TPU v7x, 32 devices: a whole 2x2x4 slice. The times are simulated.
32 devices in a mesh: seq: 4 (over z), fsdp: 8 (over y, x, core).
Axes of the slice: x: 2, y: 2, z: 4, core: 2. Of those that a mesh axis runs over, the one named last changes fastest.
Arguments:
- inputs: bfloat16 [16, 1024, 1024], P('fsdp', 'seq'), may hold values from -6 to 6
- lengths: int32 [16], P('fsdp'), may hold values from 1 to 1024, 12288 in all
- cotangent: bfloat16 [16, 1024, 1024], P('fsdp', 'seq'), may hold values from -6 to 6
- query_weight: bfloat16 [1024, 1024], P('fsdp'), may hold values from -0.046875 to 0.046875
- key_weight: bfloat16 [1024, 1024], P('fsdp'), may hold values from -0.1875 to 0.1875
- value_weight: bfloat16 [1024, 1024], P('fsdp'), may hold values from -0.1875 to 0.1875
- output_weight: bfloat16 [1024, 1024], P('fsdp'), may hold values from -0.75 to 0.75
- up_weight: bfloat16 [4096, 1024], P('fsdp'), may hold values from -0.1875 to 0.1875
- down_weight: bfloat16 [4096, 1024], P('fsdp'), may hold values from -0.125 to 0.125
- attn_gain: float32 [1024], replicated, may hold values from 0.25 to 1.75
- ffn_gain: float32 [1024], replicated, may hold values from 0.25 to 1.75
- bias_table: float32 [32, 16], replicated, may hold values from -4 to 4
Outputs:
- layer_out: bfloat16 [16, 1024, 1024], P('fsdp', 'seq')
- input_grad: float32 [16, 1024, 1024], P('fsdp', 'seq')
- query_grad: float32 [1024, 1024], P(('seq', 'fsdp'))
- key_grad: float32 [1024, 1024], P(('seq', 'fsdp'))
- value_grad: float32 [1024, 1024], P(('seq', 'fsdp'))
- output_grad: float32 [1024, 1024], P(('seq', 'fsdp'))
- up_grad: float32 [4096, 1024], P(('seq', 'fsdp'))
- down_grad: float32 [4096, 1024], P(('seq', 'fsdp'))
- attn_gain_grad: float32 [1024], P('fsdp')
- ffn_gain_grad: float32 [1024], P('fsdp')
- bias_grad: float32 [32, 16], P('fsdp')
Inputs may be any that keep to these rules, and one draw needn't show every extreme that they name: lengths of the sequences; the longest is exactly 1024, and all of them sum to 12288.
All inputs are finite; a program needn't handle non-finite values. No bound on the sum of `lengths` on one device may be relied on, other than what follows from the above.
Results may differ from a plain program's by a relative error of at most 0.014.
The roundings to bfloat16 on the way count: a program that leaves them out, or rounds other values in their place, can miss the bound.
Values may be sent and summed in bfloat16 or wider, within the bound.
A program may use at most 256 MiB of HBM per device.

v0:
```python
import jax
import jax.numpy as jnp
from jax import lax
from jax.sharding import PartitionSpec as P

HEADS = 16
HEAD_DIM = 64
BUCKETS = 32


NEGATIVE = -1000000000.0
EPSILON = 1e-06
THRESHOLDS = (1, 2, 3, 4, 5, 6, 7, 8, 12, 16, 23, 32, 46, 64, 91)
ROOT_HALF = 0.7071067811865476
NORMAL_PEAK = 0.3989422804014327


def bucket_of(relative):
    distance = jnp.abs(relative)
    magnitude = jnp.zeros(relative.shape, jnp.int32)
    for threshold in THRESHOLDS:
        magnitude = magnitude + (distance >= threshold).astype(jnp.int32)
    return magnitude + jnp.where(relative > 0, BUCKETS // 2, 0).astype(jnp.int32)


def gelu_exact(value):
    return 0.5 * value * (1.0 + lax.erf(value * ROOT_HALF))


def gelu_slope(value):
    return (
        0.5 * (1.0 + lax.erf(value * ROOT_HALF))
        + value * jnp.exp(-0.5 * value * value) * NORMAL_PEAK
    )


def against(matrix, operand):
    return lax.dot_general(
        matrix, operand, (((1,), (1,)), ((), ())), preferred_element_type=jnp.float32
    )


def across(matrix, operand):
    return lax.dot_general(
        matrix, operand, (((0,), (0,)), ((), ())), preferred_element_type=jnp.float32
    )


def bias_block(query_start, block_rows, key_total, table_cols):
    query_ids = query_start + jnp.arange(block_rows, dtype=jnp.int32)
    key_ids = jnp.arange(key_total, dtype=jnp.int32)
    buckets = bucket_of(key_ids[None, :] - query_ids[:, None])
    local_heads = table_cols.shape[1]
    bias = jnp.zeros((local_heads, block_rows, key_total), jnp.float32)
    for number in range(BUCKETS):
        bias = jnp.where((buckets == number)[None, :, :], table_cols[number][:, None, None], bias)
    return (buckets, bias)


def shards(
    inputs,
    lengths,
    cotangent,
    query_weight,
    key_weight,
    value_weight,
    output_weight,
    up_weight,
    down_weight,
    attn_gain,
    ffn_gain,
    bias_table,
):
    seq_count, span, width = inputs.shape
    groups = lax.axis_size("seq")
    rank = lax.axis_index("seq")
    row_count = seq_count * span
    key_total = span * groups
    inner = HEADS * HEAD_DIM
    local_heads = HEADS // groups
    block_rows = min(512, key_total)
    block_count = key_total // block_rows
    slot_ids = rank * span + jnp.arange(span, dtype=jnp.int32)
    mask_rows = (slot_ids[None, :] < lengths[:, None]).reshape(row_count, 1).astype(jnp.float32)
    source = inputs.reshape(row_count, width).astype(jnp.float32)
    rms_one = lax.rsqrt(jnp.mean(source * source, axis=1, keepdims=True) + EPSILON)
    scaled_one = source * rms_one
    normed_one = (scaled_one * attn_gain).astype(jnp.bfloat16)
    pieces = (
        lax.all_gather(query_weight, "fsdp", axis=0, tiled=True),
        lax.all_gather(key_weight, "fsdp", axis=0, tiled=True),
        lax.all_gather(value_weight, "fsdp", axis=0, tiled=True),
    )
    projected = tuple((against(normed_one, weight_piece) for weight_piece in pieces))
    stacked = jnp.stack([member.astype(jnp.bfloat16) for member in projected]).reshape(
        3, seq_count, span, inner
    )
    by_heads = lax.all_to_all(stacked, "seq", split_axis=3, concat_axis=2, tiled=True)
    by_heads = by_heads.reshape(3, seq_count, key_total, local_heads, HEAD_DIM).transpose(
        0, 1, 3, 2, 4
    )
    head_query, head_key, head_value = (by_heads[0], by_heads[1], by_heads[2])
    table_cols = lax.dynamic_slice_in_dim(bias_table, rank * local_heads, local_heads, 1)
    key_range = jnp.arange(key_total, dtype=jnp.int32)

    def scores_of(sequence, query_start):
        queries = lax.dynamic_slice_in_dim(head_query[sequence], query_start, block_rows, 1)
        buckets, offset_bias = bias_block(query_start, block_rows, key_total, table_cols)
        logits = jnp.einsum(
            "hqd,hkd->hqk", queries, head_key[sequence], preferred_element_type=jnp.float32
        )
        logits = logits + offset_bias
        live_keys = key_range < lengths[sequence]
        masked = jnp.where(live_keys[None, None, :], logits, NEGATIVE)
        return (queries, buckets, masked)

    def forward_block(block_index):
        sequence = block_index // block_count
        query_start = block_index % block_count * block_rows
        queries, buckets, masked = scores_of(sequence, query_start)
        row_peak = jnp.max(masked, axis=2, keepdims=True)
        exponent = jnp.exp(masked - row_peak)
        row_total = jnp.sum(exponent, axis=2, keepdims=True)
        weights_low = (exponent / row_total).astype(jnp.bfloat16)
        context_block = jnp.einsum(
            "hqk,hkd->hqd", weights_low, head_value[sequence], preferred_element_type=jnp.float32
        )
        return (context_block.astype(jnp.bfloat16), (row_peak + jnp.log(row_total))[:, :, 0])

    context_blocks, log_totals = lax.map(
        forward_block, jnp.arange(seq_count * block_count, dtype=jnp.int32)
    )
    log_totals = log_totals.reshape(seq_count, block_count, local_heads, block_rows)
    context_heads = context_blocks.reshape(
        seq_count, block_count, local_heads, block_rows, HEAD_DIM
    )
    context_heads = context_heads.transpose(0, 1, 3, 2, 4).reshape(
        seq_count, key_total, local_heads * HEAD_DIM
    )
    context = lax.all_to_all(context_heads, "seq", split_axis=1, concat_axis=2, tiled=True).reshape(
        row_count, inner
    )
    blank_wide = jnp.zeros((row_count, width), jnp.float32)
    selected = context
    attended = jnp.dot(
        selected,
        lax.all_gather(output_weight, "fsdp", axis=0, tiled=True),
        preferred_element_type=jnp.float32,
    )
    hidden_one = source + attended
    rms_two = lax.rsqrt(jnp.mean(hidden_one * hidden_one, axis=1, keepdims=True) + EPSILON)
    scaled_two = hidden_one * rms_two
    normed_two = (scaled_two * ffn_gain).astype(jnp.bfloat16)
    up_piece = lax.all_gather(up_weight, "fsdp", axis=0, tiled=True)
    down_piece = lax.all_gather(down_weight, "fsdp", axis=0, tiled=True)
    active = gelu_exact(against(normed_two, up_piece)).astype(jnp.bfloat16)
    mlp_out = jnp.dot(active, down_piece, preferred_element_type=jnp.float32)
    layer_out = (
        ((hidden_one + mlp_out) * mask_rows).reshape(seq_count, span, width).astype(jnp.bfloat16)
    )
    grad_out = cotangent.reshape(row_count, width).astype(jnp.float32) * mask_rows
    grad_low = grad_out.astype(jnp.bfloat16)
    up_piece = lax.all_gather(up_weight, "fsdp", axis=0, tiled=True)
    down_piece = lax.all_gather(down_weight, "fsdp", axis=0, tiled=True)
    before = against(normed_two, up_piece)
    active = gelu_exact(before).astype(jnp.bfloat16)
    pre_grad = (against(grad_low, down_piece) * gelu_slope(before)).astype(jnp.bfloat16)
    normed_grad = jnp.dot(pre_grad, up_piece, preferred_element_type=jnp.float32)
    ffn_grads = lax.psum_scatter(
        jnp.concatenate([across(pre_grad, normed_two), across(active, grad_low)], axis=1),
        ("seq", "fsdp"),
        scatter_dimension=0,
        tiled=True,
    )
    gained_two = ffn_gain * normed_grad
    hidden_grad = grad_out + rms_two * (
        gained_two - scaled_two * jnp.mean(gained_two * scaled_two, axis=1, keepdims=True)
    )
    ffn_gain_part = jnp.sum(normed_grad * scaled_two, axis=0)
    hidden_low = hidden_grad.astype(jnp.bfloat16)
    context_grad = against(
        hidden_low, lax.all_gather(output_weight, "fsdp", axis=0, tiled=True)
    ).astype(jnp.bfloat16)
    heads_grad = lax.all_to_all(
        context_grad.reshape(seq_count, span, inner), "seq", split_axis=2, concat_axis=1, tiled=True
    )
    heads_grad = heads_grad.reshape(seq_count, key_total, local_heads, HEAD_DIM).transpose(
        0, 2, 1, 3
    )

    def backward_sequence(sequence):

        def step(carry, block_number):
            key_acc, value_acc, bias_acc = carry
            query_start = block_number * block_rows
            queries, buckets, masked = scores_of(sequence, query_start)
            probs = jnp.exp(masked - log_totals[sequence, block_number][:, :, None])
            probs_low = probs.astype(jnp.bfloat16)
            out_block = lax.dynamic_slice_in_dim(heads_grad[sequence], query_start, block_rows, 1)
            prob_grad = jnp.einsum(
                "hqd,hkd->hqk", out_block, head_value[sequence], preferred_element_type=jnp.float32
            )
            value_acc = value_acc + jnp.einsum(
                "hqk,hqd->hkd", probs_low, out_block, preferred_element_type=jnp.float32
            )
            inner_sum = jnp.sum(probs * prob_grad, axis=2, keepdims=True)
            score_grad = (probs * (prob_grad - inner_sum)).astype(jnp.bfloat16)
            query_block = jnp.einsum(
                "hqk,hkd->hqd", score_grad, head_key[sequence], preferred_element_type=jnp.float32
            )
            key_acc = key_acc + jnp.einsum(
                "hqk,hqd->hkd", score_grad, queries, preferred_element_type=jnp.float32
            )
            score_wide = score_grad.astype(jnp.float32)
            bucket_sums = jnp.stack(
                [
                    jnp.sum(
                        jnp.where((buckets == number)[None, :, :], score_wide, 0.0), axis=(1, 2)
                    )
                    for number in range(BUCKETS)
                ],
                axis=1,
            )
            bias_acc = bias_acc + bucket_sums
            return ((key_acc, value_acc, bias_acc), query_block.astype(jnp.bfloat16))

        start_state = (
            jnp.zeros((local_heads, key_total, HEAD_DIM), jnp.float32),
            jnp.zeros((local_heads, key_total, HEAD_DIM), jnp.float32),
            jnp.zeros((local_heads, BUCKETS), jnp.float32),
        )
        final_state, query_blocks = lax.scan(
            step, start_state, jnp.arange(block_count, dtype=jnp.int32)
        )
        key_acc, value_acc, bias_acc = final_state
        query_slots = query_blocks.transpose(0, 2, 1, 3).reshape(key_total, local_heads * HEAD_DIM)
        return (
            query_slots,
            key_acc.astype(jnp.bfloat16)
            .transpose(1, 0, 2)
            .reshape(key_total, local_heads * HEAD_DIM),
            value_acc.astype(jnp.bfloat16)
            .transpose(1, 0, 2)
            .reshape(key_total, local_heads * HEAD_DIM),
            bias_acc,
        )

    query_heads, key_heads, value_heads, bias_parts = lax.map(
        backward_sequence, jnp.arange(seq_count, dtype=jnp.int32)
    )
    grad_stack = jnp.stack([query_heads, key_heads, value_heads])
    slot_grads = lax.all_to_all(grad_stack, "seq", split_axis=2, concat_axis=3, tiled=True).reshape(
        3, row_count, inner
    )
    query_low, key_low, value_low = (slot_grads[0], slot_grads[1], slot_grads[2])
    carry = blank_wide
    pieces = (
        lax.all_gather(query_weight, "fsdp", axis=0, tiled=True),
        lax.all_gather(key_weight, "fsdp", axis=0, tiled=True),
        lax.all_gather(value_weight, "fsdp", axis=0, tiled=True),
    )
    for source_grad, weight_piece in zip((query_low, key_low, value_low), pieces):
        selected = source_grad
        carry = carry + jnp.dot(selected, weight_piece, preferred_element_type=jnp.float32)
    columns = [across(source_grad, normed_one) for source_grad in (query_low, key_low, value_low)]
    columns.append(across(context, hidden_low))
    attention_grads = lax.psum_scatter(
        jnp.concatenate(columns, axis=1), ("seq", "fsdp"), scatter_dimension=0, tiled=True
    )
    gained_one = attn_gain * carry
    input_grad = hidden_grad + rms_one * (
        gained_one - scaled_one * jnp.mean(gained_one * scaled_one, axis=1, keepdims=True)
    )
    attn_gain_part = jnp.sum(carry * scaled_one, axis=0)
    bias_local = jnp.sum(bias_parts, axis=0).T
    bias_full = lax.dynamic_update_slice_in_dim(
        jnp.zeros((BUCKETS, HEADS), jnp.float32), bias_local, rank * local_heads, 1
    )
    attn_gain_sum, ffn_gain_sum, bias_sum = lax.psum(
        (attn_gain_part, ffn_gain_part, bias_full), ("seq", "fsdp")
    )
    owner = lax.axis_index("fsdp")
    owners = lax.axis_size("fsdp")
    gain_rows = width // owners
    bucket_rows = BUCKETS // owners
    attn_gain_grad = lax.dynamic_slice_in_dim(attn_gain_sum, owner * gain_rows, gain_rows, 0)
    ffn_gain_grad = lax.dynamic_slice_in_dim(ffn_gain_sum, owner * gain_rows, gain_rows, 0)
    bias_grad = lax.dynamic_slice_in_dim(bias_sum, owner * bucket_rows, bucket_rows, 0)
    return (
        layer_out,
        input_grad.reshape(seq_count, span, width),
        attention_grads[:, :width],
        attention_grads[:, width : 2 * width],
        attention_grads[:, 2 * width : 3 * width],
        attention_grads[:, 3 * width :],
        ffn_grads[:, :width],
        ffn_grads[:, width:],
        attn_gain_grad,
        ffn_gain_grad,
        bias_grad,
    )


def solution(mesh):
    placed = (
        P("fsdp", "seq", None),
        P("fsdp"),
        P("fsdp", "seq", None),
        P("fsdp", None),
        P("fsdp", None),
        P("fsdp", None),
        P("fsdp", None),
        P("fsdp", None),
        P("fsdp", None),
        P(),
        P(),
        P(),
    )
    return jax.shard_map(
        shards,
        mesh=mesh,
        in_specs=placed,
        out_specs=(
            P("fsdp", "seq", None),
            P("fsdp", "seq", None),
            P(("seq", "fsdp"), None),
            P(("seq", "fsdp"), None),
            P(("seq", "fsdp"), None),
            P(("seq", "fsdp"), None),
            P(("seq", "fsdp"), None),
            P(("seq", "fsdp"), None),
            P("fsdp"),
            P("fsdp"),
            P("fsdp", None),
        ),
        check_vma=False,
    )
```

profile of v0, /device:TPU:0, one launch (start us, length us, event | category | flops | bytes accessed | tf_op | source)
XLA Modules:
  0.0 1770.3 jit_solution(14791990930558064336)
XLA Ops:
  11.8 28.8 %all-gather.11.cloned.1.call-done = bf16[1024,1024]{1,0:T(8,128)(2,1)} async-done(((bf16[128,1024]{1,0:T(8,128)(2,1)}), bf16[1024,1024]{1,0:T(8,128)(2,1)}) %all-gather.11.cloned.1.call-update) | async-done | bytes 2097168 | tf_op jit(solution)/shard_map/all_gather | solution.py:92
  46.9 23.4 %all-gather.9.cloned.1.call-done = bf16[1024,1024]{1,0:T(8,128)(2,1)} async-done(((bf16[128,1024]{1,0:T(8,128)(2,1)}), bf16[1024,1024]{1,0:T(8,128)(2,1)}) %all-gather.9.cloned.1.call-update) | async-done | bytes 2097168 | tf_op jit(solution)/shard_map/all_gather | solution.py:91
  76.7 23.5 %all-gather.7.cloned.1.call-done = bf16[1024,1024]{1,0:T(8,128)(2,1)} async-done(((bf16[128,1024]{1,0:T(8,128)(2,1)}), bf16[1024,1024]{1,0:T(8,128)(2,1)}) %all-gather.7.cloned.1.call-update) | async-done | bytes 2097168 | tf_op jit(solution)/shard_map/all_gather | solution.py:90
  108.0 7.0 pad_maximum_fusion.2
  120.4 70.7 %all-to-all-done = bf16[3,2,256,1024]{2,1,0,3:T(2,128)(2,1)} async-done(((bf16[3,2,256,1024]{2,1,0,3:T(2,128)(2,1)}), bf16[3,2,256,1024]{2,1,0,3:T(2,128)(2,1)}, u32[]{:S(2)}, u32[]{:S(2)}) %all-to-all-start) | async-done | bytes 3145760 | tf_op jit(solution)/shard_map/all_to_all | solution.py:98
  197.2 6.1 reshape.1608
  207.0 260.2 %while.77 = (s32[]{:T(128)}, bf16[4,4,512,64]{2,3,1,0:T(8,128)(2,1)}, f32[4,4,512]{2,1,0:T(4,128)}, s32[4]{0:T(128)S(1)}, s32[2]{0:T(128)}, /*index=5*/bf16[2,4,...) while((s32[]{:T(128)}, ...), condition=%wide.region_4.5_spmd.clone, body=%wide.region_1.4_spmd.clone.sunk | while | flops 663354880 | bytes 93921296 | solution.py:130
  221.4 15.6 broadcast_compare_fusion.68
  239.6 31.3 %fusion.196 = (f32[4,512]{1,0:T(4,128)S(1)}, f32[4,512,1024]{2,1,0:T(8,128)}) fusion(f32[4]{0:T(128)S(1)} %get-tuple-element.1487, pred[512,1024]{1,0:T(8,128)(4,1)} %get-tuple-element.1488, f32[4]{0:T(128)S(1)} %get-tuple-element.1489, pred[512,1024]{1,0:T(8,128)(4,1)} %get-tuple-element.1490, f32[4]{0:T(128)S(1)} %get-tuple-element.1491, ...), kind=kOutput, calls=%fused_computation.350.clone.1 | convolution fusion | flops 341833728 | bytes 25961996 | tf_op jit(solution)/shard_map/while/body/eval_jaxpr/hqd,hkd->hqk/dot_general | solution.py:109
  283.5 15.6 broadcast_compare_fusion.68
  301.8 31.1 %fusion.196 = (f32[4,512]{1,0:T(4,128)S(1)}, f32[4,512,1024]{2,1,0:T(8,128)}) fusion(f32[4]{0:T(128)S(1)} %get-tuple-element.1487, pred[512,1024]{1,0:T(8,128)(4,1)} %get-tuple-element.1488, f32[4]{0:T(128)S(1)} %get-tuple-element.1489, pred[512,1024]{1,0:T(8,128)(4,1)} %get-tuple-element.1490, f32[4]{0:T(128)S(1)} %get-tuple-element.1491, ...), kind=kOutput, calls=%fused_computation.350.clone.1 | convolution fusion | flops 341833728 | bytes 25961996 | tf_op jit(solution)/shard_map/while/body/eval_jaxpr/hqd,hkd->hqk/dot_general | solution.py:109
  345.5 15.6 broadcast_compare_fusion.68
  363.8 31.1 %fusion.196 = (f32[4,512]{1,0:T(4,128)S(1)}, f32[4,512,1024]{2,1,0:T(8,128)}) fusion(f32[4]{0:T(128)S(1)} %get-tuple-element.1487, pred[512,1024]{1,0:T(8,128)(4,1)} %get-tuple-element.1488, f32[4]{0:T(128)S(1)} %get-tuple-element.1489, pred[512,1024]{1,0:T(8,128)(4,1)} %get-tuple-element.1490, f32[4]{0:T(128)S(1)} %get-tuple-element.1491, ...), kind=kOutput, calls=%fused_computation.350.clone.1 | convolution fusion | flops 341833728 | bytes 25961996 | tf_op jit(solution)/shard_map/while/body/eval_jaxpr/hqd,hkd->hqk/dot_general | solution.py:109
  407.6 15.6 broadcast_compare_fusion.68
  425.8 31.1 %fusion.196 = (f32[4,512]{1,0:T(4,128)S(1)}, f32[4,512,1024]{2,1,0:T(8,128)}) fusion(f32[4]{0:T(128)S(1)} %get-tuple-element.1487, pred[512,1024]{1,0:T(8,128)(4,1)} %get-tuple-element.1488, f32[4]{0:T(128)S(1)} %get-tuple-element.1489, pred[512,1024]{1,0:T(8,128)(4,1)} %get-tuple-element.1490, f32[4]{0:T(128)S(1)} %get-tuple-element.1491, ...), kind=kOutput, calls=%fused_computation.350.clone.1 | convolution fusion | flops 341833728 | bytes 25961996 | tf_op jit(solution)/shard_map/while/body/eval_jaxpr/hqd,hkd->hqk/dot_general | solution.py:109
  480.3 23.7 %all-to-all-done.1 = bf16[2,1024,256]{2,0,1:T(2,128)(2,1)S(1)} async-done(((bf16[2,1024,256]{2,0,1:T(2,128)(2,1)}), bf16[2,1024,256]{2,0,1:T(2,128)(2,1)S(1)}, u32[]{:S(2)}, u32[]{:S(2)}) %all-to-all-start.1) | async-done | bytes 1048608 | tf_op jit(solution)/shard_map/all_to_all | solution.py:140
  509.7 10.9 multiply_convert_fusion.1
  520.6 10.7 fusion.111
  545.3 25.2 %all-to-all-done.2 = bf16[2,256,1024]{1,0,2:T(2,128)(2,1)S(1)} async-done(((bf16[2,256,1024]{1,0,2:T(2,128)(2,1)}), bf16[2,256,1024]{1,0,2:T(2,128)(2,1)S(1)}, u32[]{:S(2)}, u32[]{:S(2)}) %all-to-all-start.2) | async-done | bytes 1048608 | tf_op jit(solution)/shard_map/all_to_all | solution.py:184
  573.4 522.1 %while.79 = (s32[]{:T(128)}, bf16[2,1024,256]{1,2,0:T(8,128)(2,1)}, bf16[2,1024,256]{1,2,0:T(8,128)(2,1)}, bf16[2,1024,256]{1,2,0:T(8,128)(2,1)}, f32[2,4,32]{2,...) while((s32[]{:T(128)}, bf16[2,1024,256]{1,2,0:T(8,128)(2,1)}, ...), condition=%wide.region_43.44_spmd.clone, body=%wide.region_7.43_spmd.clone.sunk | while | flops 1610743552 | bytes 302853312 | solution.py:248
  581.8 247.3 %while.80 = (s32[]{:T(128)}, f32[4,1024,64]{1,2,0:T(8,128)S(1)}, f32[4,1024,64]{1,2,0:T(8,128)}, f32[4,32]{1,0:T(4,128)S(1)}, bf16[2,4,512,64]{2,3,1,0:T(8,128)(...) while((s32[]{:T(128)}, f32[4,1024,64]{1,2,0:T(8,128)S(1)}, ...), condition=%wide.region_42.42_spmd.clone, body=%wide.region_8.41_spmd.clone.sunk | while | flops 1610219264 | bytes 271378944 | solution.py:232
  583.0 15.7 broadcast_compare_fusion.69
  607.7 33.1 %multiply_reduce_fusion.5 = (f32[4,512]{1,0:T(4,128)S(1)}, f32[4,512,1024]{2,1,0:T(8,128)S(1)}) fusion(f32[4,512,1024]{2,1,0:T(8,128)} %fusion.207, f32[4,512]{1,0:T(4,128)S(1)} %dynamic-slice_bitcast_fusion.2, f32[4]{0:T(128)S(1)} %get-tuple-element.1607, pred[512,1024]{1,0:T(8,128)(4,1)} %get-tuple-element.1608, f32[4]{0:T(128)S(1)} %get-tuple-element.1609, ...), kind=kOutput, calls=%fused_computation.169.clone.1 | convolution fusion | flops 346028032 | bytes 34359300 | tf_op jit(solution)/shard_map/while/body/eval_jaxpr/while/body/eval_jaxpr/hqd,hkd->hqk/dot_general | solution.py:109
  640.9 30.7 %fusion.208 = (f32[4]{0:T(128)S(1)}, f32[4]{0:T(128)S(1)}, f32[4]{0:T(128)S(1)}, f32[4]{0:T(128)S(1)}, f32[4]{0:T(128)S(1)}, /*index=5*/f32[4]{0:T(128)S(1)}, f3...) fusion(pred[512,1024]{1,0:T(8,128)(4,1)} %get-tuple-element.158, ...), kind=kLoop, calls=%fused_computation.167.clone.1 | loop fusion | flops 83886016 | bytes 30417184 | tf_op jit(solution)/shard_map/while/body/eval_jaxpr/while/body/eval_jaxpr/reduce_sum | solution.py:217
  680.8 17.0 fusion.210
  706.5 15.7 broadcast_compare_fusion.69
  731.2 33.1 %multiply_reduce_fusion.5 = (f32[4,512]{1,0:T(4,128)S(1)}, f32[4,512,1024]{2,1,0:T(8,128)S(1)}) fusion(f32[4,512,1024]{2,1,0:T(8,128)} %fusion.207, f32[4,512]{1,0:T(4,128)S(1)} %dynamic-slice_bitcast_fusion.2, f32[4]{0:T(128)S(1)} %get-tuple-element.1607, pred[512,1024]{1,0:T(8,128)(4,1)} %get-tuple-element.1608, f32[4]{0:T(128)S(1)} %get-tuple-element.1609, ...), kind=kOutput, calls=%fused_computation.169.clone.1 | convolution fusion | flops 346028032 | bytes 34359300 | tf_op jit(solution)/shard_map/while/body/eval_jaxpr/while/body/eval_jaxpr/hqd,hkd->hqk/dot_general | solution.py:109
  764.4 30.7 %fusion.208 = (f32[4]{0:T(128)S(1)}, f32[4]{0:T(128)S(1)}, f32[4]{0:T(128)S(1)}, f32[4]{0:T(128)S(1)}, f32[4]{0:T(128)S(1)}, /*index=5*/f32[4]{0:T(128)S(1)}, f3...) fusion(pred[512,1024]{1,0:T(8,128)(4,1)} %get-tuple-element.158, ...), kind=kLoop, calls=%fused_computation.167.clone.1 | loop fusion | flops 83886016 | bytes 30417184 | tf_op jit(solution)/shard_map/while/body/eval_jaxpr/while/body/eval_jaxpr/reduce_sum | solution.py:217
  804.6 17.0 fusion.210
  842.5 247.3 %while.80 = (s32[]{:T(128)}, f32[4,1024,64]{1,2,0:T(8,128)S(1)}, f32[4,1024,64]{1,2,0:T(8,128)}, f32[4,32]{1,0:T(4,128)S(1)}, bf16[2,4,512,64]{2,3,1,0:T(8,128)(...) while((s32[]{:T(128)}, f32[4,1024,64]{1,2,0:T(8,128)S(1)}, ...), condition=%wide.region_42.42_spmd.clone, body=%wide.region_8.41_spmd.clone.sunk | while | flops 1610219264 | bytes 271378944 | solution.py:232
  843.7 15.7 broadcast_compare_fusion.69
  868.4 33.1 %multiply_reduce_fusion.5 = (f32[4,512]{1,0:T(4,128)S(1)}, f32[4,512,1024]{2,1,0:T(8,128)S(1)}) fusion(f32[4,512,1024]{2,1,0:T(8,128)} %fusion.207, f32[4,512]{1,0:T(4,128)S(1)} %dynamic-slice_bitcast_fusion.2, f32[4]{0:T(128)S(1)} %get-tuple-element.1607, pred[512,1024]{1,0:T(8,128)(4,1)} %get-tuple-element.1608, f32[4]{0:T(128)S(1)} %get-tuple-element.1609, ...), kind=kOutput, calls=%fused_computation.169.clone.1 | convolution fusion | flops 346028032 | bytes 34359300 | tf_op jit(solution)/shard_map/while/body/eval_jaxpr/while/body/eval_jaxpr/hqd,hkd->hqk/dot_general | solution.py:109
  901.6 30.7 %fusion.208 = (f32[4]{0:T(128)S(1)}, f32[4]{0:T(128)S(1)}, f32[4]{0:T(128)S(1)}, f32[4]{0:T(128)S(1)}, f32[4]{0:T(128)S(1)}, /*index=5*/f32[4]{0:T(128)S(1)}, f3...) fusion(pred[512,1024]{1,0:T(8,128)(4,1)} %get-tuple-element.158, ...), kind=kLoop, calls=%fused_computation.167.clone.1 | loop fusion | flops 83886016 | bytes 30417184 | tf_op jit(solution)/shard_map/while/body/eval_jaxpr/while/body/eval_jaxpr/reduce_sum | solution.py:217
  941.6 17.0 fusion.210
  967.2 15.7 broadcast_compare_fusion.69
  992.0 33.1 %multiply_reduce_fusion.5 = (f32[4,512]{1,0:T(4,128)S(1)}, f32[4,512,1024]{2,1,0:T(8,128)S(1)}) fusion(f32[4,512,1024]{2,1,0:T(8,128)} %fusion.207, f32[4,512]{1,0:T(4,128)S(1)} %dynamic-slice_bitcast_fusion.2, f32[4]{0:T(128)S(1)} %get-tuple-element.1607, pred[512,1024]{1,0:T(8,128)(4,1)} %get-tuple-element.1608, f32[4]{0:T(128)S(1)} %get-tuple-element.1609, ...), kind=kOutput, calls=%fused_computation.169.clone.1 | convolution fusion | flops 346028032 | bytes 34359300 | tf_op jit(solution)/shard_map/while/body/eval_jaxpr/while/body/eval_jaxpr/hqd,hkd->hqk/dot_general | solution.py:109
  1025.2 30.7 %fusion.208 = (f32[4]{0:T(128)S(1)}, f32[4]{0:T(128)S(1)}, f32[4]{0:T(128)S(1)}, f32[4]{0:T(128)S(1)}, f32[4]{0:T(128)S(1)}, /*index=5*/f32[4]{0:T(128)S(1)}, f3...) fusion(pred[512,1024]{1,0:T(8,128)(4,1)} %get-tuple-element.158, ...), kind=kLoop, calls=%fused_computation.167.clone.1 | loop fusion | flops 83886016 | bytes 30417184 | tf_op jit(solution)/shard_map/while/body/eval_jaxpr/while/body/eval_jaxpr/reduce_sum | solution.py:217
  1065.4 17.0 fusion.210
  1118.2 63.8 %all-to-all-done.3 = bf16[3,2,1024,256]{3,1,0,2:T(2,128)(2,1)} async-done(((bf16[3,2,1024,256]{3,1,0,2:T(2,128)(2,1)}), bf16[3,2,1024,256]{3,1,0,2:T(2,128)(2,1)}, u32[]{:S(2)}, u32[]{:S(2)}) %all-to-all-start.3) | async-done | bytes 3145760 | tf_op jit(solution)/shard_map/all_to_all | solution.py:252
  1194.4 7.3 pad_maximum_fusion.1
  1201.7 17.5 copy.105
  1219.3 7.0 fusion.143
  1226.4 8.6 fusion.132
  1235.0 19.0 %pad_maximum_fusion = f32[4096,2048]{0,1:T(8,128)} fusion(f32[4096,1024]{0,1:T(8,128)S(1)} %fusion.143, f32[4096,1024]{0,1:T(8,128)} %fusion.132), kind=kLoop, calls=%fused_computation.287 | loop fusion | flops 8388608 | bytes 67108864 | tf_op jit(solution)/shard_map/concatenate | solution.py:170
  1254.6 10.8 multiply_convert_fusion.2
  1274.4 40.4 %all-reduce = (f32[1024]{0:T(1024)S(1)}, f32[1024]{0:T(1024)S(1)}, f32[32,16]{1,0:T(8,128)S(1)}) all-reduce(f32[1024]{0:T(1024)S(1)} %get-tuple-element.846, f32[1024]{0:T(1024)S(1)} %copy-done.65, f32[32,16]{1,0:T(8,128)S(1)} %dynamic_update_slice.56), channel_id=1, replica_groups=mesh['seq'=4,'fsdp'=8] {'seq','fsdp'}, use_global_device_ids=true, to_apply=%region_48.49 | all-reduce | flops 2560 | bytes 20480 | tf_op jit(solution)/shard_map/psum | solution.py:279
  1320.0 81.6 %reduce-scatter.7.cloned.1.call-done = f32[32,4096]{1,0:T(8,128)} async-done(((f32[1024,4096]{1,0:T(8,128)}), f32[32,4096]{1,0:T(8,128)}) %reduce-scatter.7.cloned.1.call-update) | async-done | bytes 524304
  1403.5 356.5 %reduce-scatter.5.cloned.1.call-done = f32[128,2048]{0,1:T(8,128)} async-done(((f32[4096,2048]{0,1:T(8,128)}), f32[128,2048]{0,1:T(8,128)}) %reduce-scatter.5.cloned.1.call-update) | async-done | bytes 1048592 | tf_op jit(solution)/shard_map/reduce_scatter | solution.py:169
  (647 shorter events, 301.7 us)
Async XLA Ops:
  7.2 113.1 %copy-start = (f32[32,16]{0,1:T(8,128)S(1)}, f32[32,16]{0,1:T(8,128)}, u32[]{:S(2)}) copy-start(f32[32,16]{0,1:T(8,128)} %param.29) | copy-start | bytes 6148
  7.2 33.4 %all-gather.11.cloned.1.call-start = ((), (), s32[]{:S(2)}) async-start(), calls=%async_computation.8 | async-start | bytes 2359296 | tf_op jit(solution)/shard_map/all_gather | solution.py:92
  8.0 62.4 %all-gather.9.cloned.1.call-start = ((), (), s32[]{:S(2)}) async-start(), calls=%async_computation.7 | async-start | bytes 2359296 | tf_op jit(solution)/shard_map/all_gather | solution.py:91
  8.7 91.5 %all-gather.7.cloned.1.call-start = ((), (), s32[]{:S(2)}) async-start(), calls=%async_computation.6 | async-start | bytes 2359296 | tf_op jit(solution)/shard_map/all_gather | solution.py:90
  9.4 495.6 %all-gather.13.cloned.1.call-start = ((), (), s32[]{:S(2)}) async-start(), calls=%async_computation.9 | async-start | bytes 2359296 | tf_op jit(solution)/shard_map/all_gather | solution.py:147
  10.0 499.7 %all-gather.15.cloned.1.call-start = ((), (), s32[]{:S(2)}) async-start(), calls=%async_computation.10 | async-start | bytes 9437184 | tf_op jit(solution)/shard_map/all_gather | solution.py:154
  11.5 32.9 %copy-start.53 = (f32[1,2,2,128]{3,1,2,0:T(2,128)}, f32[1,2,2,128]{3,1,2,0:T(2,128)S(1)}, u32[]{:S(2)}) copy-start(f32[1,2,2,128]{3,1,2,0:T(2,128)S(1)} %copy.112) | copy-start | bytes 6148
  11.8 58.6 %copy-start.45 = (bf16[512,1024]{1,0:T(8,128)(2,1)}, bf16[512,1024]{1,0:T(8,128)(2,1)S(1)}, u32[]{:S(2)}) copy-start(bf16[512,1024]{1,0:T(8,128)(2,1)S(1)} %fusion.118) | copy-start | bytes 3145732
  115.0 76.1 %all-to-all-start = ((bf16[3,2,256,1024]{2,1,0,3:T(2,128)(2,1)}), bf16[3,2,256,1024]{2,1,0,3:T(2,128)(2,1)}, u32[]{:S(2)}, u32[]{:S(2)}) async-start(bf16[3,2,256,1024]{2,1,0,3:T(2,128)(2,1)} %pad_maximum_fusion.2), calls=%async_computation | async-start | bytes 6291456 | tf_op jit(solution)/shard_map/all_to_all | solution.py:98
  119.7 400.9 %all-gather.17.cloned.1.call-start = ((), (), s32[]{:S(2)}) async-start(), calls=%async_computation.11 | async-start | bytes 9437184 | tf_op jit(solution)/shard_map/all_gather | solution.py:155
  474.8 29.2 %all-to-all-start.1 = ((bf16[2,1024,256]{2,0,1:T(2,128)(2,1)}), bf16[2,1024,256]{2,0,1:T(2,128)(2,1)S(1)}, u32[]{:S(2)}, u32[]{:S(2)}) async-start(bf16[2,1024,256]{2,0,1:T(2,128)(2,1)} %copy.90), calls=%async_computation.1 | async-start | bytes 2097152 | tf_op jit(solution)/shard_map/all_to_all | solution.py:140
  479.1 57.7 %copy-start.55 = (f32[1,2,2,128]{3,1,2,0:T(2,128)}, f32[1,2,2,128]{3,1,2,0:T(2,128)S(1)}, u32[]{:S(2)}) copy-start(f32[1,2,2,128]{3,1,2,0:T(2,128)S(1)} %copy.114) | copy-start | bytes 6148
  509.6 27.1 %copy-start.58 = (f32[512]{0:T(512)}, f32[512]{0:T(512)S(1)}, u32[]{:S(2)}) copy-start(f32[512]{0:T(512)S(1)} %add_rsqrt_fusion) | copy-start | bytes 6148
  509.7 10.9 copy-start.44
  520.6 10.7 copy-start.41
  520.6 10.7 copy-start.66
  541.7 28.7 %all-to-all-start.2 = ((bf16[2,256,1024]{1,0,2:T(2,128)(2,1)}), bf16[2,256,1024]{1,0,2:T(2,128)(2,1)S(1)}, u32[]{:S(2)}, u32[]{:S(2)}) async-start(bf16[2,256,1024]{1,0,2:T(2,128)(2,1)} %copy.92), calls=%async_computation.2 | async-start | bytes 2097152 | tf_op jit(solution)/shard_map/all_to_all | solution.py:184
  606.8 34.0 %slice-start = ((s8[8388608]{0:T(1024)(128)(4,1)}), s8[4194304]{0:T(1024)(128)(4,1)S(1)}, s32[]{:S(2)}) async-start(s8[8388608]{0:T(1024)(128)(4,1)} %bitcast.468), calls=%async_computation.14 | async-start | bytes 8388608 | tf_op jit(solution)/shard_map/while/body/eval_jaxpr/while
  607.7 33.2 %slice-start.1 = ((s8[8388608]{0:T(1024)(128)(4,1)}), s8[4194304]{0:T(1024)(128)(4,1)S(1)}, s32[]{:S(2)}) async-start(s8[8388608]{0:T(1024)(128)(4,1)} %bitcast.468), calls=%async_computation.15 | async-start | bytes 8388608 | tf_op jit(solution)/shard_map/while/body/eval_jaxpr/while
  607.7 33.2 %copy-start.5 = (pred[512,1024]{1,0:T(8,128)(4,1)S(1)}, pred[512,1024]{1,0:T(8,128)(4,1)}, u32[]{:S(2)}) copy-start(pred[512,1024]{1,0:T(8,128)(4,1)} %get-tuple-element.1602) | copy-start | bytes 1572868 | tf_op jit(solution)/shard_map/while/body/eval_jaxpr/while
  640.8 30.8 %copy-start.3 = (f32[4,512,1024]{2,1,0:T(8,128)}, f32[4,512,1024]{2,1,0:T(8,128)S(1)}, u32[]{:S(2)}) copy-start(f32[4,512,1024]{2,1,0:T(8,128)S(1)} %get-tuple-element.1653) | copy-start | bytes 25165828 | tf_op jit(solution)/shard_map/while/body/eval_jaxpr/while
  680.8 20.1 %copy-start.21 = (bf16[1,4,1024,64]{2,3,1,0:T(8,128)(2,1)S(1)}, bf16[1,4,1024,64]{2,3,1,0:T(8,128)(2,1)}, u32[]{:S(2)}) copy-start(bf16[1,4,1024,64]{2,3,1,0:T(8,128)(2,1)} %get-tuple-element.1740) | copy-start | bytes 1572868 | tf_op jit(solution)/shard_map/while/body/eval_jaxpr/while
  680.8 20.1 %copy-start.32 = (bf16[2,4,512,64]{2,3,1,0:T(8,128)(2,1)S(1)}, bf16[2,4,512,64]{2,3,1,0:T(8,128)(2,1)}, u32[]{:S(2)}) copy-start(bf16[2,4,512,64]{2,3,1,0:T(8,128)(2,1)} %get-tuple-element.1713) | copy-start | bytes 1572868 | tf_op jit(solution)/shard_map/while/body/eval_jaxpr/while
  730.3 34.0 %slice-start = ((s8[8388608]{0:T(1024)(128)(4,1)}), s8[4194304]{0:T(1024)(128)(4,1)S(1)}, s32[]{:S(2)}) async-start(s8[8388608]{0:T(1024)(128)(4,1)} %bitcast.468), calls=%async_computation.14 | async-start | bytes 8388608 | tf_op jit(solution)/shard_map/while/body/eval_jaxpr/while
  731.2 33.2 %slice-start.1 = ((s8[8388608]{0:T(1024)(128)(4,1)}), s8[4194304]{0:T(1024)(128)(4,1)S(1)}, s32[]{:S(2)}) async-start(s8[8388608]{0:T(1024)(128)(4,1)} %bitcast.468), calls=%async_computation.15 | async-start | bytes 8388608 | tf_op jit(solution)/shard_map/while/body/eval_jaxpr/while
  731.2 33.2 %copy-start.5 = (pred[512,1024]{1,0:T(8,128)(4,1)S(1)}, pred[512,1024]{1,0:T(8,128)(4,1)}, u32[]{:S(2)}) copy-start(pred[512,1024]{1,0:T(8,128)(4,1)} %get-tuple-element.1602) | copy-start | bytes 1572868 | tf_op jit(solution)/shard_map/while/body/eval_jaxpr/while
  764.4 30.8 %copy-start.3 = (f32[4,512,1024]{2,1,0:T(8,128)}, f32[4,512,1024]{2,1,0:T(8,128)S(1)}, u32[]{:S(2)}) copy-start(f32[4,512,1024]{2,1,0:T(8,128)S(1)} %get-tuple-element.1653) | copy-start | bytes 25165828 | tf_op jit(solution)/shard_map/while/body/eval_jaxpr/while
  795.2 8.2 copy-start.18
  804.6 20.1 %copy-start.21 = (bf16[1,4,1024,64]{2,3,1,0:T(8,128)(2,1)S(1)}, bf16[1,4,1024,64]{2,3,1,0:T(8,128)(2,1)}, u32[]{:S(2)}) copy-start(bf16[1,4,1024,64]{2,3,1,0:T(8,128)(2,1)} %get-tuple-element.1740) | copy-start | bytes 1572868 | tf_op jit(solution)/shard_map/while/body/eval_jaxpr/while
  804.6 20.1 %copy-start.32 = (bf16[2,4,512,64]{2,3,1,0:T(8,128)(2,1)S(1)}, bf16[2,4,512,64]{2,3,1,0:T(8,128)(2,1)}, u32[]{:S(2)}) copy-start(bf16[2,4,512,64]{2,3,1,0:T(8,128)(2,1)} %get-tuple-element.1713) | copy-start | bytes 1572868 | tf_op jit(solution)/shard_map/while/body/eval_jaxpr/while
  867.6 34.0 %slice-start = ((s8[8388608]{0:T(1024)(128)(4,1)}), s8[4194304]{0:T(1024)(128)(4,1)S(1)}, s32[]{:S(2)}) async-start(s8[8388608]{0:T(1024)(128)(4,1)} %bitcast.468), calls=%async_computation.14 | async-start | bytes 8388608 | tf_op jit(solution)/shard_map/while/body/eval_jaxpr/while
  868.4 33.2 %slice-start.1 = ((s8[8388608]{0:T(1024)(128)(4,1)}), s8[4194304]{0:T(1024)(128)(4,1)S(1)}, s32[]{:S(2)}) async-start(s8[8388608]{0:T(1024)(128)(4,1)} %bitcast.468), calls=%async_computation.15 | async-start | bytes 8388608 | tf_op jit(solution)/shard_map/while/body/eval_jaxpr/while
  868.4 33.2 %copy-start.5 = (pred[512,1024]{1,0:T(8,128)(4,1)S(1)}, pred[512,1024]{1,0:T(8,128)(4,1)}, u32[]{:S(2)}) copy-start(pred[512,1024]{1,0:T(8,128)(4,1)} %get-tuple-element.1602) | copy-start | bytes 1572868 | tf_op jit(solution)/shard_map/while/body/eval_jaxpr/while
  901.6 30.8 %copy-start.3 = (f32[4,512,1024]{2,1,0:T(8,128)}, f32[4,512,1024]{2,1,0:T(8,128)S(1)}, u32[]{:S(2)}) copy-start(f32[4,512,1024]{2,1,0:T(8,128)S(1)} %get-tuple-element.1653) | copy-start | bytes 25165828 | tf_op jit(solution)/shard_map/while/body/eval_jaxpr/while
  941.6 20.1 %copy-start.21 = (bf16[1,4,1024,64]{2,3,1,0:T(8,128)(2,1)S(1)}, bf16[1,4,1024,64]{2,3,1,0:T(8,128)(2,1)}, u32[]{:S(2)}) copy-start(bf16[1,4,1024,64]{2,3,1,0:T(8,128)(2,1)} %get-tuple-element.1740) | copy-start | bytes 1572868 | tf_op jit(solution)/shard_map/while/body/eval_jaxpr/while
  941.6 20.1 %copy-start.32 = (bf16[2,4,512,64]{2,3,1,0:T(8,128)(2,1)S(1)}, bf16[2,4,512,64]{2,3,1,0:T(8,128)(2,1)}, u32[]{:S(2)}) copy-start(bf16[2,4,512,64]{2,3,1,0:T(8,128)(2,1)} %get-tuple-element.1713) | copy-start | bytes 1572868 | tf_op jit(solution)/shard_map/while/body/eval_jaxpr/while
  991.1 34.0 %slice-start = ((s8[8388608]{0:T(1024)(128)(4,1)}), s8[4194304]{0:T(1024)(128)(4,1)S(1)}, s32[]{:S(2)}) async-start(s8[8388608]{0:T(1024)(128)(4,1)} %bitcast.468), calls=%async_computation.14 | async-start | bytes 8388608 | tf_op jit(solution)/shard_map/while/body/eval_jaxpr/while
  991.9 33.2 %slice-start.1 = ((s8[8388608]{0:T(1024)(128)(4,1)}), s8[4194304]{0:T(1024)(128)(4,1)S(1)}, s32[]{:S(2)}) async-start(s8[8388608]{0:T(1024)(128)(4,1)} %bitcast.468), calls=%async_computation.15 | async-start | bytes 8388608 | tf_op jit(solution)/shard_map/while/body/eval_jaxpr/while
  991.9 33.2 %copy-start.5 = (pred[512,1024]{1,0:T(8,128)(4,1)S(1)}, pred[512,1024]{1,0:T(8,128)(4,1)}, u32[]{:S(2)}) copy-start(pred[512,1024]{1,0:T(8,128)(4,1)} %get-tuple-element.1602) | copy-start | bytes 1572868 | tf_op jit(solution)/shard_map/while/body/eval_jaxpr/while
  1025.1 30.8 %copy-start.3 = (f32[4,512,1024]{2,1,0:T(8,128)}, f32[4,512,1024]{2,1,0:T(8,128)S(1)}, u32[]{:S(2)}) copy-start(f32[4,512,1024]{2,1,0:T(8,128)S(1)} %get-tuple-element.1653) | copy-start | bytes 25165828 | tf_op jit(solution)/shard_map/while/body/eval_jaxpr/while
  1055.9 8.2 copy-start.18
  1065.3 20.1 %copy-start.21 = (bf16[1,4,1024,64]{2,3,1,0:T(8,128)(2,1)S(1)}, bf16[1,4,1024,64]{2,3,1,0:T(8,128)(2,1)}, u32[]{:S(2)}) copy-start(bf16[1,4,1024,64]{2,3,1,0:T(8,128)(2,1)} %get-tuple-element.1740) | copy-start | bytes 1572868 | tf_op jit(solution)/shard_map/while/body/eval_jaxpr/while
  1065.3 20.1 %copy-start.32 = (bf16[2,4,512,64]{2,3,1,0:T(8,128)(2,1)S(1)}, bf16[2,4,512,64]{2,3,1,0:T(8,128)(2,1)}, u32[]{:S(2)}) copy-start(bf16[2,4,512,64]{2,3,1,0:T(8,128)(2,1)} %get-tuple-element.1713) | copy-start | bytes 1572868 | tf_op jit(solution)/shard_map/while/body/eval_jaxpr/while
  1107.0 75.0 %all-to-all-start.3 = ((bf16[3,2,1024,256]{3,1,0,2:T(2,128)(2,1)}), bf16[3,2,1024,256]{3,1,0,2:T(2,128)(2,1)}, u32[]{:S(2)}, u32[]{:S(2)}) async-start(bf16[3,2,1024,256]{3,1,0,2:T(2,128)(2,1)} %pad_maximum_fusion.3), calls=%async_computation.3 | async-start | bytes 6291456 | tf_op jit(solution)/shard_map/all_to_all | solution.py:252
  1111.7 289.8 %reduce-scatter.7.cloned.1.call-start = ((), (), s32[]{:S(2)}) async-start(), calls=%async_computation.13 | async-start | bytes 17301504
  1219.2 540.7 %reduce-scatter.5.cloned.1.call-start = ((), (), s32[]{:S(2)}) async-start(), calls=%async_computation.12 | async-start | bytes 34603008 | tf_op jit(solution)/shard_map/reduce_scatter | solution.py:169
  1254.6 10.8 copy-start.64
  1401.6 361.6 %copy-start.1 = (f32[32,16]{0,1:T(8,128)S(1)}, f32[32,16]{0,1:T(8,128)}, u32[]{:S(2)}) copy-start(f32[32,16]{0,1:T(8,128)} %param.29) | copy-start | bytes 6148
  (116 other events, 423.7 us)
Sparse Core Ops, SparseCore 0:
  9.9 30.5 all-gather.10
  42.5 27.8 all-gather.8
  72.3 27.8 all-gather.6
  101.9 27.8 all-gather.12
  131.6 54.3 all-gather.14
  187.8 54.3 all-gather.16
  1219.3 182.2 reduce-scatter.6
  1403.9 356.0 reduce-scatter.4
where the time goes:
time: 1780 us; the launch traced here: 1770 us
  waiting for transfers between devices  701 us (39%)
  matrix products  423 us (24%)
  other arithmetic  390 us (22%)
  local copies, waits for them, and re-layouts  147 us (8%)
  blocking collectives  40.4 us (2%)
  loops' own time  37.7 us (2%)
    reduce_scatter x1, waiting for transfers between devices, shards(): lax.psum_scatter(jnp.concatenate([across(pre_grad, normed_two), across(ac...  356 us
    dot_general x8, matrix products, scores_of(): jnp.einsum('hqd,hkd->hqk', queries, head_key[sequence], preferred_element...  257 us
    reduce_sum x8, other arithmetic, step(): jnp.sum(jnp.where((buckets == number)[None, :, :], score_wide, 0.0), axis...  191 us
    eq x8, other arithmetic, bias_block(): buckets == number  125 us
    unnamed x9, waiting for transfers between devices  85.3 us
    all_to_all x1, waiting for transfers between devices, shards(): lax.all_to_all(stacked, 'seq', split_axis=3, concat_axis=2, tiled=True)  70.7 us
    all_to_all x1, waiting for transfers between devices, shards(): lax.all_to_all(grad_stack, 'seq', split_axis=2, concat_axis=3, tiled=True)  63.8 us
    psum x1, blocking collectives, shards(): lax.psum((attn_gain_part, ffn_gain_part, bias_full), ('seq', 'fsdp'))  40.4 us
  transfers between devices with their start and end apart: 12, of which 9 were waited for; matrix products, arithmetic and copies ran while one was open for 21% of the time, Pallas kernels for 0%

commit v1 on v0

v1 whole, which is shorter than its diff:
```python
import jax
import jax.numpy as jnp
from jax import lax
from jax.experimental import pallas as pl
from jax.experimental.pallas import tpu as pltpu
from jax.sharding import PartitionSpec as P

HEADS = 16
HEAD_DIM = 64
BUCKETS = 32
NEGATIVE = -1000000000.0
EPSILON = 1e-06
THRESHOLDS = (1, 2, 3, 4, 5, 6, 7, 8, 12, 16, 23, 32, 46, 64, 91)
ROOT_HALF = 0.7071067811865476
NORMAL_PEAK = 0.3989422804014327
LANES = 128
QUERY_ROWS = 256
HALF_ROWS = QUERY_ROWS // 2
LOW = jnp.bfloat16
WIDE = jnp.float32
BOTH = ("seq", "fsdp")

NN = (((1,), (0,)), ((), ()))
NT = (((1,), (1,)), ((), ()))
TN = (((0,), (0,)), ((), ()))


def dot(left, right, dims=NN):
    return lax.dot_general(left, right, dims, preferred_element_type=WIDE)


def bucket_of(relative):
    distance = jnp.abs(relative)
    magnitude = jnp.zeros(relative.shape, jnp.int32)
    for threshold in THRESHOLDS:
        magnitude = magnitude + (distance >= threshold).astype(jnp.int32)
    return magnitude + jnp.where(relative > 0, BUCKETS // 2, 0).astype(jnp.int32)


def gelu_parts(value):
    cumulative = 0.5 * (1.0 + lax.erf(value * ROOT_HALF))
    slope = cumulative + value * jnp.exp(-0.5 * value * value) * NORMAL_PEAK
    return (value * cumulative, slope)


def near_tables(columns):
    side = jnp.arange(HALF_ROWS, dtype=jnp.int32)
    tiles = []
    for shift in (-1, 0, 1):
        buckets = bucket_of(side[None, :] - side[:, None] + HALF_ROWS * shift)
        tile = jnp.zeros((columns.shape[1],) + buckets.shape, WIDE)
        for number in range(BUCKETS):
            tile = jnp.where((buckets == number)[None], columns[number][:, None, None], tile)
        tiles.append(tile)
    flat = [jnp.broadcast_to(columns[number][:, None, None], tiles[0].shape) for number in (15, 31)]
    before, centre, after = tiles
    wide = jnp.concatenate(
        [
            jnp.concatenate([before, centre, after, flat[1]], axis=2),
            jnp.concatenate([flat[0], before, centre, after], axis=2),
        ],
        axis=1,
    )
    return (wide, jnp.swapaxes(wide, 1, 2))


def spare_lanes(length, rows):
    blocks = rows // QUERY_ROWS
    key = lax.broadcasted_iota(jnp.int32, (rows, LANES), 0)
    lane = lax.rem(lax.broadcasted_iota(jnp.int32, (rows, LANES), 1), HEAD_DIM)
    hidden = jnp.where((lane == 0) & (key >= length), NEGATIVE, 0.0)
    left = (lane >= 1) & (lane <= blocks) & (key < QUERY_ROWS * (lane - 1) - HALF_ROWS)
    start = QUERY_ROWS * (lane - 1 - blocks) + 3 * HALF_ROWS
    right = (lane > blocks) & (lane <= 2 * blocks) & (key >= start)
    return jnp.where(left | right, 1.0, hidden).astype(LOW)


def split_heads(pair, spare, out):
    low_half = lax.broadcasted_iota(jnp.int32, pair.shape, 1) < HEAD_DIM
    out[0] = jnp.where(low_half, pair, spare)
    out[1] = jnp.where(low_half, spare, pair)


def attend_kernel(
    length_ref, ends_ref, query_ref, key_ref, value_ref, near_ref, context_ref, log_ref, bias, keys, values
):
    rows = query_ref.shape[0]
    pair = pl.program_id(0)
    split_heads(key_ref[...], spare_lanes(length_ref[0], rows), keys)
    split_heads(value_ref[...], jnp.zeros((rows, LANES), LOW), values)
    near_start = rows - QUERY_ROWS - HALF_ROWS
    near_end = near_start + 2 * QUERY_ROWS
    for head in range(2):
        left, right = (ends_ref[2 * pair + head, 0], ends_ref[2 * pair + head, 1])
        bias[head, :, :near_start] = jnp.full((QUERY_ROWS, near_start), left, WIDE)
        bias[head, :, near_start:near_end] = near_ref[head]
        bias[head, :, near_end:] = jnp.full((QUERY_ROWS, bias.shape[2] - near_end), right, WIDE)
    lane = lax.broadcasted_iota(jnp.int32, (QUERY_ROWS, LANES), 1)
    ones = jnp.where(lax.rem(lane, HEAD_DIM) == 0, 1.0, 0.0).astype(LOW)

    def block(number, carry):
        start = pl.multiple_of(number * QUERY_ROWS, QUERY_ROWS)
        offset = pl.multiple_of(rows - QUERY_ROWS - number * QUERY_ROWS, LANES)
        both = query_ref[pl.ds(start, QUERY_ROWS), :]
        total = jnp.zeros((QUERY_ROWS, LANES), WIDE)
        for head in range(2):
            mine = lane < HEAD_DIM if head == 0 else lane >= HEAD_DIM
            logits = dot(jnp.where(mine, both, ones), keys[head], NT)
            logits = logits + bias[head, :, pl.ds(offset, rows)]
            peak = jnp.max(logits, axis=1, keepdims=True)
            exponent = jnp.exp(logits - peak)
            row_sum = jnp.sum(exponent, axis=1, keepdims=True)
            weights_low = (exponent * (1.0 / row_sum)).astype(LOW)
            total = total + dot(weights_low, values[head])
            logs = jnp.broadcast_to(peak + jnp.log(row_sum), (QUERY_ROWS, LANES))
            log_ref[0, head : head + 1, pl.ds(start, QUERY_ROWS)] = logs.T[0:1, :]
        context_ref[pl.ds(start, QUERY_ROWS), :] = total.astype(LOW)
        return carry

    lax.fori_loop(0, rows // QUERY_ROWS, block, 0)


def attend(length, ends, query, key, value, near):
    rows, width = query.shape
    pairs = width // LANES
    smem = pl.BlockSpec(memory_space=pltpu.SMEM)
    columns = pl.BlockSpec((rows, LANES), lambda pair: (0, pair))
    return pl.pallas_call(
        attend_kernel,
        grid=(pairs,),
        in_specs=[smem, smem, columns, columns, columns]
        + [pl.BlockSpec((2, QUERY_ROWS, 2 * QUERY_ROWS), lambda pair: (pair, 0, 0))],
        out_specs=[columns, pl.BlockSpec((1, 2, rows), lambda pair: (pair, 0, 0))],
        out_shape=[
            jax.ShapeDtypeStruct((rows, width), LOW),
            jax.ShapeDtypeStruct((pairs, 2, rows), WIDE),
        ],
        scratch_shapes=[
            pltpu.VMEM((2, QUERY_ROWS, 2 * rows - QUERY_ROWS), WIDE),
            pltpu.VMEM((2, rows, LANES), LOW),
            pltpu.VMEM((2, rows, LANES), LOW),
        ],
        compiler_params=pltpu.CompilerParams(vmem_limit_bytes=40 << 20),
        cost_estimate=pl.CostEstimate(
            flops=24 * rows * rows * width, bytes_accessed=8 * rows * width, transcendentals=2 * pairs * rows * rows
        ),
        name="attend",
    )(length, ends, query, key, value, near)


def attend_grad_kernel(
    length_ref,
    ends_ref,
    query_ref,
    key_ref,
    value_ref,
    grad_ref,
    log_ref,
    near_ref,
    query_grad_ref,
    key_grad_ref,
    value_grad_ref,
    tiles_ref,
    far_ref,
    bias,
    keys,
    values,
    padded,
    key_total,
    value_total,
):
    rows = query_ref.shape[0]
    blocks = rows // QUERY_ROWS
    pair = pl.program_id(0)
    split_heads(key_ref[...], spare_lanes(length_ref[0], rows), keys)
    split_heads(value_ref[...], jnp.zeros((rows, LANES), LOW), values)
    near_start = rows - QUERY_ROWS - HALF_ROWS
    near_end = near_start + 2 * QUERY_ROWS
    for head in range(2):
        left, right = (ends_ref[2 * pair + head, 0], ends_ref[2 * pair + head, 1])
        bias[head, :near_start, :] = jnp.full((near_start, QUERY_ROWS), left, WIDE)
        bias[head, near_start:near_end, :] = near_ref[head]
        bias[head, near_end:, :] = jnp.full((bias.shape[1] - near_end, QUERY_ROWS), right, WIDE)
        padded[head, :HALF_ROWS, :] = jnp.zeros((HALF_ROWS, QUERY_ROWS), LOW)
        padded[head, rows + HALF_ROWS :, :] = jnp.zeros((HALF_ROWS, QUERY_ROWS), LOW)
    key_total[...] = jnp.zeros_like(key_total)
    value_total[...] = jnp.zeros_like(value_total)
    tiles_ref[...] = jnp.zeros_like(tiles_ref)
    lane = lax.broadcasted_iota(jnp.int32, (QUERY_ROWS, LANES), 1)
    ones = jnp.where(lax.rem(lane, HEAD_DIM) == 0, 1.0, 0.0).astype(LOW)
    zero = jnp.zeros((), LOW)

    def block(number, carry):
        start = pl.multiple_of(number * QUERY_ROWS, QUERY_ROWS)
        offset = pl.multiple_of(rows - QUERY_ROWS - number * QUERY_ROWS, LANES)
        both = query_ref[pl.ds(start, QUERY_ROWS), :]
        grad = grad_ref[pl.ds(start, QUERY_ROWS), :]
        parts = []
        for head in range(2):
            mine = lane < HEAD_DIM if head == 0 else lane >= HEAD_DIM
            logits = dot(keys[head], jnp.where(mine, both, ones), NT)
            logits = logits + bias[head, pl.ds(offset, rows), :]
            probs = jnp.exp(logits - log_ref[0, head : head + 1, pl.ds(start, QUERY_ROWS)])
            prob_grad = dot(values[head], grad, NT)
            weighted = probs * prob_grad
            inner = jnp.sum(weighted, axis=0, keepdims=True)
            score = (weighted - probs * inner).astype(LOW)
            value_total[...] += dot(probs.astype(LOW), jnp.where(mine, grad, zero))
            key_total[...] += dot(score, jnp.where(mine, both, zero))
            padded[head, HALF_ROWS : HALF_ROWS + rows, :] = score
            part = dot(score, keys[head], TN)
            parts.append(part)
            far_ref[0, head, pl.ds(number, 1), :] = jnp.sum(part, axis=0, keepdims=True)
            close = padded[head, pl.ds(start, 2 * QUERY_ROWS), :].astype(WIDE)
            quarter = [close[HALF_ROWS * step : HALF_ROWS * (step + 1)] for step in range(4)]
            for step in range(3):
                tiles_ref[head, step] += quarter[step][:, :HALF_ROWS] + quarter[step + 1][:, HALF_ROWS:]
            corner = jnp.sum(quarter[0][:, HALF_ROWS:], axis=0, keepdims=True)
            far_ref[0, head, pl.ds(blocks + number, 1), :] = corner
            corner = jnp.sum(quarter[3][:, :HALF_ROWS], axis=0, keepdims=True)
            far_ref[0, head, pl.ds(2 * blocks + number, 1), :] = corner
        chosen = jnp.where(lane < HEAD_DIM, parts[0], parts[1])
        query_grad_ref[pl.ds(start, QUERY_ROWS), :] = chosen.astype(LOW)
        return carry

    lax.fori_loop(0, blocks, block, 0)
    key_grad_ref[...] = key_total[...].astype(LOW)
    value_grad_ref[...] = value_total[...].astype(LOW)


def attend_grad(length, ends, query, key, value, grad, logs, near):
    rows, width = query.shape
    pairs = width // LANES
    blocks = rows // QUERY_ROWS
    smem = pl.BlockSpec(memory_space=pltpu.SMEM)
    columns = pl.BlockSpec((rows, LANES), lambda pair: (0, pair))
    shape = jax.ShapeDtypeStruct
    return pl.pallas_call(
        attend_grad_kernel,
        grid=(pairs,),
        in_specs=[smem, smem, columns, columns, columns, columns]
        + [pl.BlockSpec((1, 2, rows), lambda pair: (pair, 0, 0))]
        + [pl.BlockSpec((2, 2 * QUERY_ROWS, QUERY_ROWS), lambda pair: (pair, 0, 0))],
        out_specs=[columns, columns, columns]
        + [pl.BlockSpec((2, 3, HALF_ROWS, HALF_ROWS), lambda pair: (pair, 0, 0, 0))]
        + [pl.BlockSpec((1, 2, 3 * blocks, LANES), lambda pair: (pair, 0, 0, 0))],
        out_shape=[shape((rows, width), LOW)] * 3
        + [shape((2 * pairs, 3, HALF_ROWS, HALF_ROWS), WIDE), shape((pairs, 2, 3 * blocks, LANES), WIDE)],
        scratch_shapes=[
            pltpu.VMEM((2, 2 * rows - QUERY_ROWS, QUERY_ROWS), WIDE),
            pltpu.VMEM((2, rows, LANES), LOW),
            pltpu.VMEM((2, rows, LANES), LOW),
            pltpu.VMEM((2, rows + QUERY_ROWS, QUERY_ROWS), LOW),
            pltpu.VMEM((rows, LANES), WIDE),
            pltpu.VMEM((rows, LANES), WIDE),
        ],
        compiler_params=pltpu.CompilerParams(vmem_limit_bytes=48 << 20),
        cost_estimate=pl.CostEstimate(
            flops=44 * rows * rows * width, bytes_accessed=14 * rows * width, transcendentals=2 * pairs * rows * rows
        ),
        name="attend_grad",
    )(length, ends, query, key, value, grad, logs, near)


def bucket_sums(tiles, far):
    heads = tiles.shape[0]
    pairs = far.shape[0]
    blocks = far.shape[2] // 3
    side = jnp.arange(HALF_ROWS, dtype=jnp.int32)
    relative = jnp.stack([side[:, None] - side[None, :] + HALF_ROWS * shift for shift in (-1, 0, 1)])
    buckets = bucket_of(relative)
    sums = jnp.stack(
        [jnp.sum(jnp.where((buckets == number)[None], tiles, 0.0), axis=(1, 2, 3)) for number in range(BUCKETS)]
    )
    corners = jnp.sum(far.reshape(pairs, 2, 3, blocks, LANES)[:, :, 1:], axis=(3, 4))
    left, right = (corners[:, :, 0], corners[:, :, 1])
    for number in range(blocks):
        spare = [far[:, head, number, HEAD_DIM * (1 - head) + 1 :] for head in range(2)]
        left = left + jnp.stack([one[:, number] for one in spare], axis=1)
        right = right + jnp.stack([one[:, blocks + number] for one in spare], axis=1)
    ends = jnp.zeros((BUCKETS, heads), WIDE)
    ends = ends.at[BUCKETS // 2 - 1].set(left.reshape(heads)).at[BUCKETS - 1].set(right.reshape(heads))
    return sums + ends


def flip(value, bit):
    size = lax.axis_size("fsdp")
    return lax.ppermute(value, "fsdp", [(one, one ^ bit) for one in range(size)])


def other_core(value):
    return flip(value, 1)


def after(value, *first):
    return lax.optimization_barrier((value,) + first)[0]


def rounds_of(inverse):
    depth, size = (lax.axis_size("seq"), lax.axis_size("fsdp"))
    held = depth // 2
    rounds = []
    for step in range(held):
        pairs = []
        for place in range(depth):
            for index in range(size):
                target = (index % 2) * held + (place + step) % held
                there = target * size + index - index % 2 + place // held
                here = place * size + index
                pairs.append((there, here) if inverse else (here, there))
        rounds.append(pairs)
    return rounds


def to_sequence(blocks):
    held, span, width = blocks.shape
    place = lax.axis_index("seq")
    out = jnp.zeros((held, span, width), blocks.dtype)
    for step, pairs in enumerate(rounds_of(False)):
        sent = lax.dynamic_index_in_dim(blocks, (place + step) % held, 0, keepdims=False)
        got = lax.ppermute(sent, BOTH, pairs)
        out = lax.dynamic_update_index_in_dim(out, got, (place + held - step) % held, 0)
    return out.reshape(held * span, width)


def to_slots(rows, held):
    span, width = (rows.shape[0] // held, rows.shape[1])
    place = lax.axis_index("seq")
    blocks = rows.reshape(held, span, width)
    out = jnp.zeros(blocks.shape, rows.dtype)
    for step, pairs in enumerate(rounds_of(True)):
        sent = lax.dynamic_index_in_dim(blocks, (place + held - step) % held, 0, keepdims=False)
        got = lax.ppermute(sent, BOTH, pairs)
        out = lax.dynamic_update_index_in_dim(out, got, (place + step) % held, 0)
    return out


def whole(mine, core):
    other = other_core(mine)
    return jnp.where(
        core == 0, jnp.concatenate([mine, other], axis=0), jnp.concatenate([other, mine], axis=0)
    )


def fold(partial, core):
    half = partial.shape[0] // 2
    sent = lax.dynamic_slice_in_dim(partial, (1 - core) * half, half, 0)
    kept = lax.dynamic_slice_in_dim(partial, core * half, half, 0)
    return kept + other_core(sent)


def gather_plane(mine, first=()):
    mine = after(mine, *first)
    chip = lax.axis_index("fsdp") // 2
    half = mine.shape[0] // 2
    beside = flip(mine, 2)
    above = flip(mine, 4)
    across_one = flip(above[:half], 2)
    across_two = flip(beside[half:], 4)
    out = jnp.zeros((4,) + mine.shape, mine.dtype)
    out = lax.dynamic_update_index_in_dim(out, mine, chip, 0)
    out = lax.dynamic_update_index_in_dim(out, beside, chip ^ 1, 0)
    out = lax.dynamic_update_index_in_dim(out, above, chip ^ 2, 0)
    out = lax.dynamic_update_slice(out, across_one[None], (chip ^ 3, 0, 0))
    out = lax.dynamic_update_slice(out, across_two[None], (chip ^ 3, half, 0))
    return (out, (across_one, across_two))


def fast_plane():
    return lax.axis_size("fsdp") == 8 and lax.axis_size("seq") == 4


def own_head_rows(weight, core):
    width = weight.shape[1]
    return lax.dynamic_index_in_dim(weight.reshape(4, 2, -1, width), core, 1, keepdims=False).reshape(-1, width)


def add_low(left, right):
    return (left.astype(WIDE) + right.astype(WIDE)).astype(LOW)


def pick(value, index, axis):
    return lax.dynamic_index_in_dim(value, index, axis, keepdims=False)


def spread_depth(value):
    depth = lax.axis_size("seq")
    place = lax.axis_index("seq")
    total = pick(value, place, 0).astype(WIDE)
    for step in range(1, depth):
        sent = pick(value, (place + step) % depth, 0)
        got = lax.ppermute(sent, "seq", [(one, (one + step) % depth) for one in range(depth)])
        total = total + got.astype(WIDE)
    return total


def scatter_plane(parts, first=()):
    chip = lax.axis_index("fsdp") // 2
    x, y = (chip % 2, chip // 2)
    one, two = parts
    one_got = flip(after(pick(one, 1 - x, 2), *first), 2)
    two_got = flip(after(pick(two, 1 - y, 1), *first), 4)
    one = add_low(pick(one, x, 2), one_got)
    two = add_low(pick(two, y, 1), two_got)
    one_last = flip(pick(one, 1 - y, 1), 4)
    two_last = flip(pick(two, 1 - x, 1), 2)
    return (add_low(pick(one, y, 1), one_last), add_low(pick(two, x, 1), two_last)), (one_last, two_last)


def shards(
    inputs,
    lengths,
    cotangent,
    query_weight,
    key_weight,
    value_weight,
    output_weight,
    up_weight,
    down_weight,
    attn_gain,
    ffn_gain,
    bias_table,
):
    held, span, width = inputs.shape
    depth, size = (lax.axis_size("seq"), lax.axis_size("fsdp"))
    place, index = (lax.axis_index("seq"), lax.axis_index("fsdp"))
    core = index % 2
    rows = held * span
    inner = HEADS * HEAD_DIM
    fast = fast_plane()

    near_lengths = jnp.where(
        core == 0,
        jnp.concatenate([lengths, other_core(lengths)]),
        jnp.concatenate([other_core(lengths), lengths]),
    )
    length = lax.dynamic_slice_in_dim(near_lengths, place, 1, 0)
    slots = core * rows + jnp.arange(rows, dtype=jnp.int32)
    mask_rows = (slots < length[0])[:, None].astype(WIDE)

    own_table = lax.dynamic_index_in_dim(bias_table.reshape(BUCKETS, 4, 2, 2), core, 2, keepdims=False)
    own_table = own_table.reshape(BUCKETS, HEADS // 2)
    near, near_turned = near_tables(own_table)
    ends = jnp.stack([own_table[BUCKETS // 2 - 1], own_table[BUCKETS - 1]], axis=1)

    ffn = up_weight.shape[0]
    if fast:
        stacked = jnp.concatenate([query_weight, key_weight, value_weight], axis=0)
        heads_low, done = gather_plane(stacked)
        heads_low = heads_low.reshape(4, 3, -1, width)
        own_three = [heads_low[:, number].reshape(-1, width) for number in range(3)]
        own_output, done = gather_plane(output_weight, done)
        own_output = own_output.reshape(-1, width)
        far_output = other_core(own_output)
        cut = jnp.stack([up_weight, down_weight]).reshape(2, 2, 2, -1, width)
        swapped = other_core(pick(cut, 1 - core, 2))
        kept = pick(cut, core, 2)
        cut = jnp.where(
            core == 0, jnp.stack([kept, swapped], axis=1), jnp.stack([swapped, kept], axis=1)
        )
        own_up, done = gather_plane(cut[0].reshape(-1, width), done)
        own_down, done = gather_plane(cut[1].reshape(-1, width), done)
        own_up = own_up.reshape(-1, width)
        own_down = own_down.reshape(-1, width)
    else:
        own_three = [
            own_head_rows(lax.all_gather(one, "fsdp", axis=0, tiled=True), core)
            for one in (query_weight, key_weight, value_weight)
        ]
        full = lax.all_gather(output_weight, "fsdp", axis=0, tiled=True)
        own_output = own_head_rows(full, core)
        far_output = own_head_rows(full, 1 - core)
        own_up, own_down = (
            pick(
                lax.all_gather(one, "fsdp", axis=0, tiled=True).reshape(depth, size // 2, 2, -1, width), core, 2
            ).reshape(-1, width)
            for one in (up_weight, down_weight)
        )

    source_low = to_sequence(inputs)
    source = source_low.astype(WIDE)
    rms_one = lax.rsqrt(jnp.mean(source * source, axis=1, keepdims=True) + EPSILON)
    scaled_one = source * rms_one
    normed_one = whole((scaled_one * attn_gain).astype(LOW), core)
    query, key, value = [dot(normed_one, one, NT).astype(LOW) for one in own_three]
    context, logs = attend(length, ends, query, key, value, near)
    near_context = lax.dynamic_slice_in_dim(context, core * rows, rows, 0)
    far_context = other_core(lax.dynamic_slice_in_dim(context, (1 - core) * rows, rows, 0))
    hidden_one = source + (dot(near_context, own_output) + dot(far_context, far_output))
    rms_two = lax.rsqrt(jnp.mean(hidden_one * hidden_one, axis=1, keepdims=True) + EPSILON)
    scaled_two = hidden_one * rms_two
    normed_two = whole((scaled_two * ffn_gain).astype(LOW), core)
    grad_out = to_sequence(cotangent).astype(WIDE) * mask_rows
    grad_low = whole(grad_out.astype(LOW), core)
    active, slope = gelu_parts(dot(normed_two, own_up, NT))
    active = active.astype(LOW)
    mlp_out = fold(dot(active, own_down), core)
    layer_rows = ((hidden_one + mlp_out) * mask_rows).astype(LOW)
    layer_out = to_slots(layer_rows, held)

    pre_grad = (dot(grad_low, own_down, NT) * slope).astype(LOW)
    normed_grad = fold(dot(pre_grad, own_up), core)
    up_part = dot(pre_grad, normed_two, TN).astype(LOW)
    down_part = dot(active, grad_low, TN).astype(LOW)
    gained_two = ffn_gain * normed_grad
    hidden_grad = grad_out + rms_two * (
        gained_two - scaled_two * jnp.mean(gained_two * scaled_two, axis=1, keepdims=True)
    )
    ffn_gain_part = jnp.sum(normed_grad * scaled_two, axis=0)
    hidden_low = hidden_grad.astype(LOW)
    near_grad = dot(hidden_low, own_output, NT).astype(LOW)
    far_grad = other_core(dot(hidden_low, far_output, NT).astype(LOW))
    context_grad = jnp.where(
        core == 0,
        jnp.concatenate([near_grad, far_grad], axis=0),
        jnp.concatenate([far_grad, near_grad], axis=0),
    )
    near_output_part = dot(near_context, hidden_low, TN).astype(LOW)
    far_output_part = dot(far_context, hidden_low, TN).astype(LOW)

    query_low, key_low, value_low, tiles, far = attend_grad(
        length, ends, query, key, value, context_grad, logs, near_turned
    )
    lows = (query_low, key_low, value_low)
    normed_one_grad = dot(query_low, own_three[0]) + dot(key_low, own_three[1]) + dot(value_low, own_three[2])
    normed_one_grad = fold(normed_one_grad, core)
    three_parts = [dot(one, normed_one, TN).astype(LOW) for one in lows]
    gained_one = attn_gain * normed_one_grad
    input_grad = hidden_grad + rms_one * (
        gained_one - scaled_one * jnp.mean(gained_one * scaled_one, axis=1, keepdims=True)
    )
    attn_gain_part = jnp.sum(normed_one_grad * scaled_one, axis=0)
    input_grad = to_slots(input_grad.astype(LOW), held).astype(WIDE)

    if fast:
        blocks = (depth, 2, 2, -1, width)
        (up_some, down_some), done = scatter_plane((up_part.reshape(blocks), down_part.reshape(blocks)))
        up_grad, down_grad = (spread_depth(up_some), spread_depth(down_some))

        def to_parity(kept, sent):
            return jnp.where(
                core == 0, jnp.stack([kept, sent], axis=1), jnp.stack([sent, kept], axis=1)
            )

        three = jnp.stack(three_parts).reshape(3, 4, 2, 2, -1, width)
        three_got = other_core(pick(three, 1 - core, 3))
        three_kept = pick(three, core, 3)
        outs = [to_parity(three_kept[number], three_got[number]) for number in range(3)]
        near_part = near_output_part.reshape(4, 2, 2, -1, width)
        far_part = far_output_part.reshape(4, 2, 2, -1, width)
        got = other_core(jnp.stack([pick(far_part, 1 - core, 2), pick(near_part, 1 - core, 2)]))
        outs.append(
            to_parity(add_low(pick(near_part, core, 2), got[0]), add_low(pick(far_part, core, 2), got[1]))
        )
        one = jnp.concatenate(outs[:2], axis=3)
        two = jnp.concatenate(outs[2:], axis=3)
        (one, two), done = scatter_plane((one, two), done)
        attention = spread_depth(jnp.concatenate([one, two], axis=1))
        attention = attention.reshape(4, -1, width)
        query_grad, key_grad, value_grad, output_grad = [attention[number] for number in range(4)]
    else:

        def summed(value):
            return lax.psum_scatter(value, BOTH, scatter_dimension=0, tiled=True).astype(WIDE)

        def own_only(value, shape):
            blank = jnp.zeros_like(value)
            pair = jnp.where(core == 0, jnp.stack([value, blank], axis=1), jnp.stack([blank, value], axis=1))
            return pair.reshape(-1, width)

        up_grad, down_grad = [
            summed(own_only(one.reshape(depth * (size // 2), -1, width), None)) for one in (up_part, down_part)
        ]
        query_grad, key_grad, value_grad = [summed(own_only(one.reshape(4, -1, width), None)) for one in three_parts]
        near_part, far_part = (near_output_part.reshape(4, -1, width), far_output_part.reshape(4, -1, width))
        pair = jnp.where(
            core == 0, jnp.stack([near_part, far_part], axis=1), jnp.stack([far_part, near_part], axis=1)
        )
        output_grad = summed(pair.reshape(-1, width))

    bias_own = bucket_sums(tiles, far).reshape(BUCKETS, 4, 1, 2)
    bias_full = lax.dynamic_update_slice(
        jnp.zeros((BUCKETS, 4, 2, 2), WIDE), bias_own, (0, 0, core, 0)
    ).reshape(BUCKETS, HEADS)
    attn_gain_sum, ffn_gain_sum, bias_sum = lax.psum((attn_gain_part, ffn_gain_part, bias_full), BOTH)
    gain_rows = width // size
    bucket_rows = BUCKETS // size
    attn_gain_grad = lax.dynamic_slice_in_dim(attn_gain_sum, index * gain_rows, gain_rows, 0)
    ffn_gain_grad = lax.dynamic_slice_in_dim(ffn_gain_sum, index * gain_rows, gain_rows, 0)
    bias_grad = lax.dynamic_slice_in_dim(bias_sum, index * bucket_rows, bucket_rows, 0)
    return (
        layer_out,
        input_grad,
        query_grad,
        key_grad,
        value_grad,
        output_grad,
        up_grad,
        down_grad,
        attn_gain_grad,
        ffn_gain_grad,
        bias_grad,
    )


def solution(mesh):
    placed = (
        P("fsdp", "seq", None),
        P("fsdp"),
        P("fsdp", "seq", None),
        P("fsdp", None),
        P("fsdp", None),
        P("fsdp", None),
        P("fsdp", None),
        P("fsdp", None),
        P("fsdp", None),
        P(),
        P(),
        P(),
    )
    return jax.shard_map(
        shards,
        mesh=mesh,
        in_specs=placed,
        out_specs=(
            P("fsdp", "seq", None),
            P("fsdp", "seq", None),
            P(("seq", "fsdp"), None),
            P(("seq", "fsdp"), None),
            P(("seq", "fsdp"), None),
            P(("seq", "fsdp"), None),
            P(("seq", "fsdp"), None),
            P(("seq", "fsdp"), None),
            P("fsdp"),
            P("fsdp"),
            P("fsdp", None),
        ),
        check_vma=False,
    )
```

time: 1780 us -> 686 us (0.39)
  waiting for transfers between devices: 701 us -> 188 us
  matrix products: 423 us -> 71.8 us
  other arithmetic: 390 us -> 118 us
  starting transfers between devices: 16.8 us -> 93.7 us
  Pallas kernels: 0 us -> 69.6 us
  local copies, waits for them, and re-layouts: 147 us -> 88.5 us
  loops' own time: 37.7 us -> 0 us
    reduce_scatter x1 -> x0, waiting for transfers between devices: 356 us -> none  [shards(): lax.psum_scatter(jnp.concatenate([across(pre_grad, normed_two), across(ac...]
    dot_general x46 -> x21, matrix products: 423 us -> 71.8 us  [dot(): return lax.dot_general(left, right, dims, preferred_element_type=WIDE)]
    reduce_sum x13 -> x5, other arithmetic: 209 us -> 15.3 us  [the longest x2 9.05 us: bucket_sums(): jnp.sum(jnp.where((buckets == number)[None], tiles, 0.0), axis=(1, 2, 3))]
    ppermute x0 -> x54, waiting for transfers between devices: none -> 188 us  [the longest x37 148 us: flip(): lax.ppermute(value, 'fsdp', [(one, one ^ bit) for one in range(size)])]
    all_to_all x4 -> x0, waiting for transfers between devices: 183 us -> none  [the longest x1 70.7 us: shards(): lax.all_to_all(stacked, 'seq', split_axis=3, concat_axis=2, tiled=True)]
    ppermute x0 -> x54, starting transfers between devices: none -> 93.7 us  [the longest x37 46.9 us: flip(): lax.ppermute(value, 'fsdp', [(one, one ^ bit) for one in range(size)])]
    unnamed x9 -> x0, waiting for transfers between devices: 85.3 us -> none
    all_gather x6 -> x0, waiting for transfers between devices: 75.7 us -> none  [the longest x1 28.8 us: shards(): lax.all_gather(value_weight, 'fsdp', axis=0, tiled=True)]
  transfers between devices with their start and end apart: 12 -> 54, of which waited for: 9 -> 20; matrix products, arithmetic and copies ran while one was open for 21% -> 40% of each run, Pallas kernels for 0% -> 10%
where the time goes in v1:
time: 686 us; the launch traced here: 675 us
  waiting for transfers between devices  188 us (27%)
  other arithmetic  118 us (17%)
  starting transfers between devices  93.7 us (14%)
  local copies, waits for them, and re-layouts  88.5 us (13%)
  matrix products  71.8 us (10%)
  Pallas kernels  69.6 us (10%)
  blocking collectives  41.4 us (6%)
    ppermute x37, waiting for transfers between devices, flip(): lax.ppermute(value, 'fsdp', [(one, one ^ bit) for one in range(size)])  148 us
    dot_general x21, matrix products, dot(): return lax.dot_general(left, right, dims, preferred_element_type=WIDE)  71.8 us
    eq x96, other arithmetic, near_tables(): buckets == number  52.1 us
    ppermute x37, starting transfers between devices, flip(): lax.ppermute(value, 'fsdp', [(one, one ^ bit) for one in range(size)])  46.9 us
    pallas_call x1, Pallas kernels, attend_grad(): pl.pallas_call(attend_grad_kernel, grid=(pairs,), in_specs=[smem, smem, c...  44.1 us
    psum x1, blocking collectives, shards(): lax.psum((attn_gain_part, ffn_gain_part, bias_full), BOTH)  41.4 us
    ppermute x9, waiting for transfers between devices, spread_depth(): lax.ppermute(sent, 'seq', [(one, (one + step) % depth) for one in range(d...  40.3 us
    pallas_call x1, Pallas kernels, attend(): pl.pallas_call(attend_kernel, grid=(pairs,), in_specs=[smem, smem, column...  25.5 us
  transfers between devices with their start and end apart: 54, of which 20 were waited for; matrix products, arithmetic and copies ran while one was open for 40% of the time, Pallas kernels for 10%

profile of v1, /device:TPU:0, one launch (start us, length us, event | category | flops | bytes accessed | tf_op | source)
XLA Modules:
  0.0 674.6 jit_solution(384236747496672957)
XLA Ops:
  0.7 2.2 pad_maximum_fusion.2
  2.8 2.9 collective-permute-start.4
  8.3 5.4 collective-permute-start
  88.4 2.2 broadcast_compare_fusion.14
  92.7 2.9 select_select_fusion
  95.9 2.7 select_select_fusion.1
  98.7 2.7 select_select_fusion.2
  101.7 3.6 fusion.151
  106.5 3.0 fusion.37
  109.7 5.4 copy.124.near_ref
  122.5 18.0 %collective-permute-start.3 = (bf16[512,1024]{1,0:T(8,128)(2,1)S(1)}, bf16[512,1024]{1,0:T(8,128)(2,1)S(1)}, u32[]{:S(2)}, u32[]{:S(2)}) collective-permute-start(bf16[512,1024]{1,0:T(8,128)(2,1)S(1)} %fusion.18), channel_id=1, source_target_pairs={{0,1},{1,0},{2,3},{3,2},{4,5},{5,4},{6,7},{7,6},{8,9},{9,8},{10,11... | collective-permute-start | bytes 3145736 | tf_op jit(solution)/shard_map/ppermute | solution.py:288
  146.9 5.9 collective-permute-done.6
  156.8 5.6 collective-permute-done.9
  169.4 25.5 %attend.1 = (bf16[1024,512]{1,0:T(8,128)(2,1)S(1)}, f32[4,2,1024]{2,1,0:T(2,128)S(1)}) custom-call(s32[1]{0:T(128)} %dynamic_slice.185.length_ref, f32[8,2]{1,0:T(8,128)S(1)} %copy.123.ends_ref, bf16[1024,512]{1,0:T(8,128)(2,1)S(1)} %convolution_convert_fusion.7.query_ref, bf16[1024,512]{1,0:T(8,128)(2,1)S(1)} %convolution_convert_fusion.6.key_ref, ...), custom_call_target="tpu_custom_call" | custom-call | flops 12884901888 | bytes 4194304 | tf_op jit(solution)/shard_map/attend/pallas_call | solution.py:128
  201.2 21.5 %collective-permute-done.16 = bf16[512,1024]{1,0:T(8,128)(2,1)S(1)} collective-permute-done((bf16[512,1024]{1,0:T(8,128)(2,1)S(1)}, bf16[512,1024]{1,0:T(8,128)(2,1)S(1)}, u32[]{:S(2)}, u32[]{:S(2)}) %collective-permute-start.16) | collective-permute-done | bytes 1048608 | tf_op jit(solution)/shard_map/ppermute | solution.py:288
  224.3 8.9 %collective-permute-done.18 = bf16[256,1024]{1,0:T(8,128)(2,1)S(1)} collective-permute-done((bf16[256,1024]{1,0:T(8,128)(2,1)S(1)}, bf16[256,1024]{1,0:T(8,128)(2,1)S(1)}, u32[]{:S(2)}, u32[]{:S(2)}) %collective-permute-start.18) | collective-permute-done | bytes 524320 | tf_op jit(solution)/shard_map/ppermute | solution.py:288
  233.2 2.0 collective-permute-done.19
  239.8 12.0 %multiply_convert_fusion = (bf16[1024,2048]{1,0:T(8,128)(2,1)}, f32[1024,2048]{1,0:T(8,128)}) fusion(bf16[2048,1024]{1,0:T(8,128)(2,1)} %bitcast.354, bf16[512,1024]{1,0:T(8,128)(2,1)S(1)} %collective-permute-done.14, bf16[512,1024]{1,0:T(8,128)(2,1)S(1)} %multiply_convert_fusion.2, pred[]{:T(512)S(6)} %eq.997), kind=kOutput, calls=%fused_computation.7 | convolution fusion | flops 4314890240 | bytes 18874368 | tf_op jit(solution)/shard_map/dot_general | solution.py:29
  251.8 8.2 %convolution_convert_fusion = bf16[2048,1024]{1,0:T(8,128)(2,1)S(1)} fusion(bf16[1024,2048]{1,0:T(8,128)(2,1)} %get-tuple-element.275, bf16[512,1024]{1,0:T(8,128)(2,1)} %collective-permute-done.29, bf16[512,1024]{1,0:T(8,128)(2,1)} %fusion.13, pred[]{:T(512)S(6)} %eq.997), kind=kOutput, calls=%fused_computation.15 | convolution fusion | flops 4306501632 | bytes 10485761 | tf_op jit(solution)/shard_map/dot_general | solution.py:29
  265.0 8.9 %collective-permute-done.22 = bf16[256,1024]{1,0:T(8,128)(2,1)S(1)} collective-permute-done((bf16[256,1024]{1,0:T(8,128)(2,1)S(1)}, bf16[256,1024]{1,0:T(8,128)(2,1)S(1)}, u32[]{:S(2)}, u32[]{:S(2)}) %collective-permute-start.22) | collective-permute-done | bytes 524320 | tf_op jit(solution)/shard_map/ppermute | solution.py:288
  273.9 44.1 %collective-permute-done.23 = bf16[256,1024]{1,0:T(8,128)(2,1)S(1)} collective-permute-done((bf16[256,1024]{1,0:T(8,128)(2,1)S(1)}, bf16[256,1024]{1,0:T(8,128)(2,1)S(1)}, u32[]{:S(2)}, u32[]{:S(2)}) %collective-permute-start.23) | collective-permute-done | bytes 524320 | tf_op jit(solution)/shard_map/ppermute | solution.py:288
  318.2 6.1 fusion.167
  324.3 13.0 %fusion.5 = bf16[1024,2048]{1,0:T(8,128)(2,1)} fusion(f32[1024,2048]{1,0:T(8,128)} %get-tuple-element.276, bf16[2048,1024]{1,0:T(8,128)(2,1)} %bitcast.353, bf16[512,1024]{1,0:T(8,128)(2,1)} %collective-permute-done.29, bf16[512,1024]{1,0:T(8,128)(2,1)} %fusion.13, pred[]{:T(512)S(6)} %eq.997), kind=kOutput, calls=%fused_computation.6 | convolution fusion | flops 4325376000 | bytes 18874368 | tf_op jit(solution)/shard_map/dot_general | solution.py:29
  337.3 7.7 %fusion.168 = f32[1024,1024]{1,0:T(8,128)S(1)} fusion(bf16[1024,2048]{1,0:T(8,128)(2,1)} %fusion.5, bf16[2048,1024]{1,0:T(8,128)(2,1)} %bitcast.355), kind=kOutput, calls=%fused_computation.555 | convolution fusion | flops 4294967296 | bytes 12582912 | tf_op jit(solution)/shard_map/dot_general | solution.py:29
  349.4 8.4 %convolution_convert_fusion.1 = bf16[2048,1024]{1,0:T(8,128)(2,1)} fusion(bf16[1024,2048]{1,0:T(8,128)(2,1)} %fusion.5, bf16[512,1024]{1,0:T(8,128)(2,1)S(1)} %copy-done.135, bf16[512,1024]{1,0:T(8,128)(2,1)S(1)} %copy-done.21, pred[]{:T(512)S(6)} %eq.997), kind=kOutput, calls=%fused_computation.16 | convolution fusion | flops 4306501632 | bytes 10485761 | tf_op jit(solution)/shard_map/dot_general | solution.py:29
  357.8 2.7 constant_dynamic-slice_fusion.41
  362.5 2.6 fusion.6
  367.7 2.9 multiply_reduce_fusion
  370.6 4.0 fusion.152
  375.6 5.4 collective-permute-start.25
  386.6 24.0 %collective-permute-done.36 = bf16[4,2,128,1024]{3,2,0,1:T(8,128)(2,1)S(1)} collective-permute-done((bf16[4,2,128,1024]{3,2,0,1:T(8,128)(2,1)}, bf16[4,2,128,1024]{3,2,0,1:T(8,128)(2,1)S(1)}, u32[]{:S(2)}, u32[]{:S(2)}) %collective-permute-start.36) | collective-permute-done | bytes 2097184 | tf_op jit(solution)/shard_map/ppermute | solution.py:288
  412.8 20.0 %collective-permute-done.39 = bf16[4,128,1024]{2,1,0:T(8,128)(2,1)} collective-permute-done((bf16[4,128,1024]{2,1,0:T(8,128)(2,1)}, bf16[4,128,1024]{2,1,0:T(8,128)(2,1)}, u32[]{:S(2)}, u32[]{:S(2)}) %collective-permute-start.39) | collective-permute-done | bytes 1048608 | tf_op jit(solution)/shard_map/ppermute | solution.py:288
  436.3 4.4 collective-permute-start.52
  445.5 13.9 %collective-permute-start.26 = (bf16[256,1024]{1,0:T(8,128)(2,1)}, bf16[256,1024]{1,0:T(8,128)(2,1)}, u32[]{:S(2)}, u32[]{:S(2)}) collective-permute-start(bf16[256,1024]{1,0:T(8,128)(2,1)} %get-tuple-element.208), channel_id=1, source_target_pairs={{8,0},{24,1},{10,2},{26,3},{12,4},{28,5},{14,6},{30,7},{0,8},{16,9... | collective-permute-start | bytes 1572872 | tf_op jit(solution)/shard_map/ppermute | solution.py:333
  459.4 8.3 %collective-permute-done.52 = bf16[128,1024]{1,0:T(8,128)(2,1)S(1)} collective-permute-done((bf16[128,1024]{1,0:T(8,128)(2,1)S(1)}, bf16[128,1024]{1,0:T(8,128)(2,1)S(1)}, u32[]{:S(2)}, u32[]{:S(2)}) %collective-permute-start.52) | collective-permute-done | bytes 262176 | tf_op jit(solution)/shard_map/ppermute | solution.py:392
  470.1 44.1 %attend_grad.1 = (bf16[1024,512]{1,0:T(8,128)(2,1)S(1)}, bf16[1024,512]{1,0:T(8,128)(2,1)S(1)}, bf16[1024,512]{1,0:T(8,128)(2,1)S(1)}, f32[8,3,128,128]{3,2,1,0:T(8,128)}, f32[4,2,12,128]{3,2,1,0:T(8,128)S(1)}) custom-call(s32[1]{0:T(128)} %dynamic_slice.185.length_ref, f32[8,2]{1,0:T(8,128)S(1)} %copy.123.ends_ref, ...), custom_call_target="tpu_custom_call" | custom-call | flops 23622320128 | bytes 7340032 | tf_op jit(solution)/shard_map/attend_grad/pallas_call | solution.py:238
  543.5 5.7 select_reduce_fusion
  549.4 3.4 select_reduce_fusion.18
  571.9 2.0 collective-permute-start.43
  573.9 11.8 %collective-permute-done.49 = bf16[128,1024]{1,0:T(8,128)(2,1)S(1)} collective-permute-done((bf16[128,1024]{1,0:T(8,128)(2,1)S(1)}, bf16[128,1024]{1,0:T(8,128)(2,1)S(1)}, u32[]{:S(2)}, u32[]{:S(2)}) %collective-permute-start.49) | collective-permute-done | bytes 262176 | tf_op jit(solution)/shard_map/ppermute | solution.py:392
  586.8 2.5 fusion.24
  589.2 3.4 collective-permute-done.40
  594.0 2.0 collective-permute-start.41
  600.3 5.4 collective-permute-start.33
  606.1 41.4 %all-reduce.1 = (f32[1024]{0:T(1024)S(1)}, f32[1024]{0:T(1024)S(1)}, f32[32,16]{0,1:T(8,128)S(1)}) all-reduce(f32[1024]{0:T(1024)S(1)} %get-tuple-element.94, f32[1024]{0:T(1024)S(1)} %copy-done.90, f32[32,16]{0,1:T(8,128)S(1)} %bitcast.383), channel_id=1, replica_groups=mesh['seq'=4,'fsdp'=8] {'seq','fsdp'}, use_global_device_ids=true, to_apply=%region_5.6 | all-reduce | flops 2560 | bytes 20480 | tf_op jit(solution)/shard_map/psum | solution.py:585
  649.9 2.4 collective-permute-start.47
  656.8 2.3 collective-permute-done.47
  659.1 14.4 %collective-permute-done.46 = bf16[128,1024]{1,0:T(8,128)(2,1)S(1)} collective-permute-done((bf16[128,1024]{1,0:T(8,128)(2,1)S(1)}, bf16[128,1024]{1,0:T(8,128)(2,1)S(1)}, u32[]{:S(2)}, u32[]{:S(2)}) %collective-permute-start.46) | collective-permute-done | bytes 262176 | tf_op jit(solution)/shard_map/ppermute | solution.py:392
  (665 shorter events, 213.1 us)
Async XLA Ops:
  2.8 139.5 %collective-permute-start.4 = (bf16[384,1024]{1,0:T(8,128)(2,1)}, bf16[384,1024]{1,0:T(8,128)(2,1)}, u32[]{:S(2)}, u32[]{:S(2)}) collective-permute-start(bf16[384,1024]{1,0:T(8,128)(2,1)} %pad_maximum_fusion.2), channel_id=1, source_target_pairs={{0,2},{1,3},{2,0},{3,1},{4,6},{5,7},{6,4},{7,5},{8,10},{9,11},{10,... | collective-permute-start | bytes 2359304 | tf_op jit(solution)/shard_map/ppermute | solution.py:288
  5.8 134.9 %collective-permute-start.5 = (bf16[384,1024]{1,0:T(8,128)(2,1)}, bf16[384,1024]{1,0:T(8,128)(2,1)}, u32[]{:S(2)}, u32[]{:S(2)}) collective-permute-start(bf16[384,1024]{1,0:T(8,128)(2,1)} %pad_maximum_fusion.2), channel_id=1, source_target_pairs={{0,4},{1,5},{2,6},{3,7},{4,0},{5,1},{6,2},{7,3},{8,12},{9,13},{10,... | collective-permute-start | bytes 2359304 | tf_op jit(solution)/shard_map/ppermute | solution.py:288
  7.3 107.8 %collective-permute-start.2 = (s32[2]{0:T(128)}, s32[2]{0:T(128)}, u32[]{:S(2)}, u32[]{:S(2)}) collective-permute-start(s32[2]{0:T(128)} %param.17), channel_id=1, source_target_pairs={{0,1},{1,0},{2,3},{3,2},{4,5},{5,4},{6,7},{7,6},{8,9},{9,8},{10,11... | collective-permute-start | bytes 32 | tf_op jit(solution)/shard_map/ppermute | solution.py:288
  8.3 108.7 %collective-permute-start = (bf16[256,1024]{1,0:T(8,128)(2,1)}, bf16[256,1024]{1,0:T(8,128)(2,1)}, u32[]{:S(2)}, u32[]{:S(2)}) collective-permute-start(bf16[256,1024]{1,0:T(8,128)(2,1)} %get-tuple-element.211), channel_id=1, source_target_pairs={{0,0},{1,16},{2,2},{3,18},{4,4},{5,20},{6,6},{7,22},{8,8},{9,24},{... | collective-permute-start | bytes 1572872 | tf_op jit(solution)/shard_map/ppermute | solution.py:321
  13.7 106.5 %collective-permute-start.1 = (bf16[256,1024]{1,0:T(8,128)(2,1)}, bf16[256,1024]{1,0:T(8,128)(2,1)}, u32[]{:S(2)}, u32[]{:S(2)}) collective-permute-start(bf16[256,1024]{1,0:T(8,128)(2,1)} %get-tuple-element.210), channel_id=1, source_target_pairs={{0,8},{1,24},{2,10},{3,26},{4,12},{5,28},{6,14},{7,30},{8,0},{9,16... | collective-permute-start | bytes 1572872 | tf_op jit(solution)/shard_map/ppermute | solution.py:321
  115.1 31.3 %collective-permute-start.15 = (bf16[2,2,128,1024]{3,2,1,0:T(8,128)(2,1)}, bf16[2,2,128,1024]{3,2,1,0:T(8,128)(2,1)S(1)}, u32[]{:S(2)}, u32[]{:S(2)}) collective-permute-start(bf16[2,2,128,1024]{3,2,1,0:T(8,128)(2,1)} %get-tuple-element.185), channel_id=1, source_target_pairs={{0,1},{1,0},{2,3},{3,2},{4,5},{5,4},{6,7},{7,6},{8,9},{9,8},{10,11... | collective-permute-start | bytes 3145736 | tf_op jit(solution)/shard_map/ppermute | solution.py:288
  120.2 20.5 %collective-permute-start.28 = (bf16[256,1024]{1,0:T(8,128)(2,1)S(1)}, bf16[256,1024]{1,0:T(8,128)(2,1)S(1)}, u32[]{:S(2)}, u32[]{:S(2)}) collective-permute-start(bf16[256,1024]{1,0:T(8,128)(2,1)S(1)} %copy-done.28), channel_id=1, source_target_pairs={{0,8},{1,24},{2,10},{3,26},{4,12},{5,28},{6,14},{7,30},{8,0},{9,16... | collective-permute-start | bytes 1572872 | tf_op jit(solution)/shard_map/ppermute | solution.py:321
  122.5 41.0 %collective-permute-start.3 = (bf16[512,1024]{1,0:T(8,128)(2,1)S(1)}, bf16[512,1024]{1,0:T(8,128)(2,1)S(1)}, u32[]{:S(2)}, u32[]{:S(2)}) collective-permute-start(bf16[512,1024]{1,0:T(8,128)(2,1)S(1)} %fusion.18), channel_id=1, source_target_pairs={{0,1},{1,0},{2,3},{3,2},{4,5},{5,4},{6,7},{7,6},{8,9},{9,8},{10,11... | collective-permute-start | bytes 3145736 | tf_op jit(solution)/shard_map/ppermute | solution.py:288
  141.8 11.0 %collective-permute-start.6 = (bf16[192,1024]{1,0:T(8,128)(2,1)S(1)}, bf16[192,1024]{1,0:T(8,128)(2,1)S(1)}, u32[]{:S(2)}, u32[]{:S(2)}) collective-permute-start(bf16[192,1024]{1,0:T(8,128)(2,1)S(1)} %slice.472), channel_id=1, source_target_pairs={{0,2},{1,3},{2,0},{3,1},{4,6},{5,7},{6,4},{7,5},{8,10},{9,11},{10,... | collective-permute-start | bytes 1179656 | tf_op jit(solution)/shard_map/ppermute | solution.py:288
  143.4 10.8 %collective-permute-start.7 = (bf16[192,1024]{1,0:T(8,128)(2,1)S(1)}, bf16[192,1024]{1,0:T(8,128)(2,1)S(1)}, u32[]{:S(2)}, u32[]{:S(2)}) collective-permute-start(bf16[192,1024]{1,0:T(8,128)(2,1)S(1)} %slice.473), channel_id=1, source_target_pairs={{0,4},{1,5},{2,6},{3,7},{4,0},{5,1},{6,2},{7,3},{8,12},{9,13},{10,... | collective-permute-start | bytes 1179656 | tf_op jit(solution)/shard_map/ppermute | solution.py:288
  168.1 31.4 %collective-permute-start.13 = (bf16[512,1024]{1,0:T(8,128)(2,1)S(1)}, bf16[512,1024]{1,0:T(8,128)(2,1)S(1)}, u32[]{:S(2)}, u32[]{:S(2)}) collective-permute-start(bf16[512,1024]{1,0:T(8,128)(2,1)S(1)} %bitcast.346), channel_id=1, source_target_pairs={{0,1},{1,0},{2,3},{3,2},{4,5},{5,4},{6,7},{7,6},{8,9},{9,8},{10,11... | collective-permute-start | bytes 3145736 | tf_op jit(solution)/shard_map/ppermute | solution.py:288
  168.1 30.7 %collective-permute-start.17 = (bf16[512,1024]{1,0:T(8,128)(2,1)S(1)}, bf16[512,1024]{1,0:T(8,128)(2,1)S(1)}, u32[]{:S(2)}, u32[]{:S(2)}) collective-permute-start(bf16[512,1024]{1,0:T(8,128)(2,1)S(1)} %bitcast.359), channel_id=1, source_target_pairs={{0,4},{1,5},{2,6},{3,7},{4,0},{5,1},{6,2},{7,3},{8,12},{9,13},{10,... | collective-permute-start | bytes 3145736 | tf_op jit(solution)/shard_map/ppermute | solution.py:288
  196.3 55.5 %collective-permute-start.29 = (bf16[512,1024]{1,0:T(8,128)(2,1)}, bf16[512,1024]{1,0:T(8,128)(2,1)}, u32[]{:S(2)}, u32[]{:S(2)}) collective-permute-start(bf16[512,1024]{1,0:T(8,128)(2,1)} %fusion.13), channel_id=1, source_target_pairs={{0,1},{1,0},{2,3},{3,2},{4,5},{5,4},{6,7},{7,6},{8,9},{9,8},{10,11... | collective-permute-start | bytes 3145736 | tf_op jit(solution)/shard_map/ppermute | solution.py:288
  196.7 26.0 %collective-permute-start.16 = (bf16[512,1024]{1,0:T(8,128)(2,1)S(1)}, bf16[512,1024]{1,0:T(8,128)(2,1)S(1)}, u32[]{:S(2)}, u32[]{:S(2)}) collective-permute-start(bf16[512,1024]{1,0:T(8,128)(2,1)S(1)} %bitcast.360), channel_id=1, source_target_pairs={{0,2},{1,3},{2,0},{3,1},{4,6},{5,7},{6,4},{7,5},{8,10},{9,11},{10,... | collective-permute-start | bytes 3145736 | tf_op jit(solution)/shard_map/ppermute | solution.py:288
  198.9 34.3 %collective-permute-start.18 = (bf16[256,1024]{1,0:T(8,128)(2,1)S(1)}, bf16[256,1024]{1,0:T(8,128)(2,1)S(1)}, u32[]{:S(2)}, u32[]{:S(2)}) collective-permute-start(bf16[256,1024]{1,0:T(8,128)(2,1)S(1)} %slice.480), channel_id=1, source_target_pairs={{0,2},{1,3},{2,0},{3,1},{4,6},{5,7},{6,4},{7,5},{8,10},{9,11},{10,... | collective-permute-start | bytes 1572872 | tf_op jit(solution)/shard_map/ppermute | solution.py:288
  222.7 12.5 %collective-permute-start.19 = (bf16[256,1024]{1,0:T(8,128)(2,1)S(1)}, bf16[256,1024]{1,0:T(8,128)(2,1)S(1)}, u32[]{:S(2)}, u32[]{:S(2)}) collective-permute-start(bf16[256,1024]{1,0:T(8,128)(2,1)S(1)} %slice.481), channel_id=1, source_target_pairs={{0,4},{1,5},{2,6},{3,7},{4,0},{5,1},{6,2},{7,3},{8,12},{9,13},{10,... | collective-permute-start | bytes 1572872 | tf_op jit(solution)/shard_map/ppermute | solution.py:288
  223.9 15.8 %collective-permute-start.14 = (bf16[512,1024]{1,0:T(8,128)(2,1)S(1)}, bf16[512,1024]{1,0:T(8,128)(2,1)S(1)}, u32[]{:S(2)}, u32[]{:S(2)}) collective-permute-start(bf16[512,1024]{1,0:T(8,128)(2,1)S(1)} %multiply_convert_fusion.2), channel_id=1, source_target_pairs={{0,1},{1,0},{2,3},{3,2},{4,5},{5,4},{6,7},{7,6},{8,9},{9,8},{10,11... | collective-permute-start | bytes 3145736 | tf_op jit(solution)/shard_map/ppermute | solution.py:288
  235.2 28.6 %collective-permute-start.20 = (bf16[512,1024]{1,0:T(8,128)(2,1)S(1)}, bf16[512,1024]{1,0:T(8,128)(2,1)S(1)}, u32[]{:S(2)}, u32[]{:S(2)}) collective-permute-start(bf16[512,1024]{1,0:T(8,128)(2,1)S(1)} %bitcast.356), channel_id=1, source_target_pairs={{0,2},{1,3},{2,0},{3,1},{4,6},{5,7},{6,4},{7,5},{8,10},{9,11},{10,... | collective-permute-start | bytes 3145736 | tf_op jit(solution)/shard_map/ppermute | solution.py:288
  236.7 26.4 %collective-permute-start.21 = (bf16[512,1024]{1,0:T(8,128)(2,1)S(1)}, bf16[512,1024]{1,0:T(8,128)(2,1)S(1)}, u32[]{:S(2)}, u32[]{:S(2)}) collective-permute-start(bf16[512,1024]{1,0:T(8,128)(2,1)S(1)} %bitcast.357), channel_id=1, source_target_pairs={{0,4},{1,5},{2,6},{3,7},{4,0},{5,1},{6,2},{7,3},{8,12},{9,13},{10,... | collective-permute-start | bytes 3145736 | tf_op jit(solution)/shard_map/ppermute | solution.py:288
  262.0 100.5 %collective-permute-start.38 = (bf16[4,2,128,1024]{3,2,0,1:T(8,128)(2,1)}, bf16[4,2,128,1024]{3,2,0,1:T(8,128)(2,1)}, u32[]{:S(2)}, u32[]{:S(2)}) collective-permute-start(bf16[4,2,128,1024]{3,2,0,1:T(8,128)(2,1)} %bitcast.336), channel_id=1, source_target_pairs={{0,4},{1,5},{2,6},{3,7},{4,0},{5,1},{6,2},{7,3},{8,12},{9,13},{10,... | collective-permute-start | bytes 6291464 | tf_op jit(solution)/shard_map/ppermute | solution.py:288
  263.2 10.7 %collective-permute-start.22 = (bf16[256,1024]{1,0:T(8,128)(2,1)S(1)}, bf16[256,1024]{1,0:T(8,128)(2,1)S(1)}, u32[]{:S(2)}, u32[]{:S(2)}) collective-permute-start(bf16[256,1024]{1,0:T(8,128)(2,1)S(1)} %slice.483), channel_id=1, source_target_pairs={{0,2},{1,3},{2,0},{3,1},{4,6},{5,7},{6,4},{7,5},{8,10},{9,11},{10,... | collective-permute-start | bytes 1572872 | tf_op jit(solution)/shard_map/ppermute | solution.py:288
  263.8 54.3 %collective-permute-start.23 = (bf16[256,1024]{1,0:T(8,128)(2,1)S(1)}, bf16[256,1024]{1,0:T(8,128)(2,1)S(1)}, u32[]{:S(2)}, u32[]{:S(2)}) collective-permute-start(bf16[256,1024]{1,0:T(8,128)(2,1)S(1)} %slice.484), channel_id=1, source_target_pairs={{0,4},{1,5},{2,6},{3,7},{4,0},{5,1},{6,2},{7,3},{8,12},{9,13},{10,... | collective-permute-start | bytes 1572872 | tf_op jit(solution)/shard_map/ppermute | solution.py:288
  346.4 21.2 %collective-permute-start.30 = (f32[512,1024]{1,0:T(8,128)}, f32[512,1024]{1,0:T(8,128)}, u32[]{:S(2)}, u32[]{:S(2)}) collective-permute-start(f32[512,1024]{1,0:T(8,128)} %constant_dynamic-slice_fusion.45), channel_id=1, source_target_pairs={{0,1},{1,0},{2,3},{3,2},{4,5},{5,4},{6,7},{7,6},{8,9},{9,8},{10,11... | collective-permute-start | bytes 6291464 | tf_op jit(solution)/shard_map/ppermute | solution.py:288
  349.4 21.2 %collective-permute-start.24 = (f32[512,1024]{1,0:T(8,128)}, f32[512,1024]{1,0:T(8,128)}, u32[]{:S(2)}, u32[]{:S(2)}) collective-permute-start(f32[512,1024]{1,0:T(8,128)} %constant_dynamic-slice_fusion.46), channel_id=1, source_target_pairs={{0,1},{1,0},{2,3},{3,2},{4,5},{5,4},{6,7},{7,6},{8,9},{9,8},{10,11... | collective-permute-start | bytes 6291464 | tf_op jit(solution)/shard_map/ppermute | solution.py:288
  362.0 48.6 %collective-permute-start.36 = (bf16[4,2,128,1024]{3,2,0,1:T(8,128)(2,1)}, bf16[4,2,128,1024]{3,2,0,1:T(8,128)(2,1)S(1)}, u32[]{:S(2)}, u32[]{:S(2)}) collective-permute-start(bf16[4,2,128,1024]{3,2,0,1:T(8,128)(2,1)} %bitcast.337), channel_id=1, source_target_pairs={{0,2},{1,3},{2,0},{3,1},{4,6},{5,7},{6,4},{7,5},{8,10},{9,11},{10,... | collective-permute-start | bytes 6291464 | tf_op jit(solution)/shard_map/ppermute | solution.py:288
  366.2 66.6 %collective-permute-start.39 = (bf16[4,128,1024]{2,1,0:T(8,128)(2,1)}, bf16[4,128,1024]{2,1,0:T(8,128)(2,1)}, u32[]{:S(2)}, u32[]{:S(2)}) collective-permute-start(bf16[4,128,1024]{2,1,0:T(8,128)(2,1)} %dynamic-slice_bitcast_fusion), channel_id=1, source_target_pairs={{0,2},{1,3},{2,0},{3,1},{4,6},{5,7},{6,4},{7,5},{8,10},{9,11},{10,... | collective-permute-start | bytes 3145736 | tf_op jit(solution)/shard_map/ppermute | solution.py:288
  375.6 177.2 %collective-permute-start.25 = (bf16[256,1024]{1,0:T(8,128)(2,1)}, bf16[256,1024]{1,0:T(8,128)(2,1)}, u32[]{:S(2)}, u32[]{:S(2)}) collective-permute-start(bf16[256,1024]{1,0:T(8,128)(2,1)} %get-tuple-element.209), channel_id=1, source_target_pairs={{0,0},{16,1},{2,2},{18,3},{4,4},{20,5},{6,6},{22,7},{8,8},{24,9},{... | collective-permute-start | bytes 1572872 | tf_op jit(solution)/shard_map/ppermute | solution.py:333
  381.7 87.0 %collective-permute-start.31 = (bf16[512,512]{1,0:T(8,128)(2,1)S(1)}, bf16[512,512]{1,0:T(8,128)(2,1)S(1)}, u32[]{:S(2)}, u32[]{:S(2)}) collective-permute-start(bf16[512,512]{1,0:T(8,128)(2,1)S(1)} %convolution_convert_fusion.10), channel_id=1, source_target_pairs={{0,1},{1,0},{2,3},{3,2},{4,5},{5,4},{6,7},{7,6},{8,9},{9,8},{10,11... | collective-permute-start | bytes 1572872 | tf_op jit(solution)/shard_map/ppermute | solution.py:288
  434.5 11.0 %collective-permute-start.53 = (bf16[128,1024]{1,0:T(8,128)(2,1)S(1)}, bf16[128,1024]{1,0:T(8,128)(2,1)S(1)}, u32[]{:S(2)}, u32[]{:S(2)}) collective-permute-start(bf16[128,1024]{1,0:T(8,128)(2,1)S(1)} %get-tuple-element.190), channel_id=1, source_target_pairs={{0,24},{8,0},{16,8},{24,16},{1,25},{9,1},{17,9},{25,17},{2,26},{10... | collective-permute-start | bytes 786440 | tf_op jit(solution)/shard_map/ppermute | solution.py:392
  436.3 31.4 %collective-permute-start.52 = (bf16[128,1024]{1,0:T(8,128)(2,1)S(1)}, bf16[128,1024]{1,0:T(8,128)(2,1)S(1)}, u32[]{:S(2)}, u32[]{:S(2)}) collective-permute-start(bf16[128,1024]{1,0:T(8,128)(2,1)S(1)} %get-tuple-element.191), channel_id=1, source_target_pairs={{0,16},{8,24},{16,0},{24,8},{1,17},{9,25},{17,1},{25,9},{2,18},{10... | collective-permute-start | bytes 786440 | tf_op jit(solution)/shard_map/ppermute | solution.py:392
  440.7 27.0 %collective-permute-start.51 = (bf16[128,1024]{1,0:T(8,128)(2,1)S(1)}, bf16[128,1024]{1,0:T(8,128)(2,1)S(1)}, u32[]{:S(2)}, u32[]{:S(2)}) collective-permute-start(bf16[128,1024]{1,0:T(8,128)(2,1)S(1)} %get-tuple-element.189), channel_id=1, source_target_pairs={{0,8},{8,16},{16,24},{24,0},{1,9},{9,17},{17,25},{25,1},{2,10},{10... | collective-permute-start | bytes 786440 | tf_op jit(solution)/shard_map/ppermute | solution.py:392
  445.5 110.7 %collective-permute-start.26 = (bf16[256,1024]{1,0:T(8,128)(2,1)}, bf16[256,1024]{1,0:T(8,128)(2,1)}, u32[]{:S(2)}, u32[]{:S(2)}) collective-permute-start(bf16[256,1024]{1,0:T(8,128)(2,1)} %get-tuple-element.208), channel_id=1, source_target_pairs={{8,0},{24,1},{10,2},{26,3},{12,4},{28,5},{14,6},{30,7},{0,8},{16,9... | collective-permute-start | bytes 1572872 | tf_op jit(solution)/shard_map/ppermute | solution.py:333
  467.7 92.4 %collective-permute-start.37 = (bf16[4,128,1024]{2,1,0:T(8,128)(2,1)}, bf16[4,128,1024]{2,1,0:T(8,128)(2,1)}, u32[]{:S(2)}, u32[]{:S(2)}) collective-permute-start(bf16[4,128,1024]{2,1,0:T(8,128)(2,1)} %dynamic-slice_bitcast_fusion.1), channel_id=1, source_target_pairs={{0,4},{1,5},{2,6},{3,7},{4,0},{5,1},{6,2},{7,3},{8,12},{9,13},{10,... | collective-permute-start | bytes 3145736 | tf_op jit(solution)/shard_map/ppermute | solution.py:288
  467.7 94.6 %collective-permute-start.42 = (bf16[2,4,2,32,1024]{4,3,1,2,0:T(8,128)(2,1)}, bf16[2,4,2,32,1024]{4,3,1,2,0:T(8,128)(2,1)}, u32[]{:S(2)}, u32[]{:S(2)}) collective-permute-start(bf16[2,4,2,32,1024]{4,3,1,2,0:T(8,128)(2,1)} %pad_maximum_fusion.1), channel_id=1, source_target_pairs={{0,1},{1,0},{2,3},{3,2},{4,5},{5,4},{6,7},{7,6},{8,9},{9,8},{10,11... | collective-permute-start | bytes 3145736 | tf_op jit(solution)/shard_map/ppermute | solution.py:288
  521.7 65.0 %collective-permute-start.32 = (f32[512,1024]{1,0:T(8,128)}, f32[512,1024]{1,0:T(8,128)}, u32[]{:S(2)}, u32[]{:S(2)}) collective-permute-start(f32[512,1024]{1,0:T(8,128)} %constant_dynamic-slice_fusion.44), channel_id=1, source_target_pairs={{0,1},{1,0},{2,3},{3,2},{4,5},{5,4},{6,7},{7,6},{8,9},{9,8},{10,11... | collective-permute-start | bytes 6291464 | tf_op jit(solution)/shard_map/ppermute | solution.py:288
  552.7 13.1 %collective-permute-start.35 = (bf16[3,4,2,32,1024]{4,3,1,2,0:T(8,128)(2,1)}, bf16[3,4,2,32,1024]{4,3,1,2,0:T(8,128)(2,1)}, u32[]{:S(2)}, u32[]{:S(2)}) collective-permute-start(bf16[3,4,2,32,1024]{4,3,1,2,0:T(8,128)(2,1)} %copy_bitcast_fusion.4), channel_id=1, source_target_pairs={{0,1},{1,0},{2,3},{3,2},{4,5},{5,4},{6,7},{7,6},{8,9},{9,8},{10,11... | collective-permute-start | bytes 4718600 | tf_op jit(solution)/shard_map/ppermute | solution.py:288
  562.1 9.8 %collective-permute-start.50 = (bf16[128,1024]{1,0:T(8,128)(2,1)S(1)}, bf16[128,1024]{1,0:T(8,128)(2,1)S(1)}, u32[]{:S(2)}, u32[]{:S(2)}) collective-permute-start(bf16[128,1024]{1,0:T(8,128)(2,1)S(1)} %get-tuple-element.193), channel_id=1, source_target_pairs={{0,24},{8,0},{16,8},{24,16},{1,25},{9,1},{17,9},{25,17},{2,26},{10... | collective-permute-start | bytes 786440 | tf_op jit(solution)/shard_map/ppermute | solution.py:392
  562.2 23.6 %collective-permute-start.49 = (bf16[128,1024]{1,0:T(8,128)(2,1)S(1)}, bf16[128,1024]{1,0:T(8,128)(2,1)S(1)}, u32[]{:S(2)}, u32[]{:S(2)}) collective-permute-start(bf16[128,1024]{1,0:T(8,128)(2,1)S(1)} %get-tuple-element.194), channel_id=1, source_target_pairs={{0,16},{8,24},{16,0},{24,8},{1,17},{9,25},{17,1},{25,9},{2,18},{10... | collective-permute-start | bytes 786440 | tf_op jit(solution)/shard_map/ppermute | solution.py:392
  562.3 23.5 %collective-permute-start.48 = (bf16[128,1024]{1,0:T(8,128)(2,1)S(1)}, bf16[128,1024]{1,0:T(8,128)(2,1)S(1)}, u32[]{:S(2)}, u32[]{:S(2)}) collective-permute-start(bf16[128,1024]{1,0:T(8,128)(2,1)S(1)} %get-tuple-element.192), channel_id=1, source_target_pairs={{0,8},{8,16},{16,24},{24,0},{1,9},{9,17},{17,25},{25,1},{2,10},{10... | collective-permute-start | bytes 786440 | tf_op jit(solution)/shard_map/ppermute | solution.py:392
  567.9 24.8 %collective-permute-start.40 = (bf16[4,2,64,1024]{3,2,0,1:T(8,128)(2,1)S(1)}, bf16[4,2,64,1024]{3,2,0,1:T(8,128)(2,1)S(1)}, u32[]{:S(2)}, u32[]{:S(2)}) collective-permute-start(bf16[4,2,64,1024]{3,2,0,1:T(8,128)(2,1)S(1)} %fusion.31), channel_id=1, source_target_pairs={{0,2},{1,3},{2,0},{3,1},{4,6},{5,7},{6,4},{7,5},{8,10},{9,11},{10,... | collective-permute-start | bytes 3145736 | tf_op jit(solution)/shard_map/ppermute | solution.py:288
  571.9 25.5 %collective-permute-start.43 = (bf16[4,2,64,1024]{3,2,0,1:T(8,128)(2,1)S(1)}, bf16[4,2,64,1024]{3,2,0,1:T(8,128)(2,1)S(1)}, u32[]{:S(2)}, u32[]{:S(2)}) collective-permute-start(bf16[4,2,64,1024]{3,2,0,1:T(8,128)(2,1)S(1)} %fusion.27), channel_id=1, source_target_pairs={{0,4},{1,5},{2,6},{3,7},{4,0},{5,1},{6,2},{7,3},{8,12},{9,13},{10,... | collective-permute-start | bytes 3145736 | tf_op jit(solution)/shard_map/ppermute | solution.py:288
  594.0 55.4 %collective-permute-start.41 = (bf16[4,64,1024]{2,1,0:T(8,128)(2,1)}, bf16[4,64,1024]{2,1,0:T(8,128)(2,1)S(1)}, u32[]{:S(2)}, u32[]{:S(2)}) collective-permute-start(bf16[4,64,1024]{2,1,0:T(8,128)(2,1)} %dynamic-slice_bitcast_fusion.3), channel_id=1, source_target_pairs={{0,4},{1,5},{2,6},{3,7},{4,0},{5,1},{6,2},{7,3},{8,12},{9,13},{10,... | collective-permute-start | bytes 1572872 | tf_op jit(solution)/shard_map/ppermute | solution.py:288
  598.7 51.0 %collective-permute-start.44 = (bf16[4,64,1024]{2,1,0:T(8,128)(2,1)}, bf16[4,64,1024]{2,1,0:T(8,128)(2,1)S(1)}, u32[]{:S(2)}, u32[]{:S(2)}) collective-permute-start(bf16[4,64,1024]{2,1,0:T(8,128)(2,1)} %dynamic-slice_bitcast_fusion.2), channel_id=1, source_target_pairs={{0,2},{1,3},{2,0},{3,1},{4,6},{5,7},{6,4},{7,5},{8,10},{9,11},{10,... | collective-permute-start | bytes 1572872 | tf_op jit(solution)/shard_map/ppermute | solution.py:288
  600.3 52.6 %collective-permute-start.33 = (bf16[256,1024]{1,0:T(8,128)(2,1)}, bf16[256,1024]{1,0:T(8,128)(2,1)}, u32[]{:S(2)}, u32[]{:S(2)}) collective-permute-start(bf16[256,1024]{1,0:T(8,128)(2,1)} %get-tuple-element.205), channel_id=1, source_target_pairs={{0,0},{16,1},{2,2},{18,3},{4,4},{20,5},{6,6},{22,7},{8,8},{24,9},{... | collective-permute-start | bytes 1572872 | tf_op jit(solution)/shard_map/ppermute | solution.py:333
  605.7 48.5 %collective-permute-start.34 = (bf16[256,1024]{1,0:T(8,128)(2,1)}, bf16[256,1024]{1,0:T(8,128)(2,1)}, u32[]{:S(2)}, u32[]{:S(2)}) collective-permute-start(bf16[256,1024]{1,0:T(8,128)(2,1)} %get-tuple-element.204), channel_id=1, source_target_pairs={{8,0},{24,1},{10,2},{26,3},{12,4},{28,5},{14,6},{30,7},{0,8},{16,9... | collective-permute-start | bytes 1572872 | tf_op jit(solution)/shard_map/ppermute | solution.py:333
  649.9 9.2 %collective-permute-start.47 = (bf16[128,1024]{1,0:T(8,128)(2,1)S(1)}, bf16[128,1024]{1,0:T(8,128)(2,1)S(1)}, u32[]{:S(2)}, u32[]{:S(2)}) collective-permute-start(bf16[128,1024]{1,0:T(8,128)(2,1)S(1)} %get-tuple-element.197), channel_id=1, source_target_pairs={{0,24},{8,0},{16,8},{24,16},{1,25},{9,1},{17,9},{25,17},{2,26},{10... | collective-permute-start | bytes 786440 | tf_op jit(solution)/shard_map/ppermute | solution.py:392
  652.3 21.2 %collective-permute-start.46 = (bf16[128,1024]{1,0:T(8,128)(2,1)S(1)}, bf16[128,1024]{1,0:T(8,128)(2,1)S(1)}, u32[]{:S(2)}, u32[]{:S(2)}) collective-permute-start(bf16[128,1024]{1,0:T(8,128)(2,1)S(1)} %get-tuple-element.196), channel_id=1, source_target_pairs={{0,16},{8,24},{16,0},{24,8},{1,17},{9,25},{17,1},{25,9},{2,18},{10... | collective-permute-start | bytes 786440 | tf_op jit(solution)/shard_map/ppermute | solution.py:392
  652.3 21.2 %collective-permute-start.45 = (bf16[128,1024]{1,0:T(8,128)(2,1)S(1)}, bf16[128,1024]{1,0:T(8,128)(2,1)S(1)}, u32[]{:S(2)}, u32[]{:S(2)}) collective-permute-start(bf16[128,1024]{1,0:T(8,128)(2,1)S(1)} %get-tuple-element.195), channel_id=1, source_target_pairs={{0,8},{8,16},{16,24},{24,0},{1,9},{9,17},{17,25},{25,1},{2,10},{10... | collective-permute-start | bytes 786440 | tf_op jit(solution)/shard_map/ppermute | solution.py:392
  (143 other events, 1142.4 us)

commit v2 on v1

--- a/solution.py
+++ b/solution.py
@@ -1,5 +1,8 @@
+import functools
+
 import jax
 import jax.numpy as jnp
+import numpy as np
 from jax import lax
 from jax.experimental import pallas as pl
 from jax.experimental.pallas import tpu as pltpu
@@ -29,39 +32,76 @@
     return lax.dot_general(left, right, dims, preferred_element_type=WIDE)
 
 
-def bucket_of(relative):
-    distance = jnp.abs(relative)
-    magnitude = jnp.zeros(relative.shape, jnp.int32)
-    for threshold in THRESHOLDS:
-        magnitude = magnitude + (distance >= threshold).astype(jnp.int32)
-    return magnitude + jnp.where(relative > 0, BUCKETS // 2, 0).astype(jnp.int32)
-
-
 def gelu_parts(value):
     cumulative = 0.5 * (1.0 + lax.erf(value * ROOT_HALF))
     slope = cumulative + value * jnp.exp(-0.5 * value * value) * NORMAL_PEAK
     return (value * cumulative, slope)
 
 
-def near_tables(columns):
-    side = jnp.arange(HALF_ROWS, dtype=jnp.int32)
-    tiles = []
-    for shift in (-1, 0, 1):
-        buckets = bucket_of(side[None, :] - side[:, None] + HALF_ROWS * shift)
-        tile = jnp.zeros((columns.shape[1],) + buckets.shape, WIDE)
-        for number in range(BUCKETS):
-            tile = jnp.where((buckets == number)[None], columns[number][:, None, None], tile)
-        tiles.append(tile)
-    flat = [jnp.broadcast_to(columns[number][:, None, None], tiles[0].shape) for number in (15, 31)]
-    before, centre, after = tiles
-    wide = jnp.concatenate(
-        [
-            jnp.concatenate([before, centre, after, flat[1]], axis=2),
-            jnp.concatenate([flat[0], before, centre, after], axis=2),
-        ],
-        axis=1,
-    )
-    return (wide, jnp.swapaxes(wide, 1, 2))
+CORE, ALONG_X, ALONG_Y = (1, 2, 4)
+
+
+def partner(bit):
+    index = lax.axis_index("fsdp")
+    return index + bit - 2 * bit * ((index // bit) % 2)
+
+
+def chip_of(*bits):
+    index = lax.axis_index("fsdp")
+    for bit in bits:
+        index = index + bit - 2 * bit * ((index // bit) % 2)
+    return index // 2
+
+
+def send(source, target, sems, number, bit):
+    return pltpu.make_async_remote_copy(
+        src_ref=source,
+        dst_ref=target,
+        send_sem=sems.at[0, number],
+        recv_sem=sems.at[1, number],
+        device_id={"fsdp": partner(bit)},
+        device_id_type=pl.DeviceIdType.MESH,
+    )
+
+
+def greet(bits):
+    barrier = pltpu.get_barrier_semaphore()
+    for bit in bits:
+        pl.semaphore_signal(
+            barrier, inc=1, device_id={"fsdp": partner(bit)}, device_id_type=pl.DeviceIdType.MESH
+        )
+    pl.semaphore_wait(barrier, len(bits))
+
+
+def bucket_columns(distances):
+    distances = np.asarray(distances)
+    magnitude = sum((np.abs(distances) >= threshold).astype(np.int32) for threshold in THRESHOLDS)
+    buckets = magnitude + np.where(distances > 0, BUCKETS // 2, 0)
+    return (buckets[None, :] == np.arange(BUCKETS)[:, None]).astype(np.float32)
+
+
+def near_bias(columns):
+    chosen = jnp.asarray(bucket_columns(np.arange(2 * QUERY_ROWS) - HALF_ROWS))
+    line = lax.dot_general(columns, chosen, TN, precision=lax.Precision.HIGHEST, preferred_element_type=WIDE)
+    return line[:, None, :]
+
+
+def near_block(line):
+    shape = (QUERY_ROWS, 2 * QUERY_ROWS)
+    turned = pltpu.roll(jnp.broadcast_to(line, shape), 0, 1, stride=1, stride_axis=0)
+    row = lax.broadcasted_iota(jnp.int32, shape, 0)
+    column = lax.broadcasted_iota(jnp.int32, shape, 1)
+    return jnp.where(column < row, line[:, :1], turned)
+
+
+def diagonal_sums(tile):
+    side = tile.shape[1]
+    row = lax.broadcasted_iota(jnp.int32, tile.shape, 0)
+    step = 1
+    while step < side:
+        tile = jnp.where((row // step) % 2 == 1, pltpu.roll(tile, side - step, 1), tile)
+        step *= 2
+    return jnp.sum(tile, axis=0, keepdims=True)
 
 
 def spare_lanes(length, rows):
@@ -81,20 +121,66 @@
     out[1] = jnp.where(low_half, spare, pair)
 
 
-def attend_kernel(
-    length_ref, ends_ref, query_ref, key_ref, value_ref, near_ref, context_ref, log_ref, bias, keys, values
-):
+def gather_moves(mine, wholes, sems):
+    chip = chip_of()
+    direct = []
+    for number, (one, whole_one) in enumerate(zip(mine, wholes)):
+        for place, bit in enumerate((ALONG_X, ALONG_Y)):
+            direct.append(send(one, whole_one.at[chip], sems, 2 * number + place, bit))
+    first = wholes[0]
+    half = first.shape[1] // 2
+    onward = []
+    for place, (bit, came) in enumerate(((ALONG_X, ALONG_Y), (ALONG_Y, ALONG_X))):
+        piece = first.at[chip_of(came), pl.ds(place * half, half)]
+        onward.append(send(piece, piece, sems, 2 * len(mine) + place, bit))
+    return (direct, onward)
+
+
+def attend_kernel(gathered, length_ref, query_ref, key_ref, value_ref, near_ref, *refs):
+    mine, refs = (refs[:gathered], refs[gathered:])
+    context_ref, log_ref = refs[:2]
+    wholes, refs = (refs[2 : 2 + gathered], refs[2 + gathered :])
+    bias, keys, values = refs[:3]
     rows = query_ref.shape[0]
-    pair = pl.program_id(0)
+    if gathered:
+        sems, local = refs[3:]
+        pair = pl.program_id(0)
+        direct, onward = gather_moves(mine, wholes, sems)
+        own = pltpu.make_async_copy(mine[0], wholes[0].at[chip_of()], local)
+
+        @pl.when(pair == 0)
+        def _():
+            greet((ALONG_X, ALONG_Y))
+            own.start()
+            for one in direct:
+                one.start()
+
+        @pl.when(pair == 1)
+        def _():
+            for one in direct[:2]:
+                one.wait_recv()
+            for one in onward:
+                one.start()
+
+        @pl.when(pair == pl.num_programs(0) - 1)
+        def _():
+            own.wait()
+            for one in direct:
+                one.wait_send()
+            for one in direct[2:]:
+                one.wait_recv()
+            for one in onward:
+                one.wait()
+
     split_heads(key_ref[...], spare_lanes(length_ref[0], rows), keys)
     split_heads(value_ref[...], jnp.zeros((rows, LANES), LOW), values)
     near_start = rows - QUERY_ROWS - HALF_ROWS
     near_end = near_start + 2 * QUERY_ROWS
     for head in range(2):
-        left, right = (ends_ref[2 * pair + head, 0], ends_ref[2 * pair + head, 1])
-        bias[head, :, :near_start] = jnp.full((QUERY_ROWS, near_start), left, WIDE)
-        bias[head, :, near_start:near_end] = near_ref[head]
-        bias[head, :, near_end:] = jnp.full((QUERY_ROWS, bias.shape[2] - near_end), right, WIDE)
+        line = near_ref[head]
+        bias[head, :, :near_start] = jnp.broadcast_to(line[:, :1], (QUERY_ROWS, near_start))
+        bias[head, :, near_start:near_end] = near_block(line)
+        bias[head, :, near_end:] = jnp.broadcast_to(line[:, -1:], (QUERY_ROWS, bias.shape[2] - near_end))
     lane = lax.broadcasted_iota(jnp.int32, (QUERY_ROWS, LANES), 1)
     ones = jnp.where(lax.rem(lane, HEAD_DIM) == 0, 1.0, 0.0).astype(LOW)
 
@@ -120,37 +206,44 @@
     lax.fori_loop(0, rows // QUERY_ROWS, block, 0)
 
 
-def attend(length, ends, query, key, value, near):
+def attend(length, query, key, value, near, mine=()):
     rows, width = query.shape
     pairs = width // LANES
+    anywhere = pl.BlockSpec(memory_space=pl.ANY)
+    gathered = len(mine)
     smem = pl.BlockSpec(memory_space=pltpu.SMEM)
     columns = pl.BlockSpec((rows, LANES), lambda pair: (0, pair))
     return pl.pallas_call(
-        attend_kernel,
+        functools.partial(attend_kernel, gathered),
         grid=(pairs,),
-        in_specs=[smem, smem, columns, columns, columns]
-        + [pl.BlockSpec((2, QUERY_ROWS, 2 * QUERY_ROWS), lambda pair: (pair, 0, 0))],
-        out_specs=[columns, pl.BlockSpec((1, 2, rows), lambda pair: (pair, 0, 0))],
+        in_specs=[smem, columns, columns, columns]
+        + [pl.BlockSpec((2, 1, 2 * QUERY_ROWS), lambda pair: (pair, 0, 0))]
+        + [anywhere] * gathered,
+        out_specs=[columns, pl.BlockSpec((1, 2, rows), lambda pair: (pair, 0, 0))] + [anywhere] * gathered,
         out_shape=[
             jax.ShapeDtypeStruct((rows, width), LOW),
             jax.ShapeDtypeStruct((pairs, 2, rows), WIDE),
-        ],
+        ]
+        + [jax.ShapeDtypeStruct((4,) + one.shape, LOW) for one in mine],
         scratch_shapes=[
             pltpu.VMEM((2, QUERY_ROWS, 2 * rows - QUERY_ROWS), WIDE),
             pltpu.VMEM((2, rows, LANES), LOW),
             pltpu.VMEM((2, rows, LANES), LOW),
-        ],
-        compiler_params=pltpu.CompilerParams(vmem_limit_bytes=40 << 20),
+        ]
+        + ([pltpu.SemaphoreType.DMA((2, 2 * gathered + 2)), pltpu.SemaphoreType.DMA] if gathered else []),
+        compiler_params=pltpu.CompilerParams(
+            vmem_limit_bytes=40 << 20,
+            **({"collective_id": 1, "has_side_effects": True} if gathered else {}),
+        ),
         cost_estimate=pl.CostEstimate(
             flops=24 * rows * rows * width, bytes_accessed=8 * rows * width, transcendentals=2 * pairs * rows * rows
         ),
         name="attend",
-    )(length, ends, query, key, value, near)
+    )(length, query, key, value, near, *mine)
 
 
 def attend_grad_kernel(
     length_ref,
-    ends_ref,
     query_ref,
     key_ref,
     value_ref,
@@ -160,32 +253,33 @@
     query_grad_ref,
     key_grad_ref,
     value_grad_ref,
-    tiles_ref,
-    far_ref,
+    sums_ref,
     bias,
     keys,
     values,
     padded,
     key_total,
     value_total,
+    tiles,
 ):
     rows = query_ref.shape[0]
     blocks = rows // QUERY_ROWS
-    pair = pl.program_id(0)
     split_heads(key_ref[...], spare_lanes(length_ref[0], rows), keys)
     split_heads(value_ref[...], jnp.zeros((rows, LANES), LOW), values)
     near_start = rows - QUERY_ROWS - HALF_ROWS
     near_end = near_start + 2 * QUERY_ROWS
     for head in range(2):
-        left, right = (ends_ref[2 * pair + head, 0], ends_ref[2 * pair + head, 1])
-        bias[head, :near_start, :] = jnp.full((near_start, QUERY_ROWS), left, WIDE)
-        bias[head, near_start:near_end, :] = near_ref[head]
-        bias[head, near_end:, :] = jnp.full((bias.shape[1] - near_end, QUERY_ROWS), right, WIDE)
+        line = near_ref[head]
+        bias[head, :near_start, :] = jnp.broadcast_to(line[:, :1], (near_start, QUERY_ROWS))
+        bias[head, near_start:near_end, :] = near_block(line).T
+        bias[head, near_end:, :] = jnp.broadcast_to(line[:, -1:], (bias.shape[1] - near_end, QUERY_ROWS))
         padded[head, :HALF_ROWS, :] = jnp.zeros((HALF_ROWS, QUERY_ROWS), LOW)
         padded[head, rows + HALF_ROWS :, :] = jnp.zeros((HALF_ROWS, QUERY_ROWS), LOW)
     key_total[...] = jnp.zeros_like(key_total)
     value_total[...] = jnp.zeros_like(value_total)
-    tiles_ref[...] = jnp.zeros_like(tiles_ref)
+    tiles[...] = jnp.zeros_like(tiles)
+    sums_ref[...] = jnp.zeros_like(sums_ref)
+    spot = lax.broadcasted_iota(jnp.int32, (1, LANES), 1)
     lane = lax.broadcasted_iota(jnp.int32, (QUERY_ROWS, LANES), 1)
     ones = jnp.where(lax.rem(lane, HEAD_DIM) == 0, 1.0, 0.0).astype(LOW)
     zero = jnp.zeros((), LOW)
@@ -210,15 +304,18 @@
             padded[head, HALF_ROWS : HALF_ROWS + rows, :] = score
             part = dot(score, keys[head], TN)
             parts.append(part)
-            far_ref[0, head, pl.ds(number, 1), :] = jnp.sum(part, axis=0, keepdims=True)
+            columns = jnp.sum(part, axis=0, keepdims=True)
+            spare = HEAD_DIM * (1 - head) + 1 + number
             close = padded[head, pl.ds(start, 2 * QUERY_ROWS), :].astype(WIDE)
             quarter = [close[HALF_ROWS * step : HALF_ROWS * (step + 1)] for step in range(4)]
             for step in range(3):
-                tiles_ref[head, step] += quarter[step][:, :HALF_ROWS] + quarter[step + 1][:, HALF_ROWS:]
-            corner = jnp.sum(quarter[0][:, HALF_ROWS:], axis=0, keepdims=True)
-            far_ref[0, head, pl.ds(blocks + number, 1), :] = corner
-            corner = jnp.sum(quarter[3][:, :HALF_ROWS], axis=0, keepdims=True)
-            far_ref[0, head, pl.ds(2 * blocks + number, 1), :] = corner
+                tiles[head, step] += quarter[step][:, :HALF_ROWS] + quarter[step + 1][:, HALF_ROWS:]
+            left = jnp.sum(quarter[0][:, HALF_ROWS:], axis=0, keepdims=True)
+            right = jnp.sum(quarter[3][:, :HALF_ROWS], axis=0, keepdims=True)
+            left = left + jnp.where(spot == spare, columns, 0.0)
+            right = right + jnp.where(spot == spare + blocks, columns, 0.0)
+            sums_ref[0, 4 * head + 2 : 4 * head + 3, :] += left
+            sums_ref[0, 4 * head + 3 : 4 * head + 4, :] += right
         chosen = jnp.where(lane < HEAD_DIM, parts[0], parts[1])
         query_grad_ref[pl.ds(start, QUERY_ROWS), :] = chosen.astype(LOW)
         return carry
@@ -226,26 +323,32 @@
     lax.fori_loop(0, blocks, block, 0)
     key_grad_ref[...] = key_total[...].astype(LOW)
     value_grad_ref[...] = value_total[...].astype(LOW)
-
-
-def attend_grad(length, ends, query, key, value, grad, logs, near):
+    shape = (HALF_ROWS, HALF_ROWS)
+    upper = lax.broadcasted_iota(jnp.int32, shape, 0) <= lax.broadcasted_iota(jnp.int32, shape, 1)
+    for head in range(2):
+        before, centre, behind = (tiles[head, step] for step in range(3))
+        sums_ref[0, 4 * head : 4 * head + 1, :] = diagonal_sums(jnp.where(upper, centre, before))
+        sums_ref[0, 4 * head + 1 : 4 * head + 2, :] = diagonal_sums(jnp.where(upper, behind, centre))
+        left = jnp.sum(jnp.where(upper, before, 0.0), axis=0, keepdims=True)
+        right = jnp.sum(jnp.where(upper, 0.0, behind), axis=0, keepdims=True)
+        sums_ref[0, 4 * head + 2 : 4 * head + 3, :] += left
+        sums_ref[0, 4 * head + 3 : 4 * head + 4, :] += right
+
+
+def attend_grad(length, query, key, value, grad, logs, near):
     rows, width = query.shape
     pairs = width // LANES
-    blocks = rows // QUERY_ROWS
     smem = pl.BlockSpec(memory_space=pltpu.SMEM)
     columns = pl.BlockSpec((rows, LANES), lambda pair: (0, pair))
     shape = jax.ShapeDtypeStruct
     return pl.pallas_call(
         attend_grad_kernel,
         grid=(pairs,),
-        in_specs=[smem, smem, columns, columns, columns, columns]
+        in_specs=[smem, columns, columns, columns, columns]
         + [pl.BlockSpec((1, 2, rows), lambda pair: (pair, 0, 0))]
-        + [pl.BlockSpec((2, 2 * QUERY_ROWS, QUERY_ROWS), lambda pair: (pair, 0, 0))],
-        out_specs=[columns, columns, columns]
-        + [pl.BlockSpec((2, 3, HALF_ROWS, HALF_ROWS), lambda pair: (pair, 0, 0, 0))]
-        + [pl.BlockSpec((1, 2, 3 * blocks, LANES), lambda pair: (pair, 0, 0, 0))],
-        out_shape=[shape((rows, width), LOW)] * 3
-        + [shape((2 * pairs, 3, HALF_ROWS, HALF_ROWS), WIDE), shape((pairs, 2, 3 * blocks, LANES), WIDE)],
+        + [pl.BlockSpec((2, 1, 2 * QUERY_ROWS), lambda pair: (pair, 0, 0))],
+        out_specs=[columns, columns, columns] + [pl.BlockSpec((1, 8, LANES), lambda pair: (pair, 0, 0))],
+        out_shape=[shape((rows, width), LOW)] * 3 + [shape((pairs, 8, LANES), WIDE)],
         scratch_shapes=[
             pltpu.VMEM((2, 2 * rows - QUERY_ROWS, QUERY_ROWS), WIDE),
             pltpu.VMEM((2, rows, LANES), LOW),
@@ -253,34 +356,172 @@
             pltpu.VMEM((2, rows + QUERY_ROWS, QUERY_ROWS), LOW),
             pltpu.VMEM((rows, LANES), WIDE),
             pltpu.VMEM((rows, LANES), WIDE),
+            pltpu.VMEM((2, 3, HALF_ROWS, HALF_ROWS), WIDE),
         ],
         compiler_params=pltpu.CompilerParams(vmem_limit_bytes=48 << 20),
         cost_estimate=pl.CostEstimate(
             flops=44 * rows * rows * width, bytes_accessed=14 * rows * width, transcendentals=2 * pairs * rows * rows
         ),
         name="attend_grad",
-    )(length, ends, query, key, value, grad, logs, near)
-
-
-def bucket_sums(tiles, far):
-    heads = tiles.shape[0]
-    pairs = far.shape[0]
-    blocks = far.shape[2] // 3
-    side = jnp.arange(HALF_ROWS, dtype=jnp.int32)
-    relative = jnp.stack([side[:, None] - side[None, :] + HALF_ROWS * shift for shift in (-1, 0, 1)])
-    buckets = bucket_of(relative)
-    sums = jnp.stack(
-        [jnp.sum(jnp.where((buckets == number)[None], tiles, 0.0), axis=(1, 2, 3)) for number in range(BUCKETS)]
-    )
-    corners = jnp.sum(far.reshape(pairs, 2, 3, blocks, LANES)[:, :, 1:], axis=(3, 4))
-    left, right = (corners[:, :, 0], corners[:, :, 1])
-    for number in range(blocks):
-        spare = [far[:, head, number, HEAD_DIM * (1 - head) + 1 :] for head in range(2)]
-        left = left + jnp.stack([one[:, number] for one in spare], axis=1)
-        right = right + jnp.stack([one[:, blocks + number] for one in spare], axis=1)
-    ends = jnp.zeros((BUCKETS, heads), WIDE)
-    ends = ends.at[BUCKETS // 2 - 1].set(left.reshape(heads)).at[BUCKETS - 1].set(right.reshape(heads))
-    return sums + ends
+    )(length, query, key, value, grad, logs, near)
+
+
+def bucket_sums(sums):
+    pairs = sums.shape[0]
+    side = np.arange(LANES)
+    far = np.full((LANES,), 2 * HALF_ROWS)
+    chosen = bucket_columns(np.concatenate([-side, HALF_ROWS - side, -far, far]))
+    return lax.dot_general(
+        jnp.asarray(chosen),
+        sums.reshape(2 * pairs, 4 * LANES),
+        NT,
+        precision=lax.Precision.HIGHEST,
+        preferred_element_type=WIDE,
+    )
+
+
+def feed_kernel(pieces, normed_ref, grad_ref, *refs):
+    moved = pieces > 1
+    kinds = 2
+    mine, refs = (refs[:kinds], refs[kinds:])
+    if moved:
+        wholes, refs = (refs[:kinds], refs[kinds:])
+    parts, refs = (refs[:kinds], refs[kinds:])
+    out_ref, back_ref = refs[:2]
+    refs = refs[2:]
+    if moved:
+        fars, refs = (refs[:kinds], refs[kinds:])
+    slots, stages, refs = (refs[:2], refs[2:4], refs[4:])
+    arrived, stored = refs[:2]
+    step, steps = (pl.program_id(0), pl.num_programs(0))
+    unit = slots[0].shape[1]
+    slot = lax.rem(step, 2)
+
+    if moved:
+        sems = refs[2]
+        half = unit // 2
+        moves = []
+        for kind in range(kinds):
+            for place, (bit, came) in enumerate(((ALONG_X, ALONG_Y), (ALONG_Y, ALONG_X))):
+                there = pl.ds(place * half, half)
+                source = wholes[kind].at[chip_of(came), there]
+                moves.append(send(source, fars[kind].at[there], sems, 2 * kind + place, bit))
+        sources = [
+            mine,
+            [one.at[chip_of(ALONG_X)] for one in wholes],
+            [one.at[chip_of(ALONG_Y)] for one in wholes],
+            fars,
+        ]
+        places = [chip_of(), chip_of(ALONG_X), chip_of(ALONG_Y), chip_of(ALONG_X, ALONG_Y)]
+
+        def fetch(block, into):
+            for number, pair in enumerate(sources):
+
+                @pl.when(block == number)
+                def _():
+                    for kind in range(kinds):
+                        pltpu.make_async_copy(pair[kind], slots[kind].at[into], arrived.at[kind, into]).start()
+
+        def store(block, kind, from_slot, act):
+            for number, place in enumerate(places):
+
+                @pl.when(block == number)
+                def _():
+                    act(
+                        pltpu.make_async_copy(
+                            stages[kind].at[from_slot],
+                            parts[kind].at[pl.ds(pl.multiple_of(place * unit, unit), unit)],
+                            stored.at[kind, from_slot],
+                        )
+                    )
+    else:
+
+        def fetch(block, into):
+            rows = pl.ds(pl.multiple_of(block * unit, unit), unit)
+            for kind in range(kinds):
+                pltpu.make_async_copy(mine[kind].at[rows], slots[kind].at[into], arrived.at[kind, into]).start()
+
+        def store(block, kind, from_slot, act):
+            rows = pl.ds(pl.multiple_of(block * unit, unit), unit)
+            act(pltpu.make_async_copy(stages[kind].at[from_slot], parts[kind].at[rows], stored.at[kind, from_slot]))
+
+    @pl.when(step == 0)
+    def _():
+        if moved:
+            greet((ALONG_X, ALONG_Y))
+            for one in moves:
+                one.start()
+        fetch(0, 0)
+        out_ref[...] = jnp.zeros_like(out_ref)
+        back_ref[...] = jnp.zeros_like(back_ref)
+
+    @pl.when(step + 1 < steps - moved)
+    def _():
+        fetch(step + 1, 1 - slot)
+
+    for kind in range(kinds):
+        pltpu.make_async_copy(slots[kind].at[slot], slots[kind].at[slot], arrived.at[kind, slot]).wait()
+    up, down = (slots[0][slot], slots[1][slot])
+    normed, grad = (normed_ref[...], grad_ref[...])
+    active, slope = gelu_parts(dot(normed, up, NT))
+    active = active.astype(LOW)
+    pre_grad = (dot(grad, down, NT) * slope).astype(LOW)
+    out_ref[...] += dot(active, down)
+    back_ref[...] += dot(pre_grad, up)
+
+    @pl.when(step >= 2)
+    def _():
+        for kind in range(kinds):
+            store(step - 2, kind, slot, lambda copy: copy.wait())
+
+    stages[0][slot] = dot(pre_grad, normed, TN).astype(LOW)
+    stages[1][slot] = dot(active, grad, TN).astype(LOW)
+    for kind in range(kinds):
+        store(step, kind, slot, lambda copy: copy.start())
+
+    if moved:
+
+        @pl.when(step == steps - 2)
+        def _():
+            for one in moves:
+                one.wait()
+            fetch(step + 1, 1 - slot)
+
+    @pl.when(step == steps - 1)
+    def _():
+        for kind in range(kinds):
+            store(step - 1, kind, 1 - slot, lambda copy: copy.wait())
+            store(step, kind, slot, lambda copy: copy.wait())
+
+
+def feed(normed, grad, mine, wholes=()):
+    rows, width = normed.shape
+    moved = bool(wholes)
+    unit = mine[0].shape[0] if moved else mine[0].shape[0] // 4
+    anywhere = pl.BlockSpec(memory_space=pl.ANY)
+    fixed = pl.BlockSpec((rows, width), lambda step: (0, 0))
+    return pl.pallas_call(
+        functools.partial(feed_kernel, 4 if moved else 1),
+        grid=(4,),
+        in_specs=[fixed, fixed] + [anywhere] * (4 if moved else 2),
+        out_specs=[anywhere, anywhere, fixed, fixed] + ([anywhere, anywhere] if moved else []),
+        out_shape=[jax.ShapeDtypeStruct((4 * unit, width), LOW)] * 2
+        + [jax.ShapeDtypeStruct((rows, width), WIDE)] * 2
+        + ([jax.ShapeDtypeStruct((unit, width), LOW)] * 2 if moved else []),
+        scratch_shapes=[pltpu.VMEM((2, unit, width), LOW)] * 4
+        + [pltpu.SemaphoreType.DMA((2, 2)), pltpu.SemaphoreType.DMA((2, 2))]
+        + ([pltpu.SemaphoreType.DMA((2, 4))] if moved else []),
+        compiler_params=pltpu.CompilerParams(
+            vmem_limit_bytes=56 << 20,
+            **({"collective_id": 2, "has_side_effects": True} if moved else {}),
+        ),
+        cost_estimate=pl.CostEstimate(
+            flops=48 * unit * rows * width,
+            bytes_accessed=32 * unit * width + 12 * rows * width,
+            transcendentals=8 * unit * rows,
+        ),
+        name="feed",
+    )(normed, grad, *mine, *wholes)[:4]
 
 
 def flip(value, bit):
@@ -349,21 +590,23 @@
     return kept + other_core(sent)
 
 
-def gather_plane(mine, first=()):
-    mine = after(mine, *first)
+def gather_near(mine):
+    return (flip(mine, 2), flip(mine, 4))
+
+
+def gather_far(beside, above):
+    half = beside.shape[0] // 2
+    return (flip(above[:half], 2), flip(beside[half:], 4))
+
+
+def in_order(mine, beside, above, far):
     chip = lax.axis_index("fsdp") // 2
-    half = mine.shape[0] // 2
-    beside = flip(mine, 2)
-    above = flip(mine, 4)
-    across_one = flip(above[:half], 2)
-    across_two = flip(beside[half:], 4)
     out = jnp.zeros((4,) + mine.shape, mine.dtype)
     out = lax.dynamic_update_index_in_dim(out, mine, chip, 0)
     out = lax.dynamic_update_index_in_dim(out, beside, chip ^ 1, 0)
     out = lax.dynamic_update_index_in_dim(out, above, chip ^ 2, 0)
-    out = lax.dynamic_update_slice(out, across_one[None], (chip ^ 3, 0, 0))
-    out = lax.dynamic_update_slice(out, across_two[None], (chip ^ 3, half, 0))
-    return (out, (across_one, across_two))
+    out = lax.dynamic_update_slice(out, far[0][None], (chip ^ 3, 0, 0))
+    return lax.dynamic_update_slice(out, far[1][None], (chip ^ 3, mine.shape[0] // 2, 0))
 
 
 def fast_plane():
@@ -394,17 +637,16 @@
     return total
 
 
-def scatter_plane(parts, first=()):
+def scatter_plane(one, two):
     chip = lax.axis_index("fsdp") // 2
     x, y = (chip % 2, chip // 2)
-    one, two = parts
-    one_got = flip(after(pick(one, 1 - x, 2), *first), 2)
-    two_got = flip(after(pick(two, 1 - y, 1), *first), 4)
+    one_got = flip(pick(one, 1 - x, 2), 2)
+    two_got = flip(pick(two, 1 - y, 1), 4)
     one = add_low(pick(one, x, 2), one_got)
     two = add_low(pick(two, y, 1), two_got)
     one_last = flip(pick(one, 1 - y, 1), 4)
     two_last = flip(pick(two, 1 - x, 1), 2)
-    return (add_low(pick(one, y, 1), one_last), add_low(pick(two, x, 1), two_last)), (one_last, two_last)
+    return (add_low(pick(one, y, 1), one_last), add_low(pick(two, x, 1), two_last))
 
 
 def shards(
@@ -440,28 +682,22 @@
 
     own_table = lax.dynamic_index_in_dim(bias_table.reshape(BUCKETS, 4, 2, 2), core, 2, keepdims=False)
     own_table = own_table.reshape(BUCKETS, HEADS // 2)
-    near, near_turned = near_tables(own_table)
-    ends = jnp.stack([own_table[BUCKETS // 2 - 1], own_table[BUCKETS - 1]], axis=1)
+    near = near_bias(own_table)
 
     ffn = up_weight.shape[0]
     if fast:
         stacked = jnp.concatenate([query_weight, key_weight, value_weight], axis=0)
-        heads_low, done = gather_plane(stacked)
-        heads_low = heads_low.reshape(4, 3, -1, width)
-        own_three = [heads_low[:, number].reshape(-1, width) for number in range(3)]
-        own_output, done = gather_plane(output_weight, done)
-        own_output = own_output.reshape(-1, width)
-        far_output = other_core(own_output)
         cut = jnp.stack([up_weight, down_weight]).reshape(2, 2, 2, -1, width)
         swapped = other_core(pick(cut, 1 - core, 2))
         kept = pick(cut, core, 2)
         cut = jnp.where(
             core == 0, jnp.stack([kept, swapped], axis=1), jnp.stack([swapped, kept], axis=1)
-        )
-        own_up, done = gather_plane(cut[0].reshape(-1, width), done)
-        own_down, done = gather_plane(cut[1].reshape(-1, width), done)
-        own_up = own_up.reshape(-1, width)
-        own_down = own_down.reshape(-1, width)
+        ).reshape(2, -1, width)
+        up_mine, down_mine = (cut[0], cut[1])
+        beside, above = gather_near(stacked)
+        far = gather_far(beside, above)
+        heads_low = in_order(stacked, beside, above, far).reshape(4, 3, -1, width)
+        own_three = [heads_low[:, number].reshape(-1, width) for number in range(3)]
     else:
         own_three = [
             own_head_rows(lax.all_gather(one, "fsdp", axis=0, tiled=True), core)
@@ -483,7 +719,15 @@
     scaled_one = source * rms_one
     normed_one = whole((scaled_one * attn_gain).astype(LOW), core)
     query, key, value = [dot(normed_one, one, NT).astype(LOW) for one in own_three]
-    context, logs = attend(length, ends, query, key, value, near)
+    if fast:
+        mine = (output_weight, up_mine, down_mine)
+        context, logs, own_output, *wholes = attend(length, query, key, value, near, mine)
+        own_output = own_output.reshape(-1, width)
+        far_output = other_core(own_output)
+        mine = mine[1:]
+    else:
+        context, logs = attend(length, query, key, value, near)
+        mine, wholes = ((own_up, own_down), ())
     near_context = lax.dynamic_slice_in_dim(context, core * rows, rows, 0)
     far_context = other_core(lax.dynamic_slice_in_dim(context, (1 - core) * rows, rows, 0))
     hidden_one = source + (dot(near_context, own_output) + dot(far_context, far_output))
@@ -492,16 +736,12 @@
     normed_two = whole((scaled_two * ffn_gain).astype(LOW), core)
     grad_out = to_sequence(cotangent).astype(WIDE) * mask_rows
     grad_low = whole(grad_out.astype(LOW), core)
-    active, slope = gelu_parts(dot(normed_two, own_up, NT))
-    active = active.astype(LOW)
-    mlp_out = fold(dot(active, own_down), core)
+    up_part, down_part, mlp_part, normed_part = feed(normed_two, grad_low, mine, wholes)
+    normed_grad = fold(normed_part, core)
+    mlp_out = fold(mlp_part, core)
     layer_rows = ((hidden_one + mlp_out) * mask_rows).astype(LOW)
     layer_out = to_slots(layer_rows, held)
 
-    pre_grad = (dot(grad_low, own_down, NT) * slope).astype(LOW)
-    normed_grad = fold(dot(pre_grad, own_up), core)
-    up_part = dot(pre_grad, normed_two, TN).astype(LOW)
-    down_part = dot(active, grad_low, TN).astype(LOW)
     gained_two = ffn_gain * normed_grad
     hidden_grad = grad_out + rms_two * (
         gained_two - scaled_two * jnp.mean(gained_two * scaled_two, axis=1, keepdims=True)
@@ -518,8 +758,8 @@
     near_output_part = dot(near_context, hidden_low, TN).astype(LOW)
     far_output_part = dot(far_context, hidden_low, TN).astype(LOW)
 
-    query_low, key_low, value_low, tiles, far = attend_grad(
-        length, ends, query, key, value, context_grad, logs, near_turned
+    query_low, key_low, value_low, distance_sums = attend_grad(
+        length, query, key, value, context_grad, logs, near
     )
     lows = (query_low, key_low, value_low)
     normed_one_grad = dot(query_low, own_three[0]) + dot(key_low, own_three[1]) + dot(value_low, own_three[2])
@@ -534,7 +774,7 @@
 
     if fast:
         blocks = (depth, 2, 2, -1, width)
-        (up_some, down_some), done = scatter_plane((up_part.reshape(blocks), down_part.reshape(blocks)))
+        up_some, down_some = scatter_plane(up_part.reshape(blocks), down_part.reshape(blocks))
         up_grad, down_grad = (spread_depth(up_some), spread_depth(down_some))
 
         def to_parity(kept, sent):
@@ -554,7 +794,7 @@
         )
         one = jnp.concatenate(outs[:2], axis=3)
         two = jnp.concatenate(outs[2:], axis=3)
-        (one, two), done = scatter_plane((one, two), done)
+        one, two = scatter_plane(one, two)
         attention = spread_depth(jnp.concatenate([one, two], axis=1))
         attention = attention.reshape(4, -1, width)
         query_grad, key_grad, value_grad, output_grad = [attention[number] for number in range(4)]
@@ -578,11 +818,23 @@
         )
         output_grad = summed(pair.reshape(-1, width))
 
-    bias_own = bucket_sums(tiles, far).reshape(BUCKETS, 4, 1, 2)
+    bias_own = bucket_sums(distance_sums).reshape(BUCKETS, 4, 1, 2)
     bias_full = lax.dynamic_update_slice(
         jnp.zeros((BUCKETS, 4, 2, 2), WIDE), bias_own, (0, 0, core, 0)
     ).reshape(BUCKETS, HEADS)
-    attn_gain_sum, ffn_gain_sum, bias_sum = lax.psum((attn_gain_part, ffn_gain_part, bias_full), BOTH)
+    if fast:
+        small = jnp.concatenate([attn_gain_part, ffn_gain_part, bias_full.reshape(-1)]).reshape(-1, LANES)
+        for bit in (1, 2, 4):
+            small = small + flip(small, bit)
+        moved = [
+            lax.ppermute(small, "seq", [(one, (one + step) % depth) for one in range(depth)])
+            for step in range(1, depth)
+        ]
+        small = sum(moved, small).reshape(-1)
+        attn_gain_sum, ffn_gain_sum = (small[:width], small[width : 2 * width])
+        bias_sum = small[2 * width :].reshape(BUCKETS, HEADS)
+    else:
+        attn_gain_sum, ffn_gain_sum, bias_sum = lax.psum((attn_gain_part, ffn_gain_part, bias_full), BOTH)
     gain_rows = width // size
     bucket_rows = BUCKETS // size
     attn_gain_grad = lax.dynamic_slice_in_dim(attn_gain_sum, index * gain_rows, gain_rows, 0)

time: 686 us -> 492 us (0.72)
  Pallas kernels: 69.6 us -> 152 us
  other arithmetic: 118 us -> 39.1 us
  waiting for transfers between devices: 188 us -> 136 us
  matrix products: 71.8 us -> 26.3 us
  blocking collectives: 41.4 us -> 0 us
  local copies, waits for them, and re-layouts: 88.5 us -> 54.9 us
  starting transfers between devices: 93.7 us -> 72.5 us
    pallas_call x2 -> x3, Pallas kernels: 69.6 us -> 152 us  [the longest x1 62.4 us: attend(): pl.pallas_call(functools.partial(attend_kernel, gathered), grid=(pairs,),...]
    ppermute x37 -> x28, waiting for transfers between devices: 148 us -> 78.4 us  [flip(): lax.ppermute(value, 'fsdp', [(one, one ^ bit) for one in range(size)])]
    eq x98 -> x0, other arithmetic: 55.3 us -> none  [the longest x96 52.1 us: near_tables(): buckets == number]
    dot_general x21 -> x15, matrix products: 71.8 us -> 26 us  [dot(): return lax.dot_general(left, right, dims, preferred_element_type=WIDE)]
    psum x1 -> x0, blocking collectives: 41.4 us -> none  [shards(): lax.psum((attn_gain_part, ffn_gain_part, bias_full), BOTH)]
    ppermute x37 -> x28, starting transfers between devices: 46.9 us -> 20.8 us  [flip(): lax.ppermute(value, 'fsdp', [(one, one ^ bit) for one in range(size)])]
    broadcast_in_dim x36 -> x2, local copies, waits for them, and re-layouts: 19.7 us -> 2.06 us  [the longest x1 2.05 us: in_order(): out = jnp.zeros((4,) + mine.shape, mine.dtype)]
    ppermute x9, waiting for transfers between devices: 40.3 us -> 51.4 us  [spread_depth(): lax.ppermute(sent, 'seq', [(one, (one + step) % depth) for one in range(d...]
  transfers between devices with their start and end apart: 54 -> 48, of which waited for: 20 -> 17; matrix products, arithmetic and copies ran while one was open for 40% -> 21% of each run, Pallas kernels for 10% -> 23%
where the time goes in v2:
time: 492 us; the launch traced here: 483 us
  Pallas kernels  152 us (31%)
  waiting for transfers between devices  136 us (28%)
  starting transfers between devices  72.5 us (15%)
  local copies, waits for them, and re-layouts  54.9 us (11%)
  other arithmetic  39.1 us (8%)
  matrix products  26.3 us (5%)
    ppermute x28, waiting for transfers between devices, flip(): lax.ppermute(value, 'fsdp', [(one, one ^ bit) for one in range(size)])  78.4 us
    pallas_call x1, Pallas kernels, attend(): pl.pallas_call(functools.partial(attend_kernel, gathered), grid=(pairs,),...  62.4 us
    ppermute x9, waiting for transfers between devices, spread_depth(): lax.ppermute(sent, 'seq', [(one, (one + step) % depth) for one in range(d...  51.4 us
    pallas_call x1, Pallas kernels, attend_grad(): pl.pallas_call(attend_grad_kernel, grid=(pairs,), in_specs=[smem, columns...  48.1 us
    pallas_call x1, Pallas kernels, feed(): pl.pallas_call(functools.partial(feed_kernel, 4 if moved else 1), grid=(4...  41.5 us
    dot_general x15, matrix products, dot(): return lax.dot_general(left, right, dims, preferred_element_type=WIDE)  26 us
    ppermute x4, starting transfers between devices, to_slots(): got = lax.ppermute(sent, BOTH, pairs)  25.1 us
    ppermute x28, starting transfers between devices, flip(): lax.ppermute(value, 'fsdp', [(one, one ^ bit) for one in range(size)])  20.8 us
  transfers between devices with their start and end apart: 48, of which 17 were waited for; matrix products, arithmetic and copies ran while one was open for 21% of the time, Pallas kernels for 23%

profile of v2, /device:TPU:0, one launch (start us, length us, event | category | flops | bytes accessed | tf_op | source)
XLA Modules:
  0.0 483.3 jit_solution(646858240377212684)
XLA Ops:
  3.7 3.0 collective-permute-start.4
  9.2 5.4 %collective-permute-start = (bf16[256,1024]{1,0:T(8,128)(2,1)}, bf16[256,1024]{1,0:T(8,128)(2,1)}, u32[]{:S(2)}, u32[]{:S(2)}) collective-permute-start(bf16[256,1024]{1,0:T(8,128)(2,1)} %get-tuple-element.85), channel_id=1, source_target_pairs={{0,0},{1,16},{2,2},{3,18},{4,4},{5,20},{6,6},{7,22},{8,8},{9,24},{... | collective-permute-start | bytes 1572872 | tf_op jit(solution)/shard_map/ppermute | solution.py:562
  16.2 2.1 broadcast_in_dim.61
  20.4 2.7 fusion.31
  25.0 1.7 collective-permute-start.12
  27.9 6.3 %collective-permute-done.1 = bf16[256,1024]{1,0:T(8,128)(2,1)} collective-permute-done((bf16[256,1024]{1,0:T(8,128)(2,1)}, bf16[256,1024]{1,0:T(8,128)(2,1)}, u32[]{:S(2)}, u32[]{:S(2)}) %collective-permute-start.1) | collective-permute-done | bytes 524320 | tf_op jit(solution)/shard_map/ppermute | solution.py:562
  36.0 2.5 collective-permute-start.3
  42.1 7.5 %collective-permute-done.6 = bf16[192,1024]{1,0:T(8,128)(2,1)S(1)} collective-permute-done((bf16[192,1024]{1,0:T(8,128)(2,1)S(1)}, bf16[192,1024]{1,0:T(8,128)(2,1)S(1)}, u32[]{:S(2)}, u32[]{:S(2)}) %collective-permute-start.6) | collective-permute-done | bytes 393248 | tf_op jit(solution)/shard_map/ppermute | solution.py:529
  52.6 2.2 fusion.59
  58.8 62.4 %attend.1 = (bf16[1024,512]{1,0:T(8,128)(2,1)S(1)}, f32[4,2,1024]{2,1,0:T(2,128)S(1)}, bf16[4,128,1024]{2,1,0:T(8,128)(2,1)S(1)}, bf16[4,512,1024]{2,1,0:T(8,128)(2,1)S(1)}, bf16[4,512,1024]{2,1,0:T(8,128)(2,1)}) custom-call(s32[1]{0:T(128)} %dynamic_slice.185.length_ref, bf16[1024,512]{1,0:T(8,128)(2,1)S(1)} %convolution_convert_fusion.5.query_ref, ...), custom_call_target="tpu_custom_call" | custom-call | flops 12884901888 | bytes 4194304 | tf_op jit(solution)/shard_map/attend/pallas_call | solution.py:216
  128.2 2.4 maximum_select_fusion.3.grad_ref
  130.7 2.3 maximum_select_fusion.2.normed_ref
  133.0 41.5 %feed.1 = (bf16[2048,1024]{1,0:T(8,128)(2,1)}, bf16[2048,1024]{1,0:T(8,128)(2,1)}, f32[1024,1024]{1,0:T(8,128)}, f32[1024,1024]{1,0:T(8,128)}, bf16[512,1024]{1,0:T(8,128)(2,1)}, /*index=5*/bf16[512,1024]{1,0:T(8,128)(2,1)}) custom-call(bf16[1024,1024]{1,0:T(8,128)(2,1)} %maximum_select_fusion.2.normed_ref, ...), custom_call_target="tpu_custom_call" | custom-call | flops 25769803776 | bytes 29360128 | tf_op jit(solution)/shard_map/feed/pallas_call | solution.py:503
  174.5 3.3 constant_dynamic-slice_fusion.14
  179.9 4.0 constant_dynamic-slice_fusion.4
  186.9 2.9 constant_dynamic-slice_fusion.6
  191.5 2.8 multiply_reduce_fusion
  194.3 4.1 fusion.57
  199.2 34.0 %collective-permute-done.37 = bf16[4,2,128,1024]{3,2,0,1:T(8,128)(2,1)} collective-permute-done((bf16[4,2,128,1024]{3,2,0,1:T(8,128)(2,1)}, bf16[4,2,128,1024]{3,2,0,1:T(8,128)(2,1)}, u32[]{:S(2)}, u32[]{:S(2)}) %collective-permute-start.37) | collective-permute-done | bytes 2097184 | tf_op jit(solution)/shard_map/ppermute | solution.py:529
  233.3 2.6 fusion
  246.5 5.5 %collective-permute-start.16 = (bf16[256,1024]{1,0:T(8,128)(2,1)}, bf16[256,1024]{1,0:T(8,128)(2,1)}, u32[]{:S(2)}, u32[]{:S(2)}) collective-permute-start(bf16[256,1024]{1,0:T(8,128)(2,1)} %get-tuple-element.81), channel_id=1, source_target_pairs={{0,0},{16,1},{2,2},{18,3},{4,4},{20,5},{6,6},{22,7},{8,8},{24,9},{... | collective-permute-start | bytes 1572872 | tf_op jit(solution)/shard_map/ppermute | solution.py:574
  252.8 14.2 %collective-permute-start.17 = (bf16[256,1024]{1,0:T(8,128)(2,1)}, bf16[256,1024]{1,0:T(8,128)(2,1)}, u32[]{:S(2)}, u32[]{:S(2)}) collective-permute-start(bf16[256,1024]{1,0:T(8,128)(2,1)} %get-tuple-element.80), channel_id=1, source_target_pairs={{8,0},{24,1},{10,2},{26,3},{12,4},{28,5},{14,6},{30,7},{0,8},{16,9... | collective-permute-start | bytes 1572872 | tf_op jit(solution)/shard_map/ppermute | solution.py:574
  268.4 48.1 %attend_grad.1 = (bf16[1024,512]{1,0:T(8,128)(2,1)S(1)}, bf16[1024,512]{1,0:T(8,128)(2,1)S(1)}, bf16[1024,512]{1,0:T(8,128)(2,1)S(1)}, f32[4,8,128]{2,1,0:T(8,128)S(1)}) custom-call(s32[1]{0:T(128)} %dynamic_slice.185.length_ref, bf16[1024,512]{1,0:T(8,128)(2,1)S(1)} %copy-done.11, bf16[1024,512]{1,0:T(8,128)(2,1)S(1)} %copy-done.9, ...), custom_call_target="tpu_custom_call" | custom-call | flops 23622320128 | bytes 7340032 | tf_op jit(solution)/shard_map/attend_grad/pallas_call | solution.py:344
  316.6 3.3 fusion.64
  319.9 3.3 fusion.63
  323.3 6.9 %add_add_fusion = f32[1024,1024]{1,0:T(8,128)} fusion(f32[1024,1024]{1,0:T(8,128)} %fusion.63, f32[1024,1024]{1,0:T(8,128)} %fusion.64, bf16[1024,512]{1,0:T(8,128)(2,1)S(1)} %get-tuple-element.33, bf16[512,1024]{1,0:T(8,128)(2,1)S(1)} %bitcast.269), kind=kOutput, calls=%fused_computation.4 | convolution fusion | flops 1075838976 | bytes 14680064 | tf_op jit(solution)/shard_map/dot_general | solution.py:32
  337.0 1.9 copy-done.17
  343.2 1.7 fusion.2
  345.0 2.2 collective-permute-start.40
  347.3 1.7 collective-permute-start.41
  350.5 5.6 %collective-permute-done.39 = bf16[128,1024]{1,0:T(8,128)(2,1)S(1)} collective-permute-done((bf16[128,1024]{1,0:T(8,128)(2,1)S(1)}, bf16[128,1024]{1,0:T(8,128)(2,1)S(1)}, u32[]{:S(2)}, u32[]{:S(2)}) %collective-permute-start.39) | collective-permute-done | bytes 262176 | tf_op jit(solution)/shard_map/ppermute | solution.py:635
  356.1 11.1 %collective-permute-done.40 = bf16[128,1024]{1,0:T(8,128)(2,1)S(1)} collective-permute-done((bf16[128,1024]{1,0:T(8,128)(2,1)S(1)}, bf16[128,1024]{1,0:T(8,128)(2,1)S(1)}, u32[]{:S(2)}, u32[]{:S(2)}) %collective-permute-start.40) | collective-permute-done | bytes 262176 | tf_op jit(solution)/shard_map/ppermute | solution.py:635
  367.2 5.8 %collective-permute-start.36 = (bf16[128,1024]{1,0:T(8,128)(2,1)S(1)}, bf16[128,1024]{1,0:T(8,128)(2,1)S(1)}, u32[]{:S(2)}, u32[]{:S(2)}) collective-permute-start(bf16[128,1024]{1,0:T(8,128)(2,1)S(1)} %get-tuple-element.67), channel_id=1, source_target_pairs={{0,24},{8,0},{16,8},{24,16},{1,25},{9,1},{17,9},{25,17},{2,26},{10... | collective-permute-start | bytes 786440 | tf_op jit(solution)/shard_map/ppermute | solution.py:635
  375.4 13.5 %collective-permute-done.35 = bf16[128,1024]{1,0:T(8,128)(2,1)S(1)} collective-permute-done((bf16[128,1024]{1,0:T(8,128)(2,1)S(1)}, bf16[128,1024]{1,0:T(8,128)(2,1)S(1)}, u32[]{:S(2)}, u32[]{:S(2)}) %collective-permute-start.35) | collective-permute-done | bytes 262176 | tf_op jit(solution)/shard_map/ppermute | solution.py:635
  388.9 4.7 collective-permute-done.36
  399.4 2.1 collective-permute-start.24
  401.6 24.2 %collective-permute-done.43 = f32[20,128]{1,0:T(8,128)S(1)} collective-permute-done((f32[20,128]{1,0:T(8,128)S(1)}, f32[20,128]{1,0:T(8,128)S(1)}, u32[]{:S(2)}, u32[]{:S(2)}) %collective-permute-start.43) | collective-permute-done | bytes 10272 | tf_op jit(solution)/shard_map/ppermute | solution.py:529
  425.7 1.7 collective-permute-start.44
  429.4 1.9 collective-permute-start.45
  431.9 1.8 collective-permute-start.47
  434.9 5.4 %collective-permute-start.21 = (bf16[256,1024]{1,0:T(8,128)(2,1)}, bf16[256,1024]{1,0:T(8,128)(2,1)}, u32[]{:S(2)}, u32[]{:S(2)}) collective-permute-start(bf16[256,1024]{1,0:T(8,128)(2,1)} %get-tuple-element.79), channel_id=1, source_target_pairs={{0,0},{16,1},{2,2},{18,3},{4,4},{20,5},{6,6},{22,7},{8,8},{24,9},{... | collective-permute-start | bytes 1572872 | tf_op jit(solution)/shard_map/ppermute | solution.py:574
  440.4 1.7 fusion.4
  442.2 1.8 collective-permute-start.28
  447.8 6.8 %collective-permute-done.28 = bf16[4,64,1024]{2,1,0:T(8,128)(2,1)S(1)} collective-permute-done((bf16[4,64,1024]{2,1,0:T(8,128)(2,1)S(1)}, bf16[4,64,1024]{2,1,0:T(8,128)(2,1)S(1)}, u32[]{:S(2)}, u32[]{:S(2)}) %collective-permute-start.28) | collective-permute-done | bytes 524320 | tf_op jit(solution)/shard_map/ppermute | solution.py:529
  454.8 2.6 collective-permute-done.25
  458.3 2.2 collective-permute-start.30
  465.6 3.2 collective-permute-done.29
  468.8 13.4 %collective-permute-done.30 = bf16[128,1024]{1,0:T(8,128)(2,1)S(1)} collective-permute-done((bf16[128,1024]{1,0:T(8,128)(2,1)S(1)}, bf16[128,1024]{1,0:T(8,128)(2,1)S(1)}, u32[]{:S(2)}, u32[]{:S(2)}) %collective-permute-start.30) | collective-permute-done | bytes 262176 | tf_op jit(solution)/shard_map/ppermute | solution.py:635
  (295 shorter events, 87.8 us)
Async XLA Ops:
  3.7 34.8 %collective-permute-start.4 = (bf16[384,1024]{1,0:T(8,128)(2,1)S(1)}, bf16[384,1024]{1,0:T(8,128)(2,1)S(1)}, u32[]{:S(2)}, u32[]{:S(2)}) collective-permute-start(bf16[384,1024]{1,0:T(8,128)(2,1)S(1)} %constant_dynamic-update-slice_fusion), channel_id=1, source_target_pairs={{0,2},{1,3},{2,0},{3,1},{4,6},{5,7},{6,4},{7,5},{8,10},{9,11},{10,... | collective-permute-start | bytes 2359304 | tf_op jit(solution)/shard_map/ppermute | solution.py:529
  6.7 29.3 %collective-permute-start.5 = (bf16[384,1024]{1,0:T(8,128)(2,1)S(1)}, bf16[384,1024]{1,0:T(8,128)(2,1)S(1)}, u32[]{:S(2)}, u32[]{:S(2)}) collective-permute-start(bf16[384,1024]{1,0:T(8,128)(2,1)S(1)} %constant_dynamic-update-slice_fusion), channel_id=1, source_target_pairs={{0,4},{1,5},{2,6},{3,7},{4,0},{5,1},{6,2},{7,3},{8,12},{9,13},{10,... | collective-permute-start | bytes 2359304 | tf_op jit(solution)/shard_map/ppermute | solution.py:529
  9.2 15.8 %collective-permute-start = (bf16[256,1024]{1,0:T(8,128)(2,1)}, bf16[256,1024]{1,0:T(8,128)(2,1)}, u32[]{:S(2)}, u32[]{:S(2)}) collective-permute-start(bf16[256,1024]{1,0:T(8,128)(2,1)} %get-tuple-element.85), channel_id=1, source_target_pairs={{0,0},{1,16},{2,2},{3,18},{4,4},{5,20},{6,6},{7,22},{8,8},{9,24},{... | collective-permute-start | bytes 1572872 | tf_op jit(solution)/shard_map/ppermute | solution.py:562
  14.6 19.6 %collective-permute-start.1 = (bf16[256,1024]{1,0:T(8,128)(2,1)}, bf16[256,1024]{1,0:T(8,128)(2,1)}, u32[]{:S(2)}, u32[]{:S(2)}) collective-permute-start(bf16[256,1024]{1,0:T(8,128)(2,1)} %get-tuple-element.84), channel_id=1, source_target_pairs={{0,8},{1,24},{2,10},{3,26},{4,12},{5,28},{6,14},{7,30},{8,0},{9,16... | collective-permute-start | bytes 1572872 | tf_op jit(solution)/shard_map/ppermute | solution.py:562
  16.2 6.9 %collective-permute-start.2 = (s32[2]{0:T(128)S(1)}, s32[2]{0:T(128)S(1)}, u32[]{:S(2)}, u32[]{:S(2)}) collective-permute-start(s32[2]{0:T(128)S(1)} %copy-done.54), channel_id=1, source_target_pairs={{0,1},{1,0},{2,3},{3,2},{4,5},{5,4},{6,7},{7,6},{8,9},{9,8},{10,11... | collective-permute-start | bytes 32 | tf_op jit(solution)/shard_map/ppermute | solution.py:529
  23.1 17.9 %collective-permute-start.8 = (bf16[2,2,128,1024]{3,2,1,0:T(8,128)(2,1)}, bf16[2,2,128,1024]{3,2,1,0:T(8,128)(2,1)S(1)}, u32[]{:S(2)}, u32[]{:S(2)}) collective-permute-start(bf16[2,2,128,1024]{3,2,1,0:T(8,128)(2,1)} %get-tuple-element.59), channel_id=1, source_target_pairs={{0,1},{1,0},{2,3},{3,2},{4,5},{5,4},{6,7},{7,6},{8,9},{9,8},{10,11... | collective-permute-start | bytes 3145736 | tf_op jit(solution)/shard_map/ppermute | solution.py:529
  25.0 96.3 %collective-permute-start.12 = (bf16[256,1024]{1,0:T(8,128)(2,1)}, bf16[256,1024]{1,0:T(8,128)(2,1)S(1)}, u32[]{:S(2)}, u32[]{:S(2)}) collective-permute-start(bf16[256,1024]{1,0:T(8,128)(2,1)} %get-tuple-element.83), channel_id=1, source_target_pairs={{0,0},{1,16},{2,2},{3,18},{4,4},{5,20},{6,6},{7,22},{8,8},{9,24},{... | collective-permute-start | bytes 1572872 | tf_op jit(solution)/shard_map/ppermute | solution.py:562
  34.2 87.3 %collective-permute-start.13 = (bf16[256,1024]{1,0:T(8,128)(2,1)S(1)}, bf16[256,1024]{1,0:T(8,128)(2,1)S(1)}, u32[]{:S(2)}, u32[]{:S(2)}) collective-permute-start(bf16[256,1024]{1,0:T(8,128)(2,1)S(1)} %copy-done.46), channel_id=1, source_target_pairs={{0,8},{1,24},{2,10},{3,26},{4,12},{5,28},{6,14},{7,30},{8,0},{9,16... | collective-permute-start | bytes 1572872 | tf_op jit(solution)/shard_map/ppermute | solution.py:562
  36.0 18.8 %collective-permute-start.3 = (bf16[512,1024]{1,0:T(8,128)(2,1)S(1)}, bf16[512,1024]{1,0:T(8,128)(2,1)S(1)}, u32[]{:S(2)}, u32[]{:S(2)}) collective-permute-start(bf16[512,1024]{1,0:T(8,128)(2,1)S(1)} %fusion.12), channel_id=1, source_target_pairs={{0,1},{1,0},{2,3},{3,2},{4,5},{5,4},{6,7},{7,6},{8,9},{9,8},{10,11... | collective-permute-start | bytes 3145736 | tf_op jit(solution)/shard_map/ppermute | solution.py:529
  38.5 11.1 %collective-permute-start.6 = (bf16[192,1024]{1,0:T(8,128)(2,1)S(1)}, bf16[192,1024]{1,0:T(8,128)(2,1)S(1)}, u32[]{:S(2)}, u32[]{:S(2)}) collective-permute-start(bf16[192,1024]{1,0:T(8,128)(2,1)S(1)} %slice.106), channel_id=1, source_target_pairs={{0,2},{1,3},{2,0},{3,1},{4,6},{5,7},{6,4},{7,5},{8,10},{9,11},{10,... | collective-permute-start | bytes 1179656 | tf_op jit(solution)/shard_map/ppermute | solution.py:529
  41.1 10.8 %collective-permute-start.7 = (bf16[192,1024]{1,0:T(8,128)(2,1)S(1)}, bf16[192,1024]{1,0:T(8,128)(2,1)S(1)}, u32[]{:S(2)}, u32[]{:S(2)}) collective-permute-start(bf16[192,1024]{1,0:T(8,128)(2,1)S(1)} %slice.107), channel_id=1, source_target_pairs={{0,4},{1,5},{2,6},{3,7},{4,0},{5,1},{6,2},{7,3},{8,12},{9,13},{10,... | collective-permute-start | bytes 1179656 | tf_op jit(solution)/shard_map/ppermute | solution.py:529
  121.3 3.9 collective-permute-start.10
  123.3 1.9 collective-permute-start.9
  123.6 4.6 collective-permute-start.14
  128.0 2.7 collective-permute-start.11
  177.8 12.8 %collective-permute-start.18 = (f32[512,1024]{1,0:T(8,128)}, f32[512,1024]{1,0:T(8,128)}, u32[]{:S(2)}, u32[]{:S(2)}) collective-permute-start(f32[512,1024]{1,0:T(8,128)} %constant_dynamic-slice_fusion.14), channel_id=1, source_target_pairs={{0,1},{1,0},{2,3},{3,2},{4,5},{5,4},{6,7},{7,6},{8,9},{9,8},{10,11... | collective-permute-start | bytes 6291464 | tf_op jit(solution)/shard_map/ppermute | solution.py:529
  179.4 14.9 %collective-permute-start.15 = (f32[512,1024]{1,0:T(8,128)}, f32[512,1024]{1,0:T(8,128)}, u32[]{:S(2)}, u32[]{:S(2)}) collective-permute-start(f32[512,1024]{1,0:T(8,128)} %constant_dynamic-slice_fusion.15), channel_id=1, source_target_pairs={{0,1},{1,0},{2,3},{3,2},{4,5},{5,4},{6,7},{7,6},{8,9},{9,8},{10,11... | collective-permute-start | bytes 6291464 | tf_op jit(solution)/shard_map/ppermute | solution.py:529
  185.4 47.9 %collective-permute-start.37 = (bf16[4,2,128,1024]{3,2,0,1:T(8,128)(2,1)}, bf16[4,2,128,1024]{3,2,0,1:T(8,128)(2,1)}, u32[]{:S(2)}, u32[]{:S(2)}) collective-permute-start(bf16[4,2,128,1024]{3,2,0,1:T(8,128)(2,1)} %bitcast.253), channel_id=1, source_target_pairs={{0,4},{1,5},{2,6},{3,7},{4,0},{5,1},{6,2},{7,3},{8,12},{9,13},{10,... | collective-permute-start | bytes 6291464 | tf_op jit(solution)/shard_map/ppermute | solution.py:529
  190.0 49.2 %collective-permute-start.32 = (bf16[4,2,128,1024]{3,2,0,1:T(8,128)(2,1)S(1)}, bf16[4,2,128,1024]{3,2,0,1:T(8,128)(2,1)S(1)}, u32[]{:S(2)}, u32[]{:S(2)}) collective-permute-start(bf16[4,2,128,1024]{3,2,0,1:T(8,128)(2,1)S(1)} %bitcast.277), channel_id=1, source_target_pairs={{0,2},{1,3},{2,0},{3,1},{4,6},{5,7},{6,4},{7,5},{8,10},{9,11},{10,... | collective-permute-start | bytes 6291464 | tf_op jit(solution)/shard_map/ppermute | solution.py:529
  199.1 53.7 %collective-permute-start.19 = (bf16[512,512]{1,0:T(8,128)(2,1)S(1)}, bf16[512,512]{1,0:T(8,128)(2,1)S(1)}, u32[]{:S(2)}, u32[]{:S(2)}) collective-permute-start(bf16[512,512]{1,0:T(8,128)(2,1)S(1)} %convolution_convert_fusion.8), channel_id=1, source_target_pairs={{0,1},{1,0},{2,3},{3,2},{4,5},{5,4},{6,7},{7,6},{8,9},{9,8},{10,11... | collective-permute-start | bytes 1572872 | tf_op jit(solution)/shard_map/ppermute | solution.py:529
  237.0 106.3 %collective-permute-start.38 = (bf16[4,128,1024]{2,1,0:T(8,128)(2,1)}, bf16[4,128,1024]{2,1,0:T(8,128)(2,1)}, u32[]{:S(2)}, u32[]{:S(2)}) collective-permute-start(bf16[4,128,1024]{2,1,0:T(8,128)(2,1)} %dynamic-slice_bitcast_fusion), channel_id=1, source_target_pairs={{0,2},{1,3},{2,0},{3,1},{4,6},{5,7},{6,4},{7,5},{8,10},{9,11},{10,... | collective-permute-start | bytes 3145736 | tf_op jit(solution)/shard_map/ppermute | solution.py:529
  241.3 103.8 %collective-permute-start.33 = (bf16[4,128,1024]{2,1,0:T(8,128)(2,1)}, bf16[4,128,1024]{2,1,0:T(8,128)(2,1)}, u32[]{:S(2)}, u32[]{:S(2)}) collective-permute-start(bf16[4,128,1024]{2,1,0:T(8,128)(2,1)} %dynamic-slice_bitcast_fusion.1), channel_id=1, source_target_pairs={{0,4},{1,5},{2,6},{3,7},{4,0},{5,1},{6,2},{7,3},{8,12},{9,13},{10,... | collective-permute-start | bytes 3145736 | tf_op jit(solution)/shard_map/ppermute | solution.py:529
  245.5 101.8 %collective-permute-start.26 = (bf16[2,4,2,32,1024]{4,3,1,2,0:T(8,128)(2,1)}, bf16[2,4,2,32,1024]{4,3,1,2,0:T(8,128)(2,1)}, u32[]{:S(2)}, u32[]{:S(2)}) collective-permute-start(bf16[2,4,2,32,1024]{4,3,1,2,0:T(8,128)(2,1)} %pad_maximum_fusion.1), channel_id=1, source_target_pairs={{0,1},{1,0},{2,3},{3,2},{4,5},{5,4},{6,7},{7,6},{8,9},{9,8},{10,11... | collective-permute-start | bytes 3145736 | tf_op jit(solution)/shard_map/ppermute | solution.py:529
  246.5 92.7 %collective-permute-start.16 = (bf16[256,1024]{1,0:T(8,128)(2,1)}, bf16[256,1024]{1,0:T(8,128)(2,1)}, u32[]{:S(2)}, u32[]{:S(2)}) collective-permute-start(bf16[256,1024]{1,0:T(8,128)(2,1)} %get-tuple-element.81), channel_id=1, source_target_pairs={{0,0},{16,1},{2,2},{18,3},{4,4},{20,5},{6,6},{22,7},{8,8},{24,9},{... | collective-permute-start | bytes 1572872 | tf_op jit(solution)/shard_map/ppermute | solution.py:574
  252.8 87.9 %collective-permute-start.17 = (bf16[256,1024]{1,0:T(8,128)(2,1)}, bf16[256,1024]{1,0:T(8,128)(2,1)}, u32[]{:S(2)}, u32[]{:S(2)}) collective-permute-start(bf16[256,1024]{1,0:T(8,128)(2,1)} %get-tuple-element.80), channel_id=1, source_target_pairs={{8,0},{24,1},{10,2},{26,3},{12,4},{28,5},{14,6},{30,7},{0,8},{16,9... | collective-permute-start | bytes 1572872 | tf_op jit(solution)/shard_map/ppermute | solution.py:574
  339.3 57.2 %collective-permute-start.20 = (f32[512,1024]{1,0:T(8,128)S(1)}, f32[512,1024]{1,0:T(8,128)S(1)}, u32[]{:S(2)}, u32[]{:S(2)}) collective-permute-start(f32[512,1024]{1,0:T(8,128)S(1)} %constant_dynamic-slice_fusion.13), channel_id=1, source_target_pairs={{0,1},{1,0},{2,3},{3,2},{4,5},{5,4},{6,7},{7,6},{8,9},{9,8},{10,11... | collective-permute-start | bytes 6291464 | tf_op jit(solution)/shard_map/ppermute | solution.py:529
  340.7 53.9 %collective-permute-start.23 = (bf16[3,4,2,32,1024]{4,3,1,2,0:T(8,128)(2,1)S(1)}, bf16[3,4,2,32,1024]{4,3,1,2,0:T(8,128)(2,1)S(1)}, u32[]{:S(2)}, u32[]{:S(2)}) collective-permute-start(bf16[3,4,2,32,1024]{4,3,1,2,0:T(8,128)(2,1)S(1)} %copy_bitcast_fusion.4), channel_id=1, source_target_pairs={{0,1},{1,0},{2,3},{3,2},{4,5},{5,4},{6,7},{7,6},{8,9},{9,8},{10,11... | collective-permute-start | bytes 4718600 | tf_op jit(solution)/shard_map/ppermute | solution.py:529
  345.0 11.1 %collective-permute-start.39 = (bf16[128,1024]{1,0:T(8,128)(2,1)S(1)}, bf16[128,1024]{1,0:T(8,128)(2,1)S(1)}, u32[]{:S(2)}, u32[]{:S(2)}) collective-permute-start(bf16[128,1024]{1,0:T(8,128)(2,1)S(1)} %get-tuple-element.63), channel_id=1, source_target_pairs={{0,8},{8,16},{16,24},{24,0},{1,9},{9,17},{17,25},{25,1},{2,10},{10... | collective-permute-start | bytes 786440 | tf_op jit(solution)/shard_map/ppermute | solution.py:635
  345.0 22.1 %collective-permute-start.40 = (bf16[128,1024]{1,0:T(8,128)(2,1)S(1)}, bf16[128,1024]{1,0:T(8,128)(2,1)S(1)}, u32[]{:S(2)}, u32[]{:S(2)}) collective-permute-start(bf16[128,1024]{1,0:T(8,128)(2,1)S(1)} %get-tuple-element.65), channel_id=1, source_target_pairs={{0,16},{8,24},{16,0},{24,8},{1,17},{9,25},{17,1},{25,9},{2,18},{10... | collective-permute-start | bytes 786440 | tf_op jit(solution)/shard_map/ppermute | solution.py:635
  347.3 19.9 %collective-permute-start.41 = (bf16[128,1024]{1,0:T(8,128)(2,1)S(1)}, bf16[128,1024]{1,0:T(8,128)(2,1)S(1)}, u32[]{:S(2)}, u32[]{:S(2)}) collective-permute-start(bf16[128,1024]{1,0:T(8,128)(2,1)S(1)} %get-tuple-element.64), channel_id=1, source_target_pairs={{0,24},{8,0},{16,8},{24,16},{1,25},{9,1},{17,9},{25,17},{2,26},{10... | collective-permute-start | bytes 786440 | tf_op jit(solution)/shard_map/ppermute | solution.py:635
  356.1 19.3 %collective-permute-start.34 = (bf16[128,1024]{1,0:T(8,128)(2,1)S(1)}, bf16[128,1024]{1,0:T(8,128)(2,1)S(1)}, u32[]{:S(2)}, u32[]{:S(2)}) collective-permute-start(bf16[128,1024]{1,0:T(8,128)(2,1)S(1)} %get-tuple-element.66), channel_id=1, source_target_pairs={{0,8},{8,16},{16,24},{24,0},{1,9},{9,17},{17,25},{25,1},{2,10},{10... | collective-permute-start | bytes 786440 | tf_op jit(solution)/shard_map/ppermute | solution.py:635
  367.2 21.8 %collective-permute-start.35 = (bf16[128,1024]{1,0:T(8,128)(2,1)S(1)}, bf16[128,1024]{1,0:T(8,128)(2,1)S(1)}, u32[]{:S(2)}, u32[]{:S(2)}) collective-permute-start(bf16[128,1024]{1,0:T(8,128)(2,1)S(1)} %get-tuple-element.68), channel_id=1, source_target_pairs={{0,16},{8,24},{16,0},{24,8},{1,17},{9,25},{17,1},{25,9},{2,18},{10... | collective-permute-start | bytes 786440 | tf_op jit(solution)/shard_map/ppermute | solution.py:635
  367.2 26.5 %collective-permute-start.36 = (bf16[128,1024]{1,0:T(8,128)(2,1)S(1)}, bf16[128,1024]{1,0:T(8,128)(2,1)S(1)}, u32[]{:S(2)}, u32[]{:S(2)}) collective-permute-start(bf16[128,1024]{1,0:T(8,128)(2,1)S(1)} %get-tuple-element.67), channel_id=1, source_target_pairs={{0,24},{8,0},{16,8},{24,16},{1,25},{9,1},{17,9},{25,17},{2,26},{10... | collective-permute-start | bytes 786440 | tf_op jit(solution)/shard_map/ppermute | solution.py:635
  396.2 44.3 %collective-permute-start.27 = (bf16[4,2,64,1024]{3,2,0,1:T(8,128)(2,1)}, bf16[4,2,64,1024]{3,2,0,1:T(8,128)(2,1)}, u32[]{:S(2)}, u32[]{:S(2)}) collective-permute-start(bf16[4,2,64,1024]{3,2,0,1:T(8,128)(2,1)} %fusion.21), channel_id=1, source_target_pairs={{0,4},{1,5},{2,6},{3,7},{4,0},{5,1},{6,2},{7,3},{8,12},{9,13},{10,... | collective-permute-start | bytes 3145736 | tf_op jit(solution)/shard_map/ppermute | solution.py:529
  398.2 3.2 collective-permute-start.42
  399.4 44.6 %collective-permute-start.24 = (bf16[4,2,64,1024]{3,2,0,1:T(8,128)(2,1)}, bf16[4,2,64,1024]{3,2,0,1:T(8,128)(2,1)}, u32[]{:S(2)}, u32[]{:S(2)}) collective-permute-start(bf16[4,2,64,1024]{3,2,0,1:T(8,128)(2,1)} %fusion.25), channel_id=1, source_target_pairs={{0,2},{1,3},{2,0},{3,1},{4,6},{5,7},{6,4},{7,5},{8,10},{9,11},{10,... | collective-permute-start | bytes 3145736 | tf_op jit(solution)/shard_map/ppermute | solution.py:529
  401.5 24.3 %collective-permute-start.43 = (f32[20,128]{1,0:T(8,128)S(1)}, f32[20,128]{1,0:T(8,128)S(1)}, u32[]{:S(2)}, u32[]{:S(2)}) collective-permute-start(f32[20,128]{1,0:T(8,128)S(1)} %fusion.56), channel_id=1, source_target_pairs={{0,2},{1,3},{2,0},{3,1},{4,6},{5,7},{6,4},{7,5},{8,10},{9,11},{10,... | collective-permute-start | bytes 30728 | tf_op jit(solution)/shard_map/ppermute | solution.py:529
  425.7 3.7 collective-permute-start.44
  429.4 5.5 %collective-permute-start.45 = (f32[20,128]{1,0:T(8,128)S(1)}, f32[20,128]{1,0:T(8,128)S(1)}, u32[]{:S(2)}, u32[]{:S(2)}) collective-permute-start(f32[20,128]{1,0:T(8,128)S(1)} %add.418), channel_id=1, source_target_pairs={{0,8},{8,16},{16,24},{24,0},{1,9},{9,17},{17,25},{25,1},{2,10},{10... | collective-permute-start | bytes 30728 | tf_op jit(solution)/shard_map/ppermute | solution.py:830
  431.3 9.0 %collective-permute-start.46 = (f32[20,128]{1,0:T(8,128)S(1)}, f32[20,128]{1,0:T(8,128)S(1)}, u32[]{:S(2)}, u32[]{:S(2)}) collective-permute-start(f32[20,128]{1,0:T(8,128)S(1)} %add.418), channel_id=1, source_target_pairs={{0,16},{8,24},{16,0},{24,8},{1,17},{9,25},{17,1},{25,9},{2,18},{10... | collective-permute-start | bytes 30728 | tf_op jit(solution)/shard_map/ppermute | solution.py:830
  431.9 8.5 %collective-permute-start.47 = (f32[20,128]{1,0:T(8,128)S(1)}, f32[20,128]{1,0:T(8,128)S(1)}, u32[]{:S(2)}, u32[]{:S(2)}) collective-permute-start(f32[20,128]{1,0:T(8,128)S(1)} %add.418), channel_id=1, source_target_pairs={{0,24},{8,0},{16,8},{24,16},{1,25},{9,1},{17,9},{25,17},{2,26},{10... | collective-permute-start | bytes 30728 | tf_op jit(solution)/shard_map/ppermute | solution.py:830
  434.9 26.8 %collective-permute-start.21 = (bf16[256,1024]{1,0:T(8,128)(2,1)}, bf16[256,1024]{1,0:T(8,128)(2,1)}, u32[]{:S(2)}, u32[]{:S(2)}) collective-permute-start(bf16[256,1024]{1,0:T(8,128)(2,1)} %get-tuple-element.79), channel_id=1, source_target_pairs={{0,0},{16,1},{2,2},{18,3},{4,4},{20,5},{6,6},{22,7},{8,8},{24,9},{... | collective-permute-start | bytes 1572872 | tf_op jit(solution)/shard_map/ppermute | solution.py:574
  440.3 22.7 %collective-permute-start.22 = (bf16[256,1024]{1,0:T(8,128)(2,1)}, bf16[256,1024]{1,0:T(8,128)(2,1)}, u32[]{:S(2)}, u32[]{:S(2)}) collective-permute-start(bf16[256,1024]{1,0:T(8,128)(2,1)} %get-tuple-element.78), channel_id=1, source_target_pairs={{8,0},{24,1},{10,2},{26,3},{12,4},{28,5},{14,6},{30,7},{0,8},{16,9... | collective-permute-start | bytes 1572872 | tf_op jit(solution)/shard_map/ppermute | solution.py:574
  442.2 12.4 %collective-permute-start.28 = (bf16[4,64,1024]{2,1,0:T(8,128)(2,1)S(1)}, bf16[4,64,1024]{2,1,0:T(8,128)(2,1)S(1)}, u32[]{:S(2)}, u32[]{:S(2)}) collective-permute-start(bf16[4,64,1024]{2,1,0:T(8,128)(2,1)S(1)} %dynamic-slice_bitcast_fusion.2), channel_id=1, source_target_pairs={{0,2},{1,3},{2,0},{3,1},{4,6},{5,7},{6,4},{7,5},{8,10},{9,11},{10,... | collective-permute-start | bytes 1572872 | tf_op jit(solution)/shard_map/ppermute | solution.py:529
  445.6 11.8 %collective-permute-start.25 = (bf16[4,64,1024]{2,1,0:T(8,128)(2,1)S(1)}, bf16[4,64,1024]{2,1,0:T(8,128)(2,1)S(1)}, u32[]{:S(2)}, u32[]{:S(2)}) collective-permute-start(bf16[4,64,1024]{2,1,0:T(8,128)(2,1)S(1)} %dynamic-slice_bitcast_fusion.3), channel_id=1, source_target_pairs={{0,4},{1,5},{2,6},{3,7},{4,0},{5,1},{6,2},{7,3},{8,12},{9,13},{10,... | collective-permute-start | bytes 1572872 | tf_op jit(solution)/shard_map/ppermute | solution.py:529
  457.7 11.1 %collective-permute-start.29 = (bf16[128,1024]{1,0:T(8,128)(2,1)S(1)}, bf16[128,1024]{1,0:T(8,128)(2,1)S(1)}, u32[]{:S(2)}, u32[]{:S(2)}) collective-permute-start(bf16[128,1024]{1,0:T(8,128)(2,1)S(1)} %get-tuple-element.69), channel_id=1, source_target_pairs={{0,8},{8,16},{16,24},{24,0},{1,9},{9,17},{17,25},{25,1},{2,10},{10... | collective-permute-start | bytes 786440 | tf_op jit(solution)/shard_map/ppermute | solution.py:635
  458.3 23.8 %collective-permute-start.30 = (bf16[128,1024]{1,0:T(8,128)(2,1)S(1)}, bf16[128,1024]{1,0:T(8,128)(2,1)S(1)}, u32[]{:S(2)}, u32[]{:S(2)}) collective-permute-start(bf16[128,1024]{1,0:T(8,128)(2,1)S(1)} %get-tuple-element.70), channel_id=1, source_target_pairs={{0,16},{8,24},{16,0},{24,8},{1,17},{9,25},{17,1},{25,9},{2,18},{10... | collective-permute-start | bytes 786440 | tf_op jit(solution)/shard_map/ppermute | solution.py:635
  460.5 21.6 %collective-permute-start.31 = (bf16[128,1024]{1,0:T(8,128)(2,1)S(1)}, bf16[128,1024]{1,0:T(8,128)(2,1)S(1)}, u32[]{:S(2)}, u32[]{:S(2)}) collective-permute-start(bf16[128,1024]{1,0:T(8,128)(2,1)S(1)} %get-tuple-element.71), channel_id=1, source_target_pairs={{0,24},{8,0},{16,8},{24,16},{1,25},{9,1},{17,9},{25,17},{2,26},{10... | collective-permute-start | bytes 786440 | tf_op jit(solution)/shard_map/ppermute | solution.py:635
  (57 other events, 612.9 us)

commit v3 on v2

--- a/solution.py
+++ b/solution.py
@@ -367,16 +367,11 @@
 
 
 def bucket_sums(sums):
-    pairs = sums.shape[0]
     side = np.arange(LANES)
     far = np.full((LANES,), 2 * HALF_ROWS)
     chosen = bucket_columns(np.concatenate([-side, HALF_ROWS - side, -far, far]))
     return lax.dot_general(
-        jnp.asarray(chosen),
-        sums.reshape(2 * pairs, 4 * LANES),
-        NT,
-        precision=lax.Precision.HIGHEST,
-        preferred_element_type=WIDE,
+        jnp.asarray(chosen), sums, NT, precision=lax.Precision.HIGHEST, preferred_element_type=WIDE
     )
 
 
@@ -524,6 +519,499 @@
     )(normed, grad, *mine, *wholes)[:4]
 
 
+def push(source, target, sems, number, place, index):
+    return pltpu.make_async_remote_copy(
+        src_ref=source,
+        dst_ref=target,
+        send_sem=sems.at[(0,) + number],
+        recv_sem=sems.at[(1,) + number],
+        device_id={"seq": place, "fsdp": index},
+        device_id_type=pl.DeviceIdType.MESH,
+    )
+
+
+def greet_column(depth):
+    barrier = pltpu.get_barrier_semaphore()
+    place, index = (lax.axis_index("seq"), lax.axis_index("fsdp"))
+
+    def signal(there, which):
+        pl.semaphore_signal(
+            barrier, inc=1, device_id={"seq": there, "fsdp": which}, device_id_type=pl.DeviceIdType.MESH
+        )
+
+    signal(place, partner(ALONG_X))
+    signal(place, partner(ALONG_Y))
+    signal(place, partner(CORE))
+    for step in range(1, depth):
+        signal(lax.rem(place + step, depth), index)
+        signal(lax.rem(place + step, depth), partner(CORE))
+    pl.semaphore_wait(barrier, 2 * depth + 1)
+
+
+def add_rows(target, source):
+    target[...] = (target[...].astype(WIDE) + source[...].astype(WIDE)).astype(LOW)
+
+
+def backward_kernel(
+    depth,
+    length_ref,
+    query_ref,
+    key_ref,
+    value_ref,
+    grad_ref,
+    log_ref,
+    near_ref,
+    normed_ref,
+    weight_ref,
+    source_ref,
+    hidden_ref,
+    gain_ref,
+    small_ref,
+    output_ref,
+    layer_ref,
+    up_ref,
+    down_ref,
+    layer_out_ref,
+    input_grad_ref,
+    heads_out_ref,
+    units_out_ref,
+    small_out_ref,
+    bias,
+    spare,
+    keys,
+    values,
+    padded,
+    key_total,
+    value_total,
+    tiles,
+    lows,
+    part,
+    x_block,
+    y_block,
+    x_came,
+    y_came,
+    x_last,
+    y_last,
+    heads_came,
+    units,
+    units_came,
+    units_last,
+    units_far,
+    fold_sent,
+    fold_came,
+    row_sent,
+    row_came,
+    small,
+    small_came,
+    swap_sems,
+    first_sems,
+    second_sems,
+    third_sems,
+    unit_first_sems,
+    unit_second_sems,
+    unit_third_sems,
+    fold_sems,
+    row_sems,
+    layer_sems,
+    small_sems,
+    local_sems,
+):
+    rows = query_ref.shape[0]
+    width = normed_ref.shape[1]
+    inner = query_ref.shape[1]
+    held = depth // 2
+    step = pl.program_id(0)
+    last = depth - 1
+    place, index = (lax.axis_index("seq"), lax.axis_index("fsdp"))
+    core, x, y = (lax.rem(index, 2), lax.rem(index // 2, 2), index // 4)
+    column = index - core
+
+    def owner(block):
+        return lax.rem(place + 1 + block, depth)
+
+    def beside(source, target, sems, number, bit):
+        return push(source, target, sems, number, place, partner(bit))
+
+
+    def row_moves(source, target, sems, piece, started=True):
+        there, which = (core * held + piece, column + place // held)
+        slot = lax.rem(place, held)
+        home = (there == place) & (which == index)
+
+        @pl.when(home)
+        def _():
+            move = pltpu.make_async_copy(source, target.at[slot], sems.at[1, piece, slot])
+            if started:
+                move.start()
+
+        @pl.when(jnp.logical_not(home))
+        def _():
+            move = push(source, target.at[slot], sems, (piece, slot), there, which)
+            if started:
+                move.start()
+            else:
+                move.wait_send()
+
+    def rows_came(target, sems):
+        for slot in range(held):
+            number = (lax.rem(place, held), slot)
+            push(target.at[slot], target.at[slot], sems, number, place, partner(CORE)).wait_recv()
+
+
+    def unit_sources(block):
+        return (
+            (up_ref.at[owner(block), :, 1 - x], up_ref.at[owner(block), :, x], ALONG_X),
+            (down_ref.at[owner(block), 1 - y], down_ref.at[owner(block), y], ALONG_Y),
+        )
+
+    def units_start(block):
+        for kind, (away, own, bit) in enumerate(unit_sources(block)):
+            beside(away, units_came.at[kind, block], unit_first_sems, (kind, block), bit).start()
+            pltpu.make_async_copy(own, units.at[kind, block], local_sems.at[kind, block]).start()
+
+    def unit_seconds(block):
+        return (
+            (units.at[0, block, 1 - y], units.at[0, block, y], ALONG_Y),
+            (units.at[1, block, 1 - x], units.at[1, block, x], ALONG_X),
+        )
+
+    def units_first(block):
+        for kind, (away, own, bit) in enumerate(unit_sources(block)):
+            pltpu.make_async_copy(own, units.at[kind, block], local_sems.at[kind, block]).wait()
+            beside(away, units_came.at[kind, block], unit_first_sems, (kind, block), bit).wait()
+            add_rows(units.at[kind, block], units_came.at[kind, block])
+        for kind, (away, own, bit) in enumerate(unit_seconds(block)):
+            beside(away, units_last.at[kind, block], unit_second_sems, (kind, block), bit).start()
+
+    def unit_thirds(block):
+        return [
+            push(own, units_far.at[block, kind], unit_third_sems, (kind, block), owner(block), index)
+            for kind, (away, own, bit) in enumerate(unit_seconds(block))
+        ]
+
+    def units_second(block, mine=False):
+        for kind, (away, own, bit) in enumerate(unit_seconds(block)):
+            beside(away, units_last.at[kind, block], unit_second_sems, (kind, block), bit).wait()
+            add_rows(own, units_last.at[kind, block])
+        if not mine:
+            for one in unit_thirds(block):
+                one.start()
+
+
+    def swaps(block):
+        moves = [
+            beside(part.at[kind, :, 1 - core], x_block.at[block, :, core, kind], swap_sems, (kind, block), CORE)
+            for kind in range(2)
+        ]
+        moves.append(beside(part.at[2, :, 1 - core], y_block.at[block, core, :, 0], swap_sems, (2, block), CORE))
+        return moves
+
+    def output_copy(block):
+        return pltpu.make_async_copy(output_ref.at[owner(block)], y_block.at[block, :, :, 1], local_sems.at[2, block])
+
+    def firsts(block):
+        return (
+            beside(x_block.at[block, 1 - x], x_came.at[block], first_sems, (0, block), ALONG_X),
+            beside(y_block.at[block, 1 - y], y_came.at[block], first_sems, (1, block), ALONG_Y),
+        )
+
+    def seconds(block):
+        return (
+            beside(x_block.at[block, x, 1 - y], x_last.at[block], second_sems, (0, block), ALONG_Y),
+            beside(y_block.at[block, y, 1 - x], y_last.at[block], second_sems, (1, block), ALONG_X),
+        )
+
+    def thirds(block):
+        return [
+            push(own, heads_came.at[block, kind], third_sems, (kind, block), owner(block), index)
+            for kind, own in enumerate((x_block.at[block, x, y], y_block.at[block, y, x]))
+        ]
+
+    def heads_start(block):
+        for one in swaps(block):
+            one.wait_recv()
+        output_copy(block).wait()
+        for one in firsts(block):
+            one.start()
+
+    def heads_first(block):
+        for one in firsts(block):
+            one.wait()
+        add_rows(x_block.at[block, x], x_came.at[block])
+        add_rows(y_block.at[block, y], y_came.at[block])
+        for one in seconds(block):
+            one.start()
+
+    def heads_second(block, mine=False):
+        for one in seconds(block):
+            one.wait()
+        add_rows(x_block.at[block, x, y], x_last.at[block])
+        add_rows(y_block.at[block, y, x], y_last.at[block])
+        if not mine:
+            for one in thirds(block):
+                one.start()
+
+    @pl.when(step == 0)
+    def _():
+        greet_column(depth)
+        for block in range(depth):
+            units_start(block)
+        for block in range(depth):
+            output_copy(block).start()
+        for piece in range(held):
+            row_moves(layer_ref.at[piece], layer_out_ref, layer_sems, piece)
+        spare[...] = spare_lanes(length_ref[0], rows)
+        for head in range(2):
+            padded[head, :HALF_ROWS, :] = jnp.zeros((HALF_ROWS, QUERY_ROWS), LOW)
+            padded[head, rows + HALF_ROWS :, :] = jnp.zeros((HALF_ROWS, QUERY_ROWS), LOW)
+
+    @pl.when(step >= 1)
+    def _():
+        units_first(step - 1)
+
+    @pl.when(step >= 2)
+    def _():
+        units_second(step - 2)
+
+    pair = owner(step)
+    lanes = pl.ds(pl.multiple_of(pair * LANES, LANES), LANES)
+    split_heads(key_ref[:, lanes], spare[...], keys)
+    split_heads(value_ref[:, lanes], jnp.zeros((rows, LANES), LOW), values)
+    near_start = rows - QUERY_ROWS - HALF_ROWS
+    near_end = near_start + 2 * QUERY_ROWS
+    for head in range(2):
+        line = near_ref[2 * pair + head]
+        bias[head, :near_start, :] = jnp.broadcast_to(line[:, :1], (near_start, QUERY_ROWS))
+        bias[head, near_start:near_end, :] = near_block(line).T
+        bias[head, near_end:, :] = jnp.broadcast_to(line[:, -1:], (bias.shape[1] - near_end, QUERY_ROWS))
+    key_total[...] = jnp.zeros_like(key_total)
+    value_total[...] = jnp.zeros_like(value_total)
+    tiles[...] = jnp.zeros_like(tiles)
+    sums = small.at[0, pl.ds(pl.multiple_of(16 + 8 * pair, 8), 8)]
+    sums[...] = jnp.zeros((8, LANES), WIDE)
+    spot = lax.broadcasted_iota(jnp.int32, (1, LANES), 1)
+    lane = lax.broadcasted_iota(jnp.int32, (QUERY_ROWS, LANES), 1)
+    ones = jnp.where(lax.rem(lane, HEAD_DIM) == 0, 1.0, 0.0).astype(LOW)
+    zero = jnp.zeros((), LOW)
+    blocks = rows // QUERY_ROWS
+
+    def block(number, carry):
+        start = pl.multiple_of(number * QUERY_ROWS, QUERY_ROWS)
+        offset = pl.multiple_of(rows - QUERY_ROWS - number * QUERY_ROWS, LANES)
+        both = query_ref[pl.ds(start, QUERY_ROWS), lanes]
+        grad = grad_ref[pl.ds(start, QUERY_ROWS), lanes]
+        parts = []
+        for head in range(2):
+            mine = lane < HEAD_DIM if head == 0 else lane >= HEAD_DIM
+            logits = dot(keys[head], jnp.where(mine, both, ones), NT)
+            logits = logits + bias[head, pl.ds(offset, rows), :]
+            probs = jnp.exp(logits - log_ref[pair, head : head + 1, pl.ds(start, QUERY_ROWS)])
+            prob_grad = dot(values[head], grad, NT)
+            weighted = probs * prob_grad
+            total = jnp.sum(weighted, axis=0, keepdims=True)
+            score = (weighted - probs * total).astype(LOW)
+            value_total[...] += dot(probs.astype(LOW), jnp.where(mine, grad, zero))
+            key_total[...] += dot(score, jnp.where(mine, both, zero))
+            padded[head, HALF_ROWS : HALF_ROWS + rows, :] = score
+            one = dot(score, keys[head], TN)
+            parts.append(one)
+            columns = jnp.sum(one, axis=0, keepdims=True)
+            first = HEAD_DIM * (1 - head) + 1 + number
+            close = padded[head, pl.ds(start, 2 * QUERY_ROWS), :].astype(WIDE)
+            quarter = [close[HALF_ROWS * turn : HALF_ROWS * (turn + 1)] for turn in range(4)]
+            for turn in range(3):
+                tiles[head, turn] += quarter[turn][:, :HALF_ROWS] + quarter[turn + 1][:, HALF_ROWS:]
+            left = jnp.sum(quarter[0][:, HALF_ROWS:], axis=0, keepdims=True)
+            right = jnp.sum(quarter[3][:, :HALF_ROWS], axis=0, keepdims=True)
+            left = left + jnp.where(spot == first, columns, 0.0)
+            right = right + jnp.where(spot == first + blocks, columns, 0.0)
+            sums[4 * head + 2 : 4 * head + 3, :] += left
+            sums[4 * head + 3 : 4 * head + 4, :] += right
+        chosen = jnp.where(lane < HEAD_DIM, parts[0], parts[1])
+        lows[pl.ds(start, QUERY_ROWS), lanes] = chosen.astype(LOW)
+        return carry
+
+    lax.fori_loop(0, blocks, block, 0)
+    lows[:, pl.ds(pl.multiple_of(inner + pair * LANES, LANES), LANES)] = key_total[...].astype(LOW)
+    lows[:, pl.ds(pl.multiple_of(2 * inner + pair * LANES, LANES), LANES)] = value_total[...].astype(LOW)
+    shape = (HALF_ROWS, HALF_ROWS)
+    upper = lax.broadcasted_iota(jnp.int32, shape, 0) <= lax.broadcasted_iota(jnp.int32, shape, 1)
+    for head in range(2):
+        before, centre, behind = (tiles[head, turn] for turn in range(3))
+        sums[4 * head : 4 * head + 1, :] = diagonal_sums(jnp.where(upper, centre, before))
+        sums[4 * head + 1 : 4 * head + 2, :] = diagonal_sums(jnp.where(upper, behind, centre))
+        sums[4 * head + 2 : 4 * head + 3, :] += jnp.sum(jnp.where(upper, before, 0.0), axis=0, keepdims=True)
+        sums[4 * head + 3 : 4 * head + 4, :] += jnp.sum(jnp.where(upper, 0.0, behind), axis=0, keepdims=True)
+
+    @pl.when(step >= 1)
+    def _():
+        for one in swaps(step - 1):
+            one.wait_send()
+
+    for kind in range(3):
+        columns = lows[:, pl.ds(pl.multiple_of(kind * inner + pair * LANES, LANES), LANES)]
+        product = dot(columns, normed_ref[...], TN).astype(LOW)
+        part[kind] = product.reshape(part.shape[1:])
+    for one in swaps(step):
+        one.start()
+    for half in range(2):
+        for kind in range(2):
+            x_block[step, half, core, kind] = part[kind, half, core]
+        y_block[step, core, half, 0] = part[2, half, core]
+
+    @pl.when(step >= 1)
+    def _():
+        heads_start(step - 1)
+
+    @pl.when(step >= 2)
+    def _():
+        heads_first(step - 2)
+
+    @pl.when(step >= 3)
+    def _():
+        heads_second(step - 3)
+
+    @pl.when(step == last)
+    def _():
+        span = rows // 2 // held
+        for piece in range(held):
+            away = pl.ds(pl.multiple_of((1 - core) * (rows // 2) + piece * span, span), span)
+            fold_sent[piece] = dot(lows[away, :], weight_ref[...]).astype(LOW)
+            beside(fold_sent.at[piece], fold_came.at[piece], fold_sems, (piece,), CORE).start()
+        for one in swaps(last):
+            one.wait_send()
+        heads_start(last)
+        units_first(last)
+        units_second(last - 1)
+        heads_first(last - 1)
+        heads_second(last - 2)
+
+        gain_total = jnp.zeros((1, width), WIDE)
+        for piece in range(held):
+            here = pl.ds(pl.multiple_of(core * (rows // 2) + piece * span, span), span)
+            product = dot(lows[here, :], weight_ref[...])
+            beside(fold_sent.at[piece], fold_came.at[piece], fold_sems, (piece,), CORE).wait()
+            product = product + fold_came[piece].astype(WIDE)
+            local = slice(piece * span, (piece + 1) * span)
+            source = source_ref[local, :].astype(WIDE)
+            rms = lax.rsqrt(jnp.mean(source * source, axis=1, keepdims=True) + EPSILON)
+            scaled = source * rms
+            gain_total = gain_total + jnp.sum(product * scaled, axis=0, keepdims=True)
+            gained = gain_ref[...] * product
+            inside = jnp.mean(gained * scaled, axis=1, keepdims=True)
+            row_sent[piece] = (hidden_ref[local, :] + rms * (gained - scaled * inside)).astype(LOW)
+            row_moves(row_sent.at[piece], row_came, row_sems, piece)
+            if piece == 0:
+                heads_first(last)
+                units_second(last, True)
+                heads_second(last - 1)
+        heads_second(last, True)
+
+        for number in range(width // LANES):
+            small[0, number : number + 1, :] = gain_total[:, number * LANES : (number + 1) * LANES]
+        small[0, 8:16, :] = small_ref[...]
+        for turn, bit in enumerate((ALONG_X, ALONG_Y)):
+            move = beside(small.at[turn], small_came.at[turn], small_sems, (turn,), bit)
+            move.start()
+            move.wait()
+            small[turn + 1] = small[turn] + small_came[turn]
+        moves = [
+            push(small.at[2], small_came.at[1 + turn], small_sems, (1 + turn,), lax.rem(place + turn, depth), index)
+            for turn in range(1, depth)
+        ]
+        for one in moves:
+            one.start()
+
+        for block in range(last):
+            for one in unit_thirds(block) + thirds(block):
+                one.wait()
+        units_out_ref[0] = units[0, last, y].astype(WIDE) + sum(units_far[one, 0].astype(WIDE) for one in range(depth - 1))
+        units_out_ref[1] = units[1, last, x].astype(WIDE) + sum(units_far[one, 1].astype(WIDE) for one in range(depth - 1))
+        heads_out_ref[0:2] = x_block[last, x, y].astype(WIDE) + sum(
+            heads_came[one, 0].astype(WIDE) for one in range(depth - 1)
+        )
+        heads_out_ref[2:4] = y_block[last, y, x].astype(WIDE) + sum(
+            heads_came[one, 1].astype(WIDE) for one in range(depth - 1)
+        )
+        for one in moves:
+            one.wait()
+        small[3] = small[2] + sum(small_came[1 + turn] for turn in range(1, depth))
+        move = beside(small.at[3], small_came.at[depth + 1], small_sems, (depth + 1,), CORE)
+        move.start()
+        move.wait()
+        small_out_ref[0] = small[3]
+        small_out_ref[1] = small_came[depth + 1]
+
+        for piece in range(held):
+            row_moves(layer_ref.at[piece], layer_out_ref, layer_sems, piece, False)
+            row_moves(row_sent.at[piece], row_came, row_sems, piece, False)
+        rows_came(layer_out_ref, layer_sems)
+        rows_came(row_came, row_sems)
+        input_grad_ref[...] = row_came[...].astype(WIDE)
+
+
+def backward(
+    length, query, key, value, grad, logs, near, normed, weights, source, hidden, gain, ffn_gain_part, output_part, layer, ups, downs
+):
+    rows, inner = query.shape
+    width = normed.shape[1]
+    depth = lax.axis_size("seq")
+    held = depth // 2
+    span = rows // depth
+    slim, thick = (output_part.shape[3], ups.shape[3])
+    vmem, anywhere = (pl.BlockSpec(memory_space=pltpu.VMEM), pl.BlockSpec(memory_space=pl.ANY))
+    shape = jax.ShapeDtypeStruct
+    small_rows = 2 * (width // LANES) + 8 * depth
+    sems = [(3, depth), (2, depth), (2, depth), (2, depth), (2, depth), (2, depth), (2, depth)]
+    sems += [(held,), (held, held), (held, held), (depth + 2,)]
+    return pl.pallas_call(
+        functools.partial(backward_kernel, depth),
+        grid=(depth,),
+        in_specs=[pl.BlockSpec(memory_space=pltpu.SMEM)] + [vmem] * 12 + [anywhere] * 4,
+        out_specs=[anywhere] + [vmem] * 4,
+        out_shape=[
+            shape((held, span, width), LOW),
+            shape((held, span, width), WIDE),
+            shape((4, slim, width), WIDE),
+            shape((2, thick, width), WIDE),
+            shape((2, small_rows, LANES), WIDE),
+        ],
+        scratch_shapes=[
+            pltpu.VMEM((2, 2 * rows - QUERY_ROWS, QUERY_ROWS), WIDE),
+            pltpu.VMEM((rows, LANES), LOW),
+            pltpu.VMEM((2, rows, LANES), LOW),
+            pltpu.VMEM((2, rows, LANES), LOW),
+            pltpu.VMEM((2, rows + QUERY_ROWS, QUERY_ROWS), LOW),
+            pltpu.VMEM((rows, LANES), WIDE),
+            pltpu.VMEM((rows, LANES), WIDE),
+            pltpu.VMEM((2, 3, HALF_ROWS, HALF_ROWS), WIDE),
+            pltpu.VMEM((rows, 3 * inner), LOW),
+            pltpu.VMEM((3, 2, 2, slim, width), LOW),
+        ]
+        + [pltpu.VMEM((depth, 2, 2, 2, slim, width), LOW)] * 2
+        + [pltpu.VMEM((depth, 2, 2, slim, width), LOW)] * 2
+        + [pltpu.VMEM((depth, 2, slim, width), LOW)] * 2
+        + [
+            pltpu.VMEM((depth - 1, 2, 2, slim, width), LOW),
+            pltpu.VMEM((2, depth, 2, thick, width), LOW),
+            pltpu.VMEM((2, depth, 2, thick, width), LOW),
+            pltpu.VMEM((2, depth, thick, width), LOW),
+            pltpu.VMEM((depth - 1, 2, thick, width), LOW),
+        ]
+        + [pltpu.VMEM((held, span, width), LOW)] * 4
+        + [pltpu.VMEM((4, small_rows, LANES), WIDE), pltpu.VMEM((depth + 2, small_rows, LANES), WIDE)]
+        + [pltpu.SemaphoreType.DMA((2,) + one) for one in sems]
+        + [pltpu.SemaphoreType.DMA((3, depth))],
+        compiler_params=pltpu.CompilerParams(
+            vmem_limit_bytes=62 << 20, collective_id=3, has_side_effects=True
+        ),
+        cost_estimate=pl.CostEstimate(
+            flops=60 * rows * rows * inner, bytes_accessed=14 * rows * inner, transcendentals=rows * rows * inner // 64
+        ),
+        name="backward",
+    )(length, query, key, value, grad, logs, near, normed, weights, source, hidden, gain, ffn_gain_part, output_part, layer, ups, downs)
+
+
 def flip(value, bit):
     size = lax.axis_size("fsdp")
     return lax.ppermute(value, "fsdp", [(one, one ^ bit) for one in range(size)])
@@ -624,29 +1112,6 @@
 
 def pick(value, index, axis):
     return lax.dynamic_index_in_dim(value, index, axis, keepdims=False)
-
-
-def spread_depth(value):
-    depth = lax.axis_size("seq")
-    place = lax.axis_index("seq")
-    total = pick(value, place, 0).astype(WIDE)
-    for step in range(1, depth):
-        sent = pick(value, (place + step) % depth, 0)
-        got = lax.ppermute(sent, "seq", [(one, (one + step) % depth) for one in range(depth)])
-        total = total + got.astype(WIDE)
-    return total
-
-
-def scatter_plane(one, two):
-    chip = lax.axis_index("fsdp") // 2
-    x, y = (chip % 2, chip // 2)
-    one_got = flip(pick(one, 1 - x, 2), 2)
-    two_got = flip(pick(two, 1 - y, 1), 4)
-    one = add_low(pick(one, x, 2), one_got)
-    two = add_low(pick(two, y, 1), two_got)
-    one_last = flip(pick(one, 1 - y, 1), 4)
-    two_last = flip(pick(two, 1 - x, 1), 2)
-    return (add_low(pick(one, y, 1), one_last), add_low(pick(two, x, 1), two_last))
 
 
 def shards(
@@ -740,7 +1205,6 @@
     normed_grad = fold(normed_part, core)
     mlp_out = fold(mlp_part, core)
     layer_rows = ((hidden_one + mlp_out) * mask_rows).astype(LOW)
-    layer_out = to_slots(layer_rows, held)
 
     gained_two = ffn_gain * normed_grad
     hidden_grad = grad_out + rms_two * (
@@ -758,83 +1222,82 @@
     near_output_part = dot(near_context, hidden_low, TN).astype(LOW)
     far_output_part = dot(far_context, hidden_low, TN).astype(LOW)
 
-    query_low, key_low, value_low, distance_sums = attend_grad(
-        length, query, key, value, context_grad, logs, near
-    )
-    lows = (query_low, key_low, value_low)
-    normed_one_grad = dot(query_low, own_three[0]) + dot(key_low, own_three[1]) + dot(value_low, own_three[2])
-    normed_one_grad = fold(normed_one_grad, core)
-    three_parts = [dot(one, normed_one, TN).astype(LOW) for one in lows]
-    gained_one = attn_gain * normed_one_grad
-    input_grad = hidden_grad + rms_one * (
-        gained_one - scaled_one * jnp.mean(gained_one * scaled_one, axis=1, keepdims=True)
-    )
-    attn_gain_part = jnp.sum(normed_one_grad * scaled_one, axis=0)
-    input_grad = to_slots(input_grad.astype(LOW), held).astype(WIDE)
-
     if fast:
         blocks = (depth, 2, 2, -1, width)
-        up_some, down_some = scatter_plane(up_part.reshape(blocks), down_part.reshape(blocks))
-        up_grad, down_grad = (spread_depth(up_some), spread_depth(down_some))
 
         def to_parity(kept, sent):
-            return jnp.where(
-                core == 0, jnp.stack([kept, sent], axis=1), jnp.stack([sent, kept], axis=1)
-            )
-
-        three = jnp.stack(three_parts).reshape(3, 4, 2, 2, -1, width)
-        three_got = other_core(pick(three, 1 - core, 3))
-        three_kept = pick(three, core, 3)
-        outs = [to_parity(three_kept[number], three_got[number]) for number in range(3)]
+            return jnp.where(core == 0, jnp.stack([kept, sent], axis=1), jnp.stack([sent, kept], axis=1))
+
         near_part = near_output_part.reshape(4, 2, 2, -1, width)
         far_part = far_output_part.reshape(4, 2, 2, -1, width)
         got = other_core(jnp.stack([pick(far_part, 1 - core, 2), pick(near_part, 1 - core, 2)]))
-        outs.append(
-            to_parity(add_low(pick(near_part, core, 2), got[0]), add_low(pick(far_part, core, 2), got[1]))
+        output_part = to_parity(
+            add_low(pick(near_part, core, 2), got[0]), add_low(pick(far_part, core, 2), got[1])
         )
-        one = jnp.concatenate(outs[:2], axis=3)
-        two = jnp.concatenate(outs[2:], axis=3)
-        one, two = scatter_plane(one, two)
-        attention = spread_depth(jnp.concatenate([one, two], axis=1))
-        attention = attention.reshape(4, -1, width)
-        query_grad, key_grad, value_grad, output_grad = [attention[number] for number in range(4)]
+        layer_out, input_grad, heads_grad, units_grad, small = backward(
+            length,
+            query,
+            key,
+            value,
+            context_grad,
+            logs,
+            near,
+            normed_one,
+            jnp.concatenate(own_three, axis=0),
+            source_low,
+            hidden_grad,
+            attn_gain[None, :],
+            ffn_gain_part.reshape(-1, LANES),
+            output_part,
+            layer_rows.reshape(held, span, width),
+            up_part.reshape(blocks),
+            down_part.reshape(blocks),
+        )
+        query_grad, key_grad, value_grad, output_grad = (heads_grad[number] for number in range(4))
+        up_grad, down_grad = (units_grad[0], units_grad[1])
+        gain_lines = width // LANES
+        gains = (small[0] + small[1])[: 2 * gain_lines].reshape(2, width)
+        attn_gain_sum, ffn_gain_sum = (gains[0], gains[1])
+        sums = jnp.where(core == 0, small, small[::-1])[:, 2 * gain_lines :]
+        sums = jnp.swapaxes(sums.reshape(2, 4, 2, 4 * LANES), 0, 1)
+        bias_sum = bucket_sums(sums.reshape(HEADS, 4 * LANES))
     else:
+        query_low, key_low, value_low, distance_sums = attend_grad(
+            length, query, key, value, context_grad, logs, near
+        )
+        lows = (query_low, key_low, value_low)
+        normed_one_grad = dot(query_low, own_three[0]) + dot(key_low, own_three[1]) + dot(value_low, own_three[2])
+        normed_one_grad = fold(normed_one_grad, core)
+        three_parts = [dot(one, normed_one, TN).astype(LOW) for one in lows]
+        gained_one = attn_gain * normed_one_grad
+        input_grad = hidden_grad + rms_one * (
+            gained_one - scaled_one * jnp.mean(gained_one * scaled_one, axis=1, keepdims=True)
+        )
+        attn_gain_part = jnp.sum(normed_one_grad * scaled_one, axis=0)
+        input_grad = to_slots(input_grad.astype(LOW), held).astype(WIDE)
+        layer_out = to_slots(layer_rows, held)
 
         def summed(value):
             return lax.psum_scatter(value, BOTH, scatter_dimension=0, tiled=True).astype(WIDE)
 
-        def own_only(value, shape):
+        def own_only(value):
             blank = jnp.zeros_like(value)
             pair = jnp.where(core == 0, jnp.stack([value, blank], axis=1), jnp.stack([blank, value], axis=1))
-            return pair.reshape(-1, width)
-
-        up_grad, down_grad = [
-            summed(own_only(one.reshape(depth * (size // 2), -1, width), None)) for one in (up_part, down_part)
-        ]
-        query_grad, key_grad, value_grad = [summed(own_only(one.reshape(4, -1, width), None)) for one in three_parts]
+            return summed(pair.reshape(-1, width))
+
+        up_grad, down_grad = [own_only(one.reshape(depth * (size // 2), -1, width)) for one in (up_part, down_part)]
+        query_grad, key_grad, value_grad = [own_only(one.reshape(4, -1, width)) for one in three_parts]
         near_part, far_part = (near_output_part.reshape(4, -1, width), far_output_part.reshape(4, -1, width))
         pair = jnp.where(
             core == 0, jnp.stack([near_part, far_part], axis=1), jnp.stack([far_part, near_part], axis=1)
         )
         output_grad = summed(pair.reshape(-1, width))
-
-    bias_own = bucket_sums(distance_sums).reshape(BUCKETS, 4, 1, 2)
-    bias_full = lax.dynamic_update_slice(
-        jnp.zeros((BUCKETS, 4, 2, 2), WIDE), bias_own, (0, 0, core, 0)
-    ).reshape(BUCKETS, HEADS)
-    if fast:
-        small = jnp.concatenate([attn_gain_part, ffn_gain_part, bias_full.reshape(-1)]).reshape(-1, LANES)
-        for bit in (1, 2, 4):
-            small = small + flip(small, bit)
-        moved = [
-            lax.ppermute(small, "seq", [(one, (one + step) % depth) for one in range(depth)])
-            for step in range(1, depth)
-        ]
-        small = sum(moved, small).reshape(-1)
-        attn_gain_sum, ffn_gain_sum = (small[:width], small[width : 2 * width])
-        bias_sum = small[2 * width :].reshape(BUCKETS, HEADS)
-    else:
+        bias_own = bucket_sums(distance_sums.reshape(HEADS // 2, 4 * LANES)).reshape(BUCKETS, 4, 1, 2)
+        bias_full = lax.dynamic_update_slice(
+            jnp.zeros((BUCKETS, 4, 2, 2), WIDE), bias_own, (0, 0, core, 0)
+        ).reshape(BUCKETS, HEADS)
         attn_gain_sum, ffn_gain_sum, bias_sum = lax.psum((attn_gain_part, ffn_gain_part, bias_full), BOTH)
+
     gain_rows = width // size
     bucket_rows = BUCKETS // size
     attn_gain_grad = lax.dynamic_slice_in_dim(attn_gain_sum, index * gain_rows, gain_rows, 0)

time: 492 us -> 392 us (0.80)
  Pallas kernels: 152 us -> 276 us
  waiting for transfers between devices: 136 us -> 18.1 us
  starting transfers between devices: 72.5 us -> 19.1 us
  local copies, waits for them, and re-layouts: 54.9 us -> 35.4 us
  matrix products: 26.3 us -> 8.87 us
  other arithmetic: 39.1 us -> 25.6 us
    pallas_call x1, Pallas kernels: 48.1 us -> 173 us  [backward(): pl.pallas_call(functools.partial(backward_kernel, depth), grid=(depth,),...]
    ppermute x28 -> x15, waiting for transfers between devices: 78.4 us -> 11.9 us  [flip(): lax.ppermute(value, 'fsdp', [(one, one ^ bit) for one in range(size)])]
    ppermute x16 -> x0, waiting for transfers between devices: 51.7 us -> none  [the longest x9 51.4 us: spread_depth(): lax.ppermute(sent, 'seq', [(one, (one + step) % depth) for one in range(d...]
    ppermute x16 -> x0, starting transfers between devices: 43 us -> none  [the longest x4 25.1 us: to_slots(): got = lax.ppermute(sent, BOTH, pairs)]
    dot_general x15 -> x9, matrix products: 26 us -> 8.53 us  [dot(): return lax.dot_general(left, right, dims, preferred_element_type=WIDE)]
    convert_element_type x9 -> x2, other arithmetic: 12 us -> 0.41 us  [add_low(): return (left.astype(WIDE) + right.astype(WIDE)).astype(LOW)]
    dynamic_slice x8 -> x0, local copies, waits for them, and re-layouts: 10.4 us -> none  [pick(): return lax.dynamic_index_in_dim(value, index, axis, keepdims=False)]
    ppermute x28 -> x15, starting transfers between devices: 20.8 us -> 10.4 us  [flip(): lax.ppermute(value, 'fsdp', [(one, one ^ bit) for one in range(size)])]
  transfers between devices with their start and end apart: 48 -> 19, of which waited for: 17 -> 6; matrix products, arithmetic and copies ran while one was open for 21% -> 10% of each run, Pallas kernels for 23% -> 16%
where the time goes in v3:
time: 392 us; the launch traced here: 385 us
  Pallas kernels  276 us (70%)
  local copies, waits for them, and re-layouts  35.4 us (9%)
  other arithmetic  25.6 us (7%)
  starting transfers between devices  19.1 us (5%)
  waiting for transfers between devices  18.1 us (5%)
  matrix products  8.87 us (2%)
    pallas_call x1, Pallas kernels, backward(): pl.pallas_call(functools.partial(backward_kernel, depth), grid=(depth,),...  173 us
    pallas_call x1, Pallas kernels, attend(): pl.pallas_call(functools.partial(attend_kernel, gathered), grid=(pairs,),...  62.4 us
    pallas_call x1, Pallas kernels, feed(): pl.pallas_call(functools.partial(feed_kernel, 4 if moved else 1), grid=(4...  40.9 us
    ppermute x15, waiting for transfers between devices, flip(): lax.ppermute(value, 'fsdp', [(one, one ^ bit) for one in range(size)])  11.9 us
    ppermute x15, starting transfers between devices, flip(): lax.ppermute(value, 'fsdp', [(one, one ^ bit) for one in range(size)])  10.4 us
    unnamed x81, local copies, waits for them, and re-layouts  9.32 us
    ppermute x4, starting transfers between devices, to_sequence(): got = lax.ppermute(sent, BOTH, pairs)  8.63 us
    dot_general x9, matrix products, dot(): return lax.dot_general(left, right, dims, preferred_element_type=WIDE)  8.53 us
  transfers between devices with their start and end apart: 19, of which 6 were waited for; matrix products, arithmetic and copies ran while one was open for 10% of the time, Pallas kernels for 16%

profile of v3, /device:TPU:0, one launch (start us, length us, event | category | flops | bytes accessed | tf_op | source)
XLA Modules:
  0.0 385.0 jit_solution(15577926964051361306)
XLA Ops:
  0.7 1.1 constant_dynamic-update-slice_fusion.2
  1.7 1.0 constant_dynamic-update-slice_fusion.1
  2.7 1.0 constant_dynamic-update-slice_fusion
  3.7 3.0 collective-permute-start.4
  6.7 1.5 collective-permute-start.5
  8.2 1.0 dynamic-slice_bitcast_fusion.4
  9.2 5.4 %collective-permute-start.1 = (bf16[256,1024]{1,0:T(8,128)(2,1)}, bf16[256,1024]{1,0:T(8,128)(2,1)}, u32[]{:S(2)}, u32[]{:S(2)}) collective-permute-start(bf16[256,1024]{1,0:T(8,128)(2,1)} %get-tuple-element.57), channel_id=1, source_target_pairs={{0,0},{1,16},{2,2},{3,18},{4,4},{5,20},{6,6},{7,22},{8,8},{9,24},{... | collective-permute-start | bytes 1572872 | tf_op jit(solution)/shard_map/ppermute | solution.py:1050
  14.6 1.6 collective-permute-start.2
  16.2 2.0 broadcast_in_dim.47
  18.2 1.0 bitcast_dynamic-update-slice_fusion.2
  19.3 1.1 dynamic-slice_bitcast_fusion.2
  20.4 2.7 fusion.7
  25.1 1.7 collective-permute-start.8
  26.9 1.1 bitcast_dynamic-update-slice_fusion.6
  28.0 6.3 %collective-permute-done.2 = bf16[256,1024]{1,0:T(8,128)(2,1)} collective-permute-done((bf16[256,1024]{1,0:T(8,128)(2,1)}, bf16[256,1024]{1,0:T(8,128)(2,1)}, u32[]{:S(2)}, u32[]{:S(2)}) %collective-permute-start.2) | collective-permute-done | bytes 524320 | tf_op jit(solution)/shard_map/ppermute | solution.py:1050
  34.2 1.1 bitcast_dynamic-update-slice_fusion.5
  36.0 2.5 collective-permute-start.3
  39.1 0.9 bitcast_dynamic-update-slice_fusion.1
  40.1 0.9 bitcast_dynamic-update-slice_fusion
  42.2 7.4 %collective-permute-done.6 = bf16[192,1024]{1,0:T(8,128)(2,1)S(1)} collective-permute-done((bf16[192,1024]{1,0:T(8,128)(2,1)S(1)}, bf16[192,1024]{1,0:T(8,128)(2,1)S(1)}, u32[]{:S(2)}, u32[]{:S(2)}) %collective-permute-start.6) | collective-permute-done | bytes 393248 | tf_op jit(solution)/shard_map/ppermute | solution.py:1017
  50.4 1.4 collective-permute-done.7
  51.8 0.8 bitcast_dynamic-update-slice_fusion.7
  52.6 2.4 fusion.20
  55.0 1.0 maximum_select_fusion.normed_ref
  56.1 1.3 convolution_convert_fusion.value_ref
  57.4 1.3 convolution_convert_fusion.1.key_ref
  58.7 1.3 convolution_convert_fusion.2.query_ref
  60.1 62.4 %attend.1 = (bf16[1024,512]{1,0:T(8,128)(2,1)S(1)}, f32[4,2,1024]{2,1,0:T(2,128)S(1)}, bf16[4,128,1024]{2,1,0:T(8,128)(2,1)S(1)}, bf16[4,512,1024]{2,1,0:T(8,128)(2,1)S(1)}, bf16[4,512,1024]{2,1,0:T(8,128)(2,1)}) custom-call(s32[1]{0:T(128)} %dynamic_slice.67.length_ref, bf16[1024,512]{1,0:T(8,128)(2,1)S(1)} %convolution_convert_fusion.2.query_ref, ...), custom_call_target="tpu_custom_call" | custom-call | flops 12884901888 | bytes 4194304 | tf_op jit(solution)/shard_map/attend/pallas_call | solution.py:216
  123.4 1.7 copy-done.9
  127.0 0.9 multiply_reduce_fusion.2
  128.1 1.3 copy-done.11
  129.9 2.3 maximum_select_fusion.3.grad_ref
  132.4 2.4 maximum_select_fusion.2.normed_ref
  134.9 40.9 %feed.1 = (bf16[2048,1024]{1,0:T(8,128)(2,1)}, bf16[2048,1024]{1,0:T(8,128)(2,1)}, f32[1024,1024]{1,0:T(8,128)}, f32[1024,1024]{1,0:T(8,128)}, bf16[512,1024]{1,0:T(8,128)(2,1)}, /*index=5*/bf16[512,1024]{1,0:T(8,128)(2,1)}) custom-call(bf16[1024,1024]{1,0:T(8,128)(2,1)} %maximum_select_fusion.2.normed_ref, ...), custom_call_target="tpu_custom_call" | custom-call | flops 25769803776 | bytes 29360128 | tf_op jit(solution)/shard_map/feed/pallas_call | solution.py:498
  175.8 3.4 constant_dynamic-slice_fusion.2
  179.2 1.5 constant_dynamic-slice_fusion.1
  181.2 2.5 collective-permute-done.15
  183.7 4.2 %multiply_reduce_fusion = (f32[1024]{0:T(1024)}, f32[512]{0:T(512)S(1)}, f32[512,1024]{1,0:T(8,128)S(1)}) fusion(f32[512,1024]{1,0:T(8,128)} %copy-done.11, f32[512]{0:T(512)S(1)} %add_rsqrt_fusion, f32[1024]{0:T(1024)S(1)} %copy-done.35, f32[512,1024]{1,0:T(8,128)} %collective-permute-done.15, f32[1024,1024]{1,0:T(8,128)} %get-tuple-element.29, ...), kind=kLoop, calls=%fused_computation.17 | loop fusion | flops 3668480 | bytes 8400900 | tf_op jit(solution)/shard_map/reduce_sum | solution.py:1213
  187.9 4.4 %fusion.18 = (bf16[512,1024]{1,0:T(8,128)(2,1)S(1)}, f32[512,1024]{1,0:T(8,128)}, bf16[512,1024]{1,0:T(8,128)(2,1)}) fusion(f32[512]{0:T(512)S(1)} %broadcast_multiply_fusion, f32[512,1024]{1,0:T(8,128)S(1)} %copy-done.12, f32[512,1024]{1,0:T(8,128)S(1)} %get-tuple-element.43, f32[1024]{0:T(1024)S(1)} %copy-done.35, f32[512]{0:T(512)S(1)} %add_rsqrt_fusion, ...), kind=kLoop, calls=%fused_computation.90 | loop fusion | flops 6815744 | bytes 13641732 | tf_op jit(solution)/shard_map/convert_element_type | solution.py:1214
  196.3 1.9 pad_maximum_fusion.weight_ref
  198.9 1.4 maximum_select_fusion.4.grad_ref
  200.8 1.1 maximum_select_fusion.5.output_ref
  201.9 172.7 %backward.1 = (bf16[2,256,1024]{2,1,0:T(8,128)(2,1)}, f32[2,256,1024]{2,1,0:T(8,128)}, f32[4,32,1024]{2,1,0:T(8,128)}, f32[2,128,1024]{2,1,0:T(8,128)}, f32[2,48,128]{2,1,0:T(8,128)}) custom-call(s32[1]{0:T(128)} %dynamic_slice.67.length_ref, bf16[1024,512]{1,0:T(8,128)(2,1)} %copy-done.8, bf16[1024,512]{1,0:T(8,128)(2,1)} %copy-done.7, ...), custom_call_target="tpu_custom_call" | custom-call | flops 32212254720 | bytes 7340032 | tf_op jit(solution)/shard_map/backward/pallas_call | solution.py:967
  374.7 0.9 rev.3
  377.2 2.3 slice_bitcast_fusion.2
  379.5 0.8 slice_bitcast_fusion.4
  382.2 1.0 copy.48
  383.2 1.3 copy.49
  (145 shorter events, 18.3 us)
Async XLA Ops:
  0.6 18.5 %copy-start = (f32[32,16]{0,1:T(8,128)S(1)}, f32[32,16]{0,1:T(8,128)}, u32[]{:S(2)}) copy-start(f32[32,16]{0,1:T(8,128)} %param.25) | copy-start | bytes 6148
  0.7 7.6 %copy-start.27 = (bf16[2,256,1024]{2,1,0:T(8,128)(2,1)S(1)}, bf16[2,256,1024]{2,1,0:T(8,128)(2,1)}, u32[]{:S(2)}) copy-start(bf16[2,256,1024]{2,1,0:T(8,128)(2,1)} %param.14) | copy-start | bytes 3145732
  0.7 15.5 %copy-start.37 = (s32[2]{0:T(128)S(1)}, s32[2]{0:T(128)}, u32[]{:S(2)}) copy-start(s32[2]{0:T(128)} %param.15) | copy-start | bytes 28
  3.7 34.8 %collective-permute-start.4 = (bf16[384,1024]{1,0:T(8,128)(2,1)S(1)}, bf16[384,1024]{1,0:T(8,128)(2,1)S(1)}, u32[]{:S(2)}, u32[]{:S(2)}) collective-permute-start(bf16[384,1024]{1,0:T(8,128)(2,1)S(1)} %constant_dynamic-update-slice_fusion), channel_id=1, source_target_pairs={{0,2},{1,3},{2,0},{3,1},{4,6},{5,7},{6,4},{7,5},{8,10},{9,11},{10,... | collective-permute-start | bytes 2359304 | tf_op jit(solution)/shard_map/ppermute | solution.py:1017
  6.7 29.3 %collective-permute-start.5 = (bf16[384,1024]{1,0:T(8,128)(2,1)S(1)}, bf16[384,1024]{1,0:T(8,128)(2,1)S(1)}, u32[]{:S(2)}, u32[]{:S(2)}) collective-permute-start(bf16[384,1024]{1,0:T(8,128)(2,1)S(1)} %constant_dynamic-update-slice_fusion), channel_id=1, source_target_pairs={{0,4},{1,5},{2,6},{3,7},{4,0},{5,1},{6,2},{7,3},{8,12},{9,13},{10,... | collective-permute-start | bytes 2359304 | tf_op jit(solution)/shard_map/ppermute | solution.py:1017
  9.2 15.8 %collective-permute-start.1 = (bf16[256,1024]{1,0:T(8,128)(2,1)}, bf16[256,1024]{1,0:T(8,128)(2,1)}, u32[]{:S(2)}, u32[]{:S(2)}) collective-permute-start(bf16[256,1024]{1,0:T(8,128)(2,1)} %get-tuple-element.57), channel_id=1, source_target_pairs={{0,0},{1,16},{2,2},{3,18},{4,4},{5,20},{6,6},{7,22},{8,8},{9,24},{... | collective-permute-start | bytes 1572872 | tf_op jit(solution)/shard_map/ppermute | solution.py:1050
  14.6 19.6 %collective-permute-start.2 = (bf16[256,1024]{1,0:T(8,128)(2,1)}, bf16[256,1024]{1,0:T(8,128)(2,1)}, u32[]{:S(2)}, u32[]{:S(2)}) collective-permute-start(bf16[256,1024]{1,0:T(8,128)(2,1)} %get-tuple-element.56), channel_id=1, source_target_pairs={{0,8},{1,24},{2,10},{3,26},{4,12},{5,28},{6,14},{7,30},{8,0},{9,16... | collective-permute-start | bytes 1572872 | tf_op jit(solution)/shard_map/ppermute | solution.py:1050
  16.2 7.0 %collective-permute-start = (s32[2]{0:T(128)S(1)}, s32[2]{0:T(128)S(1)}, u32[]{:S(2)}, u32[]{:S(2)}) collective-permute-start(s32[2]{0:T(128)S(1)} %copy-done.37), channel_id=1, source_target_pairs={{0,1},{1,0},{2,3},{3,2},{4,5},{5,4},{6,7},{7,6},{8,9},{9,8},{10,11... | collective-permute-start | bytes 32 | tf_op jit(solution)/shard_map/ppermute | solution.py:1017
  16.2 3.0 copy-start.34
  16.2 3.1 copy-start.28
  23.1 36.9 %copy-start.4 = (f32[8,1,512]{2,1,0:T(1,128)}, f32[8,1,512]{2,1,0:T(1,128)S(1)}, u32[]{:S(2)}) copy-start(f32[8,1,512]{2,1,0:T(1,128)S(1)} %broadcast_in_dim.55.near_ref) | copy-start | bytes 49156
  23.1 11.1 %copy-start.32 = (bf16[256,1024]{1,0:T(8,128)(2,1)S(1)}, bf16[256,1024]{1,0:T(8,128)(2,1)}, u32[]{:S(2)}) copy-start(bf16[256,1024]{1,0:T(8,128)(2,1)} %get-tuple-element.54) | copy-start | bytes 1572868
  23.1 17.9 %collective-permute-start.10 = (bf16[2,2,128,1024]{3,2,1,0:T(8,128)(2,1)}, bf16[2,2,128,1024]{3,2,1,0:T(8,128)(2,1)S(1)}, u32[]{:S(2)}, u32[]{:S(2)}) collective-permute-start(bf16[2,2,128,1024]{3,2,1,0:T(8,128)(2,1)} %get-tuple-element.51), channel_id=1, source_target_pairs={{0,1},{1,0},{2,3},{3,2},{4,5},{5,4},{6,7},{7,6},{8,9},{9,8},{10,11... | collective-permute-start | bytes 3145736 | tf_op jit(solution)/shard_map/ppermute | solution.py:1017
  25.0 10.6 %copy-start.36 = (f32[1024]{0:T(1024)S(1)}, f32[1024]{0:T(1024)}, u32[]{:S(2)}) copy-start(f32[1024]{0:T(1024)} %param.23) | copy-start | bytes 12292
  25.1 98.0 %collective-permute-start.8 = (bf16[256,1024]{1,0:T(8,128)(2,1)}, bf16[256,1024]{1,0:T(8,128)(2,1)S(1)}, u32[]{:S(2)}, u32[]{:S(2)}) collective-permute-start(bf16[256,1024]{1,0:T(8,128)(2,1)} %get-tuple-element.55), channel_id=1, source_target_pairs={{0,0},{1,16},{2,2},{3,18},{4,4},{5,20},{6,6},{7,22},{8,8},{9,24},{... | collective-permute-start | bytes 1572872 | tf_op jit(solution)/shard_map/ppermute | solution.py:1050
  34.2 89.1 %collective-permute-start.9 = (bf16[256,1024]{1,0:T(8,128)(2,1)S(1)}, bf16[256,1024]{1,0:T(8,128)(2,1)S(1)}, u32[]{:S(2)}, u32[]{:S(2)}) collective-permute-start(bf16[256,1024]{1,0:T(8,128)(2,1)S(1)} %copy-done.32), channel_id=1, source_target_pairs={{0,8},{1,24},{2,10},{3,26},{4,12},{5,28},{6,14},{7,30},{8,0},{9,16... | collective-permute-start | bytes 1572872 | tf_op jit(solution)/shard_map/ppermute | solution.py:1050
  35.3 91.7 %copy-start.13 = (bf16[2,256,1024]{2,1,0:T(8,128)(2,1)}, bf16[2,256,1024]{2,1,0:T(8,128)(2,1)S(1)}, u32[]{:S(2)}) copy-start(bf16[2,256,1024]{2,1,0:T(8,128)(2,1)S(1)} %bitcast_dynamic-update-slice_fusion.5) | copy-start | bytes 3145732
  36.0 19.1 %collective-permute-start.3 = (bf16[512,1024]{1,0:T(8,128)(2,1)S(1)}, bf16[512,1024]{1,0:T(8,128)(2,1)S(1)}, u32[]{:S(2)}, u32[]{:S(2)}) collective-permute-start(bf16[512,1024]{1,0:T(8,128)(2,1)S(1)} %fusion.1), channel_id=1, source_target_pairs={{0,1},{1,0},{2,3},{3,2},{4,5},{5,4},{6,7},{7,6},{8,9},{9,8},{10,11... | collective-permute-start | bytes 3145736 | tf_op jit(solution)/shard_map/ppermute | solution.py:1017
  38.5 11.1 %collective-permute-start.6 = (bf16[192,1024]{1,0:T(8,128)(2,1)S(1)}, bf16[192,1024]{1,0:T(8,128)(2,1)S(1)}, u32[]{:S(2)}, u32[]{:S(2)}) collective-permute-start(bf16[192,1024]{1,0:T(8,128)(2,1)S(1)} %slice.89), channel_id=1, source_target_pairs={{0,2},{1,3},{2,0},{3,1},{4,6},{5,7},{6,4},{7,5},{8,10},{9,11},{10,... | collective-permute-start | bytes 1179656 | tf_op jit(solution)/shard_map/ppermute | solution.py:1017
  41.0 10.8 %collective-permute-start.7 = (bf16[192,1024]{1,0:T(8,128)(2,1)S(1)}, bf16[192,1024]{1,0:T(8,128)(2,1)S(1)}, u32[]{:S(2)}, u32[]{:S(2)}) collective-permute-start(bf16[192,1024]{1,0:T(8,128)(2,1)S(1)} %slice.90), channel_id=1, source_target_pairs={{0,4},{1,5},{2,6},{3,7},{4,0},{5,1},{6,2},{7,3},{8,12},{9,13},{10,... | collective-permute-start | bytes 1179656 | tf_op jit(solution)/shard_map/ppermute | solution.py:1017
  42.2 17.8 %copy-start.2 = (bf16[1,2,2,128,1024]{4,3,2,1,0:T(8,128)(2,1)}, bf16[1,2,2,128,1024]{4,3,2,1,0:T(8,128)(2,1)S(1)}, u32[]{:S(2)}) copy-start(bf16[1,2,2,128,1024]{4,3,2,1,0:T(8,128)(2,1)S(1)} %get-tuple-element.48) | copy-start | bytes 3145732
  42.2 17.8 %copy-start.3 = (bf16[1,2,2,128,1024]{4,3,2,1,0:T(8,128)(2,1)}, bf16[1,2,2,128,1024]{4,3,2,1,0:T(8,128)(2,1)S(1)}, u32[]{:S(2)}) copy-start(bf16[1,2,2,128,1024]{4,3,2,1,0:T(8,128)(2,1)S(1)} %get-tuple-element.49) | copy-start | bytes 3145732
  55.0 2.4 copy-start.18
  55.0 3.7 copy-start.20
  56.0 2.6 copy-start.22
  57.3 2.7 copy-start.6
  60.0 62.5 %copy-start.8 = (bf16[1024,512]{1,0:T(8,128)(2,1)}, bf16[1024,512]{1,0:T(8,128)(2,1)S(1)}, u32[]{:S(2)}) copy-start(bf16[1024,512]{1,0:T(8,128)(2,1)S(1)} %convolution_convert_fusion.2.query_ref) | copy-start | bytes 3145732
  123.1 3.9 %collective-permute-start.12 = (bf16[512,1024]{1,0:T(8,128)(2,1)S(1)}, bf16[512,1024]{1,0:T(8,128)(2,1)S(1)}, u32[]{:S(2)}, u32[]{:S(2)}) collective-permute-start(bf16[512,1024]{1,0:T(8,128)(2,1)S(1)} %bitcast.130), channel_id=1, source_target_pairs={{0,1},{1,0},{2,3},{3,2},{4,5},{5,4},{6,7},{7,6},{8,9},{9,8},{10,11... | collective-permute-start | bytes 3145736 | tf_op jit(solution)/shard_map/ppermute | solution.py:1017
  123.3 3.3 copy-start.14
  125.1 1.9 collective-permute-start.11
  125.4 4.5 %collective-permute-start.14 = (bf16[512,1024]{1,0:T(8,128)(2,1)S(1)}, bf16[512,1024]{1,0:T(8,128)(2,1)S(1)}, u32[]{:S(2)}, u32[]{:S(2)}) collective-permute-start(bf16[512,1024]{1,0:T(8,128)(2,1)S(1)} %fusion.3), channel_id=1, source_target_pairs={{0,1},{1,0},{2,3},{3,2},{4,5},{5,4},{6,7},{7,6},{8,9},{9,8},{10,11... | collective-permute-start | bytes 3145736 | tf_op jit(solution)/shard_map/ppermute | solution.py:1017
  127.0 2.4 copy-start.35
  129.7 2.7 collective-permute-start.13
  175.8 3.4 copy-start.16
  179.2 4.5 %collective-permute-start.15 = (f32[512,1024]{1,0:T(8,128)}, f32[512,1024]{1,0:T(8,128)}, u32[]{:S(2)}, u32[]{:S(2)}) collective-permute-start(f32[512,1024]{1,0:T(8,128)} %constant_dynamic-slice_fusion.2), channel_id=1, source_target_pairs={{0,1},{1,0},{2,3},{3,2},{4,5},{5,4},{6,7},{7,6},{8,9},{9,8},{10,11... | collective-permute-start | bytes 6291464 | tf_op jit(solution)/shard_map/ppermute | solution.py:1017
  180.7 7.2 %collective-permute-start.18 = (f32[512,1024]{1,0:T(8,128)}, f32[512,1024]{1,0:T(8,128)}, u32[]{:S(2)}, u32[]{:S(2)}) collective-permute-start(f32[512,1024]{1,0:T(8,128)} %constant_dynamic-slice_fusion.1), channel_id=1, source_target_pairs={{0,1},{1,0},{2,3},{3,2},{4,5},{5,4},{6,7},{7,6},{8,9},{9,8},{10,11... | collective-permute-start | bytes 6291464 | tf_op jit(solution)/shard_map/ppermute | solution.py:1017
  181.2 6.7 %copy-start.12 = (f32[512,1024]{1,0:T(8,128)S(1)}, f32[512,1024]{1,0:T(8,128)}, u32[]{:S(2)}) copy-start(f32[512,1024]{1,0:T(8,128)} %copy-done.11) | copy-start | bytes 6291460
  181.2 6.7 %copy-start.15 = (bf16[2,256,1024]{2,1,0:T(8,128)(2,1)S(1)}, bf16[2,256,1024]{2,1,0:T(8,128)(2,1)}, u32[]{:S(2)}) copy-start(bf16[2,256,1024]{2,1,0:T(8,128)(2,1)} %copy-done.14) | copy-start | bytes 3145732
  181.2 6.7 %copy-start.17 = (f32[1024,1024]{1,0:T(8,128)S(1)}, f32[1024,1024]{1,0:T(8,128)}, u32[]{:S(2)}) copy-start(f32[1024,1024]{1,0:T(8,128)} %get-tuple-element.31) | copy-start | bytes 12582916
  194.3 2.0 copy-start.19
  194.3 2.0 copy-start.21
  194.3 6.1 %collective-permute-start.17 = (bf16[2,4,2,32,1024]{4,3,2,1,0:T(8,128)(2,1)S(1)}, bf16[2,4,2,32,1024]{4,3,2,1,0:T(8,128)(2,1)S(1)}, u32[]{:S(2)}, u32[]{:S(2)}) collective-permute-start(bf16[2,4,2,32,1024]{4,3,2,1,0:T(8,128)(2,1)S(1)} %pad_maximum_fusion.1), channel_id=1, source_target_pairs={{0,1},{1,0},{2,3},{3,2},{4,5},{5,4},{6,7},{7,6},{8,9},{9,8},{10,11... | collective-permute-start | bytes 3145736 | tf_op jit(solution)/shard_map/ppermute | solution.py:1017
  196.0 2.8 collective-permute-start.16
  374.6 4.8 %copy-start.31 = (f32[4,32,1024]{2,1,0:T(8,128)S(1)}, f32[4,32,1024]{2,1,0:T(8,128)}, u32[]{:S(2)}) copy-start(f32[4,32,1024]{2,1,0:T(8,128)} %get-tuple-element.36) | copy-start | bytes 1572868
  374.7 6.8 %copy-start.33 = (f32[32,512]{1,0:T(8,128)S(1)}, f32[32,512]{1,0:T(8,128)}, u32[]{:S(2)}) copy-start(f32[32,512]{1,0:T(8,128)} %constant.140.clone) | copy-start | bytes 196612
  374.7 7.6 %copy-start.26 = (bf16[2,256,1024]{2,1,0:T(8,128)(2,1)S(1)}, bf16[2,256,1024]{2,1,0:T(8,128)(2,1)}, u32[]{:S(2)}) copy-start(bf16[2,256,1024]{2,1,0:T(8,128)(2,1)} %get-tuple-element.79) | copy-start | bytes 3145732
  379.5 3.7 copy-start.23
  382.2 2.3 copy-start.1
  (9 other events, 11.0 us)

commit v4 on v3

--- a/solution.py
+++ b/solution.py
@@ -32,6 +32,11 @@
     return lax.dot_general(left, right, dims, preferred_element_type=WIDE)
 
 
+def inverse_root(value):
+    root = lax.rsqrt(value)
+    return root * (1.5 - 0.5 * value * root * root)
+
+
 def gelu_parts(value):
     cumulative = 0.5 * (1.0 + lax.erf(value * ROOT_HALF))
     slope = cumulative + value * jnp.exp(-0.5 * value * value) * NORMAL_PEAK
@@ -121,57 +126,10 @@
     out[1] = jnp.where(low_half, spare, pair)
 
 
-def gather_moves(mine, wholes, sems):
-    chip = chip_of()
-    direct = []
-    for number, (one, whole_one) in enumerate(zip(mine, wholes)):
-        for place, bit in enumerate((ALONG_X, ALONG_Y)):
-            direct.append(send(one, whole_one.at[chip], sems, 2 * number + place, bit))
-    first = wholes[0]
-    half = first.shape[1] // 2
-    onward = []
-    for place, (bit, came) in enumerate(((ALONG_X, ALONG_Y), (ALONG_Y, ALONG_X))):
-        piece = first.at[chip_of(came), pl.ds(place * half, half)]
-        onward.append(send(piece, piece, sems, 2 * len(mine) + place, bit))
-    return (direct, onward)
-
-
-def attend_kernel(gathered, length_ref, query_ref, key_ref, value_ref, near_ref, *refs):
-    mine, refs = (refs[:gathered], refs[gathered:])
-    context_ref, log_ref = refs[:2]
-    wholes, refs = (refs[2 : 2 + gathered], refs[2 + gathered :])
-    bias, keys, values = refs[:3]
+def attend_kernel(
+    length_ref, query_ref, key_ref, value_ref, near_ref, context_ref, log_ref, bias, keys, values
+):
     rows = query_ref.shape[0]
-    if gathered:
-        sems, local = refs[3:]
-        pair = pl.program_id(0)
-        direct, onward = gather_moves(mine, wholes, sems)
-        own = pltpu.make_async_copy(mine[0], wholes[0].at[chip_of()], local)
-
-        @pl.when(pair == 0)
-        def _():
-            greet((ALONG_X, ALONG_Y))
-            own.start()
-            for one in direct:
-                one.start()
-
-        @pl.when(pair == 1)
-        def _():
-            for one in direct[:2]:
-                one.wait_recv()
-            for one in onward:
-                one.start()
-
-        @pl.when(pair == pl.num_programs(0) - 1)
-        def _():
-            own.wait()
-            for one in direct:
-                one.wait_send()
-            for one in direct[2:]:
-                one.wait_recv()
-            for one in onward:
-                one.wait()
-
     split_heads(key_ref[...], spare_lanes(length_ref[0], rows), keys)
     split_heads(value_ref[...], jnp.zeros((rows, LANES), LOW), values)
     near_start = rows - QUERY_ROWS - HALF_ROWS
@@ -206,40 +164,32 @@
     lax.fori_loop(0, rows // QUERY_ROWS, block, 0)
 
 
-def attend(length, query, key, value, near, mine=()):
+def attend(length, query, key, value, near):
     rows, width = query.shape
     pairs = width // LANES
-    anywhere = pl.BlockSpec(memory_space=pl.ANY)
-    gathered = len(mine)
     smem = pl.BlockSpec(memory_space=pltpu.SMEM)
     columns = pl.BlockSpec((rows, LANES), lambda pair: (0, pair))
     return pl.pallas_call(
-        functools.partial(attend_kernel, gathered),
+        attend_kernel,
         grid=(pairs,),
         in_specs=[smem, columns, columns, columns]
-        + [pl.BlockSpec((2, 1, 2 * QUERY_ROWS), lambda pair: (pair, 0, 0))]
-        + [anywhere] * gathered,
-        out_specs=[columns, pl.BlockSpec((1, 2, rows), lambda pair: (pair, 0, 0))] + [anywhere] * gathered,
+        + [pl.BlockSpec((2, 1, 2 * QUERY_ROWS), lambda pair: (pair, 0, 0))],
+        out_specs=[columns, pl.BlockSpec((1, 2, rows), lambda pair: (pair, 0, 0))],
         out_shape=[
             jax.ShapeDtypeStruct((rows, width), LOW),
             jax.ShapeDtypeStruct((pairs, 2, rows), WIDE),
-        ]
-        + [jax.ShapeDtypeStruct((4,) + one.shape, LOW) for one in mine],
+        ],
         scratch_shapes=[
             pltpu.VMEM((2, QUERY_ROWS, 2 * rows - QUERY_ROWS), WIDE),
             pltpu.VMEM((2, rows, LANES), LOW),
             pltpu.VMEM((2, rows, LANES), LOW),
-        ]
-        + ([pltpu.SemaphoreType.DMA((2, 2 * gathered + 2)), pltpu.SemaphoreType.DMA] if gathered else []),
-        compiler_params=pltpu.CompilerParams(
-            vmem_limit_bytes=40 << 20,
-            **({"collective_id": 1, "has_side_effects": True} if gathered else {}),
-        ),
+        ],
+        compiler_params=pltpu.CompilerParams(vmem_limit_bytes=40 << 20),
         cost_estimate=pl.CostEstimate(
             flops=24 * rows * rows * width, bytes_accessed=8 * rows * width, transcendentals=2 * pairs * rows * rows
         ),
         name="attend",
-    )(length, query, key, value, near, *mine)
+    )(length, query, key, value, near)
 
 
 def attend_grad_kernel(
@@ -375,156 +325,46 @@
     )
 
 
-def feed_kernel(pieces, normed_ref, grad_ref, *refs):
-    moved = pieces > 1
-    kinds = 2
-    mine, refs = (refs[:kinds], refs[kinds:])
-    if moved:
-        wholes, refs = (refs[:kinds], refs[kinds:])
-    parts, refs = (refs[:kinds], refs[kinds:])
-    out_ref, back_ref = refs[:2]
-    refs = refs[2:]
-    if moved:
-        fars, refs = (refs[:kinds], refs[kinds:])
-    slots, stages, refs = (refs[:2], refs[2:4], refs[4:])
-    arrived, stored = refs[:2]
-    step, steps = (pl.program_id(0), pl.num_programs(0))
-    unit = slots[0].shape[1]
-    slot = lax.rem(step, 2)
-
-    if moved:
-        sems = refs[2]
-        half = unit // 2
-        moves = []
-        for kind in range(kinds):
-            for place, (bit, came) in enumerate(((ALONG_X, ALONG_Y), (ALONG_Y, ALONG_X))):
-                there = pl.ds(place * half, half)
-                source = wholes[kind].at[chip_of(came), there]
-                moves.append(send(source, fars[kind].at[there], sems, 2 * kind + place, bit))
-        sources = [
-            mine,
-            [one.at[chip_of(ALONG_X)] for one in wholes],
-            [one.at[chip_of(ALONG_Y)] for one in wholes],
-            fars,
-        ]
-        places = [chip_of(), chip_of(ALONG_X), chip_of(ALONG_Y), chip_of(ALONG_X, ALONG_Y)]
-
-        def fetch(block, into):
-            for number, pair in enumerate(sources):
-
-                @pl.when(block == number)
-                def _():
-                    for kind in range(kinds):
-                        pltpu.make_async_copy(pair[kind], slots[kind].at[into], arrived.at[kind, into]).start()
-
-        def store(block, kind, from_slot, act):
-            for number, place in enumerate(places):
-
-                @pl.when(block == number)
-                def _():
-                    act(
-                        pltpu.make_async_copy(
-                            stages[kind].at[from_slot],
-                            parts[kind].at[pl.ds(pl.multiple_of(place * unit, unit), unit)],
-                            stored.at[kind, from_slot],
-                        )
-                    )
-    else:
-
-        def fetch(block, into):
-            rows = pl.ds(pl.multiple_of(block * unit, unit), unit)
-            for kind in range(kinds):
-                pltpu.make_async_copy(mine[kind].at[rows], slots[kind].at[into], arrived.at[kind, into]).start()
-
-        def store(block, kind, from_slot, act):
-            rows = pl.ds(pl.multiple_of(block * unit, unit), unit)
-            act(pltpu.make_async_copy(stages[kind].at[from_slot], parts[kind].at[rows], stored.at[kind, from_slot]))
-
-    @pl.when(step == 0)
+def feed_kernel(normed_ref, grad_ref, up_ref, down_ref, up_part_ref, down_part_ref, out_ref, back_ref):
+    @pl.when(pl.program_id(0) == 0)
     def _():
-        if moved:
-            greet((ALONG_X, ALONG_Y))
-            for one in moves:
-                one.start()
-        fetch(0, 0)
         out_ref[...] = jnp.zeros_like(out_ref)
         back_ref[...] = jnp.zeros_like(back_ref)
 
-    @pl.when(step + 1 < steps - moved)
-    def _():
-        fetch(step + 1, 1 - slot)
-
-    for kind in range(kinds):
-        pltpu.make_async_copy(slots[kind].at[slot], slots[kind].at[slot], arrived.at[kind, slot]).wait()
-    up, down = (slots[0][slot], slots[1][slot])
+    up, down = (up_ref[...], down_ref[...])
     normed, grad = (normed_ref[...], grad_ref[...])
     active, slope = gelu_parts(dot(normed, up, NT))
     active = active.astype(LOW)
     pre_grad = (dot(grad, down, NT) * slope).astype(LOW)
     out_ref[...] += dot(active, down)
     back_ref[...] += dot(pre_grad, up)
-
-    @pl.when(step >= 2)
-    def _():
-        for kind in range(kinds):
-            store(step - 2, kind, slot, lambda copy: copy.wait())
-
-    stages[0][slot] = dot(pre_grad, normed, TN).astype(LOW)
-    stages[1][slot] = dot(active, grad, TN).astype(LOW)
-    for kind in range(kinds):
-        store(step, kind, slot, lambda copy: copy.start())
-
-    if moved:
-
-        @pl.when(step == steps - 2)
-        def _():
-            for one in moves:
-                one.wait()
-            fetch(step + 1, 1 - slot)
-
-    @pl.when(step == steps - 1)
-    def _():
-        for kind in range(kinds):
-            store(step - 1, kind, 1 - slot, lambda copy: copy.wait())
-            store(step, kind, slot, lambda copy: copy.wait())
-
-
-def feed(normed, grad, mine, wholes=()):
+    up_part_ref[...] = dot(pre_grad, normed, TN).astype(LOW)
+    down_part_ref[...] = dot(active, grad, TN).astype(LOW)
+
+
+def feed(normed, grad, up, down):
     rows, width = normed.shape
-    moved = bool(wholes)
-    unit = mine[0].shape[0] if moved else mine[0].shape[0] // 4
-    anywhere = pl.BlockSpec(memory_space=pl.ANY)
+    unit = up.shape[0] // 4
     fixed = pl.BlockSpec((rows, width), lambda step: (0, 0))
+    block = pl.BlockSpec((unit, width), lambda step: (step, 0))
     return pl.pallas_call(
-        functools.partial(feed_kernel, 4 if moved else 1),
+        feed_kernel,
         grid=(4,),
-        in_specs=[fixed, fixed] + [anywhere] * (4 if moved else 2),
-        out_specs=[anywhere, anywhere, fixed, fixed] + ([anywhere, anywhere] if moved else []),
+        in_specs=[fixed, fixed, block, block],
+        out_specs=[block, block, fixed, fixed],
         out_shape=[jax.ShapeDtypeStruct((4 * unit, width), LOW)] * 2
-        + [jax.ShapeDtypeStruct((rows, width), WIDE)] * 2
-        + ([jax.ShapeDtypeStruct((unit, width), LOW)] * 2 if moved else []),
-        scratch_shapes=[pltpu.VMEM((2, unit, width), LOW)] * 4
-        + [pltpu.SemaphoreType.DMA((2, 2)), pltpu.SemaphoreType.DMA((2, 2))]
-        + ([pltpu.SemaphoreType.DMA((2, 4))] if moved else []),
-        compiler_params=pltpu.CompilerParams(
-            vmem_limit_bytes=56 << 20,
-            **({"collective_id": 2, "has_side_effects": True} if moved else {}),
-        ),
-        cost_estimate=pl.CostEstimate(
-            flops=48 * unit * rows * width,
-            bytes_accessed=32 * unit * width + 12 * rows * width,
-            transcendentals=8 * unit * rows,
-        ),
+        + [jax.ShapeDtypeStruct((rows, width), WIDE)] * 2,
+        compiler_params=pltpu.CompilerParams(vmem_limit_bytes=56 << 20),
         name="feed",
-    )(normed, grad, *mine, *wholes)[:4]
-
-
-def push(source, target, sems, number, place, index):
+    )(normed, grad, up, down)
+
+
+def push(source, target, sems, number, place, index, there=None):
     return pltpu.make_async_remote_copy(
         src_ref=source,
         dst_ref=target,
         send_sem=sems.at[(0,) + number],
-        recv_sem=sems.at[(1,) + number],
+        recv_sem=sems.at[(1,) + (there or number)],
         device_id={"seq": place, "fsdp": index},
         device_id_type=pl.DeviceIdType.MESH,
     )
@@ -546,6 +386,677 @@
         signal(lax.rem(place + step, depth), index)
         signal(lax.rem(place + step, depth), partner(CORE))
     pl.semaphore_wait(barrier, 2 * depth + 1)
+
+
+def slots_moves(source, target, sems, depth, act):
+    held = depth // 2
+    place, index = (lax.axis_index("seq"), lax.axis_index("fsdp"))
+    core = lax.rem(index, 2)
+    slot = lax.rem(place, held)
+    for sequence in range(held):
+        there, which = (core * held + sequence, index - core + place // held)
+        home = (there == place) & (which == index)
+
+        @pl.when(home)
+        def _():
+            if act == "start":
+                pltpu.make_async_copy(source.at[sequence], target.at[slot], sems.at[1, slot]).start()
+
+        @pl.when(jnp.logical_not(home))
+        def _():
+            move = push(source.at[sequence], target.at[slot], sems, (sequence,), there, which, (slot,))
+            if act == "start":
+                move.start()
+            else:
+                move.wait_send()
+
+
+def slots_came(target, sems, slot):
+    push(target.at[slot], target.at[slot], sems, (slot,), lax.axis_index("seq"), partner(CORE)).wait_recv()
+
+
+def enter_kernel(
+    depth,
+    inputs_ref,
+    query_ref,
+    key_ref,
+    value_ref,
+    up_ref,
+    down_ref,
+    gain_ref,
+    normed_out_ref,
+    query_out_ref,
+    key_out_ref,
+    value_out_ref,
+    source_out_ref,
+    weights_out_ref,
+    up_out_ref,
+    down_out_ref,
+    normed_ref,
+    source_ref,
+    weights_ref,
+    slot_sems,
+    near_sems,
+    far_sems,
+    cut_sems,
+    row_sems,
+    local_sems,
+):
+    held = depth // 2
+    span = source_ref.shape[1]
+    rows = normed_ref.shape[0]
+    index = lax.axis_index("fsdp")
+    core = lax.rem(index, 2)
+    chip = chip_of()
+    mine = (query_ref, key_ref, value_ref)
+    half = query_ref.shape[0] // 2
+    greet_column(depth)
+    slots_moves(inputs_ref, source_ref, slot_sems, depth, "start")
+    direct = [
+        send(one, weights_ref.at[chip, kind], near_sems, 2 * kind + turn, bit)
+        for kind, one in enumerate(mine)
+        for turn, bit in enumerate((ALONG_X, ALONG_Y))
+    ]
+    for one in direct:
+        one.start()
+    local = [
+        pltpu.make_async_copy(one, weights_ref.at[chip, kind], local_sems.at[kind]) for kind, one in enumerate(mine)
+    ]
+    cuts = []
+    for kind, (whole_one, out) in enumerate(((up_ref, up_out_ref), (down_ref, down_out_ref))):
+        cuts.append(send(whole_one.at[:, 1 - core], out.at[core], cut_sems, kind, CORE))
+        local.append(pltpu.make_async_copy(whole_one.at[:, core], out.at[core], local_sems.at[3 + kind]))
+    for one in cuts + local:
+        one.start()
+    for one in direct:
+        one.wait_recv()
+    onward = []
+    for turn, (bit, came) in enumerate(((ALONG_X, ALONG_Y), (ALONG_Y, ALONG_X))):
+        piece = weights_ref.at[chip_of(came), :, pl.ds(turn * half, half)]
+        onward.append(send(piece, piece, far_sems, turn, bit))
+    for one in onward:
+        one.start()
+
+    moves = []
+    for slot in range(held):
+        slots_came(source_ref, slot_sems, slot)
+        source = source_ref[slot].astype(WIDE)
+        rms = inverse_root(jnp.mean(source * source, axis=1, keepdims=True) + EPSILON)
+        here = pl.ds(pl.multiple_of(core * (rows // 2) + slot * span, span), span)
+        normed_ref[here, :] = (source * rms * gain_ref[...]).astype(LOW)
+        moves.append(send(normed_ref.at[here], normed_ref.at[here], row_sems, slot, CORE))
+        moves[-1].start()
+    for one in moves:
+        one.wait()
+    for one in local[:3]:
+        one.wait()
+
+    def project(number):
+        weight = weights_ref[number].reshape(-1, weights_ref.shape[3])
+        product = dot(normed_ref[...], weight, NT).astype(LOW)
+        lanes = pl.ds(pl.multiple_of(number * LANES, LANES), LANES)
+        for kind, out in enumerate((query_out_ref, key_out_ref, value_out_ref)):
+            out[:, lanes] = product[:, kind * LANES : (kind + 1) * LANES]
+
+    def some(turn, carry):
+        project(lax.rem(chip + turn, 4))
+        return carry
+
+    for one in onward:
+        one.wait()
+    stored = [
+        pltpu.make_async_copy(one, there, local_sems.at[5 + number])
+        for number, (one, there) in enumerate(
+            ((normed_ref, normed_out_ref), (source_ref, source_out_ref), (weights_ref, weights_out_ref))
+        )
+    ]
+    for one in stored:
+        one.start()
+    lax.fori_loop(0, 4, some, 0)
+    for one in stored:
+        one.wait()
+    for one in direct:
+        one.wait_send()
+    for one in cuts + local[3:]:
+        one.wait()
+    slots_moves(inputs_ref, source_ref, slot_sems, depth, "end")
+
+
+def enter(inputs, projections, up, down, gain):
+    held, span, width = inputs.shape
+    depth = lax.axis_size("seq")
+    rows = 2 * held * span
+    slim = projections[0].shape[0]
+    thick = up.shape[0] // 4
+    vmem, anywhere = (pl.BlockSpec(memory_space=pltpu.VMEM), pl.BlockSpec(memory_space=pltpu.HBM))
+    shape = jax.ShapeDtypeStruct
+    return pl.pallas_call(
+        functools.partial(enter_kernel, depth),
+        in_specs=[anywhere] * 6 + [vmem],
+        out_specs=[anywhere] + [vmem] * 3 + [anywhere] * 4,
+        out_shape=[shape((rows, width), LOW)]
+        + [shape((rows, 4 * slim), LOW)] * 3
+        + [shape((held, span, width), LOW), shape((4, 3, slim, width), LOW)]
+        + [shape((2, 2, thick, width), LOW)] * 2,
+        scratch_shapes=[
+            pltpu.VMEM((rows, width), LOW),
+            pltpu.VMEM((held, span, width), LOW),
+            pltpu.VMEM((4, 3, slim, width), LOW),
+            pltpu.SemaphoreType.DMA((2, held)),
+            pltpu.SemaphoreType.DMA((2, 6)),
+            pltpu.SemaphoreType.DMA((2, 2)),
+            pltpu.SemaphoreType.DMA((2, 2)),
+            pltpu.SemaphoreType.DMA((2, held)),
+            pltpu.SemaphoreType.DMA((8,)),
+        ],
+        compiler_params=pltpu.CompilerParams(vmem_limit_bytes=62 << 20, collective_id=4, has_side_effects=True),
+        cost_estimate=pl.CostEstimate(flops=24 * rows * slim * width, bytes_accessed=16 << 20, transcendentals=0),
+        name="enter",
+    )(inputs, *projections, up.reshape(2, 2, thick, width), down.reshape(2, 2, thick, width), gain)
+
+
+def through_kernel(
+    depth,
+    length_ref,
+    query_ref,
+    key_ref,
+    value_ref,
+    near_ref,
+    source_ref,
+    gain_ref,
+    output_ref,
+    up_ref,
+    down_ref,
+    cotangent_ref,
+    log_ref,
+    context_ref,
+    hidden_ref,
+    far_context_out_ref,
+    own_output_out_ref,
+    far_output_out_ref,
+    normed_ref,
+    grad_ref,
+    ups_ref,
+    downs_ref,
+    bias,
+    keys,
+    values,
+    context,
+    came,
+    far_context_ref,
+    own_output_ref,
+    far_output_ref,
+    normed,
+    grad,
+    slot_sems,
+    near_sems,
+    far_sems,
+    core_sems,
+    context_sems,
+    local,
+):
+    rows = query_ref.shape[0]
+    width = source_ref.shape[1]
+    pair = pl.program_id(0)
+    last = depth - 1
+    held = depth // 2
+    core = lax.rem(lax.axis_index("fsdp"), 2)
+    chip = chip_of()
+    own = pl.ds(pl.multiple_of(core * (rows // 2), rows // 2), rows // 2)
+    other = pl.ds(pl.multiple_of((1 - core) * (rows // 2), rows // 2), rows // 2)
+    half = output_ref.shape[0] // 2
+    direct = []
+    unit = up_ref.shape[0] // 2
+    for first in (None, 0, unit):
+        for one, there in ((output_ref, own_output_ref),) if first is None else ((up_ref, ups_ref), (down_ref, downs_ref)):
+            for bit in (ALONG_X, ALONG_Y):
+                source, target = (one, there.at[chip])
+                if first is not None:
+                    source, target = (source.at[pl.ds(first, unit)], target.at[pl.ds(first, unit)])
+                direct.append(send(source, target, near_sems, len(direct), bit))
+    onward = []
+    for turn, (bit, from_bit) in enumerate(((ALONG_X, ALONG_Y), (ALONG_Y, ALONG_X))):
+        piece = own_output_ref.at[chip_of(from_bit), pl.ds(turn * half, half)]
+        onward.append(send(piece, piece, far_sems, turn, bit))
+    keep = pltpu.make_async_copy(output_ref, own_output_ref.at[chip], local.at[0])
+    swap = send(own_output_ref, far_output_ref, core_sems, 0, CORE)
+    both_cores = [
+        (send(one, there.at[own], core_sems, 1 + number, CORE), pltpu.make_async_copy(one, there.at[own], local.at[1 + number]))
+        for number, (one, there) in enumerate(((grad, grad_ref), (normed, normed_ref)))
+    ]
+    stored = [
+        pltpu.make_async_copy(one, there, local.at[3 + number])
+        for number, (one, there) in enumerate(
+            (
+                (own_output_ref, own_output_out_ref),
+                (far_output_ref, far_output_out_ref),
+                (far_context_ref, far_context_out_ref),
+            )
+        )
+    ]
+
+    def context_move(number):
+        lanes = pl.ds(pl.multiple_of(number * LANES, LANES), LANES)
+        return send(context.at[other, lanes], far_context_ref.at[:, lanes], context_sems, number, CORE)
+
+    @pl.when(pair == 0)
+    def _():
+        greet_column(depth)
+        for one in direct[:4]:
+            one.start()
+        keep.start()
+        slots_moves(cotangent_ref, came, slot_sems, depth, "start")
+
+    @pl.when(pair == 1)
+    def _():
+        for one in direct[:2]:
+            one.wait_recv()
+        for one in onward + direct[4:]:
+            one.start()
+
+    @pl.when(pair == last)
+    def _():
+        for one in onward:
+            one.wait()
+        keep.wait()
+        swap.start()
+        stored[0].start()
+        slot_ids = core * (rows // 2) + lax.broadcasted_iota(jnp.int32, (rows // 2, 1), 0)
+        valid = (slot_ids < length_ref[0]).astype(WIDE)
+        for slot in range(held):
+            slots_came(came, slot_sems, slot)
+        grad[...] = (came[...].reshape(rows // 2, width).astype(WIDE) * valid).astype(LOW)
+        for one in both_cores[0]:
+            one.start()
+
+    lanes = pl.ds(pl.multiple_of(pair * LANES, LANES), LANES)
+    split_heads(key_ref[...], spare_lanes(length_ref[0], rows), keys)
+    split_heads(value_ref[...], jnp.zeros((rows, LANES), LOW), values)
+    near_start = rows - QUERY_ROWS - HALF_ROWS
+    near_end = near_start + 2 * QUERY_ROWS
+    for head in range(2):
+        line = near_ref[head]
+        bias[head, :, :near_start] = jnp.broadcast_to(line[:, :1], (QUERY_ROWS, near_start))
+        bias[head, :, near_start:near_end] = near_block(line)
+        bias[head, :, near_end:] = jnp.broadcast_to(line[:, -1:], (QUERY_ROWS, bias.shape[2] - near_end))
+    lane = lax.broadcasted_iota(jnp.int32, (QUERY_ROWS, LANES), 1)
+    ones = jnp.where(lax.rem(lane, HEAD_DIM) == 0, 1.0, 0.0).astype(LOW)
+
+    def block(number, carry):
+        start = pl.multiple_of(number * QUERY_ROWS, QUERY_ROWS)
+        offset = pl.multiple_of(rows - QUERY_ROWS - number * QUERY_ROWS, LANES)
+        both = query_ref[pl.ds(start, QUERY_ROWS), :]
+        total = jnp.zeros((QUERY_ROWS, LANES), WIDE)
+        for head in range(2):
+            mine = lane < HEAD_DIM if head == 0 else lane >= HEAD_DIM
+            logits = dot(jnp.where(mine, both, ones), keys[head], NT)
+            logits = logits + bias[head, :, pl.ds(offset, rows)]
+            peak = jnp.max(logits, axis=1, keepdims=True)
+            exponent = jnp.exp(logits - peak)
+            row_sum = jnp.sum(exponent, axis=1, keepdims=True)
+            weights_low = (exponent * (1.0 / row_sum)).astype(LOW)
+            total = total + dot(weights_low, values[head])
+            logs = jnp.broadcast_to(peak + jnp.log(row_sum), (QUERY_ROWS, LANES))
+            log_ref[0, head : head + 1, pl.ds(start, QUERY_ROWS)] = logs.T[0:1, :]
+        context[pl.ds(start, QUERY_ROWS), lanes] = total.astype(LOW)
+        return carry
+
+    lax.fori_loop(0, rows // QUERY_ROWS, block, 0)
+    context_move(pair).start()
+    context_ref[:, lanes] = context[own, lanes]
+
+    @pl.when(pair == last)
+    def _():
+        swap.wait()
+        for number in range(last + 1):
+            context_move(number).wait()
+        for one in stored[1:]:
+            one.start()
+        inner = context_ref.shape[1]
+        attended = dot(context_ref[...], own_output_ref[...].reshape(inner, width))
+        attended = attended + dot(far_context_ref[...], far_output_ref[...].reshape(inner, width))
+        hidden = source_ref[...].astype(WIDE) + attended
+        hidden_ref[...] = hidden
+        rms = inverse_root(jnp.mean(hidden * hidden, axis=1, keepdims=True) + EPSILON)
+        normed[...] = (hidden * rms * gain_ref[...]).astype(LOW)
+        for one in both_cores[1]:
+            one.start()
+        for one in direct:
+            one.wait_send()
+        for one in direct[2:]:
+            one.wait_recv()
+        slots_moves(cotangent_ref, came, slot_sems, depth, "end")
+        for one in both_cores[0] + both_cores[1]:
+            one.wait()
+        for one in stored:
+            one.wait()
+
+
+def through(length, query, key, value, near, source, gain, output, up, down, cotangent):
+    rows, inner = query.shape
+    held, span, width = cotangent.shape
+    depth = lax.axis_size("seq")
+    pairs = inner // LANES
+    vmem, anywhere = (pl.BlockSpec(memory_space=pltpu.VMEM), pl.BlockSpec(memory_space=pltpu.HBM))
+    columns = pl.BlockSpec((rows, LANES), lambda pair: (0, pair))
+    shape = jax.ShapeDtypeStruct
+    outputs = (4,) + output.shape
+    return pl.pallas_call(
+        functools.partial(through_kernel, depth),
+        grid=(pairs,),
+        in_specs=[pl.BlockSpec(memory_space=pltpu.SMEM), columns, columns, columns]
+        + [pl.BlockSpec((2, 1, 2 * QUERY_ROWS), lambda pair: (pair, 0, 0)), vmem, vmem]
+        + [anywhere] * 4,
+        out_specs=[pl.BlockSpec((1, 2, rows), lambda pair: (pair, 0, 0))] + [vmem] * 2 + [anywhere] * 7,
+        out_shape=[shape((pairs, 2, rows), WIDE)]
+        + [shape((rows // 2, inner), LOW), shape((rows // 2, width), WIDE), shape((rows // 2, inner), LOW)]
+        + [shape(outputs, LOW)] * 2
+        + [shape((rows, width), LOW)] * 2
+        + [shape((4,) + up.shape, LOW)] * 2,
+        scratch_shapes=[
+            pltpu.VMEM((2, QUERY_ROWS, 2 * rows - QUERY_ROWS), WIDE),
+            pltpu.VMEM((2, rows, LANES), LOW),
+            pltpu.VMEM((2, rows, LANES), LOW),
+            pltpu.VMEM((rows, inner), LOW),
+            pltpu.VMEM((held, span, width), LOW),
+            pltpu.VMEM((rows // 2, inner), LOW),
+            pltpu.VMEM(outputs, LOW),
+            pltpu.VMEM(outputs, LOW),
+            pltpu.VMEM((rows // 2, width), LOW),
+            pltpu.VMEM((rows // 2, width), LOW),
+            pltpu.SemaphoreType.DMA((2, held)),
+            pltpu.SemaphoreType.DMA((2, 10)),
+            pltpu.SemaphoreType.DMA((2, 2)),
+            pltpu.SemaphoreType.DMA((2, 3)),
+            pltpu.SemaphoreType.DMA((2, pairs)),
+            pltpu.SemaphoreType.DMA((6,)),
+        ],
+        compiler_params=pltpu.CompilerParams(vmem_limit_bytes=62 << 20, collective_id=1, has_side_effects=True),
+        cost_estimate=pl.CostEstimate(
+            flops=24 * rows * rows * inner, bytes_accessed=8 * rows * inner, transcendentals=2 * pairs * rows * rows
+        ),
+        name="through",
+    )(length, query, key, value, near, source, gain, output, up, down, cotangent)
+
+
+def row_moves(source, target, sems, depth, piece, started=True):
+    held = depth // 2
+    place, index = (lax.axis_index("seq"), lax.axis_index("fsdp"))
+    core = lax.rem(index, 2)
+    there, which = (core * held + piece, index - core + place // held)
+    slot = lax.rem(place, held)
+    home = (there == place) & (which == index)
+
+    @pl.when(home)
+    def _():
+        if started:
+            pltpu.make_async_copy(source, target.at[slot], sems.at[1, piece, slot]).start()
+
+    @pl.when(jnp.logical_not(home))
+    def _():
+        move = push(source, target.at[slot], sems, (piece, slot), there, which)
+        if started:
+            move.start()
+        else:
+            move.wait_send()
+
+
+def rows_came(target, sems, depth):
+    held = depth // 2
+    place = lax.axis_index("seq")
+    for slot in range(held):
+        number = (lax.rem(place, held), slot)
+        push(target.at[slot], target.at[slot], sems, number, place, partner(CORE)).wait_recv()
+
+
+def middle_kernel(
+    depth,
+    length_ref,
+    normed_ref,
+    grad_ref,
+    hidden_ref,
+    gain_ref,
+    output_ref,
+    far_output_ref,
+    context_ref,
+    far_context_ref,
+    up_ref,
+    down_ref,
+    ups_ref,
+    downs_ref,
+    up_part_ref,
+    down_part_ref,
+    up_came_ref,
+    down_came_ref,
+    far_up_ref,
+    far_down_ref,
+    context_grad_ref,
+    hidden_grad_ref,
+    layer_ref,
+    gain_part_ref,
+    output_part_ref,
+    near_grad,
+    out_total,
+    back_total,
+    out_came,
+    back_came,
+    up_slots,
+    down_slots,
+    up_stages,
+    down_stages,
+    parts,
+    parts_came,
+    far_grad,
+    arrived,
+    stored,
+    far_sems,
+    unit_sems,
+    fold_sems,
+    core_sems,
+    kept,
+):
+    rows, width = normed_ref.shape
+    mine, wholes, fars = ((up_ref, down_ref), (ups_ref, downs_ref), (far_up_ref, far_down_ref))
+    results, came = ((up_part_ref, down_part_ref), (up_came_ref, down_came_ref))
+    slots, stages = ((up_slots, down_slots), (up_stages, down_stages))
+    kinds = range(2)
+    step = pl.program_id(0)
+    last = depth - 1
+    index = lax.axis_index("fsdp")
+    core, x, y = (lax.rem(index, 2), lax.rem(index // 2, 2), index // 4)
+    unit = up_slots.shape[1]
+    half = unit // 2
+    slot = lax.rem(step, 2)
+    places = [chip_of(), chip_of(ALONG_X), chip_of(ALONG_Y), chip_of(ALONG_X, ALONG_Y)]
+
+    moves = []
+    for kind in kinds:
+        for place, (bit, from_bit) in enumerate(((ALONG_X, ALONG_Y), (ALONG_Y, ALONG_X))):
+            there = pl.ds(place * half, half)
+            source = wholes[kind].at[chip_of(from_bit), there]
+            moves.append(send(source, fars[kind].at[there], far_sems, 2 * kind + place, bit))
+    sources = [
+        mine,
+        [one.at[places[1]] for one in wholes],
+        [one.at[places[2]] for one in wholes],
+        fars,
+    ]
+
+    def fetch(block, into):
+        for number, pair in enumerate(sources):
+
+            @pl.when(block == number)
+            def _():
+                for kind in kinds:
+                    pltpu.make_async_copy(pair[kind], slots[kind].at[into], arrived.at[kind, into]).start()
+
+    def store(number, kind):
+        return pltpu.make_async_copy(
+            stages[kind].at[number % 2], results[kind].at[places[number]], stored.at[kind, number % 2]
+        )
+
+    def first_sum(number, kind):
+        block = places[number]
+        if kind == 0:
+            source, bit = (results[0].at[block, :, 1 - x], ALONG_X)
+        else:
+            source, bit = (results[1].at[block, 1 - y], ALONG_Y)
+        return send(source, came[kind].at[block], unit_sems, last * kind + number, bit)
+
+    def own_rows(which):
+        return pl.ds(pl.multiple_of(which * (rows // 2), rows // 2), rows // 2)
+
+    folds = [
+        send(one.at[own_rows(1 - core)], there, fold_sems, number, CORE)
+        for number, (one, there) in enumerate(((back_total, back_came), (out_total, out_came)))
+    ]
+
+    @pl.when(step == 0)
+    def _():
+        greet_column(depth)
+        for one in moves:
+            one.start()
+        fetch(0, 0)
+        out_total[...] = jnp.zeros_like(out_total)
+        back_total[...] = jnp.zeros_like(back_total)
+
+    @pl.when(step + 1 < last)
+    def _():
+        fetch(step + 1, 1 - slot)
+
+    for number in range(last):
+
+        @pl.when(step == number + 1)
+        def _():
+            for kind in kinds:
+                store(number, kind).wait()
+                first_sum(number, kind).start()
+
+    for kind in kinds:
+        pltpu.make_async_copy(slots[kind].at[slot], slots[kind].at[slot], arrived.at[kind, slot]).wait()
+    up, down = (slots[0][slot], slots[1][slot])
+    normed, grad = (normed_ref[...], grad_ref[...])
+    active, slope = gelu_parts(dot(normed, up, NT))
+    active = active.astype(LOW)
+    pre_grad = (dot(grad, down, NT) * slope).astype(LOW)
+    back_total[...] += dot(pre_grad, up)
+    out_total[...] += dot(active, down)
+    shape = up_stages.shape[1:]
+    stages[0][slot] = dot(pre_grad, normed, TN).astype(LOW).reshape(shape)
+    stages[1][slot] = dot(active, grad, TN).astype(LOW).reshape(shape)
+    for number in range(last + 1):
+
+        @pl.when(step == number)
+        def _():
+            for kind in kinds:
+                store(number, kind).start()
+
+    @pl.when(step == last - 1)
+    def _():
+        for one in moves:
+            one.wait()
+        fetch(last, last % 2)
+
+    @pl.when(step == last)
+    def _():
+        for one in folds:
+            one.start()
+        folds[0].wait()
+        normed_grad = back_total[own_rows(core), :] + back_came[...]
+        hidden = hidden_ref[...]
+        rms = inverse_root(jnp.mean(hidden * hidden, axis=1, keepdims=True) + EPSILON)
+        scaled = hidden * rms
+        gained = gain_ref[...] * normed_grad
+        inside = jnp.mean(gained * scaled, axis=1, keepdims=True)
+        hidden_grad = grad_ref[own_rows(core), :].astype(WIDE) + rms * (gained - scaled * inside)
+        gain_part_ref[...] = jnp.sum(normed_grad * scaled, axis=0, keepdims=True)
+        hidden_grad_ref[...] = hidden_grad
+        hidden_low = hidden_grad.astype(LOW)
+        far_grad[...] = dot(hidden_low, far_output_ref[...], NT).astype(LOW)
+        move = send(far_grad, context_grad_ref.at[own_rows(core)], core_sems, 0, CORE)
+        move.start()
+        part_shape = parts.shape[1:]
+        parts[0] = dot(context_ref[...], hidden_low, TN).astype(LOW).reshape(part_shape)
+        parts[1] = dot(far_context_ref[...], hidden_low, TN).astype(LOW).reshape(part_shape)
+        others = [
+            send(parts.at[kind, :, :, 1 - core], parts_came.at[kind], core_sems, 1 + kind, CORE) for kind in kinds
+        ]
+        for one in others:
+            one.start()
+        near_grad[...] = dot(hidden_low, output_ref[...], NT).astype(LOW)
+        keep = pltpu.make_async_copy(near_grad, context_grad_ref.at[own_rows(core)], kept)
+        keep.start()
+        folds[1].wait()
+        slot_ids = core * (rows // 2) + lax.broadcasted_iota(jnp.int32, (rows // 2, 1), 0)
+        valid = (slot_ids < length_ref[0]).astype(WIDE)
+        layer_rows = (hidden + (out_total[own_rows(core), :] + out_came[...])) * valid
+        layer_ref[...] = layer_rows.astype(LOW).reshape(layer_ref.shape)
+        for one in others:
+            one.wait()
+        for turn in range(depth):
+            near = parts[0, turn, :, core].astype(WIDE) + parts_came[1, turn].astype(WIDE)
+            output_part_ref[turn, core] = near.astype(LOW)
+            far = parts[1, turn, :, core].astype(WIDE) + parts_came[0, turn].astype(WIDE)
+            output_part_ref[turn, 1 - core] = far.astype(LOW)
+        for kind in kinds:
+            store(last, kind).wait()
+        move.wait()
+        keep.wait()
+        for number in range(last):
+            for kind in kinds:
+                first_sum(number, kind).wait()
+
+
+def middle(length, normed, grad, hidden, gain, outputs, contexts, mine, wholes):
+    rows, width = normed.shape
+    inner = outputs[0].shape[0]
+    unit = mine[0].shape[0]
+    depth = lax.axis_size("seq")
+    held = depth // 2
+    thick, slim = (unit // 4, inner // 16)
+    vmem, anywhere = (pl.BlockSpec(memory_space=pltpu.VMEM), pl.BlockSpec(memory_space=pltpu.HBM))
+    shape = jax.ShapeDtypeStruct
+    part = (depth, 2, 2, thick, width)
+    return pl.pallas_call(
+        functools.partial(middle_kernel, depth),
+        grid=(depth,),
+        in_specs=[pl.BlockSpec(memory_space=pltpu.SMEM)] + [vmem] * 8 + [anywhere] * 4,
+        out_specs=[anywhere] * 7 + [vmem] * 4,
+        out_shape=[shape(part, LOW)] * 2
+        + [shape((depth, 2, thick, width), LOW)] * 2
+        + [shape((unit, width), LOW)] * 2
+        + [
+            shape((rows, inner), LOW),
+            shape((rows // 2, width), WIDE),
+            shape((held, rows // depth, width), LOW),
+            shape((1, width), WIDE),
+            shape((4, 2, 2, slim, width), LOW),
+        ],
+        scratch_shapes=[pltpu.VMEM((rows // 2, inner), LOW)]
+        + [pltpu.VMEM((rows, width), WIDE)] * 2
+        + [pltpu.VMEM((rows // 2, width), WIDE)] * 2
+        + [pltpu.VMEM((2, unit, width), LOW)] * 2
+        + [pltpu.VMEM((2, 2, 2, thick, width), LOW)] * 2
+        + [
+            pltpu.VMEM((2, 4, 2, 2, slim, width), LOW),
+            pltpu.VMEM((2, 4, 2, slim, width), LOW),
+            pltpu.VMEM((rows // 2, inner), LOW),
+            pltpu.SemaphoreType.DMA((2, 2)),
+            pltpu.SemaphoreType.DMA((2, 2)),
+            pltpu.SemaphoreType.DMA((2, 4)),
+            pltpu.SemaphoreType.DMA((2, 2 * (depth - 1))),
+            pltpu.SemaphoreType.DMA((2, 2)),
+            pltpu.SemaphoreType.DMA((2, 3)),
+            pltpu.SemaphoreType.DMA,
+        ],
+        compiler_params=pltpu.CompilerParams(vmem_limit_bytes=62 << 20, collective_id=2, has_side_effects=True),
+        cost_estimate=pl.CostEstimate(
+            flops=52 * unit * rows * width,
+            bytes_accessed=32 * unit * width + 12 * rows * width,
+            transcendentals=8 * unit * rows,
+        ),
+        name="middle",
+    )(length, normed, grad, hidden, gain, *outputs, *contexts, *mine, *wholes)
 
 
 def add_rows(target, source):
@@ -571,6 +1082,8 @@
     layer_ref,
     up_ref,
     down_ref,
+    up_came_ref,
+    down_came_ref,
     layer_out_ref,
     input_grad_ref,
     heads_out_ref,
@@ -607,18 +1120,18 @@
     first_sems,
     second_sems,
     third_sems,
-    unit_first_sems,
+    late_sems,
     unit_second_sems,
     unit_third_sems,
     fold_sems,
     row_sems,
     layer_sems,
     small_sems,
+    early_sems,
     local_sems,
 ):
     rows = query_ref.shape[0]
     width = normed_ref.shape[1]
-    inner = query_ref.shape[1]
     held = depth // 2
     step = pl.program_id(0)
     last = depth - 1
@@ -633,69 +1146,113 @@
         return push(source, target, sems, number, place, partner(bit))
 
 
-    def row_moves(source, target, sems, piece, started=True):
-        there, which = (core * held + piece, column + place // held)
-        slot = lax.rem(place, held)
-        home = (there == place) & (which == index)
-
-        @pl.when(home)
+    def unit_place(hop):
+        return chip_of(*(bit for bit in (ALONG_X, ALONG_Y) if hop & (bit // 2)))
+
+    def unit_source(kind, hop):
+        block = unit_place(hop)
+        if kind == 0:
+            return (up_ref.at[block, :, 1 - x], up_ref.at[block, :, x], ALONG_X)
+        return (down_ref.at[block, 1 - y], down_ref.at[block, y], ALONG_Y)
+
+    def unit_came(kind, hop):
+        return units_came.at[kind, hop]
+
+    def unit_own(kind, hop):
+        return pltpu.make_async_copy(unit_source(kind, hop)[1], units.at[kind, hop], local_sems.at[kind, hop])
+
+    def unit_early(kind, hop):
+        there = (up_came_ref, down_came_ref)[kind].at[unit_place(hop)]
+        return pltpu.make_async_copy(there, units_came.at[kind, hop], early_sems.at[kind, hop])
+
+    def unit_late(kind, hop):
+        away, _, bit = unit_source(kind, hop)
+        return beside(away, units_came.at[kind, late[kind]], late_sems, (kind,), bit)
+
+    late = (2, 1)
+
+    def units_start():
+        for kind in range(2):
+            unit_late(kind, 3).start()
+        for kind in range(2):
+            for hop in range(4):
+                unit_own(kind, hop).start()
+                if hop != late[kind]:
+                    unit_early(kind, hop).start()
+
+    def unit_halves(kind, hop):
+        if kind == 0:
+            return (units.at[0, hop, 1 - y], units.at[0, hop, y], ALONG_Y)
+        return (units.at[1, hop, 1 - x], units.at[1, hop, x], ALONG_X)
+
+    def unit_second(kind, hop):
+        away, _, bit = unit_halves(kind, hop)
+        there = hop ^ (bit // 2)
+        return push(
+            away, units_last.at[kind, there], unit_second_sems, (kind, hop), place, partner(bit), (kind, there)
+        )
+
+    def unit_first(kind, hop):
+        unit_own(kind, hop).wait()
+        if hop == late[kind]:
+            unit_late(kind, 3).wait()
+        else:
+            unit_early(kind, hop).wait()
+        add_rows(units.at[kind, hop], units_came.at[kind, hop])
+        unit_second(kind, hop).start()
+
+
+    def unit_pass(kind, hop):
+        block = unit_place(hop)
+        ahead = block > place
+        there = jnp.where(ahead, place + 1, place - 1)
+        side = jnp.where(ahead, 0, 1)
+        own = unit_halves(kind, hop)[1]
+        far = units_far.at[kind, block, side]
+        return push(own, far, unit_third_sems, (kind, block, 0), there, index, (kind, block, side))
+
+    def unit_arrived(kind, block, side):
+        far = units_far.at[kind, block, side]
+        return push(far, far, unit_third_sems, (kind, block, side), place, partner(CORE))
+
+    def unit_summed(kind, hop):
+        unit_second(kind, hop).wait_send()
+        unit_second(kind, hop ^ (2 - kind)).wait_recv()
+        add_rows(unit_halves(kind, hop)[1], units_last.at[kind, hop])
+        block = unit_place(hop)
+
+        @pl.when(((place == 0) | (place == last)) & (block != place))
         def _():
-            move = pltpu.make_async_copy(source, target.at[slot], sems.at[1, piece, slot])
-            if started:
-                move.start()
-
-        @pl.when(jnp.logical_not(home))
+            unit_pass(kind, hop).start()
+
+    def unit_onward(kind, hop, turn):
+        block = unit_place(hop)
+        ahead = block > place
+        outer = jnp.where(ahead, place, last - place)
+
+        @pl.when((block != place) & (outer == turn + 1))
         def _():
-            move = push(source, target.at[slot], sems, (piece, slot), there, which)
-            if started:
-                move.start()
-            else:
-                move.wait_send()
-
-    def rows_came(target, sems):
-        for slot in range(held):
-            number = (lax.rem(place, held), slot)
-            push(target.at[slot], target.at[slot], sems, number, place, partner(CORE)).wait_recv()
-
-
-    def unit_sources(block):
-        return (
-            (up_ref.at[owner(block), :, 1 - x], up_ref.at[owner(block), :, x], ALONG_X),
-            (down_ref.at[owner(block), 1 - y], down_ref.at[owner(block), y], ALONG_Y),
-        )
-
-    def units_start(block):
-        for kind, (away, own, bit) in enumerate(unit_sources(block)):
-            beside(away, units_came.at[kind, block], unit_first_sems, (kind, block), bit).start()
-            pltpu.make_async_copy(own, units.at[kind, block], local_sems.at[kind, block]).start()
-
-    def unit_seconds(block):
-        return (
-            (units.at[0, block, 1 - y], units.at[0, block, y], ALONG_Y),
-            (units.at[1, block, 1 - x], units.at[1, block, x], ALONG_X),
-        )
-
-    def units_first(block):
-        for kind, (away, own, bit) in enumerate(unit_sources(block)):
-            pltpu.make_async_copy(own, units.at[kind, block], local_sems.at[kind, block]).wait()
-            beside(away, units_came.at[kind, block], unit_first_sems, (kind, block), bit).wait()
-            add_rows(units.at[kind, block], units_came.at[kind, block])
-        for kind, (away, own, bit) in enumerate(unit_seconds(block)):
-            beside(away, units_last.at[kind, block], unit_second_sems, (kind, block), bit).start()
-
-    def unit_thirds(block):
-        return [
-            push(own, units_far.at[block, kind], unit_third_sems, (kind, block), owner(block), index)
-            for kind, (away, own, bit) in enumerate(unit_seconds(block))
-        ]
-
-    def units_second(block, mine=False):
-        for kind, (away, own, bit) in enumerate(unit_seconds(block)):
-            beside(away, units_last.at[kind, block], unit_second_sems, (kind, block), bit).wait()
-            add_rows(own, units_last.at[kind, block])
-        if not mine:
-            for one in unit_thirds(block):
-                one.start()
+            side = jnp.where(ahead, 0, 1)
+            unit_arrived(kind, block, side).wait_recv()
+            add_rows(unit_halves(kind, hop)[1], units_far.at[kind, block, side])
+            unit_pass(kind, hop).start()
+
+    def unit_finish(kind, hop):
+        block = unit_place(hop)
+
+        @pl.when(block != place)
+        def _():
+            unit_pass(kind, hop).wait_send()
+
+        @pl.when(block == place)
+        def _():
+            units_out_ref[kind] = unit_halves(kind, hop)[1][...].astype(WIDE)
+            for side, there in enumerate((place > 0, place < last)):
+
+                @pl.when(there)
+                def _():
+                    unit_arrived(kind, block, side).wait_recv()
+                    units_out_ref[kind] += units_far[kind, block, side].astype(WIDE)
 
 
     def swaps(block):
@@ -754,29 +1311,54 @@
     @pl.when(step == 0)
     def _():
         greet_column(depth)
-        for block in range(depth):
-            units_start(block)
+        units_start()
         for block in range(depth):
             output_copy(block).start()
         for piece in range(held):
-            row_moves(layer_ref.at[piece], layer_out_ref, layer_sems, piece)
+            row_moves(layer_ref.at[piece], layer_out_ref, layer_sems, depth, piece)
         spare[...] = spare_lanes(length_ref[0], rows)
         for head in range(2):
             padded[head, :HALF_ROWS, :] = jnp.zeros((HALF_ROWS, QUERY_ROWS), LOW)
             padded[head, rows + HALF_ROWS :, :] = jnp.zeros((HALF_ROWS, QUERY_ROWS), LOW)
 
-    @pl.when(step >= 1)
-    def _():
-        units_first(step - 1)
-
-    @pl.when(step >= 2)
-    def _():
-        units_second(step - 2)
+    def advance(number):
+        def at(turn, tick, act):
+            @pl.when((step == turn) & (number == tick))
+            def _():
+                act()
+
+        ready = [(kind, hop) for kind in range(2) for hop in range(4) if hop != late[kind]]
+        both_ready = [(0, 1), (0, 3), (1, 2), (1, 3)]
+        others = [(0, 0), (0, 2), (1, 0), (1, 1)]
+        at(0, 1, lambda: [unit_first(*one) for one in ready])
+        at(1, 0, lambda: [unit_first(kind, late[kind]) for kind in range(2)])
+        at(1, 1, lambda: [unit_summed(*one) for one in both_ready])
+        at(2, 0, lambda: [unit_summed(*one) for one in others])
+        at(2, 1, lambda: [unit_onward(*one, 0) for one in both_ready])
+        at(3, 0, lambda: [unit_onward(*one, 0) for one in others])
+        at(3, 1, lambda: [unit_onward(*one, 1) for one in both_ready])
+        at(3, 3, lambda: [unit_onward(*one, 1) for one in others])
+
+        @pl.when((step >= 1) & (number == 1))
+        def _():
+            heads_start(step - 1)
+
+        @pl.when((step >= 2) & (number == 0))
+        def _():
+            heads_first(step - 2)
+
+        @pl.when((step >= 2) & (number == 2))
+        def _():
+            heads_second(step - 2)
 
     pair = owner(step)
     lanes = pl.ds(pl.multiple_of(pair * LANES, LANES), LANES)
     split_heads(key_ref[:, lanes], spare[...], keys)
     split_heads(value_ref[:, lanes], jnp.zeros((rows, LANES), LOW), values)
+
+    def low_lanes(kind):
+        return pl.ds(pl.multiple_of((3 * pair + kind) * LANES, LANES), LANES)
+
     near_start = rows - QUERY_ROWS - HALF_ROWS
     near_end = near_start + 2 * QUERY_ROWS
     for head in range(2):
@@ -798,6 +1380,7 @@
     def block(number, carry):
         start = pl.multiple_of(number * QUERY_ROWS, QUERY_ROWS)
         offset = pl.multiple_of(rows - QUERY_ROWS - number * QUERY_ROWS, LANES)
+        advance(number)
         both = query_ref[pl.ds(start, QUERY_ROWS), lanes]
         grad = grad_ref[pl.ds(start, QUERY_ROWS), lanes]
         parts = []
@@ -828,12 +1411,12 @@
             sums[4 * head + 2 : 4 * head + 3, :] += left
             sums[4 * head + 3 : 4 * head + 4, :] += right
         chosen = jnp.where(lane < HEAD_DIM, parts[0], parts[1])
-        lows[pl.ds(start, QUERY_ROWS), lanes] = chosen.astype(LOW)
+        lows[pl.ds(start, QUERY_ROWS), low_lanes(0)] = chosen.astype(LOW)
         return carry
 
     lax.fori_loop(0, blocks, block, 0)
-    lows[:, pl.ds(pl.multiple_of(inner + pair * LANES, LANES), LANES)] = key_total[...].astype(LOW)
-    lows[:, pl.ds(pl.multiple_of(2 * inner + pair * LANES, LANES), LANES)] = value_total[...].astype(LOW)
+    lows[:, low_lanes(1)] = key_total[...].astype(LOW)
+    lows[:, low_lanes(2)] = value_total[...].astype(LOW)
     shape = (HALF_ROWS, HALF_ROWS)
     upper = lax.broadcasted_iota(jnp.int32, shape, 0) <= lax.broadcasted_iota(jnp.int32, shape, 1)
     for head in range(2):
@@ -849,8 +1432,7 @@
             one.wait_send()
 
     for kind in range(3):
-        columns = lows[:, pl.ds(pl.multiple_of(kind * inner + pair * LANES, LANES), LANES)]
-        product = dot(columns, normed_ref[...], TN).astype(LOW)
+        product = dot(lows[:, low_lanes(kind)], normed_ref[...], TN).astype(LOW)
         part[kind] = product.reshape(part.shape[1:])
     for one in swaps(step):
         one.start()
@@ -858,18 +1440,6 @@
         for kind in range(2):
             x_block[step, half, core, kind] = part[kind, half, core]
         y_block[step, core, half, 0] = part[2, half, core]
-
-    @pl.when(step >= 1)
-    def _():
-        heads_start(step - 1)
-
-    @pl.when(step >= 2)
-    def _():
-        heads_first(step - 2)
-
-    @pl.when(step >= 3)
-    def _():
-        heads_second(step - 3)
 
     @pl.when(step == last)
     def _():
@@ -881,10 +1451,7 @@
         for one in swaps(last):
             one.wait_send()
         heads_start(last)
-        units_first(last)
-        units_second(last - 1)
         heads_first(last - 1)
-        heads_second(last - 2)
 
         gain_total = jnp.zeros((1, width), WIDE)
         for piece in range(held):
@@ -894,17 +1461,16 @@
             product = product + fold_came[piece].astype(WIDE)
             local = slice(piece * span, (piece + 1) * span)
             source = source_ref[local, :].astype(WIDE)
-            rms = lax.rsqrt(jnp.mean(source * source, axis=1, keepdims=True) + EPSILON)
+            rms = inverse_root(jnp.mean(source * source, axis=1, keepdims=True) + EPSILON)
             scaled = source * rms
             gain_total = gain_total + jnp.sum(product * scaled, axis=0, keepdims=True)
             gained = gain_ref[...] * product
             inside = jnp.mean(gained * scaled, axis=1, keepdims=True)
             row_sent[piece] = (hidden_ref[local, :] + rms * (gained - scaled * inside)).astype(LOW)
-            row_moves(row_sent.at[piece], row_came, row_sems, piece)
+            row_moves(row_sent.at[piece], row_came, row_sems, depth, piece)
             if piece == 0:
+                heads_second(last - 1)
                 heads_first(last)
-                units_second(last, True)
-                heads_second(last - 1)
         heads_second(last, True)
 
         for number in range(width // LANES):
@@ -923,10 +1489,11 @@
             one.start()
 
         for block in range(last):
-            for one in unit_thirds(block) + thirds(block):
+            for one in thirds(block):
                 one.wait()
-        units_out_ref[0] = units[0, last, y].astype(WIDE) + sum(units_far[one, 0].astype(WIDE) for one in range(depth - 1))
-        units_out_ref[1] = units[1, last, x].astype(WIDE) + sum(units_far[one, 1].astype(WIDE) for one in range(depth - 1))
+        for kind in range(2):
+            for hop in range(4):
+                unit_finish(kind, hop)
         heads_out_ref[0:2] = x_block[last, x, y].astype(WIDE) + sum(
             heads_came[one, 0].astype(WIDE) for one in range(depth - 1)
         )
@@ -943,31 +1510,31 @@
         small_out_ref[1] = small_came[depth + 1]
 
         for piece in range(held):
-            row_moves(layer_ref.at[piece], layer_out_ref, layer_sems, piece, False)
-            row_moves(row_sent.at[piece], row_came, row_sems, piece, False)
-        rows_came(layer_out_ref, layer_sems)
-        rows_came(row_came, row_sems)
+            row_moves(layer_ref.at[piece], layer_out_ref, layer_sems, depth, piece, False)
+            row_moves(row_sent.at[piece], row_came, row_sems, depth, piece, False)
+        rows_came(layer_out_ref, layer_sems, depth)
+        rows_came(row_came, row_sems, depth)
         input_grad_ref[...] = row_came[...].astype(WIDE)
 
 
 def backward(
-    length, query, key, value, grad, logs, near, normed, weights, source, hidden, gain, ffn_gain_part, output_part, layer, ups, downs
+    length, query, key, value, grad, logs, near, normed, weights, source, hidden, gain, ffn_gain_part, output_part, layer, *units
 ):
     rows, inner = query.shape
     width = normed.shape[1]
     depth = lax.axis_size("seq")
     held = depth // 2
     span = rows // depth
-    slim, thick = (output_part.shape[3], ups.shape[3])
-    vmem, anywhere = (pl.BlockSpec(memory_space=pltpu.VMEM), pl.BlockSpec(memory_space=pl.ANY))
+    slim, thick = (output_part.shape[3], units[0].shape[3])
+    vmem, anywhere = (pl.BlockSpec(memory_space=pltpu.VMEM), pl.BlockSpec(memory_space=pltpu.HBM))
     shape = jax.ShapeDtypeStruct
     small_rows = 2 * (width // LANES) + 8 * depth
-    sems = [(3, depth), (2, depth), (2, depth), (2, depth), (2, depth), (2, depth), (2, depth)]
+    sems = [(3, depth), (2, depth), (2, depth), (2, depth), (2,), (2, depth), (2, depth, 2)]
     sems += [(held,), (held, held), (held, held), (depth + 2,)]
     return pl.pallas_call(
         functools.partial(backward_kernel, depth),
         grid=(depth,),
-        in_specs=[pl.BlockSpec(memory_space=pltpu.SMEM)] + [vmem] * 12 + [anywhere] * 4,
+        in_specs=[pl.BlockSpec(memory_space=pltpu.SMEM)] + [vmem] * 12 + [anywhere] * 6,
         out_specs=[anywhere] + [vmem] * 4,
         out_shape=[
             shape((held, span, width), LOW),
@@ -996,12 +1563,12 @@
             pltpu.VMEM((2, depth, 2, thick, width), LOW),
             pltpu.VMEM((2, depth, 2, thick, width), LOW),
             pltpu.VMEM((2, depth, thick, width), LOW),
-            pltpu.VMEM((depth - 1, 2, thick, width), LOW),
+            pltpu.VMEM((2, depth, 2, thick, width), LOW),
         ]
         + [pltpu.VMEM((held, span, width), LOW)] * 4
         + [pltpu.VMEM((4, small_rows, LANES), WIDE), pltpu.VMEM((depth + 2, small_rows, LANES), WIDE)]
         + [pltpu.SemaphoreType.DMA((2,) + one) for one in sems]
-        + [pltpu.SemaphoreType.DMA((3, depth))],
+        + [pltpu.SemaphoreType.DMA((2, depth)), pltpu.SemaphoreType.DMA((3, depth))],
         compiler_params=pltpu.CompilerParams(
             vmem_limit_bytes=62 << 20, collective_id=3, has_side_effects=True
         ),
@@ -1009,7 +1576,7 @@
             flops=60 * rows * rows * inner, bytes_accessed=14 * rows * inner, transcendentals=rows * rows * inner // 64
         ),
         name="backward",
-    )(length, query, key, value, grad, logs, near, normed, weights, source, hidden, gain, ffn_gain_part, output_part, layer, ups, downs)
+    )(length, query, key, value, grad, logs, near, normed, weights, source, hidden, gain, ffn_gain_part, output_part, layer, *units)
 
 
 def flip(value, bit):
@@ -1019,10 +1586,6 @@
 
 def other_core(value):
     return flip(value, 1)
-
-
-def after(value, *first):
-    return lax.optimization_barrier((value,) + first)[0]
 
 
 def rounds_of(inverse):
@@ -1076,25 +1639,6 @@
     sent = lax.dynamic_slice_in_dim(partial, (1 - core) * half, half, 0)
     kept = lax.dynamic_slice_in_dim(partial, core * half, half, 0)
     return kept + other_core(sent)
-
-
-def gather_near(mine):
-    return (flip(mine, 2), flip(mine, 4))
-
-
-def gather_far(beside, above):
-    half = beside.shape[0] // 2
-    return (flip(above[:half], 2), flip(beside[half:], 4))
-
-
-def in_order(mine, beside, above, far):
-    chip = lax.axis_index("fsdp") // 2
-    out = jnp.zeros((4,) + mine.shape, mine.dtype)
-    out = lax.dynamic_update_index_in_dim(out, mine, chip, 0)
-    out = lax.dynamic_update_index_in_dim(out, beside, chip ^ 1, 0)
-    out = lax.dynamic_update_index_in_dim(out, above, chip ^ 2, 0)
-    out = lax.dynamic_update_slice(out, far[0][None], (chip ^ 3, 0, 0))
-    return lax.dynamic_update_slice(out, far[1][None], (chip ^ 3, mine.shape[0] // 2, 0))
 
 
 def fast_plane():
@@ -1142,27 +1686,30 @@
         jnp.concatenate([other_core(lengths), lengths]),
     )
     length = lax.dynamic_slice_in_dim(near_lengths, place, 1, 0)
-    slots = core * rows + jnp.arange(rows, dtype=jnp.int32)
-    mask_rows = (slots < length[0])[:, None].astype(WIDE)
 
     own_table = lax.dynamic_index_in_dim(bias_table.reshape(BUCKETS, 4, 2, 2), core, 2, keepdims=False)
     own_table = own_table.reshape(BUCKETS, HEADS // 2)
     near = near_bias(own_table)
 
-    ffn = up_weight.shape[0]
     if fast:
-        stacked = jnp.concatenate([query_weight, key_weight, value_weight], axis=0)
-        cut = jnp.stack([up_weight, down_weight]).reshape(2, 2, 2, -1, width)
-        swapped = other_core(pick(cut, 1 - core, 2))
-        kept = pick(cut, core, 2)
-        cut = jnp.where(
-            core == 0, jnp.stack([kept, swapped], axis=1), jnp.stack([swapped, kept], axis=1)
-        ).reshape(2, -1, width)
-        up_mine, down_mine = (cut[0], cut[1])
-        beside, above = gather_near(stacked)
-        far = gather_far(beside, above)
-        heads_low = in_order(stacked, beside, above, far).reshape(4, 3, -1, width)
-        own_three = [heads_low[:, number].reshape(-1, width) for number in range(3)]
+        normed_one, query, key, value, source_low, weights, up_mine, down_mine = enter(
+            inputs, (query_weight, key_weight, value_weight), up_weight, down_weight, attn_gain[None, :]
+        )
+        source_low = source_low.reshape(rows, width)
+        mine = (up_mine.reshape(-1, width), down_mine.reshape(-1, width))
+        logs, near_context, hidden_one, far_context, own_output, far_output, normed_two, grad_low, *wholes = through(
+            length,
+            query,
+            key,
+            value,
+            near,
+            source_low,
+            ffn_gain[None, :],
+            output_weight,
+            *mine,
+            cotangent,
+        )
+        own_output, far_output = (own_output.reshape(-1, width), far_output.reshape(-1, width))
     else:
         own_three = [
             own_head_rows(lax.all_gather(one, "fsdp", axis=0, tiled=True), core)
@@ -1177,63 +1724,57 @@
             ).reshape(-1, width)
             for one in (up_weight, down_weight)
         )
-
-    source_low = to_sequence(inputs)
-    source = source_low.astype(WIDE)
-    rms_one = lax.rsqrt(jnp.mean(source * source, axis=1, keepdims=True) + EPSILON)
-    scaled_one = source * rms_one
-    normed_one = whole((scaled_one * attn_gain).astype(LOW), core)
-    query, key, value = [dot(normed_one, one, NT).astype(LOW) for one in own_three]
+        mask_rows = (core * rows + jnp.arange(rows, dtype=jnp.int32) < length[0])[:, None].astype(WIDE)
+        source_low = to_sequence(inputs)
+        source = source_low.astype(WIDE)
+        rms_one = lax.rsqrt(jnp.mean(source * source, axis=1, keepdims=True) + EPSILON)
+        scaled_one = source * rms_one
+        normed_one = whole((scaled_one * attn_gain).astype(LOW), core)
+        query, key, value = [dot(normed_one, one, NT).astype(LOW) for one in own_three]
+        context, logs = attend(length, query, key, value, near)
+        mine = (own_up, own_down)
+        near_context = lax.dynamic_slice_in_dim(context, core * rows, rows, 0)
+        far_context = other_core(lax.dynamic_slice_in_dim(context, (1 - core) * rows, rows, 0))
+        hidden_one = source + (dot(near_context, own_output) + dot(far_context, far_output))
+        rms_two = lax.rsqrt(jnp.mean(hidden_one * hidden_one, axis=1, keepdims=True) + EPSILON)
+        scaled_two = hidden_one * rms_two
+        normed_two = whole((scaled_two * ffn_gain).astype(LOW), core)
+        grad_out = to_sequence(cotangent).astype(WIDE) * mask_rows
+        grad_low = whole(grad_out.astype(LOW), core)
+
     if fast:
-        mine = (output_weight, up_mine, down_mine)
-        context, logs, own_output, *wholes = attend(length, query, key, value, near, mine)
-        own_output = own_output.reshape(-1, width)
-        far_output = other_core(own_output)
-        mine = mine[1:]
+        up_part, down_part, up_came, down_came, _, _, context_grad, hidden_grad, layer_rows, ffn_gain_part, output_part = middle(
+            length,
+            normed_two,
+            grad_low,
+            hidden_one,
+            ffn_gain[None, :],
+            (own_output, far_output),
+            (near_context, far_context),
+            mine,
+            wholes,
+        )
     else:
-        context, logs = attend(length, query, key, value, near)
-        mine, wholes = ((own_up, own_down), ())
-    near_context = lax.dynamic_slice_in_dim(context, core * rows, rows, 0)
-    far_context = other_core(lax.dynamic_slice_in_dim(context, (1 - core) * rows, rows, 0))
-    hidden_one = source + (dot(near_context, own_output) + dot(far_context, far_output))
-    rms_two = lax.rsqrt(jnp.mean(hidden_one * hidden_one, axis=1, keepdims=True) + EPSILON)
-    scaled_two = hidden_one * rms_two
-    normed_two = whole((scaled_two * ffn_gain).astype(LOW), core)
-    grad_out = to_sequence(cotangent).astype(WIDE) * mask_rows
-    grad_low = whole(grad_out.astype(LOW), core)
-    up_part, down_part, mlp_part, normed_part = feed(normed_two, grad_low, mine, wholes)
-    normed_grad = fold(normed_part, core)
-    mlp_out = fold(mlp_part, core)
-    layer_rows = ((hidden_one + mlp_out) * mask_rows).astype(LOW)
-
-    gained_two = ffn_gain * normed_grad
-    hidden_grad = grad_out + rms_two * (
-        gained_two - scaled_two * jnp.mean(gained_two * scaled_two, axis=1, keepdims=True)
-    )
-    ffn_gain_part = jnp.sum(normed_grad * scaled_two, axis=0)
-    hidden_low = hidden_grad.astype(LOW)
-    near_grad = dot(hidden_low, own_output, NT).astype(LOW)
-    far_grad = other_core(dot(hidden_low, far_output, NT).astype(LOW))
-    context_grad = jnp.where(
-        core == 0,
-        jnp.concatenate([near_grad, far_grad], axis=0),
-        jnp.concatenate([far_grad, near_grad], axis=0),
-    )
-    near_output_part = dot(near_context, hidden_low, TN).astype(LOW)
-    far_output_part = dot(far_context, hidden_low, TN).astype(LOW)
+        up_part, down_part, mlp_part, normed_part = feed(normed_two, grad_low, *mine)
+        normed_grad = fold(normed_part, core)
+        layer_rows = ((hidden_one + fold(mlp_part, core)) * mask_rows).astype(LOW)
+        gained_two = ffn_gain * normed_grad
+        hidden_grad = grad_out + rms_two * (
+            gained_two - scaled_two * jnp.mean(gained_two * scaled_two, axis=1, keepdims=True)
+        )
+        ffn_gain_part = jnp.sum(normed_grad * scaled_two, axis=0)
+        hidden_low = hidden_grad.astype(LOW)
+        near_grad = dot(hidden_low, own_output, NT).astype(LOW)
+        far_grad = other_core(dot(hidden_low, far_output, NT).astype(LOW))
+        context_grad = jnp.where(
+            core == 0,
+            jnp.concatenate([near_grad, far_grad], axis=0),
+            jnp.concatenate([far_grad, near_grad], axis=0),
+        )
+        near_output_part = dot(near_context, hidden_low, TN).astype(LOW)
+        far_output_part = dot(far_context, hidden_low, TN).astype(LOW)
 
     if fast:
-        blocks = (depth, 2, 2, -1, width)
-
-        def to_parity(kept, sent):
-            return jnp.where(core == 0, jnp.stack([kept, sent], axis=1), jnp.stack([sent, kept], axis=1))
-
-        near_part = near_output_part.reshape(4, 2, 2, -1, width)
-        far_part = far_output_part.reshape(4, 2, 2, -1, width)
-        got = other_core(jnp.stack([pick(far_part, 1 - core, 2), pick(near_part, 1 - core, 2)]))
-        output_part = to_parity(
-            add_low(pick(near_part, core, 2), got[0]), add_low(pick(far_part, core, 2), got[1])
-        )
         layer_out, input_grad, heads_grad, units_grad, small = backward(
             length,
             query,
@@ -1243,15 +1784,17 @@
             logs,
             near,
             normed_one,
-            jnp.concatenate(own_three, axis=0),
+            weights.reshape(-1, width),
             source_low,
             hidden_grad,
             attn_gain[None, :],
             ffn_gain_part.reshape(-1, LANES),
             output_part,
-            layer_rows.reshape(held, span, width),
-            up_part.reshape(blocks),
-            down_part.reshape(blocks),
+            layer_rows,
+            up_part,
+            down_part,
+            up_came,
+            down_came,
         )
         query_grad, key_grad, value_grad, output_grad = (heads_grad[number] for number in range(4))
         up_grad, down_grad = (units_grad[0], units_grad[1])

time: 392 us -> 322 us (0.82); the launches traced: 385 us -> 321 us
  Pallas kernels: 276 us -> 308 us
  local copies, waits for them, and re-layouts: 35.4 us -> 9.51 us
  other arithmetic: 25.6 us -> 1.6 us
  starting transfers between devices: 19.1 us -> 0.52 us
  waiting for transfers between devices: 18.1 us -> 0.01 us
  matrix products: 8.87 us -> 1.18 us
    pallas_call x2 -> x3, Pallas kernels: 103 us -> 172 us  [the longest x1 69.1 us: middle(): pl.pallas_call(functools.partial(middle_kernel, depth), grid=(depth,), in...]
    pallas_call x1, Pallas kernels: 173 us -> 135 us  [backward(): pl.pallas_call(functools.partial(backward_kernel, depth), grid=(depth,),...]
    ppermute x15 -> x1, waiting for transfers between devices: 11.9 us -> 0.01 us  [flip(): lax.ppermute(value, 'fsdp', [(one, one ^ bit) for one in range(size)])]
    ppermute x15 -> x1, starting transfers between devices: 10.4 us -> 0.52 us  [flip(): lax.ppermute(value, 'fsdp', [(one, one ^ bit) for one in range(size)])]
    select_n x6 -> x0, other arithmetic: 8.66 us -> none  [the longest x3 5.74 us: whole(): jnp.where(core == 0, jnp.concatenate([mine, other], axis=0), jnp.concaten...]
    ppermute x4 -> x0, starting transfers between devices: 8.63 us -> none  [to_sequence(): got = lax.ppermute(sent, BOTH, pairs)]
    dot_general x9 -> x0, matrix products: 8.53 us -> none  [dot(): return lax.dot_general(left, right, dims, preferred_element_type=WIDE)]
    unnamed x81 -> x14, local copies, waits for them, and re-layouts: 9.32 us -> 2.49 us
  transfers between devices with their start and end apart: 19 -> 1, of which waited for: 6 -> 0; matrix products, arithmetic and copies ran while one was open for 10% -> 1% of each run, Pallas kernels for 16% -> 13%
where the time goes in v4:
time: 322 us; the launch traced here: 321 us
  Pallas kernels  308 us (96%)
  local copies, waits for them, and re-layouts  9.51 us (3%)
    pallas_call x1, Pallas kernels, backward(): pl.pallas_call(functools.partial(backward_kernel, depth), grid=(depth,),...  135 us
    pallas_call x1, Pallas kernels, middle(): pl.pallas_call(functools.partial(middle_kernel, depth), grid=(depth,), in...  69.1 us
    pallas_call x1, Pallas kernels, through(): pl.pallas_call(functools.partial(through_kernel, depth), grid=(pairs,), i...  60.2 us
    pallas_call x1, Pallas kernels, enter(): pl.pallas_call(functools.partial(enter_kernel, depth), in_specs=[anywhere...  43 us
  transfers between devices with their start and end apart: 1, of which 0 were waited for; matrix products, arithmetic and copies ran while one was open for 1% of the time, Pallas kernels for 13%

profile of v4, /device:TPU:0, one launch (start us, length us, event | category | flops | bytes accessed | tf_op | source)
XLA Modules:
  0.0 321.3 jit_solution(9648248173750049003)
XLA Ops:
  0.6 0.0 copy-start
  0.7 0.5 collective-permute-start
  1.2 0.2 copy-done
  1.3 1.0 fusion
  2.3 0.6 broadcast_in_dim.12.near_ref
  3.0 0.0 copy-start.5
  3.0 43.0 %enter.1 = (bf16[1024,1024]{1,0:T(8,128)(2,1)}, bf16[1024,512]{1,0:T(8,128)(2,1)}, bf16[1024,512]{1,0:T(8,128)(2,1)}, bf16[1024,512]{1,0:T(8,128)(2,1)}, bf16[2,...) custom-call(bf16[2,256,1024]{2,1,0:T(8,128)(2,1)} %inputs_ref.1, ...), custom_call_target="tpu_custom_call" | custom-call | flops 3221225472 | bytes 16777216 | tf_op jit(solution)/shard_map/enter/pallas_call | solution.py:533
  46.0 0.0 collective-permute-done
  46.0 0.0 copy-done.5
  46.0 0.1 broadcast_select_fusion
  46.1 0.6 dynamic_slice.16.length_ref
  46.6 60.2 %through.1 = (f32[4,2,1024]{2,1,0:T(2,128)}, bf16[512,512]{1,0:T(8,128)(2,1)}, f32[512,1024]{1,0:T(8,128)}, bf16[512,512]{1,0:T(8,128)(2,1)}, bf16[4,128,1024]{2...) custom-call(s32[1]{0:T(128)} %dynamic_slice.16.length_ref, ...), custom_call_target="tpu_custom_call" | custom-call | flops 12884901888 | bytes 4194304 | tf_op jit(solution)/shard_map/through/pallas_call | solution.py:744
  106.8 69.1 %middle.1 = (bf16[4,2,2,128,1024]{4,3,2,1,0:T(8,128)(2,1)}, bf16[4,2,2,128,1024]{4,3,2,1,0:T(8,128)(2,1)}, bf16[4,2,128,1024]{3,2,1,0:T(8,128)(2,1)}, bf16[4,2,1...) custom-call(s32[1]{0:T(128)} %dynamic_slice.16.length_ref, ...), custom_call_target="tpu_custom_call" | custom-call | flops 27917287424 | bytes 29360128 | tf_op jit(solution)/shard_map/middle/pallas_call | solution.py:1020
  175.9 135.5 %backward.1 = (bf16[2,256,1024]{2,1,0:T(8,128)(2,1)}, f32[2,256,1024]{2,1,0:T(8,128)}, f32[4,32,1024]{2,1,0:T(8,128)}, f32[2,128,1024]{2,1,0:T(8,128)}, f32[2,48,128]{2,1,0:T(8,128)}) custom-call(s32[1]{0:T(128)} %dynamic_slice.16.length_ref, bf16[1024,512]{1,0:T(8,128)(2,1)} %get-tuple-element.43.query_ref, bf16[1024,512]{1,0:T(8,128)(2,1)} %get-tuple-element.44.key_ref, ...), custom_call_target="tpu_custom_call" | custom-call | flops 32212254720 | bytes 7340032 | tf_op jit(solution)/shard_map/backward/pallas_call | solution.py:1534
  311.4 0.0 copy-start.3
  311.4 0.0 copy-start.4
  311.4 0.0 copy-start.2
  311.4 0.9 rev.3
  312.3 0.8 slice_add_fusion
  313.1 0.8 slice_select_fusion
  313.9 2.3 slice_bitcast_fusion
  316.2 0.0 copy-start.1
  316.2 0.0 copy-done.3
  316.2 0.8 slice_bitcast_fusion.2
  317.0 0.6 dynamic_slice.18
  317.6 0.6 dynamic_slice.19
  318.2 0.0 copy-done.4
  318.2 0.2 fusion.1
  318.4 0.6 dynamic-slice_bitcast_fusion
  319.0 0.0 copy-done.2
  319.0 1.0 copy.30
  319.9 0.0 copy-done.1
  319.9 1.3 copy.31
  (5 shorter events, 0.1 us)
Async XLA Ops:
  0.6 0.7 copy-start
  0.7 45.3 %collective-permute-start = (s32[2]{0:T(128)}, s32[2]{0:T(128)S(1)}, u32[]{:S(2)}, u32[]{:S(2)}) collective-permute-start(s32[2]{0:T(128)} %param.15), channel_id=1, source_target_pairs={{0,1},{1,0},{2,3},{3,2},{4,5},{5,4},{6,7},{7,6},{8,9},{9,8},{10,11... | collective-permute-start | bytes 32 | tf_op jit(solution)/shard_map/ppermute | solution.py:1584
  3.0 43.0 %copy-start.5 = (s32[2]{0:T(128)S(1)}, s32[2]{0:T(128)}, u32[]{:S(2)}) copy-start(s32[2]{0:T(128)} %param.15) | copy-start | bytes 28
  311.4 4.8 %copy-start.3 = (f32[4,32,1024]{2,1,0:T(8,128)S(1)}, f32[4,32,1024]{2,1,0:T(8,128)}, u32[]{:S(2)}) copy-start(f32[4,32,1024]{2,1,0:T(8,128)} %get-tuple-element.72) | copy-start | bytes 1572868
  311.4 6.8 %copy-start.4 = (f32[32,512]{1,0:T(8,128)S(1)}, f32[32,512]{1,0:T(8,128)}, u32[]{:S(2)}) copy-start(f32[32,512]{1,0:T(8,128)} %constant.39.clone) | copy-start | bytes 196612
  311.4 7.6 %copy-start.2 = (bf16[2,256,1024]{2,1,0:T(8,128)(2,1)S(1)}, bf16[2,256,1024]{2,1,0:T(8,128)(2,1)}, u32[]{:S(2)}) copy-start(bf16[2,256,1024]{2,1,0:T(8,128)(2,1)} %get-tuple-element.94) | copy-start | bytes 3145732
  316.2 3.7 %copy-start.1 = (f32[2,256,1024]{2,1,0:T(8,128)S(1)}, f32[2,256,1024]{2,1,0:T(8,128)}, u32[]{:S(2)}) copy-start(f32[2,256,1024]{2,1,0:T(8,128)} %get-tuple-element.95) | copy-start | bytes 6291460

commit v5 on v4

--- a/solution.py
+++ b/solution.py
@@ -435,6 +435,7 @@
     normed_ref,
     source_ref,
     weights_ref,
+    kept,
     slot_sems,
     near_sems,
     far_sems,
@@ -465,7 +466,7 @@
     cuts = []
     for kind, (whole_one, out) in enumerate(((up_ref, up_out_ref), (down_ref, down_out_ref))):
         cuts.append(send(whole_one.at[:, 1 - core], out.at[core], cut_sems, kind, CORE))
-        local.append(pltpu.make_async_copy(whole_one.at[:, core], out.at[core], local_sems.at[3 + kind]))
+        local.append(pltpu.make_async_copy(whole_one.at[:, core], kept.at[kind], local_sems.at[3 + kind]))
     for one in cuts + local:
         one.start()
     for one in direct:
@@ -488,7 +489,7 @@
         moves[-1].start()
     for one in moves:
         one.wait()
-    for one in local[:3]:
+    for one in local:
         one.wait()
 
     def project(number):
@@ -499,25 +500,32 @@
             out[:, lanes] = product[:, kind * LANES : (kind + 1) * LANES]
 
     def some(turn, carry):
-        project(lax.rem(chip + turn, 4))
+        project(jnp.where(turn == 0, chip, jnp.where(turn == 1, chip_of(ALONG_X), chip_of(ALONG_Y))))
         return carry
 
+    lax.fori_loop(0, 3, some, 0)
     for one in onward:
         one.wait()
     stored = [
         pltpu.make_async_copy(one, there, local_sems.at[5 + number])
         for number, (one, there) in enumerate(
-            ((normed_ref, normed_out_ref), (source_ref, source_out_ref), (weights_ref, weights_out_ref))
+            (
+                (normed_ref, normed_out_ref),
+                (source_ref, source_out_ref),
+                (weights_ref, weights_out_ref),
+                (kept.at[0], up_out_ref.at[core]),
+                (kept.at[1], down_out_ref.at[core]),
+            )
         )
     ]
     for one in stored:
         one.start()
-    lax.fori_loop(0, 4, some, 0)
+    project(chip_of(ALONG_X, ALONG_Y))
     for one in stored:
         one.wait()
     for one in direct:
         one.wait_send()
-    for one in cuts + local[3:]:
+    for one in cuts:
         one.wait()
     slots_moves(inputs_ref, source_ref, slot_sems, depth, "end")
 
@@ -542,12 +550,13 @@
             pltpu.VMEM((rows, width), LOW),
             pltpu.VMEM((held, span, width), LOW),
             pltpu.VMEM((4, 3, slim, width), LOW),
+            pltpu.VMEM((2, 2, thick, width), LOW),
             pltpu.SemaphoreType.DMA((2, held)),
             pltpu.SemaphoreType.DMA((2, 6)),
             pltpu.SemaphoreType.DMA((2, 2)),
             pltpu.SemaphoreType.DMA((2, 2)),
             pltpu.SemaphoreType.DMA((2, held)),
-            pltpu.SemaphoreType.DMA((8,)),
+            pltpu.SemaphoreType.DMA((10,)),
         ],
         compiler_params=pltpu.CompilerParams(vmem_limit_bytes=62 << 20, collective_id=4, has_side_effects=True),
         cost_estimate=pl.CostEstimate(flops=24 * rows * slim * width, bytes_accessed=16 << 20, transcendentals=0),
@@ -591,6 +600,7 @@
     slot_sems,
     near_sems,
     far_sems,
+    deep_sems,
     core_sems,
     context_sems,
     local,
@@ -605,15 +615,29 @@
     own = pl.ds(pl.multiple_of(core * (rows // 2), rows // 2), rows // 2)
     other = pl.ds(pl.multiple_of((1 - core) * (rows // 2), rows // 2), rows // 2)
     half = output_ref.shape[0] // 2
+    place, index = (lax.axis_index("seq"), lax.axis_index("fsdp"))
+    parity = lax.rem(place, 2)
+    unit = down_ref.shape[0] // 2
+    mine = pl.ds(pl.multiple_of(parity * unit, unit), unit)
     direct = []
-    unit = up_ref.shape[0] // 2
-    for first in (None, 0, unit):
-        for one, there in ((output_ref, own_output_ref),) if first is None else ((up_ref, ups_ref), (down_ref, downs_ref)):
-            for bit in (ALONG_X, ALONG_Y):
-                source, target = (one, there.at[chip])
-                if first is not None:
-                    source, target = (source.at[pl.ds(first, unit)], target.at[pl.ds(first, unit)])
-                direct.append(send(source, target, near_sems, len(direct), bit))
+    for one, there in (
+        (output_ref, own_output_ref.at[chip]),
+        (down_ref.at[mine], downs_ref.at[chip, mine]),
+        (up_ref, ups_ref.at[chip]),
+    ):
+        for bit in (ALONG_X, ALONG_Y):
+            direct.append(send(one, there, near_sems, len(direct), bit))
+    exchange = [
+        push(
+            downs_ref.at[chip_of(bit), mine],
+            downs_ref.at[chip_of(bit), mine],
+            deep_sems,
+            (number,),
+            place + 1 - 2 * parity,
+            index,
+        )
+        for number, bit in enumerate((ALONG_X, ALONG_Y))
+    ]
     onward = []
     for turn, (bit, from_bit) in enumerate(((ALONG_X, ALONG_Y), (ALONG_Y, ALONG_X))):
         piece = own_output_ref.at[chip_of(from_bit), pl.ds(turn * half, half)]
@@ -654,6 +678,13 @@
         for one in onward + direct[4:]:
             one.start()
 
+    @pl.when(pair == last - 1)
+    def _():
+        for one in direct[2:4]:
+            one.wait_recv()
+        for one in exchange:
+            one.start()
+
     @pl.when(pair == last)
     def _():
         for one in onward:
@@ -723,8 +754,10 @@
             one.start()
         for one in direct:
             one.wait_send()
-        for one in direct[2:]:
+        for one in direct[4:]:
             one.wait_recv()
+        for one in exchange:
+            one.wait()
         slots_moves(cotangent_ref, came, slot_sems, depth, "end")
         for one in both_cores[0] + both_cores[1]:
             one.wait()
@@ -765,7 +798,8 @@
             pltpu.VMEM((rows // 2, width), LOW),
             pltpu.VMEM((rows // 2, width), LOW),
             pltpu.SemaphoreType.DMA((2, held)),
-            pltpu.SemaphoreType.DMA((2, 10)),
+            pltpu.SemaphoreType.DMA((2, 6)),
+            pltpu.SemaphoreType.DMA((2, 2)),
             pltpu.SemaphoreType.DMA((2, 2)),
             pltpu.SemaphoreType.DMA((2, 3)),
             pltpu.SemaphoreType.DMA((2, pairs)),
@@ -838,8 +872,8 @@
     near_grad,
     out_total,
     back_total,
-    out_came,
-    back_came,
+    fold_sent,
+    fold_came,
     up_slots,
     down_slots,
     up_stages,
@@ -869,12 +903,17 @@
     slot = lax.rem(step, 2)
     places = [chip_of(), chip_of(ALONG_X), chip_of(ALONG_Y), chip_of(ALONG_X, ALONG_Y)]
 
-    moves = []
-    for kind in kinds:
-        for place, (bit, from_bit) in enumerate(((ALONG_X, ALONG_Y), (ALONG_Y, ALONG_X))):
-            there = pl.ds(place * half, half)
-            source = wholes[kind].at[chip_of(from_bit), there]
-            moves.append(send(source, fars[kind].at[there], far_sems, 2 * kind + place, bit))
+    place = lax.axis_index("seq")
+    parity = lax.rem(place, 2)
+    moves, exchange = ([], [])
+    for turn, (bit, from_bit) in enumerate(((ALONG_X, ALONG_Y), (ALONG_Y, ALONG_X))):
+        there = pl.ds(pl.multiple_of(turn * half + parity * (half // 2), half // 2), half // 2)
+        moves.append(send(downs_ref.at[chip_of(from_bit), there], far_down_ref.at[there], far_sems, turn, bit))
+        far = far_down_ref.at[there]
+        exchange.append(push(far, far, far_sems, (4 + turn,), place + 1 - 2 * parity, index))
+    for turn, (bit, from_bit) in enumerate(((ALONG_X, ALONG_Y), (ALONG_Y, ALONG_X))):
+        there = pl.ds(turn * half, half)
+        moves.append(send(ups_ref.at[chip_of(from_bit), there], far_up_ref.at[there], far_sems, 2 + turn, bit))
     sources = [
         mine,
         [one.at[places[1]] for one in wholes],
@@ -906,10 +945,7 @@
     def own_rows(which):
         return pl.ds(pl.multiple_of(which * (rows // 2), rows // 2), rows // 2)
 
-    folds = [
-        send(one.at[own_rows(1 - core)], there, fold_sems, number, CORE)
-        for number, (one, there) in enumerate(((back_total, back_came), (out_total, out_came)))
-    ]
+    folds = [send(fold_sent.at[number], fold_came.at[number], fold_sems, number, CORE) for number in range(2)]
 
     @pl.when(step == 0)
     def _():
@@ -923,6 +959,13 @@
     @pl.when(step + 1 < last)
     def _():
         fetch(step + 1, 1 - slot)
+
+    @pl.when(step == 1)
+    def _():
+        for one in moves[:2]:
+            one.wait()
+        for one in exchange:
+            one.start()
 
     for number in range(last):
 
@@ -941,6 +984,13 @@
     pre_grad = (dot(grad, down, NT) * slope).astype(LOW)
     back_total[...] += dot(pre_grad, up)
     out_total[...] += dot(active, down)
+
+    @pl.when(step == last)
+    def _():
+        for number, total in enumerate((back_total, out_total)):
+            fold_sent[number] = total[own_rows(1 - core), :].astype(LOW)
+            folds[number].start()
+
     shape = up_stages.shape[1:]
     stages[0][slot] = dot(pre_grad, normed, TN).astype(LOW).reshape(shape)
     stages[1][slot] = dot(active, grad, TN).astype(LOW).reshape(shape)
@@ -953,16 +1003,14 @@
 
     @pl.when(step == last - 1)
     def _():
-        for one in moves:
+        for one in moves[2:] + exchange:
             one.wait()
         fetch(last, last % 2)
 
     @pl.when(step == last)
     def _():
-        for one in folds:
-            one.start()
         folds[0].wait()
-        normed_grad = back_total[own_rows(core), :] + back_came[...]
+        normed_grad = back_total[own_rows(core), :] + fold_came[0].astype(WIDE)
         hidden = hidden_ref[...]
         rms = inverse_root(jnp.mean(hidden * hidden, axis=1, keepdims=True) + EPSILON)
         scaled = hidden * rms
@@ -989,7 +1037,7 @@
         folds[1].wait()
         slot_ids = core * (rows // 2) + lax.broadcasted_iota(jnp.int32, (rows // 2, 1), 0)
         valid = (slot_ids < length_ref[0]).astype(WIDE)
-        layer_rows = (hidden + (out_total[own_rows(core), :] + out_came[...])) * valid
+        layer_rows = (hidden + (out_total[own_rows(core), :] + fold_came[1].astype(WIDE))) * valid
         layer_ref[...] = layer_rows.astype(LOW).reshape(layer_ref.shape)
         for one in others:
             one.wait()
@@ -1034,7 +1082,7 @@
         ],
         scratch_shapes=[pltpu.VMEM((rows // 2, inner), LOW)]
         + [pltpu.VMEM((rows, width), WIDE)] * 2
-        + [pltpu.VMEM((rows // 2, width), WIDE)] * 2
+        + [pltpu.VMEM((2, rows // 2, width), LOW)] * 2
         + [pltpu.VMEM((2, unit, width), LOW)] * 2
         + [pltpu.VMEM((2, 2, 2, thick, width), LOW)] * 2
         + [
@@ -1043,7 +1091,7 @@
             pltpu.VMEM((rows // 2, inner), LOW),
             pltpu.SemaphoreType.DMA((2, 2)),
             pltpu.SemaphoreType.DMA((2, 2)),
-            pltpu.SemaphoreType.DMA((2, 4)),
+            pltpu.SemaphoreType.DMA((2, 6)),
             pltpu.SemaphoreType.DMA((2, 2 * (depth - 1))),
             pltpu.SemaphoreType.DMA((2, 2)),
             pltpu.SemaphoreType.DMA((2, 3)),
@@ -1202,57 +1250,41 @@
         unit_second(kind, hop).start()
 
 
-    def unit_pass(kind, hop):
+    def unit_arrived(kind, block, slot):
+        far = units_far.at[kind, block, slot]
+        return push(far, far, unit_third_sems, (kind, block, slot), place, partner(CORE))
+
+    def unit_direct(kind, hop):
         block = unit_place(hop)
-        ahead = block > place
-        there = jnp.where(ahead, place + 1, place - 1)
-        side = jnp.where(ahead, 0, 1)
+        slot = lax.rem(block + 2 * depth - place - 1, depth)
         own = unit_halves(kind, hop)[1]
-        far = units_far.at[kind, block, side]
-        return push(own, far, unit_third_sems, (kind, block, 0), there, index, (kind, block, side))
-
-    def unit_arrived(kind, block, side):
-        far = units_far.at[kind, block, side]
-        return push(far, far, unit_third_sems, (kind, block, side), place, partner(CORE))
+        return push(
+            own, units_far.at[kind, block, slot], unit_third_sems, (kind, block, 0), block, index, (kind, block, slot)
+        )
 
     def unit_summed(kind, hop):
         unit_second(kind, hop).wait_send()
         unit_second(kind, hop ^ (2 - kind)).wait_recv()
         add_rows(unit_halves(kind, hop)[1], units_last.at[kind, hop])
-        block = unit_place(hop)
-
-        @pl.when(((place == 0) | (place == last)) & (block != place))
+
+        @pl.when(unit_place(hop) != place)
         def _():
-            unit_pass(kind, hop).start()
-
-    def unit_onward(kind, hop, turn):
-        block = unit_place(hop)
-        ahead = block > place
-        outer = jnp.where(ahead, place, last - place)
-
-        @pl.when((block != place) & (outer == turn + 1))
-        def _():
-            side = jnp.where(ahead, 0, 1)
-            unit_arrived(kind, block, side).wait_recv()
-            add_rows(unit_halves(kind, hop)[1], units_far.at[kind, block, side])
-            unit_pass(kind, hop).start()
+            unit_direct(kind, hop).start()
 
     def unit_finish(kind, hop):
         block = unit_place(hop)
 
         @pl.when(block != place)
         def _():
-            unit_pass(kind, hop).wait_send()
+            unit_direct(kind, hop).wait_send()
 
         @pl.when(block == place)
         def _():
-            units_out_ref[kind] = unit_halves(kind, hop)[1][...].astype(WIDE)
-            for side, there in enumerate((place > 0, place < last)):
-
-                @pl.when(there)
-                def _():
-                    unit_arrived(kind, block, side).wait_recv()
-                    units_out_ref[kind] += units_far[kind, block, side].astype(WIDE)
+            total = unit_halves(kind, hop)[1][...].astype(WIDE)
+            for slot in range(depth - 1):
+                unit_arrived(kind, block, slot).wait_recv()
+                total = total + units_far[kind, block, slot].astype(WIDE)
+            units_out_ref[kind] = total
 
 
     def swaps(block):
@@ -1321,35 +1353,25 @@
             padded[head, :HALF_ROWS, :] = jnp.zeros((HALF_ROWS, QUERY_ROWS), LOW)
             padded[head, rows + HALF_ROWS :, :] = jnp.zeros((HALF_ROWS, QUERY_ROWS), LOW)
 
+    both_ready = [(0, 1), (0, 3), (1, 2), (1, 3)]
+    others = [(0, 0), (0, 2), (1, 0), (1, 1)]
+
     def advance(number):
         def at(turn, tick, act):
             @pl.when((step == turn) & (number == tick))
             def _():
                 act()
 
-        ready = [(kind, hop) for kind in range(2) for hop in range(4) if hop != late[kind]]
-        both_ready = [(0, 1), (0, 3), (1, 2), (1, 3)]
-        others = [(0, 0), (0, 2), (1, 0), (1, 1)]
+        ready = both_ready + [(0, 0), (1, 0)]
         at(0, 1, lambda: [unit_first(*one) for one in ready])
         at(1, 0, lambda: [unit_first(kind, late[kind]) for kind in range(2)])
-        at(1, 1, lambda: [unit_summed(*one) for one in both_ready])
-        at(2, 0, lambda: [unit_summed(*one) for one in others])
-        at(2, 1, lambda: [unit_onward(*one, 0) for one in both_ready])
-        at(3, 0, lambda: [unit_onward(*one, 0) for one in others])
-        at(3, 1, lambda: [unit_onward(*one, 1) for one in both_ready])
-        at(3, 3, lambda: [unit_onward(*one, 1) for one in others])
+        at(1, 3, lambda: [unit_summed(*one) for one in both_ready])
+        at(2, 3, lambda: [unit_summed(*one) for one in others])
+        at(3, 1, lambda: heads_first(0))
 
         @pl.when((step >= 1) & (number == 1))
         def _():
             heads_start(step - 1)
-
-        @pl.when((step >= 2) & (number == 0))
-        def _():
-            heads_first(step - 2)
-
-        @pl.when((step >= 2) & (number == 2))
-        def _():
-            heads_second(step - 2)
 
     pair = owner(step)
     lanes = pl.ds(pl.multiple_of(pair * LANES, LANES), LANES)
@@ -1448,10 +1470,11 @@
             away = pl.ds(pl.multiple_of((1 - core) * (rows // 2) + piece * span, span), span)
             fold_sent[piece] = dot(lows[away, :], weight_ref[...]).astype(LOW)
             beside(fold_sent.at[piece], fold_came.at[piece], fold_sems, (piece,), CORE).start()
+        heads_second(0)
+        heads_first(1)
         for one in swaps(last):
             one.wait_send()
         heads_start(last)
-        heads_first(last - 1)
 
         gain_total = jnp.zeros((1, width), WIDE)
         for piece in range(held):
@@ -1467,26 +1490,37 @@
             gained = gain_ref[...] * product
             inside = jnp.mean(gained * scaled, axis=1, keepdims=True)
             row_sent[piece] = (hidden_ref[local, :] + rms * (gained - scaled * inside)).astype(LOW)
+            if piece == held - 1:
+                for number in range(width // LANES):
+                    small[0, number : number + 1, :] = gain_total[:, number * LANES : (number + 1) * LANES]
+                small[0, 8:16, :] = small_ref[...]
+                moves = [
+                    push(small.at[0], small_came.at[turn], small_sems, (turn,), lax.rem(place + turn, depth), index)
+                    for turn in range(1, depth)
+                ]
+                for one in moves:
+                    one.start()
             row_moves(row_sent.at[piece], row_came, row_sems, depth, piece)
             if piece == 0:
-                heads_second(last - 1)
-                heads_first(last)
+                heads_first(last - 1)
+                heads_second(1)
+        heads_second(last - 1)
+        heads_first(last)
         heads_second(last, True)
 
-        for number in range(width // LANES):
-            small[0, number : number + 1, :] = gain_total[:, number * LANES : (number + 1) * LANES]
-        small[0, 8:16, :] = small_ref[...]
-        for turn, bit in enumerate((ALONG_X, ALONG_Y)):
-            move = beside(small.at[turn], small_came.at[turn], small_sems, (turn,), bit)
+        for one in moves:
+            one.wait()
+        small[1] = small[0] + sum(small_came[turn] for turn in range(1, depth))
+        for turn, bit in ((1, ALONG_X), (2, ALONG_Y)):
+            move = beside(small.at[turn], small_came.at[depth + turn - 1], small_sems, (depth + turn - 1,), bit)
             move.start()
             move.wait()
-            small[turn + 1] = small[turn] + small_came[turn]
-        moves = [
-            push(small.at[2], small_came.at[1 + turn], small_sems, (1 + turn,), lax.rem(place + turn, depth), index)
-            for turn in range(1, depth)
-        ]
-        for one in moves:
-            one.start()
+            small[turn + 1] = small[turn] + small_came[depth + turn - 1]
+        move = beside(small.at[3], small_came.at[0], small_sems, (0,), CORE)
+        move.start()
+        move.wait()
+        small_out_ref[core] = small[3]
+        small_out_ref[1 - core] = small_came[0]
 
         for block in range(last):
             for one in thirds(block):
@@ -1500,15 +1534,6 @@
         heads_out_ref[2:4] = y_block[last, y, x].astype(WIDE) + sum(
             heads_came[one, 1].astype(WIDE) for one in range(depth - 1)
         )
-        for one in moves:
-            one.wait()
-        small[3] = small[2] + sum(small_came[1 + turn] for turn in range(1, depth))
-        move = beside(small.at[3], small_came.at[depth + 1], small_sems, (depth + 1,), CORE)
-        move.start()
-        move.wait()
-        small_out_ref[0] = small[3]
-        small_out_ref[1] = small_came[depth + 1]
-
         for piece in range(held):
             row_moves(layer_ref.at[piece], layer_out_ref, layer_sems, depth, piece, False)
             row_moves(row_sent.at[piece], row_came, row_sems, depth, piece, False)
@@ -1529,12 +1554,12 @@
     vmem, anywhere = (pl.BlockSpec(memory_space=pltpu.VMEM), pl.BlockSpec(memory_space=pltpu.HBM))
     shape = jax.ShapeDtypeStruct
     small_rows = 2 * (width // LANES) + 8 * depth
-    sems = [(3, depth), (2, depth), (2, depth), (2, depth), (2,), (2, depth), (2, depth, 2)]
+    sems = [(3, depth), (2, depth), (2, depth), (2, depth), (2,), (2, depth), (2, depth, depth - 1)]
     sems += [(held,), (held, held), (held, held), (depth + 2,)]
     return pl.pallas_call(
         functools.partial(backward_kernel, depth),
         grid=(depth,),
-        in_specs=[pl.BlockSpec(memory_space=pltpu.SMEM)] + [vmem] * 12 + [anywhere] * 6,
+        in_specs=[pl.BlockSpec(memory_space=pltpu.SMEM)] + [vmem] * 12 + [anywhere, vmem] + [anywhere] * 4,
         out_specs=[anywhere] + [vmem] * 4,
         out_shape=[
             shape((held, span, width), LOW),
@@ -1563,7 +1588,7 @@
             pltpu.VMEM((2, depth, 2, thick, width), LOW),
             pltpu.VMEM((2, depth, 2, thick, width), LOW),
             pltpu.VMEM((2, depth, thick, width), LOW),
-            pltpu.VMEM((2, depth, 2, thick, width), LOW),
+            pltpu.VMEM((2, depth, depth - 1, thick, width), LOW),
         ]
         + [pltpu.VMEM((held, span, width), LOW)] * 4
         + [pltpu.VMEM((4, small_rows, LANES), WIDE), pltpu.VMEM((depth + 2, small_rows, LANES), WIDE)]
@@ -1801,8 +1826,7 @@
         gain_lines = width // LANES
         gains = (small[0] + small[1])[: 2 * gain_lines].reshape(2, width)
         attn_gain_sum, ffn_gain_sum = (gains[0], gains[1])
-        sums = jnp.where(core == 0, small, small[::-1])[:, 2 * gain_lines :]
-        sums = jnp.swapaxes(sums.reshape(2, 4, 2, 4 * LANES), 0, 1)
+        sums = jnp.swapaxes(small[:, 2 * gain_lines :].reshape(2, 4, 2, 4 * LANES), 0, 1)
         bias_sum = bucket_sums(sums.reshape(HEADS, 4 * LANES))
     else:
         query_low, key_low, value_low, distance_sums = attend_grad(

time: 322 us -> 300 us (0.932)
  Pallas kernels: 308 us -> 286 us
    pallas_call x1, Pallas kernels: 60.2 us -> 51.5 us  [through(): pl.pallas_call(functools.partial(through_kernel, depth), grid=(pairs,), i...]
    pallas_call x1, Pallas kernels: 135 us -> 129 us  [backward(): pl.pallas_call(functools.partial(backward_kernel, depth), grid=(depth,),...]
    pallas_call x1, Pallas kernels: 69.1 us -> 64.6 us  [middle(): pl.pallas_call(functools.partial(middle_kernel, depth), grid=(depth,), in...]
  transfers between devices with their start and end apart: 1 -> 1, of which waited for: 0 -> 0; matrix products, arithmetic and copies ran while one was open for 1% -> 1% of each run, Pallas kernels for 13% -> 14%
where the time goes in v5:
time: 300 us; the launch traced here: 298 us
  Pallas kernels  286 us (95%)
  local copies, waits for them, and re-layouts  9.47 us (3%)
    pallas_call x1, Pallas kernels, backward(): pl.pallas_call(functools.partial(backward_kernel, depth), grid=(depth,),...  129 us
    pallas_call x1, Pallas kernels, middle(): pl.pallas_call(functools.partial(middle_kernel, depth), grid=(depth,), in...  64.6 us
    pallas_call x1, Pallas kernels, through(): pl.pallas_call(functools.partial(through_kernel, depth), grid=(pairs,), i...  51.5 us
    pallas_call x1, Pallas kernels, enter(): pl.pallas_call(functools.partial(enter_kernel, depth), in_specs=[anywhere...  40.8 us
  transfers between devices with their start and end apart: 1, of which 0 were waited for; matrix products, arithmetic and copies ran while one was open for 1% of the time, Pallas kernels for 14%

profile of v5, /device:TPU:0, one launch (start us, length us, event | category | flops | bytes accessed | tf_op | source)
XLA Modules:
  0.0 298.5 jit_solution(1656630106795726367)
XLA Ops:
  0.6 0.0 copy-start
  0.7 0.5 collective-permute-start
  1.2 0.2 copy-done
  1.3 1.0 fusion
  2.3 0.6 broadcast_in_dim.12.near_ref
  3.0 0.0 copy-start.5
  3.0 40.8 %enter.1 = (bf16[1024,1024]{1,0:T(8,128)(2,1)}, bf16[1024,512]{1,0:T(8,128)(2,1)}, bf16[1024,512]{1,0:T(8,128)(2,1)}, bf16[1024,512]{1,0:T(8,128)(2,1)}, bf16[2,...) custom-call(bf16[2,256,1024]{2,1,0:T(8,128)(2,1)} %inputs_ref.1, ...), custom_call_target="tpu_custom_call" | custom-call | flops 3221225472 | bytes 16777216 | tf_op jit(solution)/shard_map/enter/pallas_call | solution.py:541
  43.8 0.0 collective-permute-done
  43.8 0.0 copy-done.5
  43.8 0.1 broadcast_select_fusion
  43.9 0.6 dynamic_slice.16.length_ref
  44.5 51.5 %through.1 = (f32[4,2,1024]{2,1,0:T(2,128)}, bf16[512,512]{1,0:T(8,128)(2,1)}, f32[512,1024]{1,0:T(8,128)}, bf16[512,512]{1,0:T(8,128)(2,1)}, bf16[4,128,1024]{2...) custom-call(s32[1]{0:T(128)} %dynamic_slice.16.length_ref, ...), custom_call_target="tpu_custom_call" | custom-call | flops 12884901888 | bytes 4194304 | tf_op jit(solution)/shard_map/through/pallas_call | solution.py:777
  96.0 64.6 %middle.1 = (bf16[4,2,2,128,1024]{4,3,2,1,0:T(8,128)(2,1)}, bf16[4,2,2,128,1024]{4,3,2,1,0:T(8,128)(2,1)}, bf16[4,2,128,1024]{3,2,1,0:T(8,128)(2,1)}, bf16[4,2,1...) custom-call(s32[1]{0:T(128)} %dynamic_slice.16.length_ref, ...), custom_call_target="tpu_custom_call" | custom-call | flops 27917287424 | bytes 29360128 | tf_op jit(solution)/shard_map/middle/pallas_call | solution.py:1068
  160.6 128.8 %backward.1 = (bf16[2,256,1024]{2,1,0:T(8,128)(2,1)}, f32[2,256,1024]{2,1,0:T(8,128)}, f32[4,32,1024]{2,1,0:T(8,128)}, f32[2,128,1024]{2,1,0:T(8,128)}, f32[2,48,128]{2,1,0:T(8,128)}) custom-call(s32[1]{0:T(128)} %dynamic_slice.16.length_ref, bf16[1024,512]{1,0:T(8,128)(2,1)} %get-tuple-element.43.query_ref, bf16[1024,512]{1,0:T(8,128)(2,1)} %get-tuple-element.44.key_ref, ...), custom_call_target="tpu_custom_call" | custom-call | flops 32212254720 | bytes 7340032 | tf_op jit(solution)/shard_map/backward/pallas_call | solution.py:1559
  289.4 0.0 copy-start.3
  289.4 0.0 copy-start.4
  289.4 0.0 copy-start.2
  289.4 0.9 slice.50
  290.3 0.8 slice_add_fusion
  291.1 2.3 slice_bitcast_fusion
  293.3 0.0 copy-start.1
  293.3 0.0 copy-done.3
  293.3 0.8 slice_bitcast_fusion.2
  294.2 0.6 dynamic_slice.18
  294.8 0.6 dynamic_slice.19
  295.4 0.0 copy-done.4
  295.4 0.2 fusion.1
  295.6 0.6 dynamic-slice_bitcast_fusion
  296.2 0.0 copy-done.2
  296.2 1.0 copy.30
  297.2 0.0 copy-done.1
  297.2 1.3 copy.31
  (5 shorter events, 0.1 us)
Async XLA Ops:
  0.6 0.7 copy-start
  0.7 43.2 %collective-permute-start = (s32[2]{0:T(128)}, s32[2]{0:T(128)S(1)}, u32[]{:S(2)}, u32[]{:S(2)}) collective-permute-start(s32[2]{0:T(128)} %param.15), channel_id=1, source_target_pairs={{0,1},{1,0},{2,3},{3,2},{4,5},{5,4},{6,7},{7,6},{8,9},{9,8},{10,11... | collective-permute-start | bytes 32 | tf_op jit(solution)/shard_map/ppermute | solution.py:1609
  3.0 40.9 %copy-start.5 = (s32[2]{0:T(128)S(1)}, s32[2]{0:T(128)}, u32[]{:S(2)}) copy-start(s32[2]{0:T(128)} %param.15) | copy-start | bytes 28
  289.4 4.0 %copy-start.3 = (f32[4,32,1024]{2,1,0:T(8,128)S(1)}, f32[4,32,1024]{2,1,0:T(8,128)}, u32[]{:S(2)}) copy-start(f32[4,32,1024]{2,1,0:T(8,128)} %get-tuple-element.72) | copy-start | bytes 1572868
  289.4 6.0 %copy-start.4 = (f32[32,512]{1,0:T(8,128)S(1)}, f32[32,512]{1,0:T(8,128)}, u32[]{:S(2)}) copy-start(f32[32,512]{1,0:T(8,128)} %constant.39.clone) | copy-start | bytes 196612
  289.4 6.8 %copy-start.2 = (bf16[2,256,1024]{2,1,0:T(8,128)(2,1)S(1)}, bf16[2,256,1024]{2,1,0:T(8,128)(2,1)}, u32[]{:S(2)}) copy-start(bf16[2,256,1024]{2,1,0:T(8,128)(2,1)} %get-tuple-element.94) | copy-start | bytes 3145732
  293.3 3.8 %copy-start.1 = (f32[2,256,1024]{2,1,0:T(8,128)S(1)}, f32[2,256,1024]{2,1,0:T(8,128)}, u32[]{:S(2)}) copy-start(f32[2,256,1024]{2,1,0:T(8,128)} %get-tuple-element.95) | copy-start | bytes 6291460

commit v6 on v5

--- a/solution.py
+++ b/solution.py
@@ -848,12 +848,12 @@
     length_ref,
     normed_ref,
     grad_ref,
-    hidden_ref,
+    hidden_in_ref,
     gain_ref,
-    output_ref,
-    far_output_ref,
-    context_ref,
-    far_context_ref,
+    output_in_ref,
+    far_output_in_ref,
+    context_in_ref,
+    far_context_in_ref,
     up_ref,
     down_ref,
     ups_ref,
@@ -869,6 +869,11 @@
     layer_ref,
     gain_part_ref,
     output_part_ref,
+    hidden_ref,
+    output_ref,
+    far_output_ref,
+    context_ref,
+    far_context_ref,
     near_grad,
     out_total,
     back_total,
@@ -888,6 +893,7 @@
     fold_sems,
     core_sems,
     kept,
+    later_sems,
 ):
     rows, width = normed_ref.shape
     mine, wholes, fars = ((up_ref, down_ref), (ups_ref, downs_ref), (far_up_ref, far_down_ref))
@@ -947,12 +953,27 @@
 
     folds = [send(fold_sent.at[number], fold_came.at[number], fold_sems, number, CORE) for number in range(2)]
 
+    later = [
+        pltpu.make_async_copy(one, there, later_sems.at[number])
+        for number, (one, there) in enumerate(
+            (
+                (hidden_in_ref, hidden_ref),
+                (output_in_ref, output_ref),
+                (far_output_in_ref, far_output_ref),
+                (context_in_ref, context_ref),
+                (far_context_in_ref, far_context_ref),
+            )
+        )
+    ]
+
     @pl.when(step == 0)
     def _():
         greet_column(depth)
         for one in moves:
             one.start()
         fetch(0, 0)
+        for one in later:
+            one.start()
         out_total[...] = jnp.zeros_like(out_total)
         back_total[...] = jnp.zeros_like(back_total)
 
@@ -1009,6 +1030,8 @@
 
     @pl.when(step == last)
     def _():
+        for one in later:
+            one.wait()
         folds[0].wait()
         normed_grad = back_total[own_rows(core), :] + fold_came[0].astype(WIDE)
         hidden = hidden_ref[...]
@@ -1068,7 +1091,7 @@
     return pl.pallas_call(
         functools.partial(middle_kernel, depth),
         grid=(depth,),
-        in_specs=[pl.BlockSpec(memory_space=pltpu.SMEM)] + [vmem] * 8 + [anywhere] * 4,
+        in_specs=[pl.BlockSpec(memory_space=pltpu.SMEM)] + [vmem] * 2 + [anywhere, vmem] + [anywhere] * 8,
         out_specs=[anywhere] * 7 + [vmem] * 4,
         out_shape=[shape(part, LOW)] * 2
         + [shape((depth, 2, thick, width), LOW)] * 2
@@ -1080,7 +1103,8 @@
             shape((1, width), WIDE),
             shape((4, 2, 2, slim, width), LOW),
         ],
-        scratch_shapes=[pltpu.VMEM((rows // 2, inner), LOW)]
+        scratch_shapes=[pltpu.VMEM(one.shape, one.dtype) for one in (hidden, *outputs, *contexts)]
+        + [pltpu.VMEM((rows // 2, inner), LOW)]
         + [pltpu.VMEM((rows, width), WIDE)] * 2
         + [pltpu.VMEM((2, rows // 2, width), LOW)] * 2
         + [pltpu.VMEM((2, unit, width), LOW)] * 2
@@ -1096,6 +1120,7 @@
             pltpu.SemaphoreType.DMA((2, 2)),
             pltpu.SemaphoreType.DMA((2, 3)),
             pltpu.SemaphoreType.DMA,
+            pltpu.SemaphoreType.DMA((5,)),
         ],
         compiler_params=pltpu.CompilerParams(vmem_limit_bytes=62 << 20, collective_id=2, has_side_effects=True),
         cost_estimate=pl.CostEstimate(
@@ -1120,10 +1145,10 @@
     grad_ref,
     log_ref,
     near_ref,
-    normed_ref,
-    weight_ref,
-    source_ref,
-    hidden_ref,
+    normed_in_ref,
+    weight_in_ref,
+    source_in_ref,
+    hidden_in_ref,
     gain_ref,
     small_ref,
     output_ref,
@@ -1133,10 +1158,15 @@
     up_came_ref,
     down_came_ref,
     layer_out_ref,
-    input_grad_ref,
+    row_came,
     heads_out_ref,
     units_out_ref,
-    small_out_ref,
+    gains_out_ref,
+    sums_out_ref,
+    normed_ref,
+    weight_ref,
+    source_ref,
+    hidden_ref,
     bias,
     spare,
     keys,
@@ -1161,7 +1191,6 @@
     fold_sent,
     fold_came,
     row_sent,
-    row_came,
     small,
     small_came,
     swap_sems,
@@ -1177,6 +1206,7 @@
     small_sems,
     early_sems,
     local_sems,
+    later_sems,
 ):
     rows = query_ref.shape[0]
     width = normed_ref.shape[1]
@@ -1340,10 +1370,24 @@
             for one in thirds(block):
                 one.start()
 
+    later = [
+        pltpu.make_async_copy(one, there, later_sems.at[number])
+        for number, (one, there) in enumerate(
+            (
+                (normed_in_ref, normed_ref),
+                (weight_in_ref, weight_ref),
+                (source_in_ref, source_ref),
+                (hidden_in_ref, hidden_ref),
+            )
+        )
+    ]
+
     @pl.when(step == 0)
     def _():
         greet_column(depth)
         units_start()
+        for one in later:
+            one.start()
         for block in range(depth):
             output_copy(block).start()
         for piece in range(held):
@@ -1453,6 +1497,10 @@
         for one in swaps(step - 1):
             one.wait_send()
 
+    @pl.when(step == 0)
+    def _():
+        later[0].wait()
+
     for kind in range(3):
         product = dot(lows[:, low_lanes(kind)], normed_ref[...], TN).astype(LOW)
         part[kind] = product.reshape(part.shape[1:])
@@ -1466,6 +1514,8 @@
     @pl.when(step == last)
     def _():
         span = rows // 2 // held
+        for one in later[1:]:
+            one.wait()
         for piece in range(held):
             away = pl.ds(pl.multiple_of((1 - core) * (rows // 2) + piece * span, span), span)
             fold_sent[piece] = dot(lows[away, :], weight_ref[...]).astype(LOW)
@@ -1519,8 +1569,12 @@
         move = beside(small.at[3], small_came.at[0], small_sems, (0,), CORE)
         move.start()
         move.wait()
-        small_out_ref[core] = small[3]
-        small_out_ref[1 - core] = small_came[0]
+        lines = width // LANES
+        for number in range(2):
+            line = pl.ds(number * lines + index, 1)
+            gains_out_ref[number : number + 1, :] = small[3, line, :] + small_came[0, line, :]
+        sums_out_ref[core] = small[3, 2 * lines :, :]
+        sums_out_ref[1 - core] = small_came[0, 2 * lines :, :]
 
         for block in range(last):
             for one in thirds(block):
@@ -1539,7 +1593,6 @@
             row_moves(row_sent.at[piece], row_came, row_sems, depth, piece, False)
         rows_came(layer_out_ref, layer_sems, depth)
         rows_came(row_came, row_sems, depth)
-        input_grad_ref[...] = row_came[...].astype(WIDE)
 
 
 def backward(
@@ -1559,16 +1612,21 @@
     return pl.pallas_call(
         functools.partial(backward_kernel, depth),
         grid=(depth,),
-        in_specs=[pl.BlockSpec(memory_space=pltpu.SMEM)] + [vmem] * 12 + [anywhere, vmem] + [anywhere] * 4,
-        out_specs=[anywhere] + [vmem] * 4,
+        in_specs=[pl.BlockSpec(memory_space=pltpu.SMEM)] + [vmem] * 6 + [anywhere] * 4 + [vmem] * 2 + [anywhere, vmem] + [anywhere] * 4,
+        out_specs=[anywhere] * 2 + [vmem] * 4,
         out_shape=[
             shape((held, span, width), LOW),
-            shape((held, span, width), WIDE),
+            shape((held, span, width), LOW),
             shape((4, slim, width), WIDE),
             shape((2, thick, width), WIDE),
-            shape((2, small_rows, LANES), WIDE),
+            shape((2, LANES), WIDE),
+            shape((2, 8 * depth, LANES), WIDE),
         ],
         scratch_shapes=[
+            pltpu.VMEM(normed.shape, LOW),
+            pltpu.VMEM(weights.shape, LOW),
+            pltpu.VMEM(source.shape, LOW),
+            pltpu.VMEM(hidden.shape, WIDE),
             pltpu.VMEM((2, 2 * rows - QUERY_ROWS, QUERY_ROWS), WIDE),
             pltpu.VMEM((rows, LANES), LOW),
             pltpu.VMEM((2, rows, LANES), LOW),
@@ -1590,10 +1648,10 @@
             pltpu.VMEM((2, depth, thick, width), LOW),
             pltpu.VMEM((2, depth, depth - 1, thick, width), LOW),
         ]
-        + [pltpu.VMEM((held, span, width), LOW)] * 4
+        + [pltpu.VMEM((held, span, width), LOW)] * 3
         + [pltpu.VMEM((4, small_rows, LANES), WIDE), pltpu.VMEM((depth + 2, small_rows, LANES), WIDE)]
         + [pltpu.SemaphoreType.DMA((2,) + one) for one in sems]
-        + [pltpu.SemaphoreType.DMA((2, depth)), pltpu.SemaphoreType.DMA((3, depth))],
+        + [pltpu.SemaphoreType.DMA((2, depth)), pltpu.SemaphoreType.DMA((3, depth)), pltpu.SemaphoreType.DMA((4,))],
         compiler_params=pltpu.CompilerParams(
             vmem_limit_bytes=62 << 20, collective_id=3, has_side_effects=True
         ),
@@ -1800,7 +1858,7 @@
         far_output_part = dot(far_context, hidden_low, TN).astype(LOW)
 
     if fast:
-        layer_out, input_grad, heads_grad, units_grad, small = backward(
+        layer_out, input_grad, heads_grad, units_grad, gains, sums = backward(
             length,
             query,
             key,
@@ -1823,10 +1881,9 @@
         )
         query_grad, key_grad, value_grad, output_grad = (heads_grad[number] for number in range(4))
         up_grad, down_grad = (units_grad[0], units_grad[1])
-        gain_lines = width // LANES
-        gains = (small[0] + small[1])[: 2 * gain_lines].reshape(2, width)
-        attn_gain_sum, ffn_gain_sum = (gains[0], gains[1])
-        sums = jnp.swapaxes(small[:, 2 * gain_lines :].reshape(2, 4, 2, 4 * LANES), 0, 1)
+        input_grad = input_grad.astype(WIDE)
+        attn_gain_grad, ffn_gain_grad = (gains[0], gains[1])
+        sums = jnp.swapaxes(sums.reshape(2, 4, 2, 4 * LANES), 0, 1)
         bias_sum = bucket_sums(sums.reshape(HEADS, 4 * LANES))
     else:
         query_low, key_low, value_low, distance_sums = attend_grad(
@@ -1865,10 +1922,10 @@
         ).reshape(BUCKETS, HEADS)
         attn_gain_sum, ffn_gain_sum, bias_sum = lax.psum((attn_gain_part, ffn_gain_part, bias_full), BOTH)
 
-    gain_rows = width // size
+        gain_rows = width // size
+        attn_gain_grad = lax.dynamic_slice_in_dim(attn_gain_sum, index * gain_rows, gain_rows, 0)
+        ffn_gain_grad = lax.dynamic_slice_in_dim(ffn_gain_sum, index * gain_rows, gain_rows, 0)
     bucket_rows = BUCKETS // size
-    attn_gain_grad = lax.dynamic_slice_in_dim(attn_gain_sum, index * gain_rows, gain_rows, 0)
-    ffn_gain_grad = lax.dynamic_slice_in_dim(ffn_gain_sum, index * gain_rows, gain_rows, 0)
     bias_grad = lax.dynamic_slice_in_dim(bias_sum, index * bucket_rows, bucket_rows, 0)
     return (
         layer_out,

time: 300 us -> 296 us (0.987)
  Pallas kernels: 286 us -> 281 us
    pallas_call x1, Pallas kernels: 129 us -> 125 us  [backward(): pl.pallas_call(functools.partial(backward_kernel, depth), grid=(depth,),...]
where the time goes in v6:
time: 296 us; the launch traced here: 294 us
  Pallas kernels  281 us (95%)
  local copies, waits for them, and re-layouts  9.16 us (3%)
    pallas_call x1, Pallas kernels, backward(): pl.pallas_call(functools.partial(backward_kernel, depth), grid=(depth,),...  125 us
    pallas_call x1, Pallas kernels, middle(): pl.pallas_call(functools.partial(middle_kernel, depth), grid=(depth,), in...  63.2 us
    pallas_call x1, Pallas kernels, through(): pl.pallas_call(functools.partial(through_kernel, depth), grid=(pairs,), i...  51.5 us
    pallas_call x1, Pallas kernels, enter(): pl.pallas_call(functools.partial(enter_kernel, depth), in_specs=[anywhere...  40.8 us
  transfers between devices with their start and end apart: 1, of which 0 were waited for; matrix products, arithmetic and copies ran while one was open for 1% of the time, Pallas kernels for 14%

profile of v6, /device:TPU:0, one launch (start us, length us, event | category | flops | bytes accessed | tf_op | source)
XLA Modules:
  0.0 294.2 jit_solution(7647357606811993105)
XLA Ops:
  0.6 0.0 copy-start
  0.7 0.5 collective-permute-start
  1.2 0.2 copy-done
  1.3 1.0 fusion
  2.3 0.6 broadcast_in_dim.12.near_ref
  3.0 0.0 copy-start.4
  3.0 40.8 %enter.1 = (bf16[1024,1024]{1,0:T(8,128)(2,1)}, bf16[1024,512]{1,0:T(8,128)(2,1)}, bf16[1024,512]{1,0:T(8,128)(2,1)}, bf16[1024,512]{1,0:T(8,128)(2,1)}, bf16[2,...) custom-call(bf16[2,256,1024]{2,1,0:T(8,128)(2,1)} %inputs_ref.1, ...), custom_call_target="tpu_custom_call" | custom-call | flops 3221225472 | bytes 16777216 | tf_op jit(solution)/shard_map/enter/pallas_call | solution.py:541
  43.8 0.0 collective-permute-done
  43.8 0.0 copy-done.4
  43.8 0.1 broadcast_select_fusion
  43.9 0.6 dynamic_slice.10.length_ref
  44.5 51.5 %through.1 = (f32[4,2,1024]{2,1,0:T(2,128)}, bf16[512,512]{1,0:T(8,128)(2,1)}, f32[512,1024]{1,0:T(8,128)}, bf16[512,512]{1,0:T(8,128)(2,1)}, bf16[4,128,1024]{2...) custom-call(s32[1]{0:T(128)} %dynamic_slice.10.length_ref, ...), custom_call_target="tpu_custom_call" | custom-call | flops 12884901888 | bytes 4194304 | tf_op jit(solution)/shard_map/through/pallas_call | solution.py:777
  96.0 63.2 %middle.1 = (bf16[4,2,2,128,1024]{4,3,2,1,0:T(8,128)(2,1)}, bf16[4,2,2,128,1024]{4,3,2,1,0:T(8,128)(2,1)}, bf16[4,2,128,1024]{3,2,1,0:T(8,128)(2,1)}, bf16[4,2,1...) custom-call(s32[1]{0:T(128)} %dynamic_slice.10.length_ref, ...), custom_call_target="tpu_custom_call" | custom-call | flops 27917287424 | bytes 29360128 | tf_op jit(solution)/shard_map/middle/pallas_call | solution.py:1091
  159.2 125.5 %backward.1 = (bf16[2,256,1024]{2,1,0:T(8,128)(2,1)}, bf16[2,256,1024]{2,1,0:T(8,128)(2,1)}, f32[4,32,1024]{2,1,0:T(8,128)}, f32[2,128,1024]{2,1,0:T(8,128)}, f32[2,128]{1,0:T(2,128)}, /*index=5*/f32[2,32,128]{2,1,0:T(8,128)}) custom-call(s32[1]{0:T(128)} %dynamic_slice.10.length_ref, bf16[1024,512]{1,0:T(8,128)(2,1)} %get-tuple-element.44.query_ref, ...), custom_call_target="tpu_custom_call" | custom-call | flops 32212254720 | bytes 7340032 | tf_op jit(solution)/shard_map/backward/pallas_call | solution.py:1612
  284.7 0.0 copy-start.1
  284.7 1.2 slice_bitcast_fusion.6
  285.9 0.8 reshape.73
  286.7 1.9 slice_bitcast_fusion.2
  288.6 2.3 slice_bitcast_fusion
  290.9 0.0 copy-start.3
  290.9 0.0 copy-start.2
  290.9 0.0 copy-done.1
  290.9 1.6 convert_element_type.3
  292.5 0.0 copy-done.3
  292.5 0.2 fusion.1
  292.7 0.6 dynamic-slice_bitcast_fusion
  293.3 0.0 copy-done.2
  293.3 1.0 copy.29
  (3 shorter events, 0.0 us)
Async XLA Ops:
  0.6 0.7 copy-start
  0.7 43.1 %collective-permute-start = (s32[2]{0:T(128)}, s32[2]{0:T(128)S(1)}, u32[]{:S(2)}, u32[]{:S(2)}) collective-permute-start(s32[2]{0:T(128)} %param.15), channel_id=1, source_target_pairs={{0,1},{1,0},{2,3},{3,2},{4,5},{5,4},{6,7},{7,6},{8,9},{9,8},{10,11... | collective-permute-start | bytes 32 | tf_op jit(solution)/shard_map/ppermute | solution.py:1667
  3.0 40.8 %copy-start.4 = (s32[2]{0:T(128)S(1)}, s32[2]{0:T(128)}, u32[]{:S(2)}) copy-start(s32[2]{0:T(128)} %param.15) | copy-start | bytes 28
  284.7 6.2 %copy-start.1 = (bf16[2,256,1024]{2,1,0:T(8,128)(2,1)S(1)}, bf16[2,256,1024]{2,1,0:T(8,128)(2,1)}, u32[]{:S(2)}) copy-start(bf16[2,256,1024]{2,1,0:T(8,128)(2,1)} %get-tuple-element.72) | copy-start | bytes 3145732
  290.9 1.6 copy-start.3
  290.9 2.4 copy-start.2

commit v7 on v6

--- a/solution.py
+++ b/solution.py
@@ -846,8 +846,8 @@
 def middle_kernel(
     depth,
     length_ref,
-    normed_ref,
-    grad_ref,
+    normed_in_ref,
+    grad_in_ref,
     hidden_in_ref,
     gain_ref,
     output_in_ref,
@@ -869,6 +869,8 @@
     layer_ref,
     gain_part_ref,
     output_part_ref,
+    normed_ref,
+    grad_ref,
     hidden_ref,
     output_ref,
     far_output_ref,
@@ -972,10 +974,16 @@
         for one in moves:
             one.start()
         fetch(0, 0)
-        for one in later:
+        soon = [
+            pltpu.make_async_copy(one, there, later_sems.at[5 + number])
+            for number, (one, there) in enumerate(((normed_in_ref, normed_ref), (grad_in_ref, grad_ref)))
+        ]
+        for one in soon + later:
             one.start()
         out_total[...] = jnp.zeros_like(out_total)
         back_total[...] = jnp.zeros_like(back_total)
+        for one in soon:
+            one.wait()
 
     @pl.when(step + 1 < last)
     def _():
@@ -1091,7 +1099,7 @@
     return pl.pallas_call(
         functools.partial(middle_kernel, depth),
         grid=(depth,),
-        in_specs=[pl.BlockSpec(memory_space=pltpu.SMEM)] + [vmem] * 2 + [anywhere, vmem] + [anywhere] * 8,
+        in_specs=[pl.BlockSpec(memory_space=pltpu.SMEM)] + [anywhere] * 3 + [vmem] + [anywhere] * 8,
         out_specs=[anywhere] * 7 + [vmem] * 4,
         out_shape=[shape(part, LOW)] * 2
         + [shape((depth, 2, thick, width), LOW)] * 2
@@ -1103,7 +1111,7 @@
             shape((1, width), WIDE),
             shape((4, 2, 2, slim, width), LOW),
         ],
-        scratch_shapes=[pltpu.VMEM(one.shape, one.dtype) for one in (hidden, *outputs, *contexts)]
+        scratch_shapes=[pltpu.VMEM(one.shape, one.dtype) for one in (normed, grad, hidden, *outputs, *contexts)]
         + [pltpu.VMEM((rows // 2, inner), LOW)]
         + [pltpu.VMEM((rows, width), WIDE)] * 2
         + [pltpu.VMEM((2, rows // 2, width), LOW)] * 2
@@ -1120,7 +1128,7 @@
             pltpu.SemaphoreType.DMA((2, 2)),
             pltpu.SemaphoreType.DMA((2, 3)),
             pltpu.SemaphoreType.DMA,
-            pltpu.SemaphoreType.DMA((5,)),
+            pltpu.SemaphoreType.DMA((7,)),
         ],
         compiler_params=pltpu.CompilerParams(vmem_limit_bytes=62 << 20, collective_id=2, has_side_effects=True),
         cost_estimate=pl.CostEstimate(
@@ -1139,10 +1147,10 @@
 def backward_kernel(
     depth,
     length_ref,
-    query_ref,
-    key_ref,
-    value_ref,
-    grad_ref,
+    query_in_ref,
+    key_in_ref,
+    value_in_ref,
+    grad_in_ref,
     log_ref,
     near_ref,
     normed_in_ref,
@@ -1163,6 +1171,10 @@
     units_out_ref,
     gains_out_ref,
     sums_out_ref,
+    query_ref,
+    key_ref,
+    value_ref,
+    grad_ref,
     normed_ref,
     weight_ref,
     source_ref,
@@ -1382,9 +1394,23 @@
         )
     ]
 
+    soon = [
+        pltpu.make_async_copy(one, there, later_sems.at[4 + number])
+        for number, (one, there) in enumerate(
+            (
+                (query_in_ref, query_ref),
+                (key_in_ref, key_ref),
+                (value_in_ref, value_ref),
+                (grad_in_ref, grad_ref),
+            )
+        )
+    ]
+
     @pl.when(step == 0)
     def _():
         greet_column(depth)
+        for one in soon:
+            one.start()
         units_start()
         for one in later:
             one.start()
@@ -1393,6 +1419,8 @@
         for piece in range(held):
             row_moves(layer_ref.at[piece], layer_out_ref, layer_sems, depth, piece)
         spare[...] = spare_lanes(length_ref[0], rows)
+        for one in soon:
+            one.wait()
         for head in range(2):
             padded[head, :HALF_ROWS, :] = jnp.zeros((HALF_ROWS, QUERY_ROWS), LOW)
             padded[head, rows + HALF_ROWS :, :] = jnp.zeros((HALF_ROWS, QUERY_ROWS), LOW)
@@ -1612,7 +1640,7 @@
     return pl.pallas_call(
         functools.partial(backward_kernel, depth),
         grid=(depth,),
-        in_specs=[pl.BlockSpec(memory_space=pltpu.SMEM)] + [vmem] * 6 + [anywhere] * 4 + [vmem] * 2 + [anywhere, vmem] + [anywhere] * 4,
+        in_specs=[pl.BlockSpec(memory_space=pltpu.SMEM)] + [anywhere] * 4 + [vmem] * 2 + [anywhere] * 4 + [vmem] * 2 + [anywhere, vmem] + [anywhere] * 4,
         out_specs=[anywhere] * 2 + [vmem] * 4,
         out_shape=[
             shape((held, span, width), LOW),
@@ -1623,6 +1651,10 @@
             shape((2, 8 * depth, LANES), WIDE),
         ],
         scratch_shapes=[
+            pltpu.VMEM(query.shape, LOW),
+            pltpu.VMEM(key.shape, LOW),
+            pltpu.VMEM(value.shape, LOW),
+            pltpu.VMEM(grad.shape, LOW),
             pltpu.VMEM(normed.shape, LOW),
             pltpu.VMEM(weights.shape, LOW),
             pltpu.VMEM(source.shape, LOW),
@@ -1651,7 +1683,7 @@
         + [pltpu.VMEM((held, span, width), LOW)] * 3
         + [pltpu.VMEM((4, small_rows, LANES), WIDE), pltpu.VMEM((depth + 2, small_rows, LANES), WIDE)]
         + [pltpu.SemaphoreType.DMA((2,) + one) for one in sems]
-        + [pltpu.SemaphoreType.DMA((2, depth)), pltpu.SemaphoreType.DMA((3, depth)), pltpu.SemaphoreType.DMA((4,))],
+        + [pltpu.SemaphoreType.DMA((2, depth)), pltpu.SemaphoreType.DMA((3, depth)), pltpu.SemaphoreType.DMA((8,))],
         compiler_params=pltpu.CompilerParams(
             vmem_limit_bytes=62 << 20, collective_id=3, has_side_effects=True
         ),

time: 296 us -> 293 us (0.990)
  Pallas kernels: 281 us -> 278 us
where the time goes in v7:
time: 293 us; the launch traced here: 292 us
  Pallas kernels  278 us (95%)
  local copies, waits for them, and re-layouts  9.16 us (3%)
    pallas_call x1, Pallas kernels, backward(): pl.pallas_call(functools.partial(backward_kernel, depth), grid=(depth,),...  124 us
    pallas_call x1, Pallas kernels, middle(): pl.pallas_call(functools.partial(middle_kernel, depth), grid=(depth,), in...  61.7 us
    pallas_call x1, Pallas kernels, through(): pl.pallas_call(functools.partial(through_kernel, depth), grid=(pairs,), i...  51.5 us
    pallas_call x1, Pallas kernels, enter(): pl.pallas_call(functools.partial(enter_kernel, depth), in_specs=[anywhere...  40.8 us
  transfers between devices with their start and end apart: 1, of which 0 were waited for; matrix products, arithmetic and copies ran while one was open for 1% of the time, Pallas kernels for 14%

profile of v7, /device:TPU:0, one launch (start us, length us, event | category | flops | bytes accessed | tf_op | source)
XLA Modules:
  0.0 291.6 jit_solution(2492549954026321246)
XLA Ops:
  0.6 0.0 copy-start
  0.7 0.5 collective-permute-start
  1.2 0.2 copy-done
  1.3 1.0 fusion
  2.3 0.6 broadcast_in_dim.12.near_ref
  3.0 0.0 copy-start.4
  3.0 40.8 %enter.1 = (bf16[1024,1024]{1,0:T(8,128)(2,1)}, bf16[1024,512]{1,0:T(8,128)(2,1)}, bf16[1024,512]{1,0:T(8,128)(2,1)}, bf16[1024,512]{1,0:T(8,128)(2,1)}, bf16[2,...) custom-call(bf16[2,256,1024]{2,1,0:T(8,128)(2,1)} %inputs_ref.1, ...), custom_call_target="tpu_custom_call" | custom-call | flops 3221225472 | bytes 16777216 | tf_op jit(solution)/shard_map/enter/pallas_call | solution.py:541
  43.8 0.0 collective-permute-done
  43.8 0.0 copy-done.4
  43.8 0.1 broadcast_select_fusion
  43.9 0.6 dynamic_slice.10.length_ref
  44.5 51.5 %through.1 = (f32[4,2,1024]{2,1,0:T(2,128)}, bf16[512,512]{1,0:T(8,128)(2,1)}, f32[512,1024]{1,0:T(8,128)}, bf16[512,512]{1,0:T(8,128)(2,1)}, bf16[4,128,1024]{2...) custom-call(s32[1]{0:T(128)} %dynamic_slice.10.length_ref, ...), custom_call_target="tpu_custom_call" | custom-call | flops 12884901888 | bytes 4194304 | tf_op jit(solution)/shard_map/through/pallas_call | solution.py:777
  96.0 61.7 %middle.1 = (bf16[4,2,2,128,1024]{4,3,2,1,0:T(8,128)(2,1)}, bf16[4,2,2,128,1024]{4,3,2,1,0:T(8,128)(2,1)}, bf16[4,2,128,1024]{3,2,1,0:T(8,128)(2,1)}, bf16[4,2,1...) custom-call(s32[1]{0:T(128)} %dynamic_slice.10.length_ref, ...), custom_call_target="tpu_custom_call" | custom-call | flops 27917287424 | bytes 29360128 | tf_op jit(solution)/shard_map/middle/pallas_call | solution.py:1099
  157.7 124.3 %backward.1 = (bf16[2,256,1024]{2,1,0:T(8,128)(2,1)}, bf16[2,256,1024]{2,1,0:T(8,128)(2,1)}, f32[4,32,1024]{2,1,0:T(8,128)}, f32[2,128,1024]{2,1,0:T(8,128)}, f32[2,128]{1,0:T(2,128)}, /*index=5*/f32[2,32,128]{2,1,0:T(8,128)}) custom-call(s32[1]{0:T(128)} %dynamic_slice.10.length_ref, bf16[1024,512]{1,0:T(8,128)(2,1)} %get-tuple-element.44.query_ref.query_in_ref, ...), custom_call_target="tpu_custom_call" | custom-call | flops 32212254720 | bytes 7340032 | tf_op jit(solution)/shard_map/backward/pallas_call | solution.py:1640
  282.0 0.0 copy-start.1
  282.0 1.2 slice_bitcast_fusion.6
  283.2 0.8 reshape.73
  284.1 1.9 slice_bitcast_fusion.2
  285.9 2.3 slice_bitcast_fusion
  288.2 0.0 copy-start.3
  288.2 0.0 copy-start.2
  288.2 0.0 copy-done.1
  288.2 1.6 convert_element_type.3
  289.8 0.0 copy-done.3
  289.8 0.2 fusion.1
  290.0 0.6 dynamic-slice_bitcast_fusion
  290.6 0.0 copy-done.2
  290.6 1.0 copy.29
  (3 shorter events, 0.0 us)
Async XLA Ops:
  0.6 0.7 copy-start
  0.7 43.1 %collective-permute-start = (s32[2]{0:T(128)}, s32[2]{0:T(128)S(1)}, u32[]{:S(2)}, u32[]{:S(2)}) collective-permute-start(s32[2]{0:T(128)} %param.15), channel_id=1, source_target_pairs={{0,1},{1,0},{2,3},{3,2},{4,5},{5,4},{6,7},{7,6},{8,9},{9,8},{10,11... | collective-permute-start | bytes 32 | tf_op jit(solution)/shard_map/ppermute | solution.py:1699
  3.0 40.8 %copy-start.4 = (s32[2]{0:T(128)S(1)}, s32[2]{0:T(128)}, u32[]{:S(2)}) copy-start(s32[2]{0:T(128)} %param.15) | copy-start | bytes 28
  282.0 6.2 %copy-start.1 = (bf16[2,256,1024]{2,1,0:T(8,128)(2,1)S(1)}, bf16[2,256,1024]{2,1,0:T(8,128)(2,1)}, u32[]{:S(2)}) copy-start(bf16[2,256,1024]{2,1,0:T(8,128)(2,1)} %get-tuple-element.72) | copy-start | bytes 3145732
  288.2 1.6 copy-start.3
  288.2 2.4 copy-start.2
